TPU v7x, 32 devices: a whole 2x2x4 slice. The times are simulated.
32 devices in a mesh: dp: 8 (over y, x, core), ctx: 4 (over z).
Axes of the slice: x: 2, y: 2, z: 4, core: 2. Of those that a mesh axis runs over, the one named last changes fastest.
Arguments:
- hidden_in: float32 [8, 512, 768], P('dp', 'ctx'), may hold values from -6 to 6
- segments: int32 [8, 512], P('dp'), may hold values from 0 to 2, as said below
- out_grad: float32 [8, 512, 768], P('dp', 'ctx'), may hold values from -6 to 6
- weights: float32 [2, 3, 768, 3072], P(None, None, 'dp', 'ctx')
- vectors: float32 [2, 12, 768], P(None, 'ctx', 'dp')
- mat_momentum: float32 [2, 3, 768, 3072], P(None, None, 'dp', 'ctx'), may hold values from -192 to 192
- vec_first: float32 [2, 12, 768], P(None, 'ctx', 'dp'), may hold values from -40 to 40
- vec_second: float32 [2, 12, 768], P(None, 'ctx', 'dp'), may hold values from 2.048 to 16.384
Outputs:
- hidden_out: float32 [8, 512, 768], P('dp', 'ctx')
- input_grad: float32 [8, 512, 768], P('dp', 'ctx')
- mat_grad: float32 [2, 3, 768, 3072], P(None, None, 'dp', 'ctx')
- mat_momentum_new: float32 [2, 3, 768, 3072], P(None, None, 'dp', 'ctx')
- weights_new: float32 [2, 3, 768, 3072], P(None, None, 'dp', 'ctx')
- vec_grad: float32 [2, 12, 768], P(None, 'ctx', 'dp')
- vec_second_new: float32 [2, 12, 768], P(None, 'ctx', 'dp')
- vectors_new: float32 [2, 12, 768], P(None, 'ctx', 'dp')
Inputs may be any that keep to these rules, and one draw needn't show every extreme that they name: `segments`: each row is nondecreasing and holds three documents 0, 1, 2; documents 0 and 2 each have 1 to 64 tokens, document 1 the rest.
All inputs are finite; a program needn't handle non-finite values.
Results may differ from a plain program's by a relative error of at most 0.014.
Values may be sent and summed in bfloat16 or wider, within the bound.
No kernel may reach another device: no remote copies, remote signals or barrier semaphores. Data moves between devices by JAX's collectives and lax.ppermute only.
A program may use at most 192 MiB of HBM per device.

v0:
```python
import math

import jax
import jax.numpy as jnp
from jax import lax
from jax.sharding import PartitionSpec as P

D = 768
HEADS = 12
HEAD = 64
FF = 3072
LAYERS = 2
NS_ITERS = 2
ADAM_STEP = 10


norm_epsilon = 1e-05
quintic_one = 3.4445
quintic_two = -4.775
quintic_three = 2.0315
momentum_decay = 0.95
matrix_rate = 0.6
matrix_decay = 0.01
first_decay = 0.9
second_decay = 0.999
vector_rate = 0.5
vector_decay = 0.01
adam_epsilon = 1e-08
masked_score = -1e30


def layer_norm(hidden, gain_vec, bias_vec):
    center = hidden - jnp.mean(hidden, axis=-1, keepdims=True)
    variance = jnp.mean(center * center, axis=-1, keepdims=True)
    return center * lax.rsqrt(variance + norm_epsilon) * gain_vec + bias_vec


def smooth_unit(preact):
    return jax.nn.gelu(preact, approximate=True)


def dot_plain(operand, other):
    return jnp.dot(operand, other, preferred_element_type=jnp.float32)


def dot_tokens(operand, other):
    return lax.dot_general(
        operand, other, (((0,), (0,)), ((), ())), preferred_element_type=jnp.float32
    )


def dot_trans(operand, other):
    return lax.dot_general(
        operand, other, (((1,), (1,)), ((), ())), preferred_element_type=jnp.float32
    )


def split_heads(matrix):
    return matrix.reshape(matrix.shape[0], HEADS, HEAD)


def masked_scores(query_heads, key_heads, allowed):
    scores = jnp.einsum(
        "qhd,khd->hqk", query_heads, key_heads, preferred_element_type=jnp.float32
    ) * HEAD ** (-0.5)
    return jnp.where(allowed[None], scores, masked_score)


def local(hidden_in, segments, out_grad, weights, vectors, mat_momentum, vec_first, vec_second):
    tokens_dev = hidden_in.shape[1]
    seq_len = segments.shape[1]
    ctx_size = lax.axis_size("ctx")
    ctx_index = lax.axis_index("ctx")
    query_pos = ctx_index * tokens_dev + jnp.arange(tokens_dev)
    segment_all = segments[0]
    segment_query = lax.dynamic_slice_in_dim(segment_all, ctx_index * tokens_dev, tokens_dev)
    allowed = (jnp.arange(seq_len)[None, :] <= query_pos[:, None]) & (
        segment_all[None, :] == segment_query[:, None]
    )
    dp_rows = weights.shape[2]
    col_width = weights.shape[3]
    hidden = hidden_in[0]
    stored = []
    for layer_index in range(LAYERS):
        local_mats = weights[layer_index].astype(jnp.bfloat16)
        local_vecs = vectors[layer_index].astype(jnp.bfloat16)
        part_mats, part_vecs = (
            lax.all_gather(local_mats, "ctx", axis=2, tiled=True),
            lax.all_gather(local_vecs, "ctx", axis=0, tiled=True),
        )
        weight_pack, vector_low = (
            lax.all_gather(part_mats, "dp", axis=1, tiled=True),
            lax.all_gather(part_vecs, "dp", axis=1, tiled=True),
        )
        vector_rows = vector_low.astype(jnp.float32)
        normed_low = layer_norm(hidden, vector_rows[0], vector_rows[1]).astype(jnp.bfloat16)
        projected = dot_plain(normed_low, weight_pack[0][:, 0 : 3 * D])
        queries = (projected[:, 0:D] + vector_rows[4]).astype(jnp.bfloat16)
        keys_local = projected[:, D : 2 * D].astype(jnp.bfloat16)
        values_local = (projected[:, 2 * D : 3 * D] + vector_rows[5]).astype(jnp.bfloat16)
        keys_all, values_all = (
            lax.all_gather(keys_local, "ctx", axis=0, tiled=True),
            lax.all_gather(values_local, "ctx", axis=0, tiled=True),
        )
        masked = masked_scores(split_heads(queries), split_heads(keys_all), allowed)
        row_max = jnp.max(masked, axis=-1, keepdims=True)
        unnormed = jnp.exp(masked - row_max)
        row_total = jnp.sum(unnormed, axis=-1, keepdims=True)
        prob_low = (unnormed / row_total).astype(jnp.bfloat16)
        log_total = row_max + jnp.log(row_total)
        attended_low = (
            jnp.einsum(
                "hqk,khd->qhd",
                prob_low,
                split_heads(values_all),
                preferred_element_type=jnp.float32,
            )
            .reshape(tokens_dev, D)
            .astype(jnp.bfloat16)
        )
        middle = hidden + (
            dot_plain(attended_low, weight_pack[0][:, 3 * D : 4 * D]) + vector_rows[6]
        )
        normed_two_low = layer_norm(middle, vector_rows[2], vector_rows[3]).astype(jnp.bfloat16)
        preact = dot_plain(normed_two_low, weight_pack[1]) + vector_rows[8:12].reshape(-1)
        activated_low = smooth_unit(preact).astype(jnp.bfloat16)
        stored.append(
            (
                hidden,
                middle,
                normed_low,
                queries,
                log_total,
                attended_low,
                normed_two_low,
                preact,
                activated_low,
                weight_pack,
                vector_rows,
                keys_all,
                values_all,
            )
        )
        hidden = middle + (dot_trans(activated_low, weight_pack[2]) + vector_rows[7])
    grad_hidden = out_grad[0]
    grad_mat_list = [None] * LAYERS
    grad_vec_list = [None] * LAYERS
    for layer_index in reversed(range(LAYERS)):
        (
            layer_in,
            middle,
            normed_low,
            queries,
            log_total,
            attended_low,
            normed_two_low,
            preact,
            activated_low,
            weight_pack,
            vector_rows,
            keys_all,
            values_all,
        ) = stored[layer_index]
        local_mats = weights[layer_index].astype(jnp.bfloat16)
        local_vecs = vectors[layer_index].astype(jnp.bfloat16)
        part_mats, part_vecs = (
            lax.all_gather(local_mats, "ctx", axis=2, tiled=True),
            lax.all_gather(local_vecs, "ctx", axis=0, tiled=True),
        )
        weight_pack, vector_low = (
            lax.all_gather(part_mats, "dp", axis=1, tiled=True),
            lax.all_gather(part_vecs, "dp", axis=1, tiled=True),
        )
        vector_rows = vector_low.astype(jnp.float32)
        query_heads = split_heads(queries)
        key_heads = split_heads(keys_all)
        value_heads = split_heads(values_all)
        grad_two = grad_hidden.astype(jnp.bfloat16)
        grad_act = dot_plain(grad_two, weight_pack[2])
        unused, gelu_pull = jax.vjp(smooth_unit, preact)
        grad_pre_low = gelu_pull(grad_act)[0].astype(jnp.bfloat16)
        grad_normed_two = dot_trans(grad_pre_low, weight_pack[1])
        unused, norm_pull_two = jax.vjp(layer_norm, middle, vector_rows[2], vector_rows[3])
        grad_mid, grad_gain_two, grad_shift_two = norm_pull_two(grad_normed_two)
        grad_middle = grad_hidden + grad_mid
        grad_one = grad_middle.astype(jnp.bfloat16)
        grad_att_heads = split_heads(
            dot_trans(grad_one, weight_pack[0][:, 3 * D : 4 * D]).astype(jnp.bfloat16)
        )
        masked = masked_scores(query_heads, key_heads, allowed)
        probability = jnp.exp(masked - log_total)
        prob_low = probability.astype(jnp.bfloat16)
        grad_prob = jnp.einsum(
            "qhd,khd->hqk", grad_att_heads, value_heads, preferred_element_type=jnp.float32
        )
        row_dot = jnp.sum(grad_prob * probability, axis=-1, keepdims=True)
        grad_scores_low = (probability * (grad_prob - row_dot)).astype(jnp.bfloat16)
        grad_query_low = (
            (
                jnp.einsum(
                    "hqk,khd->qhd", grad_scores_low, key_heads, preferred_element_type=jnp.float32
                )
                * HEAD ** (-0.5)
            )
            .reshape(tokens_dev, D)
            .astype(jnp.bfloat16)
        )

        def key_terms(
            offset,
            length,
            grad_scores_low=grad_scores_low,
            prob_low=prob_low,
            query_heads=query_heads,
            grad_att_heads=grad_att_heads,
        ):
            grad_keys = jnp.einsum(
                "hqk,qhd->khd", grad_scores_low, query_heads, preferred_element_type=jnp.float32
            ) * HEAD ** (-0.5)
            grad_values = jnp.einsum(
                "hqk,qhd->khd", prob_low, grad_att_heads, preferred_element_type=jnp.float32
            )
            return jnp.concatenate(
                [grad_keys.reshape(length, D), grad_values.reshape(length, D)], axis=1
            )

        summed = lax.psum_scatter(
            key_terms(jnp.int32(0), tokens_dev * lax.axis_size("ctx")),
            "ctx",
            scatter_dimension=0,
            tiled=True,
        )
        grad_keys_low = summed[:, 0:D].astype(jnp.bfloat16)
        grad_values_low = summed[:, D : 2 * D].astype(jnp.bfloat16)
        grad_qkv_low = jnp.concatenate([grad_query_low, grad_keys_low, grad_values_low], axis=1)
        grad_normed = dot_trans(grad_qkv_low, weight_pack[0][:, 0 : 3 * D])
        unused, norm_pull_one = jax.vjp(layer_norm, layer_in, vector_rows[0], vector_rows[1])
        grad_in, grad_gain_one, grad_shift_one = norm_pull_one(grad_normed)
        grad_hidden = grad_middle + grad_in
        bias_grads = jnp.stack(
            [
                grad_gain_one,
                grad_shift_one,
                grad_gain_two,
                grad_shift_two,
                jnp.sum(grad_query_low, axis=0, dtype=jnp.float32),
                jnp.sum(grad_values_low, axis=0, dtype=jnp.float32),
                jnp.sum(grad_one, axis=0, dtype=jnp.float32),
                jnp.sum(grad_two, axis=0, dtype=jnp.float32),
            ]
        )
        vec_term = jnp.concatenate(
            [bias_grads, jnp.sum(grad_pre_low, axis=0, dtype=jnp.float32).reshape(4, D)], axis=0
        )
        vec_share = lax.psum_scatter(vec_term, "ctx", scatter_dimension=0, tiled=True)
        vec_pad = jnp.concatenate(
            [vec_share.T, jnp.zeros((D, 128 - vec_share.shape[0]), jnp.float32)], axis=1
        )
        normed_all, attended_all, normed_two_all, grad_two_all = (
            lax.all_gather(normed_low, "ctx", axis=0, tiled=True),
            lax.all_gather(attended_low, "ctx", axis=0, tiled=True),
            lax.all_gather(normed_two_low, "ctx", axis=0, tiled=True),
            lax.all_gather(grad_two, "ctx", axis=0, tiled=True),
        )
        grad_stack = jnp.stack([grad_query_low, grad_keys_low, grad_values_low, grad_one], axis=1)
        grad_mine, pre_mine, act_mine = (
            lax.all_to_all(grad_stack, "ctx", split_axis=1, concat_axis=0, tiled=True),
            lax.all_to_all(
                grad_pre_low.reshape(tokens_dev, ctx_size, -1),
                "ctx",
                split_axis=1,
                concat_axis=0,
                tiled=True,
            ),
            lax.all_to_all(
                activated_low.reshape(tokens_dev, ctx_size, -1),
                "ctx",
                split_axis=1,
                concat_axis=0,
                tiled=True,
            ),
        )
        grad_mine = grad_mine[:, 0]
        pre_mine = pre_mine[:, 0]
        act_mine = act_mine[:, 0]
        left_attn = jnp.where(ctx_index == ctx_size - 1, attended_all, normed_all)

        def grad_terms(
            start,
            count,
            left_attn=left_attn,
            grad_mine=grad_mine,
            normed_two_all=normed_two_all,
            pre_mine=pre_mine,
            grad_two_all=grad_two_all,
            act_mine=act_mine,
            vec_pad=vec_pad,
        ):
            blocks = [
                dot_tokens(left_attn, grad_mine),
                dot_tokens(normed_two_all, pre_mine),
                dot_tokens(grad_two_all, act_mine),
                vec_pad,
            ]
            return jnp.concatenate(blocks, axis=1)

        reduced = lax.psum_scatter(
            grad_terms(jnp.int32(0), dp_rows * lax.axis_size("dp")),
            "dp",
            scatter_dimension=0,
            tiled=True,
        )
        grad_mat_list[layer_index] = (
            reduced[:, 0 : 3 * col_width].reshape(dp_rows, 3, col_width).transpose(1, 0, 2)
        )
        grad_vec_list[layer_index] = reduced[
            :, 3 * col_width : 3 * col_width + vec_share.shape[0]
        ].T
    grad_mats = jnp.stack(grad_mat_list)
    grad_vecs = jnp.stack(grad_vec_list)
    moment_new = momentum_decay * mat_momentum + grad_mats
    update_in = grad_mats + momentum_decay * moment_new
    item_count = 3 * LAYERS
    rows_dev = update_in.shape[2]
    cols_dev = update_in.shape[3]
    item_stack = update_in.astype(jnp.bfloat16).reshape(item_count, rows_dev, cols_dev)
    dp_size = lax.axis_size("dp")
    copies = -(-dp_size // item_count)
    slot_items = jnp.tile(item_stack, (copies, 1, 1))[0:dp_size]
    received = lax.all_to_all(slot_items[:, None], "dp", split_axis=0, concat_axis=1, tiled=True)
    current = received.reshape(dp_size * rows_dev, cols_dev)
    dp_index = lax.axis_index("dp")
    item_index = dp_index % item_count
    square = item_index % 3 == 0
    for iteration in range(NS_ITERS):
        gram_local = dot_trans(current, current)
        gram_part = lax.psum_scatter(
            gram_local.astype(jnp.bfloat16), "ctx", scatter_dimension=0, tiled=True
        ).astype(jnp.float32)
        gram_total = lax.all_gather(
            gram_part.astype(jnp.bfloat16), "ctx", axis=0, tiled=True
        ).astype(gram_part.dtype)
        gram_matrix = jnp.where(square, gram_local, gram_total)
        if iteration == 0:
            norm_scale = 1.0 / (jnp.sqrt(jnp.trace(gram_matrix)) + 1e-07)
        else:
            norm_scale = 1.0
        poly_base = gram_matrix * (norm_scale * norm_scale)
        base_low = poly_base.astype(jnp.bfloat16)
        bmat_low = (quintic_two * poly_base + quintic_three * dot_plain(base_low, base_low)).astype(
            jnp.bfloat16
        )
        current = (
            norm_scale * (quintic_one * current.astype(jnp.float32) + dot_plain(bmat_low, current))
        ).astype(jnp.bfloat16)
    returned = lax.all_to_all(
        current.reshape(dp_size, 1, rows_dev, cols_dev),
        "dp",
        split_axis=0,
        concat_axis=1,
        tiled=True,
    )[0]
    spread = dp_size // item_count
    chosen = [
        lax.dynamic_index_in_dim(
            returned, item_number + item_count * (dp_index % spread), 0, keepdims=False
        )
        for item_number in range(item_count)
    ]
    ortho_all = jnp.stack(chosen).reshape(LAYERS, 3, rows_dev, cols_dev).astype(jnp.float32)
    factor = jnp.array([0.2 * math.sqrt(D), 0.2 * math.sqrt(FF), 0.2 * math.sqrt(FF)], jnp.float32)
    weights_new = weights * (1.0 - matrix_rate * matrix_decay) - matrix_rate * (
        ortho_all * factor[None, :, None, None]
    )
    first_new = first_decay * vec_first + (1.0 - first_decay) * grad_vecs
    second_new = second_decay * vec_second + (1.0 - second_decay) * grad_vecs * grad_vecs
    first_hat = first_new / (1.0 - first_decay**ADAM_STEP)
    second_hat = second_new / (1.0 - second_decay**ADAM_STEP)
    vectors_new = vectors * (1.0 - vector_rate * vector_decay) - vector_rate * first_hat / (
        jnp.sqrt(second_hat) + adam_epsilon
    )
    return (
        hidden[None],
        grad_hidden[None],
        grad_mats,
        moment_new,
        weights_new,
        grad_vecs,
        second_new,
        vectors_new,
    )


def solution(mesh):
    placed = (
        P("dp", "ctx", None),
        P("dp", None),
        P("dp", "ctx", None),
        P(None, None, "dp", "ctx"),
        P(None, "ctx", "dp"),
        P(None, None, "dp", "ctx"),
        P(None, "ctx", "dp"),
        P(None, "ctx", "dp"),
    )
    return jax.shard_map(
        local,
        mesh=mesh,
        in_specs=placed,
        out_specs=(
            P("dp", "ctx", None),
            P("dp", "ctx", None),
            P(None, None, "dp", "ctx"),
            P(None, None, "dp", "ctx"),
            P(None, None, "dp", "ctx"),
            P(None, "ctx", "dp"),
            P(None, "ctx", "dp"),
            P(None, "ctx", "dp"),
        ),
        check_vma=False,
    )
```

profile of v0, /device:TPU:0, one launch (start us, length us, event | category | flops | bytes accessed | tf_op | source)
XLA Modules:
  0.0 1143.8 jit_solution(3748208447592010903)
XLA Ops:
  10.6 42.6 %all-gather.19.cloned.1.call-done = bf16[1,3,96,3072]{3,2,1,0:T(8,128)(2,1)} async-done(((bf16[1,3,96,768]{3,2,1,0:T(8,128)(2,1)}), bf16[1,3,96,3072]{3,2,1,0:T(8,128)(2,1)}) %all-gather.19.cloned.1.call-update) | async-done | bytes 1769488 | tf_op jit(solution)/shard_map/all_gather | solution.py:88
  53.3 41.3 %all-gather.23.cloned.1.call-done = bf16[1,3,96,3072]{3,2,1,0:T(8,128)(2,1)} async-done(((bf16[1,3,96,768]{3,2,1,0:T(8,128)(2,1)}), bf16[1,3,96,3072]{3,2,1,0:T(8,128)(2,1)}) %all-gather.23.cloned.1.call-update) | async-done | bytes 1769488 | tf_op jit(solution)/shard_map/all_gather | solution.py:88
  147.4 19.9 %slice_reduce_fusion.8 = (f32[768]{0:T(1024)}, f32[768]{0:T(1024)}, f32[768]{0:T(1024)S(1)}, f32[768]{0:T(1024)}, f32[768]{0:T(1024)S(1)}, /*index=5*/f32[768]{0:T(1024)S(1)}, f32[768]{0:T(1024)S(1)}, f32[768]{0:T(1024)S(1)}) fusion(f32[1,12,768]{1,0,2:T(1,128)S(1)} %convert_element_type.328), kind=kLoop, calls=%fused_computation.149 | loop fusion | bytes 49152 | tf_op jit(solution)/shard_map/slice | solution.py:144
  167.4 20.0 %slice_reduce_fusion = (f32[768]{0:T(1024)}, f32[768]{0:T(1024)}, f32[768]{0:T(1024)}, f32[768]{0:T(1024)}, f32[768]{0:T(1024)}, /*index=5*/f32[768]{0:T(1024)}, f32[768]{0:T(1024)}, f32[768]{0:T(1024)S(1)}) fusion(f32[1,12,768]{1,0,2:T(1,128)S(1)} %convert_element_type.329), kind=kLoop, calls=%fused_computation.136 | loop fusion | bytes 49152 | tf_op jit(solution)/shard_map/slice | solution.py:144
  192.8 17.8 %all_gather.78 = bf16[512,768]{1,0:T(8,128)(2,1)S(1)} all-gather(bf16[128,768]{1,0:T(8,128)(2,1)S(1)} %get-tuple-element.92), channel_id=1, replica_groups=mesh['dp'=8,'ctx'=4] {'ctx'}, dimensions={0}, use_global_device_ids=true | all-gather | bytes 983040 | tf_op jit(solution)/shard_map/all_gather | solution.py:103
  212.5 18.0 %all_gather.79 = bf16[512,768]{1,0:T(8,128)(2,1)S(1)} all-gather(bf16[128,768]{1,0:T(8,128)(2,1)S(1)} %slice.392), channel_id=1, replica_groups=mesh['dp'=8,'ctx'=4] {'ctx'}, dimensions={0}, use_global_device_ids=true | all-gather | bytes 983040 | tf_op jit(solution)/shard_map/all_gather | solution.py:102
  263.2 19.9 %all_gather.84 = bf16[512,768]{1,0:T(8,128)(2,1)} all-gather(bf16[128,768]{1,0:T(8,128)(2,1)S(1)} %get-tuple-element.90), channel_id=1, replica_groups=mesh['dp'=8,'ctx'=4] {'ctx'}, dimensions={0}, use_global_device_ids=true | all-gather | bytes 983040 | tf_op jit(solution)/shard_map/all_gather | solution.py:103
  287.2 18.8 %all_gather.85 = bf16[512,768]{1,0:T(8,128)(2,1)} all-gather(bf16[128,768]{1,0:T(8,128)(2,1)} %slice.391), channel_id=1, replica_groups=mesh['dp'=8,'ctx'=4] {'ctx'}, dimensions={0}, use_global_device_ids=true | all-gather | bytes 983040 | tf_op jit(solution)/shard_map/all_gather | solution.py:102
  364.1 53.0 %reduce-scatter.11.cloned.1.call-done = f32[128,1536]{1,0:T(8,128)} async-done(((f32[512,1536]{1,0:T(8,128)}), f32[128,1536]{1,0:T(8,128)}) %reduce-scatter.11.cloned.1.call-update) | async-done | bytes 786448 | tf_op jit(solution)/shard_map/reduce_scatter | solution.py:227
  469.7 59.9 %all_gather.91 = bf16[512,768]{1,0:T(8,128)(2,1)} all-gather(bf16[128,768]{1,0:T(8,128)(2,1)S(1)} %copy-done.41), channel_id=1, replica_groups=mesh['dp'=8,'ctx'=4] {'ctx'}, dimensions={0}, use_global_device_ids=true | all-gather | bytes 983040 | tf_op jit(solution)/shard_map/all_gather | solution.py:260
  533.3 43.1 %all_gather.92 = bf16[512,768]{1,0:T(8,128)(2,1)S(1)} all-gather(bf16[128,768]{1,0:T(8,128)(2,1)S(1)} %copy-done.65), channel_id=1, replica_groups=mesh['dp'=8,'ctx'=4] {'ctx'}, dimensions={0}, use_global_device_ids=true | all-gather | bytes 983040 | tf_op jit(solution)/shard_map/all_gather | solution.py:262
  576.4 19.2 %all_gather.90 = bf16[512,768]{1,0:T(8,128)(2,1)} all-gather(bf16[128,768]{1,0:T(8,128)(2,1)S(1)} %copy.147), channel_id=1, replica_groups=mesh['dp'=8,'ctx'=4] {'ctx'}, dimensions={0}, use_global_device_ids=true | all-gather | bytes 983040 | tf_op jit(solution)/shard_map/all_gather | solution.py:261
  654.5 32.0 %all-reduce.5.cloned.1.call-done = (f32[12,768]{1,0:T(8,128)}, f32[12,768]{1,0:T(8,128)}) async-done(((f32[12,768]{1,0:T(8,128)}, f32[12,768]{1,0:T(8,128)}), (f32[12,768]{1,0:T(8,128)}, f32[12,768]{1,0:T(8,128)})) %all-reduce.5.cloned.1.call-update) | async-done | bytes 73744
  687.3 18.7 %concatenate.31 = f32[768,2432]{0,1:T(8,128)} concatenate(f32[768,768]{0,1:T(8,128)} %fusion.68, f32[768,768]{0,1:T(8,128)S(1)} %fusion.127, f32[768,768]{0,1:T(8,128)} %convolution_bitcast_fusion, f32[768,3]{0,1:T(4,128)S(1)} %dynamic-slice_bitcast_fusion, f32[768,125]{0,1:T(8,128)S(1)} %broadcast.241), dimensions={1} | concatenate | bytes 14942208 | tf_op jit(solution)/shard_map/concatenate | solution.py:305
  742.1 33.2 %all_gather.87 = bf16[512,768]{1,0:T(8,128)(2,1)} all-gather(bf16[128,768]{1,0:T(8,128)(2,1)S(1)} %copy-done.39), channel_id=1, replica_groups=mesh['dp'=8,'ctx'=4] {'ctx'}, dimensions={0}, use_global_device_ids=true | all-gather | bytes 983040 | tf_op jit(solution)/shard_map/all_gather | solution.py:260
  776.2 17.9 %all_gather.88 = bf16[512,768]{1,0:T(8,128)(2,1)S(1)} all-gather(bf16[128,768]{1,0:T(8,128)(2,1)} %copy-done.63), channel_id=1, replica_groups=mesh['dp'=8,'ctx'=4] {'ctx'}, dimensions={0}, use_global_device_ids=true | all-gather | bytes 983040 | tf_op jit(solution)/shard_map/all_gather | solution.py:262
  800.3 30.8 %all_gather.86 = bf16[512,768]{1,0:T(8,128)(2,1)} all-gather(bf16[128,768]{1,0:T(8,128)(2,1)S(1)} %copy-done.62), channel_id=1, replica_groups=mesh['dp'=8,'ctx'=4] {'ctx'}, dimensions={0}, use_global_device_ids=true | all-gather | bytes 983040 | tf_op jit(solution)/shard_map/all_gather | solution.py:261
  855.6 18.6 %concatenate.29 = f32[768,2432]{0,1:T(8,128)} concatenate(f32[768,768]{0,1:T(8,128)} %fusion.70, f32[768,768]{0,1:T(8,128)} %fusion.125, f32[768,768]{0,1:T(8,128)S(1)} %fusion.126, f32[768,3]{0,1:T(4,128)S(1)} %dynamic-slice_bitcast_fusion.1, f32[768,125]{0,1:T(8,128)S(1)} %broadcast.241), dimensions={1} | concatenate | bytes 14942208 | tf_op jit(solution)/shard_map/concatenate | solution.py:305
  884.8 66.8 %reduce-scatter.19.cloned.1.call-done = f32[96,2432]{1,0:T(8,128)} async-done(((f32[768,2432]{1,0:T(8,128)}), f32[96,2432]{1,0:T(8,128)}) %reduce-scatter.19.cloned.1.call-update) | async-done | bytes 933904
  957.4 19.3 %all_to_all.108 = bf16[8,1,96,768]{3,2,1,0:T(8,128)(2,1)S(1)} all-to-all(bf16[8,1,96,768]{3,2,1,0:T(8,128)(2,1)S(1)} %slice_bitcast_fusion.32), channel_id=1, replica_groups=mesh['dp'=8,'ctx'=4] {'dp'}, dimensions={0} | all-to-all | bytes 2359296 | tf_op jit(solution)/shard_map/all_to_all | solution.py:330
  978.9 28.4 %reduce-scatter.15.cloned.1.call-done = bf16[192,768]{1,0:T(8,128)(2,1)} async-done(((bf16[768,768]{1,0:T(8,128)(2,1)}), bf16[192,768]{1,0:T(8,128)(2,1)}) %reduce-scatter.15.cloned.1.call-update) | async-done | bytes 294928 | tf_op jit(solution)/shard_map/reduce_scatter | solution.py:337
  1007.6 30.5 %all-gather.15.cloned.1.call-done = bf16[768,768]{1,0:T(8,128)(2,1)} async-done(((bf16[192,768]{1,0:T(8,128)(2,1)}), bf16[768,768]{1,0:T(8,128)(2,1)}) %all-gather.15.cloned.1.call-update) | async-done | bytes 1179664 | tf_op jit(solution)/shard_map/all_gather | solution.py:340
  1050.1 28.4 %reduce-scatter.17.cloned.1.call-done = bf16[192,768]{1,0:T(8,128)(2,1)} async-done(((bf16[768,768]{1,0:T(8,128)(2,1)}), bf16[192,768]{1,0:T(8,128)(2,1)}) %reduce-scatter.17.cloned.1.call-update) | async-done | bytes 294928 | tf_op jit(solution)/shard_map/reduce_scatter | solution.py:337
  1078.6 30.8 %all-gather.17.cloned.1.call-done = bf16[768,768]{1,0:T(8,128)(2,1)} async-done(((bf16[192,768]{1,0:T(8,128)(2,1)}), bf16[768,768]{1,0:T(8,128)(2,1)}) %all-gather.17.cloned.1.call-update) | async-done | bytes 1179664 | tf_op jit(solution)/shard_map/all_gather | solution.py:340
  (480 shorter events, 397.8 us)
Async XLA Ops:
  7.2 46.0 %all-gather.19.cloned.1.call-start = ((), (), s32[]{:S(2)}) async-start(), calls=%async_computation.20 | async-start | bytes 2211840 | tf_op jit(solution)/shard_map/all_gather | solution.py:88
  9.8 84.8 %all-gather.23.cloned.1.call-start = ((), (), s32[]{:S(2)}) async-start(), calls=%async_computation.22 | async-start | bytes 2211840 | tf_op jit(solution)/shard_map/all_gather | solution.py:88
  10.5 176.8 %all-gather.21.cloned.1.call-start = ((), (), s32[]{:S(2)}) async-start(), calls=%async_computation.21 | async-start | bytes 15925248 | tf_op jit(solution)/shard_map/all_gather | solution.py:92
  53.2 203.6 %all-gather.25.cloned.1.call-start = ((), (), s32[]{:S(2)}) async-start(), calls=%async_computation.23 | async-start | bytes 15925248 | tf_op jit(solution)/shard_map/all_gather | solution.py:92
  94.6 322.5 %reduce-scatter.11.cloned.1.call-start = ((), (), s32[]{:S(2)}) async-start(), calls=%async_computation.14 | async-start | bytes 3932160 | tf_op jit(solution)/shard_map/reduce_scatter | solution.py:227
  167.2 72.1 %copy-start.70 = (f32[768]{0:T(1024)}, f32[768]{0:T(1024)S(1)}, u32[]{:S(2)}) copy-start(f32[768]{0:T(1024)S(1)} %get-tuple-element.62) | copy-start | bytes 9220
  357.8 283.3 %reduce-scatter.13.cloned.1.call-start = ((), (), s32[]{:S(2)}) async-start(), calls=%async_computation.15 | async-start | bytes 3932160 | tf_op jit(solution)/shard_map/reduce_scatter | solution.py:227
  459.6 70.0 %all-to-all-start.4 = ((bf16[128,4,768]{2,0,1:T(8,128)(2,1)}), bf16[128,4,768]{2,0,1:T(8,128)(2,1)S(1)}, u32[]{:S(2)}, u32[]{:S(2)}) async-start(bf16[128,4,768]{2,0,1:T(8,128)(2,1)} %bitcast.278), calls=%async_computation.6 | async-start | bytes 1572864 | tf_op jit(solution)/shard_map/all_to_all | solution.py:268
  465.7 67.5 %copy-start.65 = (bf16[128,768]{1,0:T(8,128)(2,1)S(1)}, bf16[128,768]{1,0:T(8,128)(2,1)}, u32[]{:S(2)}) copy-start(bf16[128,768]{1,0:T(8,128)(2,1)} %copy-done.64) | copy-start | bytes 589828
  529.6 66.1 %copy-start.28 = (bf16[128,4,768]{2,0,1:T(8,128)(2,1)}, bf16[128,4,768]{2,0,1:T(8,128)(2,1)S(1)}, u32[]{:S(2)}) copy-start(bf16[128,4,768]{2,0,1:T(8,128)(2,1)S(1)} %all-to-all-done.4) | copy-start | bytes 2359300
  529.6 66.1 %copy-start.61 = (bf16[128,768]{1,0:T(8,128)(2,1)S(1)}, bf16[128,768]{1,0:T(8,128)(2,1)}, u32[]{:S(2)}) copy-start(bf16[128,768]{1,0:T(8,128)(2,1)} %get-tuple-element.78) | copy-start | bytes 589828
  529.6 85.6 %all-to-all-start.5 = ((bf16[128,4,768]{2,0,1:T(8,128)(2,1)}), bf16[128,4,768]{2,0,1:T(8,128)(2,1)S(1)}, u32[]{:S(2)}, u32[]{:S(2)}) async-start(bf16[128,4,768]{2,0,1:T(8,128)(2,1)} %bitcast.277), calls=%async_computation.7 | async-start | bytes 1572864 | tf_op jit(solution)/shard_map/all_to_all | solution.py:275
  626.6 24.3 %all-to-all-start.3 = ((bf16[128,4,768]{2,0,1:T(8,128)(2,1)}), bf16[128,4,768]{2,0,1:T(8,128)(2,1)}, u32[]{:S(2)}, u32[]{:S(2)}) async-start(bf16[128,4,768]{2,0,1:T(8,128)(2,1)} %pad_maximum_fusion.4), calls=%async_computation.5 | async-start | bytes 1572864 | tf_op jit(solution)/shard_map/all_to_all | solution.py:267
  631.2 55.3 %all-reduce.5.cloned.1.call-start = ((), (), s32[]{:S(2)}) async-start(), calls=%async_computation.26 | async-start | bytes 196608
  650.9 232.0 %reduce-scatter.21.cloned.1.call-start = ((), (), s32[]{:S(2)}) async-start(), calls=%async_computation.25 | async-start | bytes 8404992
  716.7 21.8 %all-to-all-start.2 = ((bf16[128,4,768]{2,0,1:T(8,128)(2,1)}), bf16[128,4,768]{2,0,1:T(8,128)(2,1)S(1)}, u32[]{:S(2)}, u32[]{:S(2)}) async-start(bf16[128,4,768]{2,0,1:T(8,128)(2,1)} %bitcast.279), calls=%async_computation.4 | async-start | bytes 1572864 | tf_op jit(solution)/shard_map/all_to_all | solution.py:275
  738.5 56.8 %all-to-all-start.1 = ((bf16[128,4,768]{2,0,1:T(8,128)(2,1)}), bf16[128,4,768]{2,0,1:T(8,128)(2,1)S(1)}, u32[]{:S(2)}, u32[]{:S(2)}) async-start(bf16[128,4,768]{2,0,1:T(8,128)(2,1)} %bitcast.280), calls=%async_computation.3 | async-start | bytes 1572864 | tf_op jit(solution)/shard_map/all_to_all | solution.py:268
  795.3 56.6 %all-to-all-start = ((bf16[128,4,768]{2,0,1:T(8,128)(2,1)}), bf16[128,4,768]{2,0,1:T(8,128)(2,1)}, u32[]{:S(2)}, u32[]{:S(2)}) async-start(bf16[128,4,768]{2,0,1:T(8,128)(2,1)} %pad_maximum_fusion.3), calls=%async_computation.2 | async-start | bytes 1572864 | tf_op jit(solution)/shard_map/all_to_all | solution.py:267
  800.3 151.3 %reduce-scatter.19.cloned.1.call-start = ((), (), s32[]{:S(2)}) async-start(), calls=%async_computation.24 | async-start | bytes 8404992
  882.8 124.5 %reduce-scatter.15.cloned.1.call-start = ((), (), s32[]{:S(2)}) async-start(), calls=%async_computation.16 | async-start | bytes 1474560 | tf_op jit(solution)/shard_map/reduce_scatter | solution.py:337
  978.8 59.3 %all-gather.15.cloned.1.call-start = ((), (), s32[]{:S(2)}) async-start(), calls=%async_computation.17 | async-start | bytes 1474560 | tf_op jit(solution)/shard_map/all_gather | solution.py:340
  1007.3 71.2 %reduce-scatter.17.cloned.1.call-start = ((), (), s32[]{:S(2)}) async-start(), calls=%async_computation.18 | async-start | bytes 1474560 | tf_op jit(solution)/shard_map/reduce_scatter | solution.py:337
  1050.1 59.3 %all-gather.17.cloned.1.call-start = ((), (), s32[]{:S(2)}) async-start(), calls=%async_computation.19 | async-start | bytes 1474560 | tf_op jit(solution)/shard_map/all_gather | solution.py:340
  1114.7 20.6 %all-to-all-start.7 = ((bf16[8,1,96,768]{3,2,1,0:T(8,128)(2,1)}), bf16[8,1,96,768]{3,2,1,0:T(8,128)(2,1)S(1)}, u32[]{:S(2)}, u32[]{:S(2)}) async-start(bf16[8,1,96,768]{3,2,1,0:T(8,128)(2,1)} %bitcast.320), calls=%async_computation.11 | async-start | bytes 2359296 | tf_op jit(solution)/shard_map/all_to_all | solution.py:356
  (121 other events, 1091.9 us)
Sparse Core Ops, SparseCore 0:
  10.1 43.0 all-gather.18
  55.3 39.1 all-gather.22
  96.5 80.8 all-gather.20
  179.1 77.7 all-gather.24
  358.0 59.0 reduce-scatter.10
  457.6 91.4 reduce-scatter.12
  651.0 35.4 all-reduce.4
  714.8 67.2 reduce-scatter.20
  882.9 68.6 reduce-scatter.18
  979.0 28.2 reduce-scatter.14
  1008.9 29.1 all-gather.14
  1050.2 28.2 reduce-scatter.16
  1080.2 29.1 all-gather.16
where the time goes:
time: 1150 us; the launch traced here: 1140 us
  waiting for transfers between devices  388 us (34%)
  blocking collectives  378 us (33%)
  local copies, waits for them, and re-layouts  179 us (16%)
  matrix products  114 us (10%)
  other arithmetic  38.8 us (3%)
  starting transfers between devices  28.9 us (3%)
  between operations  17.1 us (1%)
    unnamed x16, waiting for transfers between devices  99.7 us
    all_gather x2, blocking collectives, local(): lax.all_gather(normed_low, 'ctx', axis=0, tiled=True)  93.1 us
    all_gather x2, waiting for transfers between devices, local(): lax.all_gather(local_mats, 'ctx', axis=2, tiled=True)  83.9 us
    all_gather x2, waiting for transfers between devices, local(): lax.all_gather(gram_part.astype(jnp.bfloat16), 'ctx', axis=0, tiled=True)  61.3 us
    all_gather x2, blocking collectives, local(): lax.all_gather(normed_two_low, 'ctx', axis=0, tiled=True)  61 us
    reduce_scatter x2, waiting for transfers between devices, local(): lax.psum_scatter(gram_local.astype(jnp.bfloat16), 'ctx', scatter_dimensio...  56.8 us
    reduce_scatter x2, waiting for transfers between devices, local(): lax.psum_scatter(key_terms(jnp.int32(0), tokens_dev * lax.axis_size('ctx'...  53 us
    all_gather x2, blocking collectives, local(): lax.all_gather(attended_low, 'ctx', axis=0, tiled=True)  50.1 us
  transfers between devices with their start and end apart: 20, of which 12 were waited for; matrix products, arithmetic and copies ran while one was open for 14% of the time, Pallas kernels for 0%

commit v1 on v0

v1 whole, which is shorter than its diff:
```python
import math

import jax
import jax.numpy as jnp
from jax import lax
from jax.sharding import Mesh, PartitionSpec as P

D = 768
HEADS = 12
HEAD = 64
FF = 3072
LAYERS = 2
ADAM_STEP = 10
TP = 4
COLS = D // TP
TP_HEADS = HEADS // TP

norm_epsilon = 1e-05
quintic_one = 3.4445
quintic_two = -4.775
quintic_three = 2.0315
momentum_decay = 0.95
matrix_rate = 0.6
matrix_decay = 0.01
first_decay = 0.9
second_decay = 0.999
vector_rate = 0.5
vector_decay = 0.01
adam_epsilon = 1e-08
masked_score = -1e30

GROUP = ("jx", "jc")
REPLICAS = ("g", "ctx")
DP = ("g", "jx", "jc")
EVERY = ("g", "jx", "jc", "ctx")
SWAP = [(0, 1), (1, 0)]
bf16 = jnp.bfloat16
f32 = jnp.float32


def layer_norm(hidden, gain_vec, bias_vec):
    center = hidden - jnp.mean(hidden, axis=-1, keepdims=True)
    variance = jnp.mean(center * center, axis=-1, keepdims=True)
    return center * lax.rsqrt(variance + norm_epsilon) * gain_vec + bias_vec


def smooth_unit(preact):
    return jax.nn.gelu(preact, approximate=True)


def dot(operand, other):
    return jnp.dot(operand, other, preferred_element_type=f32)


def dot_tokens(operand, other):
    return lax.dot_general(operand, other, (((0,), (0,)), ((), ())), preferred_element_type=f32)


def dot_trans(operand, other):
    return lax.dot_general(operand, other, (((1,), (1,)), ((), ())), preferred_element_type=f32)


def bdot(operand, other, left, right):
    return lax.dot_general(
        operand, other, (((left,), (right,)), ((0,), (0,))), preferred_element_type=f32
    )


def heads_of(matrix):
    return matrix.reshape(matrix.shape[0], TP_HEADS, HEAD).transpose(1, 0, 2)


def merge_heads(stack):
    return stack.transpose(1, 0, 2).reshape(stack.shape[1], TP_HEADS * HEAD)


def core_gather(rows):
    return jnp.concatenate([rows, lax.ppermute(rows, "jc", SWAP)], axis=0)


def group_sum(partial):
    half = partial.shape[0] // 2
    mine = partial[:half] + lax.ppermute(partial[half:].astype(bf16), "jc", SWAP).astype(f32)
    return mine + lax.ppermute(mine.astype(bf16), "jx", SWAP).astype(f32)


def to_group(mats):
    count, rows, width = mats.shape
    split = mats.reshape(count, rows, TP, width // TP)
    return lax.all_to_all(split, GROUP, split_axis=2, concat_axis=1, tiled=True)[:, :, 0]


def from_group(mats):
    count, rows, width = mats.shape
    split = mats.reshape(count, TP, rows // TP, width)
    return lax.all_to_all(split, GROUP, split_axis=1, concat_axis=3, tiled=True)[:, 0]


def gather_mats(mats):
    parts = lax.all_gather(mats, REPLICAS, axis=0, tiled=False)
    groups = lax.axis_size("g")
    parts = parts.reshape(groups, -1, *mats.shape)
    return [
        parts[:, :, item].transpose(0, 2, 1, 3).reshape(D, -1) for item in range(mats.shape[0])
    ]


def scatter_mats(mats):
    groups = lax.axis_size("g")
    stack = jnp.stack([mat.astype(bf16) for mat in mats])
    count, rows, blocks, width = stack.shape
    stack = stack.reshape(count, groups, rows // groups, blocks, width).transpose(1, 3, 0, 2, 4)
    stack = stack.reshape(groups * blocks, count, rows // groups, width)
    return lax.psum_scatter(stack, REPLICAS, scatter_dimension=0, tiled=True)[0]


def local(hidden_in, segments, out_grad, weights, vectors, mat_momentum, vec_first, vec_second):
    tokens_dev = hidden_in.shape[1]
    seq_len = segments.shape[1]
    half = 2 * tokens_dev
    dp_rows = weights.shape[2]
    ctx_size = lax.axis_size("ctx")
    x_index = lax.axis_index("jx")
    c_index = lax.axis_index("jc")
    t_index = 2 * x_index + c_index
    z_index = lax.axis_index("ctx")
    dp_index = lax.axis_index(DP)
    dp_size = lax.axis_size(DP)

    to_seq = []
    for t in range(TP):
        for z in range(ctx_size):
            to_seq.append((t * ctx_size + z, ((z % 2) * 2 + z // 2) * ctx_size + t))
    from_seq = [(b, a) for a, b in to_seq]
    axes = ("jx", "jc", "ctx")

    def x_join(block):
        other = lax.ppermute(block, "jx", SWAP)
        first = jnp.where(x_index == 0, block, other)
        second = jnp.where(x_index == 0, other, block)
        return jnp.concatenate([first, second], axis=0)

    seg_row = jnp.pad(segments.astype(f32), ((0, 7), (0, D - seq_len)))
    moved = lax.ppermute(jnp.concatenate([hidden_in[0], seg_row], axis=0), axes, to_seq)
    hidden = x_join(moved[:tokens_dev])
    segment_row = moved[tokens_dev, :seq_len]
    vec_parts = lax.all_gather(vectors.astype(bf16), EVERY, axis=0, tiled=False)
    vec_rows = (
        vec_parts.reshape(dp_size, ctx_size, LAYERS, vectors.shape[1], vectors.shape[2])
        .transpose(2, 1, 3, 0, 4)
        .reshape(LAYERS, 12, D)
        .astype(f32)
    )
    low = weights.astype(bf16)
    swapped = [
        [to_group(low[layer, 0:1]), to_group(low[layer, 1:3])] for layer in range(LAYERS)
    ]
    grad_hidden = x_join(lax.ppermute(out_grad[0], axes, to_seq))

    order = [c_index * half, (1 - c_index) * half]
    pos = jnp.concatenate([start + jnp.arange(half) for start in order])
    seg = jnp.concatenate([lax.dynamic_slice_in_dim(segment_row, start, half) for start in order])
    allowed = (pos[None, :] <= pos[:, None]) & (seg[None, :] == seg[:, None])

    def mine(row):
        return lax.dynamic_slice_in_dim(row, t_index * COLS, COLS, axis=-1)

    def scores_of(q, k):
        return jnp.where(allowed[None], bdot(q, k, 2, 2) * HEAD ** (-0.5), masked_score)

    stored = []
    for layer in range(LAYERS):
        vec = vec_rows[layer]
        (attn_w,) = gather_mats(swapped[layer][0])
        w_up, w_down = gather_mats(swapped[layer][1])
        w_qkv = attn_w[:, : 3 * COLS]
        w_o = lax.all_to_all(
            attn_w[:, 3 * COLS :].reshape(TP, COLS, COLS),
            GROUP,
            split_axis=0,
            concat_axis=2,
            tiled=True,
        )[0]
        a_all = core_gather(layer_norm(hidden, vec[0], vec[1]).astype(bf16))
        proj = dot(a_all, w_qkv)
        q = heads_of((proj[:, :COLS] + mine(vec[4])).astype(bf16))
        k = heads_of(proj[:, COLS : 2 * COLS].astype(bf16))
        v = heads_of((proj[:, 2 * COLS :] + mine(vec[5])).astype(bf16))
        scores = scores_of(q, k)
        row_max = jnp.max(scores, axis=-1, keepdims=True)
        unnormed = jnp.exp(scores - row_max)
        total = jnp.sum(unnormed, axis=-1, keepdims=True)
        prob = (unnormed / total).astype(bf16)
        log_total = row_max + jnp.log(total)
        o = merge_heads(bdot(prob, v, 2, 1)).astype(bf16)
        middle = hidden + (group_sum(dot(o, w_o)) + vec[6])
        c_all = core_gather(layer_norm(middle, vec[2], vec[3]).astype(bf16))
        preact = dot(c_all, w_up) + mine(vec[8:12]).reshape(-1)
        act = smooth_unit(preact).astype(bf16)
        stored.append(
            (hidden, middle, a_all, q, k, v, log_total, o, c_all, preact, act, w_qkv, w_o, w_up, w_down)
        )
        hidden = middle + (group_sum(dot_trans(act, w_down)) + vec[7])

    def send_back(rows):
        block = lax.dynamic_slice_in_dim(rows, x_index * tokens_dev, tokens_dev, axis=0)
        return lax.ppermute(block, axes, from_seq)

    hidden_out = send_back(hidden)

    once = jnp.where(x_index == 0, 1.0, 0.0).astype(f32)
    mat_list = [None] * LAYERS
    vec_list = [None] * LAYERS
    for layer in reversed(range(LAYERS)):
        (h_in, middle, a_all, q, k, v, log_total, o, c_all, preact, act, w_qkv, w_o, w_up, w_down) = stored[
            layer
        ]
        vec = vec_rows[layer]
        gy = grad_hidden.astype(bf16)
        gy_all = core_gather(gy)
        gu = dot(gy_all, w_down)
        unused, gelu_pull = jax.vjp(smooth_unit, preact)
        gz = gelu_pull(gu)[0].astype(bf16)
        gc = group_sum(dot_trans(gz, w_up))
        unused, pull_two = jax.vjp(layer_norm, middle, vec[2], vec[3])
        g_mid, g_gain_two, g_shift_two = pull_two(gc)
        gm = grad_hidden + g_mid
        gb = gm.astype(bf16)
        gb_all = core_gather(gb)
        go = heads_of(dot_trans(gb_all, w_o).astype(bf16))
        prob = jnp.exp(scores_of(q, k) - log_total)
        prob_low = prob.astype(bf16)
        g_prob = bdot(go, v, 2, 2)
        row_dot = jnp.sum(g_prob * prob, axis=-1, keepdims=True)
        g_scores = (prob * (g_prob - row_dot)).astype(bf16)
        gq = merge_heads(bdot(g_scores, k, 2, 1) * HEAD ** (-0.5)).astype(bf16)
        gk = merge_heads(bdot(g_scores, q, 1, 1) * HEAD ** (-0.5)).astype(bf16)
        gv = merge_heads(bdot(prob_low, go, 1, 1)).astype(bf16)
        g_qkv = jnp.concatenate([gq, gk, gv], axis=1)
        ga = group_sum(dot_trans(g_qkv, w_qkv))
        unused, pull_one = jax.vjp(layer_norm, h_in, vec[0], vec[1])
        g_in, g_gain_one, g_shift_one = pull_one(ga)
        grad_hidden = gm + g_in

        mlp = [
            dot_tokens(c_all, gz).reshape(D, ctx_size, COLS),
            dot_tokens(gy_all, act).reshape(D, ctx_size, COLS),
        ]
        mlp_part = scatter_mats(mlp)
        g_wo = lax.all_to_all(
            dot_tokens(o, gb_all).astype(bf16).reshape(COLS, TP, COLS),
            GROUP,
            split_axis=1,
            concat_axis=0,
            tiled=True,
        )
        g_attn = jnp.concatenate(
            [dot_tokens(a_all, g_qkv).astype(bf16).reshape(D, 3, COLS), g_wo], axis=1
        )
        attn_part = scatter_mats([g_attn])
        mat_list[layer] = from_group(jnp.concatenate([attn_part, mlp_part], axis=0)).astype(f32)

        def place(values):
            wide = jnp.zeros(values.shape[:-1] + (D,), f32)
            return lax.dynamic_update_slice_in_dim(wide, values, t_index * COLS, axis=-1)

        def token_sum(values):
            return jnp.sum(values, axis=0, dtype=f32)

        b_qv = place(jnp.stack([token_sum(gq), token_sum(gv)]))
        b_up = place(token_sum(gz).reshape(ctx_size, COLS))
        shared = once * jnp.stack(
            [g_gain_one, g_shift_one, g_gain_two, g_shift_two, token_sum(gb), token_sum(gy)]
        )
        vec_term = jnp.concatenate([shared[:4], b_qv, shared[4:], b_up], axis=0)
        vec_sum = lax.psum(vec_term, EVERY)
        vec_list[layer] = lax.dynamic_slice(
            vec_sum,
            (z_index * vectors.shape[1], dp_index * vectors.shape[2]),
            (vectors.shape[1], vectors.shape[2]),
        )
    input_grad = send_back(grad_hidden)

    grad_mats = jnp.stack(mat_list)
    grad_vecs = jnp.stack(vec_list)
    moment_new = momentum_decay * mat_momentum + grad_mats
    update_in = grad_mats + momentum_decay * moment_new
    item_count = 3 * LAYERS
    cols_dev = update_in.shape[3]
    items = update_in.astype(bf16).reshape(item_count, dp_rows, cols_dev)
    copies = -(-dp_size // item_count)
    slots = jnp.tile(items, (copies, 1, 1))[0:dp_size]
    received = lax.all_to_all(slots[:, None], DP, split_axis=0, concat_axis=1, tiled=True)
    current = received.reshape(dp_size * dp_rows, cols_dev)
    square = (dp_index % item_count) % 3 == 0
    gram_local = dot_trans(current, current)
    gram_part = lax.psum_scatter(gram_local.astype(bf16), "ctx", scatter_dimension=0, tiled=True)
    gram_total = lax.all_gather(gram_part, "ctx", axis=0, tiled=True).astype(f32)
    gram = jnp.where(square, gram_local, gram_total)
    scale = 1.0 / (jnp.sqrt(jnp.trace(gram)) + 1e-07)
    base = gram * (scale * scale)
    base_low = base.astype(bf16)
    bmat = (quintic_two * base + quintic_three * dot(base_low, base_low)).astype(bf16)
    current = (scale * (quintic_one * current.astype(f32) + dot(bmat, current))).astype(bf16)

    def two_part(left, right):
        high = right.astype(bf16)
        rest = (right - high.astype(f32)).astype(bf16)
        return dot(left, high) + dot(left, rest)

    turned = two_part(bmat, base)
    base = (
        quintic_one * quintic_one * base
        + quintic_one * (turned + turned.T)
        + two_part(bmat, turned.T)
    )
    base_low = base.astype(bf16)
    bmat = (quintic_two * base + quintic_three * dot(base_low, base_low)).astype(bf16)
    current = (quintic_one * current.astype(f32) + dot(bmat, current)).astype(bf16)
    returned = lax.all_to_all(
        current.reshape(dp_size, 1, dp_rows, cols_dev), DP, split_axis=0, concat_axis=1, tiled=True
    )[0]
    spread = dp_size // item_count
    chosen = [
        lax.dynamic_index_in_dim(
            returned, item + item_count * (dp_index % spread), 0, keepdims=False
        )
        for item in range(item_count)
    ]
    ortho = jnp.stack(chosen).reshape(LAYERS, 3, dp_rows, cols_dev).astype(f32)
    factor = jnp.array([0.2 * math.sqrt(D), 0.2 * math.sqrt(FF), 0.2 * math.sqrt(FF)], f32)
    weights_new = weights * (1.0 - matrix_rate * matrix_decay) - matrix_rate * (
        ortho * factor[None, :, None, None]
    )
    first_new = first_decay * vec_first + (1.0 - first_decay) * grad_vecs
    second_new = second_decay * vec_second + (1.0 - second_decay) * grad_vecs * grad_vecs
    first_hat = first_new / (1.0 - first_decay**ADAM_STEP)
    second_hat = second_new / (1.0 - second_decay**ADAM_STEP)
    vectors_new = vectors * (1.0 - vector_rate * vector_decay) - vector_rate * first_hat / (
        jnp.sqrt(second_hat) + adam_epsilon
    )
    return (
        hidden_out[None],
        input_grad[None],
        grad_mats,
        moment_new,
        weights_new,
        grad_vecs,
        second_new,
        vectors_new,
    )


def solution(mesh):
    dp, ctx = mesh.shape["dp"], mesh.shape["ctx"]
    fine = Mesh(mesh.devices.reshape(dp // TP, 2, 2, ctx), EVERY)
    tokens = P(DP, "ctx", None)
    mats = P(None, None, DP, "ctx")
    vecs = P(None, "ctx", DP)
    return jax.shard_map(
        local,
        mesh=fine,
        in_specs=(tokens, P(DP, None), tokens, mats, vecs, mats, vecs, vecs),
        out_specs=(tokens, tokens, mats, mats, mats, vecs, vecs, vecs),
        check_vma=False,
    )
```

time: 1150 us -> 934 us (0.81)
  blocking collectives: 378 us -> 113 us
  starting transfers between devices: 28.9 us -> 67.9 us
  waiting for transfers between devices: 388 us -> 427 us
  matrix products: 114 us -> 81.9 us
  local copies, waits for them, and re-layouts: 179 us -> 151 us
  other arithmetic: 38.8 us -> 66.5 us
    all_gather x16 -> x1, blocking collectives: 358 us -> 75.6 us  [local(): vec_parts = lax.all_gather(vectors.astype(bf16), EVERY, axis=0, tiled=False)]
    psum x0 -> x1, waiting for transfers between devices: none -> 131 us  [local(): vec_sum = lax.psum(vec_term, EVERY)]
    all_gather x6 -> x5, waiting for transfers between devices: 151 us -> 44.8 us  [the longest x4 43.4 us: gather_mats(): parts = lax.all_gather(mats, REPLICAS, axis=0, tiled=False)]
    unnamed x16 -> x11, waiting for transfers between devices: 99.7 us -> 0.18 us
    reduce_scatter x4 -> x5, waiting for transfers between devices: 110 us -> 177 us  [the longest x4 171 us: scatter_mats(): return lax.psum_scatter(stack, REPLICAS, scatter_dimension=0, tiled=True)[0]]
    ppermute x0 -> x30, waiting for transfers between devices: none -> 65.4 us  [the longest x8 47.5 us: group_sum(): return mine + lax.ppermute(mine.astype(bf16), 'jx', SWAP).astype(f32)]
    slice x18 -> x26, local copies, waits for them, and re-layouts: 46.1 us -> 12.4 us  [the longest x2 3.73 us: gather_mats(): parts[:, :, item].transpose(0, 2, 1, 3).reshape(D, -1)]
    ppermute x0 -> x30, starting transfers between devices: none -> 28 us  [the longest x8 7.67 us: group_sum(): return mine + lax.ppermute(mine.astype(bf16), 'jx', SWAP).astype(f32)]
  transfers between devices with their start and end apart: 20 -> 50, of which waited for: 12 -> 26; matrix products, arithmetic and copies ran while one was open for 14% -> 24% of each run, Pallas kernels for 0% -> 0%
where the time goes in v1:
time: 934 us; the launch traced here: 924 us
  waiting for transfers between devices  427 us (46%)
  local copies, waits for them, and re-layouts  151 us (16%)
  blocking collectives  113 us (12%)
  matrix products  81.9 us (9%)
  starting transfers between devices  67.9 us (7%)
  other arithmetic  66.5 us (7%)
  between operations  17 us (2%)
    reduce_scatter x4, waiting for transfers between devices, scatter_mats(): return lax.psum_scatter(stack, REPLICAS, scatter_dimension=0, tiled=True)[0]  171 us
    psum x1, waiting for transfers between devices, local(): vec_sum = lax.psum(vec_term, EVERY)  131 us
    all_gather x1, blocking collectives, local(): vec_parts = lax.all_gather(vectors.astype(bf16), EVERY, axis=0, tiled=False)  75.6 us
    ppermute x8, waiting for transfers between devices, group_sum(): return mine + lax.ppermute(mine.astype(bf16), 'jx', SWAP).astype(f32)  47.5 us
    all_gather x4, waiting for transfers between devices, gather_mats(): parts = lax.all_gather(mats, REPLICAS, axis=0, tiled=False)  43.4 us
    dot_general x15, matrix products, dot(): return jnp.dot(operand, other, preferred_element_type=f32)  39.1 us
    unnamed x300, local copies, waits for them, and re-layouts  26.3 us
    all_to_all x1, blocking collectives, local(): lax.all_to_all(slots[:, None], DP, split_axis=0, concat_axis=1, tiled=True)  19.2 us
  transfers between devices with their start and end apart: 50, of which 26 were waited for; matrix products, arithmetic and copies ran while one was open for 24% of the time, Pallas kernels for 0%

profile of v1, /device:TPU:0, one launch (start us, length us, event | category | flops | bytes accessed | tf_op | source)
XLA Modules:
  0.0 924.2 jit_solution(10784575039196422288)
XLA Ops:
  9.6 9.3 %all_to_all.156 = bf16[1,96,4,192]{1,3,0,2:T(8,128)(2,1)S(1)} all-to-all(bf16[1,96,4,192]{1,3,0,2:T(8,128)(2,1)S(1)} %bitcast.381), channel_id=1, replica_groups=mesh['g'=2,'jx'=2,'jc'=2,'ctx'=4] {'jx','jc'}, dimensions={2} | all-to-all | bytes 294912 | tf_op jit(solution)/shard_map/all_to_all | solution.py:90
  22.9 7.3 all-to-all-start.2
  30.2 75.6 %all-gather = bf16[64,3,96]{2,1,0:T(4,128)(2,1)S(1)} all-gather(bf16[2,3,96]{2,1,0:T(4,128)(2,1)S(1)} %copy.237), channel_id=2, replica_groups=mesh['g'=2,'jx'=2,'jc'=2,'ctx'=4] {'g','jx','jc','ctx'}, dimensions={0}, use_global_device_ids=true | all-gather | bytes 38016 | tf_op jit(solution)/shard_map/all_gather | solution.py:147
  108.9 5.1 collective-permute-done.1
  140.1 10.3 %collective-permute-done.4 = bf16[256,768]{1,0:T(8,128)(2,1)S(1)} collective-permute-done((bf16[256,768]{1,0:T(8,128)(2,1)S(1)}, bf16[256,768]{1,0:T(8,128)(2,1)S(1)}, u32[]{:S(2)}, u32[]{:S(2)}) %collective-permute-start.4) | collective-permute-done | bytes 393248 | tf_op jit(solution)/shard_map/ppermute | solution.py:84
  154.8 5.0 all-gather.9.cloned.1.call-done
  171.8 8.7 all_to_all.157
  200.0 22.1 %all-gather.11.cloned.1.call-done = bf16[8,1,384,192]{2,3,1,0:T(8,128)(2,1)} async-done(((bf16[1,1,384,192]{2,3,1,0:T(8,128)(2,1)}), bf16[8,1,384,192]{2,3,1,0:T(8,128)(2,1)}) %all-gather.11.cloned.1.call-update) | async-done | bytes 1179664 | tf_op jit(solution)/shard_map/all_gather | solution.py:100
  232.6 4.6 collective-permute-start.15
  270.1 7.0 collective-permute-start.11
  278.6 16.3 %all-gather.13.cloned.1.call-done = bf16[8,2,384,192]{2,3,1,0:T(8,128)(2,1)} async-done(((bf16[1,2,384,192]{2,3,1,0:T(8,128)(2,1)}), bf16[8,2,384,192]{2,3,1,0:T(8,128)(2,1)}) %all-gather.13.cloned.1.call-update) | async-done | bytes 2359312 | tf_op jit(solution)/shard_map/all_gather | solution.py:100
  311.1 9.7 %collective-permute-done.19 = bf16[256,768]{1,0:T(8,128)(2,1)S(1)} collective-permute-done((bf16[256,768]{1,0:T(8,128)(2,1)S(1)}, bf16[256,768]{1,0:T(8,128)(2,1)S(1)}, u32[]{:S(2)}, u32[]{:S(2)}) %collective-permute-start.19) | collective-permute-done | bytes 393248 | tf_op jit(solution)/shard_map/ppermute | solution.py:84
  398.9 9.6 %collective-permute-done.25 = bf16[256,768]{1,0:T(8,128)(2,1)S(1)} collective-permute-done((bf16[256,768]{1,0:T(8,128)(2,1)S(1)}, bf16[256,768]{1,0:T(8,128)(2,1)S(1)}, u32[]{:S(2)}, u32[]{:S(2)}) %collective-permute-start.25) | collective-permute-done | bytes 393248 | tf_op jit(solution)/shard_map/ppermute | solution.py:84
  446.0 4.8 maximum_bitcast_fusion
  453.9 40.2 %reduce-scatter.12.cloned.1.call-done = bf16[1,2,384,192]{2,3,1,0:T(8,128)(2,1)} async-done(((bf16[8,2,384,192]{2,3,1,0:T(8,128)(2,1)}), bf16[1,2,384,192]{2,3,1,0:T(8,128)(2,1)}) %reduce-scatter.12.cloned.1.call-update) | async-done | bytes 294928 | tf_op jit(solution)/shard_map/reduce_scatter | solution.py:114
  500.1 60.9 %reduce-scatter.6.cloned.1.call-done = bf16[1,1,384,192]{2,3,1,0:T(8,128)(2,1)} async-done(((bf16[8,1,384,192]{2,3,1,0:T(8,128)(2,1)}), bf16[1,1,384,192]{2,3,1,0:T(8,128)(2,1)}) %reduce-scatter.6.cloned.1.call-update) | async-done | bytes 147472 | tf_op jit(solution)/shard_map/reduce_scatter | solution.py:114
  562.1 70.4 %reduce-scatter.8.cloned.1.call-done = bf16[1,2,384,192]{2,3,1,0:T(8,128)(2,1)} async-done(((bf16[8,2,384,192]{2,3,1,0:T(8,128)(2,1)}), bf16[1,2,384,192]{2,3,1,0:T(8,128)(2,1)}) %reduce-scatter.8.cloned.1.call-update) | async-done | bytes 294928 | tf_op jit(solution)/shard_map/reduce_scatter | solution.py:114
  640.6 7.5 all-to-all-done.7
  652.8 19.2 %all_to_all.158 = bf16[8,1,96,768]{3,2,1,0:T(8,128)(2,1)S(1)} all-to-all(bf16[8,1,96,768]{3,2,1,0:T(8,128)(2,1)S(1)} %slice_bitcast_fusion), channel_id=1, replica_groups=mesh['g'=2,'jx'=2,'jc'=2,'ctx'=4] {'g','jx','jc'}, dimensions={0} | all-to-all | bytes 2359296 | tf_op jit(solution)/shard_map/all_to_all | solution.py:293
  680.7 10.8 %collective-permute-done.13 = bf16[256,768]{1,0:T(8,128)(2,1)S(1)} collective-permute-done((bf16[256,768]{1,0:T(8,128)(2,1)}, bf16[256,768]{1,0:T(8,128)(2,1)S(1)}, u32[]{:S(2)}, u32[]{:S(2)}) %collective-permute-start.13) | collective-permute-done | bytes 393248 | tf_op jit(solution)/shard_map/ppermute | solution.py:84
  698.6 5.9 reduce-scatter.14.cloned.1.call-done
  758.1 6.4 fusion.6
  764.5 7.0 add_convert_fusion
  780.0 130.9 %all-reduce.4.cloned.1.call-done = (f32[12,768]{1,0:T(8,128)}, f32[12,768]{1,0:T(8,128)}) async-done(((f32[12,768]{1,0:T(8,128)}, f32[12,768]{1,0:T(8,128)}), (f32[12,768]{1,0:T(8,128)}, f32[12,768]{1,0:T(8,128)})) %all-reduce.4.cloned.1.call-update) | async-done | bytes 73744 | tf_op jit(solution)/shard_map/psum | solution.py:276
  (642 shorter events, 352.6 us)
Async XLA Ops:
  7.2 108.9 %all-gather.7.cloned.1.call-start = ((), (), s32[]{:S(2)}) async-start(), calls=%async_computation.17 | async-start | bytes 1327104 | tf_op jit(solution)/shard_map/all_gather | solution.py:100
  20.1 86.0 %collective-permute-start = (f32[136,768]{1,0:T(8,128)S(1)}, f32[136,768]{1,0:T(8,128)S(1)}, u32[]{:S(2)}, u32[]{:S(2)}) collective-permute-start(f32[136,768]{1,0:T(8,128)S(1)} %select_maximum_fusion), channel_id=1, source_target_pairs={{0,0},{1,8},{2,4},{3,12},{4,1},{5,9},{6,5},{7,13},{8,2},{9,10},{10... | collective-permute-start | bytes 1253384 | tf_op jit(solution)/shard_map/ppermute | solution.py:144
  22.9 84.6 %all-to-all-start.2 = ((bf16[2,96,4,192]{1,3,0,2:T(8,128)(2,1)}), bf16[2,96,4,192]{1,3,0,2:T(8,128)(2,1)S(1)}, u32[]{:S(2)}, u32[]{:S(2)}) async-start(bf16[2,96,4,192]{1,3,0,2:T(8,128)(2,1)} %copy.245), calls=%async_computation.2 | async-start | bytes 786432 | tf_op jit(solution)/shard_map/all_to_all | solution.py:90
  30.2 129.6 %all-gather.9.cloned.1.call-start = ((), (), s32[]{:S(2)}) async-start(), calls=%async_computation.18 | async-start | bytes 2654208 | tf_op jit(solution)/shard_map/all_gather | solution.py:100
  124.1 97.9 %all-gather.11.cloned.1.call-start = ((), (), s32[]{:S(2)}) async-start(), calls=%async_computation.19 | async-start | bytes 1327104 | tf_op jit(solution)/shard_map/all_gather | solution.py:100
  189.6 38.8 %all-to-all-start.5 = ((bf16[2,96,4,192]{1,3,0,2:T(8,128)(2,1)}), bf16[2,96,4,192]{1,3,0,2:T(8,128)(2,1)}, u32[]{:S(2)}, u32[]{:S(2)}) async-start(bf16[2,96,4,192]{1,3,0,2:T(8,128)(2,1)} %copy.255), calls=%async_computation.5 | async-start | bytes 786432 | tf_op jit(solution)/shard_map/all_to_all | solution.py:90
  200.0 46.3 %collective-permute-start.8 = (bf16[256,768]{1,0:T(8,128)(2,1)}, bf16[256,768]{1,0:T(8,128)(2,1)}, u32[]{:S(2)}, u32[]{:S(2)}) collective-permute-start(bf16[256,768]{1,0:T(8,128)(2,1)} %add_convert_fusion.5), channel_id=1, source_target_pairs={{0,4},{4,0},{1,5},{5,1},{2,6},{6,2},{3,7},{7,3},{8,12},{12,8},{9,1... | collective-permute-start | bytes 1179656 | tf_op jit(solution)/shard_map/ppermute | solution.py:78
  232.5 62.3 %all-gather.13.cloned.1.call-start = ((), (), s32[]{:S(2)}) async-start(), calls=%async_computation.20 | async-start | bytes 2654208 | tf_op jit(solution)/shard_map/all_gather | solution.py:100
  232.6 20.7 %collective-permute-start.15 = (f32[128,768]{1,0:T(8,128)}, f32[128,768]{1,0:T(8,128)}, u32[]{:S(2)}, u32[]{:S(2)}) collective-permute-start(f32[128,768]{1,0:T(8,128)} %bitcast.410), channel_id=1, source_target_pairs={{0,0},{1,8},{2,4},{3,12},{4,1},{5,9},{6,5},{7,13},{8,2},{9,10},{10... | collective-permute-start | bytes 1179656 | tf_op jit(solution)/shard_map/ppermute | solution.py:158
  270.1 29.6 %collective-permute-start.11 = (bf16[256,768]{1,0:T(8,128)(2,1)}, bf16[256,768]{1,0:T(8,128)(2,1)}, u32[]{:S(2)}, u32[]{:S(2)}) collective-permute-start(bf16[256,768]{1,0:T(8,128)(2,1)} %add_convert_fusion.4), channel_id=1, source_target_pairs={{0,4},{4,0},{1,5},{5,1},{2,6},{6,2},{3,7},{7,3},{8,12},{12,8},{9,1... | collective-permute-start | bytes 1179656 | tf_op jit(solution)/shard_map/ppermute | solution.py:78
  278.5 23.5 %collective-permute-start.17 = (bf16[256,768]{1,0:T(8,128)(2,1)}, bf16[256,768]{1,0:T(8,128)(2,1)}, u32[]{:S(2)}, u32[]{:S(2)}) collective-permute-start(bf16[256,768]{1,0:T(8,128)(2,1)} %get-tuple-element.80), channel_id=1, source_target_pairs={{0,4},{4,0},{1,5},{5,1},{2,6},{6,2},{3,7},{7,3},{8,12},{12,8},{9,1... | collective-permute-start | bytes 1179656 | tf_op jit(solution)/shard_map/ppermute | solution.py:78
  335.2 24.4 %collective-permute-start.22 = (bf16[256,768]{1,0:T(8,128)(2,1)}, bf16[256,768]{1,0:T(8,128)(2,1)}, u32[]{:S(2)}, u32[]{:S(2)}) collective-permute-start(bf16[256,768]{1,0:T(8,128)(2,1)} %fusion.66), channel_id=1, source_target_pairs={{0,8},{8,0},{1,9},{9,1},{2,10},{10,2},{3,11},{11,3},{4,12},{12,4},... | collective-permute-start | bytes 1179656 | tf_op jit(solution)/shard_map/ppermute | solution.py:84
  343.7 109.0 %reduce-scatter.10.cloned.1.call-start = ((), (), s32[]{:S(2)}) async-start(), calls=%async_computation.23 | async-start | bytes 1327104 | tf_op jit(solution)/shard_map/reduce_scatter | solution.py:114
  359.5 134.5 %reduce-scatter.12.cloned.1.call-start = ((), (), s32[]{:S(2)}) async-start(), calls=%async_computation.24 | async-start | bytes 2654208 | tf_op jit(solution)/shard_map/reduce_scatter | solution.py:114
  423.5 137.5 %reduce-scatter.6.cloned.1.call-start = ((), (), s32[]{:S(2)}) async-start(), calls=%async_computation.21 | async-start | bytes 1327104 | tf_op jit(solution)/shard_map/reduce_scatter | solution.py:114
  435.5 196.9 %reduce-scatter.8.cloned.1.call-start = ((), (), s32[]{:S(2)}) async-start(), calls=%async_computation.22 | async-start | bytes 2654208 | tf_op jit(solution)/shard_map/reduce_scatter | solution.py:114
  496.6 138.4 %all-to-all-start.9 = ((bf16[3,4,96,192]{2,3,0,1:T(8,128)(2,1)}), bf16[3,4,96,192]{2,3,0,1:T(8,128)(2,1)S(1)}, u32[]{:S(2)}, u32[]{:S(2)}) async-start(bf16[3,4,96,192]{2,3,0,1:T(8,128)(2,1)} %copy.281), calls=%async_computation.13 | async-start | bytes 1179648 | tf_op jit(solution)/shard_map/all_to_all | solution.py:96
  638.5 66.0 %reduce-scatter.14.cloned.1.call-start = ((), (), s32[]{:S(2)}) async-start(), calls=%async_computation.25 | async-start | bytes 1474560 | tf_op jit(solution)/shard_map/reduce_scatter | solution.py:297
  674.9 67.0 %all-gather.15.cloned.1.call-start = ((), (), s32[]{:S(2)}) async-start(), calls=%async_computation.26 | async-start | bytes 1474560 | tf_op jit(solution)/shard_map/all_gather | solution.py:298
  692.3 19.5 %collective-permute-start.14 = (f32[128,768]{1,0:T(8,128)}, f32[128,768]{1,0:T(8,128)S(1)}, u32[]{:S(2)}, u32[]{:S(2)}) collective-permute-start(f32[128,768]{1,0:T(8,128)} %dynamic-slice_add_fusion.2), channel_id=1, source_target_pairs={{0,0},{8,1},{4,2},{12,3},{1,4},{9,5},{5,6},{13,7},{2,8},{10,9},{6,... | collective-permute-start | bytes 1179656 | tf_op jit(solution)/shard_map/ppermute | solution.py:207
  696.6 23.6 %collective-permute-start.27 = (bf16[256,768]{1,0:T(8,128)(2,1)S(1)}, bf16[256,768]{1,0:T(8,128)(2,1)S(1)}, u32[]{:S(2)}, u32[]{:S(2)}) collective-permute-start(bf16[256,768]{1,0:T(8,128)(2,1)S(1)} %slice.443), channel_id=1, source_target_pairs={{0,4},{4,0},{1,5},{5,1},{2,6},{6,2},{3,7},{7,3},{8,12},{12,8},{9,1... | collective-permute-start | bytes 1179656 | tf_op jit(solution)/shard_map/ppermute | solution.py:83
  771.6 142.7 %all-to-all-start.11 = ((bf16[8,1,96,768]{3,2,1,0:T(8,128)(2,1)}), bf16[8,1,96,768]{3,2,1,0:T(8,128)(2,1)S(1)}, u32[]{:S(2)}, u32[]{:S(2)}) async-start(bf16[8,1,96,768]{3,2,1,0:T(8,128)(2,1)} %bitcast.108), calls=%async_computation.16 | async-start | bytes 2359296 | tf_op jit(solution)/shard_map/all_to_all | solution.py:320
  775.4 135.5 %all-reduce.4.cloned.1.call-start = ((), (), s32[]{:S(2)}) async-start(), calls=%async_computation.27 | async-start | bytes 196608 | tf_op jit(solution)/shard_map/psum | solution.py:276
  778.3 135.9 %collective-permute-start.29 = (f32[128,768]{1,0:T(8,128)}, f32[128,768]{1,0:T(8,128)S(1)}, u32[]{:S(2)}, u32[]{:S(2)}) collective-permute-start(f32[128,768]{1,0:T(8,128)} %dynamic-slice_add_fusion), channel_id=1, source_target_pairs={{0,0},{8,1},{4,2},{12,3},{1,4},{9,5},{5,6},{13,7},{2,8},{10,9},{6,... | collective-permute-start | bytes 1179656 | tf_op jit(solution)/shard_map/ppermute | solution.py:207
  (166 other events, 1750.4 us)
Sparse Core Ops, SparseCore 0:
  20.1 46.4 all-gather.6
  109.0 50.7 all-gather.8
  183.2 38.8 all-gather.10
  242.3 52.5 all-gather.12
  359.6 62.8 reduce-scatter.9
  425.9 68.0 reduce-scatter.11
  498.0 62.9 reduce-scatter.5
  564.5 67.9 reduce-scatter.7
  675.0 29.5 reduce-scatter.13
  705.9 35.8 all-gather.14
  782.4 128.3 all-reduce.3

commit v2 on v1

--- a/solution.py
+++ b/solution.py
@@ -96,22 +96,180 @@
     return lax.all_to_all(split, GROUP, split_axis=1, concat_axis=3, tiled=True)[:, 0]
 
 
-def gather_mats(mats):
-    parts = lax.all_gather(mats, REPLICAS, axis=0, tiled=False)
+def rotate(block, axis, step):
+    size = lax.axis_size(axis)
+    return lax.ppermute(block, axis, [((i + step) % size, i) for i in range(size)])
+
+
+def pair_join(block, axis, dim):
+    other = lax.ppermute(block, axis, SWAP)
+    first = lax.axis_index(axis) == 0
+    return jnp.concatenate(
+        [jnp.where(first, block, other), jnp.where(first, other, block)], axis=dim
+    )
+
+
+def from_own(stack):
+    double = jnp.concatenate([stack, stack], axis=0)
+    return lax.dynamic_slice_in_dim(double, lax.axis_index("ctx"), stack.shape[0], axis=0)
+
+
+def to_absolute(stack):
+    count = stack.shape[0]
+    double = jnp.concatenate([stack, stack], axis=0)
+    return lax.dynamic_slice_in_dim(double, count - lax.axis_index("ctx"), count, axis=0)
+
+
+def out_moves():
+    last = lax.axis_size("ctx") - 1
+    size = last + 1
+    moves = []
+    for y in range(2):
+        for x in range(2):
+            for core in range(2):
+                moves.append(
+                    ((4 * y + 2 * x + core) * size + last, (4 * core + 2 * y + x) * size + last)
+                )
+    return moves
+
+
+def attn_piece(mat, piece):
+    half = mat.shape[1] // 2
+    core = lax.axis_index("jc")
+    mine = lax.dynamic_slice_in_dim(mat, core * half, half, axis=1)
+    give = lax.dynamic_slice_in_dim(mat, (1 - core) * half, half, axis=1)
+    got = lax.ppermute(give, "jc", SWAP)
+    rows = jnp.concatenate(
+        [jnp.where(core == 0, mine, got), jnp.where(core == 0, got, mine)], axis=0
+    )
+    rows = lax.ppermute(rows, EVERY, out_moves())
+    return jnp.where(lax.axis_index("ctx") == lax.axis_size("ctx") - 1, rows, piece)
+
+
+def out_back(piece):
+    core = lax.axis_index("jc")
+    rows = lax.ppermute(piece, EVERY, [(b, a) for a, b in out_moves()])
+    half = rows.shape[0] // 2
+    mine = lax.dynamic_slice_in_dim(rows, core * half, half, axis=0)
+    give = lax.dynamic_slice_in_dim(rows, (1 - core) * half, half, axis=0)
+    got = lax.ppermute(give, "jc", SWAP)
+    return jnp.concatenate(
+        [jnp.where(core == 0, mine, got), jnp.where(core == 0, got, mine)], axis=1
+    )
+
+
+def gather_weights(low):
+    if lax.axis_size("g") != 2:
+        return gather_weights_wide(low)
+    layers = low.shape[0]
+    first = to_group(low[0, 0:1])
+    rest = to_group(jnp.concatenate([low[0, 1:3], low[1:].reshape(-1, *low.shape[2:])]))
+    pieces = [attn_piece(low[0, 0], first[0].T), jnp.swapaxes(rest[0:2], 1, 2)]
+    for layer in range(1, layers):
+        base = 3 * layer - 1
+        pieces.append(attn_piece(low[layer, 0], rest[base].T))
+        pieces.append(jnp.swapaxes(rest[base + 1 : base + 3], 1, 2))
+    full = []
+    for number, piece in enumerate(pieces):
+        if number:
+            piece, full[-1][1:] = lax.optimization_barrier((piece, full[-1][1:]))
+        full.append([piece] + [rotate(piece, "ctx", step) for step in range(1, 4)])
+    result = []
+    for layer in range(layers):
+        attn, mlp = [
+            jnp.stack([pair_join(block, "g", block.ndim - 1) for block in blocks])
+            for blocks in full[2 * layer : 2 * layer + 2]
+        ]
+        result.append((to_absolute(attn), mlp[:, 0].reshape(D, D), mlp[:, 1].reshape(D, D)))
+    return result
+
+
+def gather_weights_wide(low):
+    result = []
+    for layer in range(low.shape[0]):
+        mats = to_group(low[layer])
+        parts = lax.all_gather(mats, REPLICAS, axis=0, tiled=False)
+        parts = parts.reshape(lax.axis_size("g"), -1, *mats.shape)
+        full = [parts[:, :, item].transpose(1, 3, 0, 2).reshape(D, D) for item in range(3)]
+        w_o = lax.all_to_all(
+            full[0][3 * COLS :].T.reshape(TP, COLS, COLS),
+            GROUP,
+            split_axis=0,
+            concat_axis=2,
+            tiled=True,
+        )
+        attn = jnp.concatenate([full[0][: 3 * COLS].reshape(3, COLS, D), w_o], axis=0)
+        result.append((attn, full[1], full[2]))
+    return result
+
+
+def replica_sum(blocks, ahead):
+    half = D // 2
+    group = lax.axis_index("g")
+    last = blocks.ndim - 1
+    mine = lax.dynamic_slice_in_dim(blocks, group * half, half, axis=last)
+    give = lax.dynamic_slice_in_dim(blocks, (1 - group) * half, half, axis=last)
+    summed = mine.astype(f32) + lax.ppermute(give.astype(bf16), "g", SWAP).astype(f32)
+    if not ahead:
+        summed = from_own(summed)
+    total = summed[0]
+    for step in range(1, 4):
+        total = total + rotate(summed[step].astype(bf16), "ctx", -step).astype(f32)
+    return total
+
+
+def scatter_attn(grads):
+    if lax.axis_size("g") != 2:
+        g_wo = lax.all_to_all(
+            grads[3].reshape(COLS, TP, COLS), GROUP, split_axis=1, concat_axis=0, tiled=True
+        )[:, 0]
+        mats = jnp.concatenate([grads[:3], g_wo.T[None]], axis=0)
+        return scatter_wide(mats[:, None])[0]
+    part = replica_sum(grads, False).astype(bf16)
+    columns = from_group(part.T[None])[0]
+    last = lax.axis_index("ctx") == lax.axis_size("ctx") - 1
+    return jnp.where(last, out_back(part), columns).astype(f32)
+
+
+def scatter_mlp(grads):
+    if lax.axis_size("g") != 2:
+        return scatter_wide(grads)
+    part = replica_sum(grads, True).astype(bf16)
+    return from_group(jnp.swapaxes(part, 1, 2)).astype(f32)
+
+
+def scatter_wide(mats):
     groups = lax.axis_size("g")
-    parts = parts.reshape(groups, -1, *mats.shape)
-    return [
-        parts[:, :, item].transpose(0, 2, 1, 3).reshape(D, -1) for item in range(mats.shape[0])
-    ]
-
-
-def scatter_mats(mats):
-    groups = lax.axis_size("g")
-    stack = jnp.stack([mat.astype(bf16) for mat in mats])
-    count, rows, blocks, width = stack.shape
-    stack = stack.reshape(count, groups, rows // groups, blocks, width).transpose(1, 3, 0, 2, 4)
-    stack = stack.reshape(groups * blocks, count, rows // groups, width)
-    return lax.psum_scatter(stack, REPLICAS, scatter_dimension=0, tiled=True)[0]
+    blocks, count, width, depth = mats.shape
+    stack = mats.astype(bf16).reshape(blocks, count, width, groups, depth // groups)
+    stack = stack.transpose(3, 0, 1, 4, 2).reshape(groups * blocks, count, -1, width)
+    part = lax.psum_scatter(stack, REPLICAS, scatter_dimension=0, tiled=True)[0]
+    return from_group(part).astype(f32)
+
+
+def gather_vectors(vectors):
+    low = vectors.astype(bf16)
+    low = pair_join(pair_join(low, "jc", 2), "jx", 2)
+    if lax.axis_size("g") == 2:
+        low = pair_join(low, "g", 2)
+    else:
+        low = lax.all_gather(low, "g", axis=2, tiled=True)
+    stack = jnp.stack([low] + [rotate(low, "ctx", step) for step in range(1, 4)])
+    return to_absolute(stack).transpose(1, 0, 2, 3).reshape(low.shape[0], -1, D).astype(f32)
+
+
+def sum_vectors(terms):
+    if lax.axis_size("g") == 2:
+        terms = terms + lax.ppermute(terms, "g", SWAP)
+    else:
+        terms = lax.psum(terms, "g")
+    layers, rows, width = terms.shape
+    blocks = from_own(terms.reshape(layers, 4, rows // 4, width).transpose(1, 0, 2, 3))
+    total = blocks[0]
+    for step in range(1, 4):
+        total = total + rotate(blocks[step], "ctx", -step)
+    total = total + lax.ppermute(total, "jc", SWAP)
+    return total + lax.ppermute(total, "jx", SWAP)
 
 
 def local(hidden_in, segments, out_grad, weights, vectors, mat_momentum, vec_first, vec_second):
@@ -135,27 +293,16 @@
     axes = ("jx", "jc", "ctx")
 
     def x_join(block):
-        other = lax.ppermute(block, "jx", SWAP)
-        first = jnp.where(x_index == 0, block, other)
-        second = jnp.where(x_index == 0, other, block)
-        return jnp.concatenate([first, second], axis=0)
+        return pair_join(block, "jx", 0)
 
     seg_row = jnp.pad(segments.astype(f32), ((0, 7), (0, D - seq_len)))
     moved = lax.ppermute(jnp.concatenate([hidden_in[0], seg_row], axis=0), axes, to_seq)
     hidden = x_join(moved[:tokens_dev])
     segment_row = moved[tokens_dev, :seq_len]
-    vec_parts = lax.all_gather(vectors.astype(bf16), EVERY, axis=0, tiled=False)
-    vec_rows = (
-        vec_parts.reshape(dp_size, ctx_size, LAYERS, vectors.shape[1], vectors.shape[2])
-        .transpose(2, 1, 3, 0, 4)
-        .reshape(LAYERS, 12, D)
-        .astype(f32)
-    )
-    low = weights.astype(bf16)
-    swapped = [
-        [to_group(low[layer, 0:1]), to_group(low[layer, 1:3])] for layer in range(LAYERS)
-    ]
+    vec_rows = gather_vectors(vectors)
+    gathered = gather_weights(weights.astype(bf16))
     grad_hidden = x_join(lax.ppermute(out_grad[0], axes, to_seq))
+    relative = lax.axis_size("g") == 2
 
     order = [c_index * half, (1 - c_index) * half]
     pos = jnp.concatenate([start + jnp.arange(half) for start in order])
@@ -170,19 +317,14 @@
 
     stored = []
     for layer in range(LAYERS):
-        vec = vec_rows[layer]
-        (attn_w,) = gather_mats(swapped[layer][0])
-        w_up, w_down = gather_mats(swapped[layer][1])
-        w_qkv = attn_w[:, : 3 * COLS]
-        w_o = lax.all_to_all(
-            attn_w[:, 3 * COLS :].reshape(TP, COLS, COLS),
-            GROUP,
-            split_axis=0,
-            concat_axis=2,
-            tiled=True,
-        )[0]
+        vec = [vec_rows[layer, row : row + 1] for row in range(8)]
+        attn_w, w_up, w_down = gathered[layer]
+        w_qkv = attn_w[:3].reshape(3 * COLS, D)
+        w_o = attn_w[3]
+        b_up = mine(vec_rows[layer, 8:12])
+        b_up = (from_own(b_up) if relative else b_up).reshape(1, D)
         a_all = core_gather(layer_norm(hidden, vec[0], vec[1]).astype(bf16))
-        proj = dot(a_all, w_qkv)
+        proj = dot_trans(a_all, w_qkv)
         q = heads_of((proj[:, :COLS] + mine(vec[4])).astype(bf16))
         k = heads_of(proj[:, COLS : 2 * COLS].astype(bf16))
         v = heads_of((proj[:, 2 * COLS :] + mine(vec[5])).astype(bf16))
@@ -195,12 +337,12 @@
         o = merge_heads(bdot(prob, v, 2, 1)).astype(bf16)
         middle = hidden + (group_sum(dot(o, w_o)) + vec[6])
         c_all = core_gather(layer_norm(middle, vec[2], vec[3]).astype(bf16))
-        preact = dot(c_all, w_up) + mine(vec[8:12]).reshape(-1)
+        preact = dot_trans(c_all, w_up) + b_up
         act = smooth_unit(preact).astype(bf16)
         stored.append(
             (hidden, middle, a_all, q, k, v, log_total, o, c_all, preact, act, w_qkv, w_o, w_up, w_down)
         )
-        hidden = middle + (group_sum(dot_trans(act, w_down)) + vec[7])
+        hidden = middle + (group_sum(dot(act, w_down)) + vec[7])
 
     def send_back(rows):
         block = lax.dynamic_slice_in_dim(rows, x_index * tokens_dev, tokens_dev, axis=0)
@@ -215,13 +357,13 @@
         (h_in, middle, a_all, q, k, v, log_total, o, c_all, preact, act, w_qkv, w_o, w_up, w_down) = stored[
             layer
         ]
-        vec = vec_rows[layer]
+        vec = [vec_rows[layer, row : row + 1] for row in range(8)]
         gy = grad_hidden.astype(bf16)
         gy_all = core_gather(gy)
-        gu = dot(gy_all, w_down)
+        gu = dot_trans(gy_all, w_down)
         unused, gelu_pull = jax.vjp(smooth_unit, preact)
         gz = gelu_pull(gu)[0].astype(bf16)
-        gc = group_sum(dot_trans(gz, w_up))
+        gc = group_sum(dot(gz, w_up))
         unused, pull_two = jax.vjp(layer_norm, middle, vec[2], vec[3])
         g_mid, g_gain_two, g_shift_two = pull_two(gc)
         gm = grad_hidden + g_mid
@@ -237,52 +379,49 @@
         gk = merge_heads(bdot(g_scores, q, 1, 1) * HEAD ** (-0.5)).astype(bf16)
         gv = merge_heads(bdot(prob_low, go, 1, 1)).astype(bf16)
         g_qkv = jnp.concatenate([gq, gk, gv], axis=1)
-        ga = group_sum(dot_trans(g_qkv, w_qkv))
+        ga = group_sum(dot(g_qkv, w_qkv))
         unused, pull_one = jax.vjp(layer_norm, h_in, vec[0], vec[1])
         g_in, g_gain_one, g_shift_one = pull_one(ga)
         grad_hidden = gm + g_in
 
-        mlp = [
-            dot_tokens(c_all, gz).reshape(D, ctx_size, COLS),
-            dot_tokens(gy_all, act).reshape(D, ctx_size, COLS),
-        ]
-        mlp_part = scatter_mats(mlp)
-        g_wo = lax.all_to_all(
-            dot_tokens(o, gb_all).astype(bf16).reshape(COLS, TP, COLS),
-            GROUP,
-            split_axis=1,
-            concat_axis=0,
-            tiled=True,
-        )
-        g_attn = jnp.concatenate(
-            [dot_tokens(a_all, g_qkv).astype(bf16).reshape(D, 3, COLS), g_wo], axis=1
-        )
-        attn_part = scatter_mats([g_attn])
-        mat_list[layer] = from_group(jnp.concatenate([attn_part, mlp_part], axis=0)).astype(f32)
+        mlp_grad = scatter_mlp(
+            jnp.stack(
+                [
+                    dot_tokens(gz, c_all).reshape(ctx_size, COLS, D),
+                    dot_tokens(act, gy_all).reshape(ctx_size, COLS, D),
+                ],
+                axis=1,
+            )
+        )
+        attn_grad = scatter_attn(
+            jnp.concatenate([dot_tokens(g_qkv, a_all), dot_tokens(o, gb_all)]).reshape(4, COLS, D)
+        )
+        mat_list[layer] = jnp.concatenate([attn_grad[None], mlp_grad], axis=0)
 
         def place(values):
-            wide = jnp.zeros(values.shape[:-1] + (D,), f32)
-            return lax.dynamic_update_slice_in_dim(wide, values, t_index * COLS, axis=-1)
+            wide = jnp.zeros((values.shape[0], D), f32)
+            return lax.dynamic_update_slice_in_dim(wide, values, t_index * COLS, axis=1)
 
         def token_sum(values):
-            return jnp.sum(values, axis=0, dtype=f32)
-
-        b_qv = place(jnp.stack([token_sum(gq), token_sum(gv)]))
-        b_up = place(token_sum(gz).reshape(ctx_size, COLS))
-        shared = once * jnp.stack(
+            return jnp.sum(values, axis=0, keepdims=True, dtype=f32)
+
+        sum_qkv = token_sum(g_qkv)
+        sum_up = token_sum(gz).reshape(ctx_size, COLS)
+        placed = place(
+            jnp.concatenate(
+                [sum_qkv[:, :COLS], sum_qkv[:, 2 * COLS :], to_absolute(sum_up) if relative else sum_up]
+            )
+        )
+        shared = once * jnp.concatenate(
             [g_gain_one, g_shift_one, g_gain_two, g_shift_two, token_sum(gb), token_sum(gy)]
         )
-        vec_term = jnp.concatenate([shared[:4], b_qv, shared[4:], b_up], axis=0)
-        vec_sum = lax.psum(vec_term, EVERY)
-        vec_list[layer] = lax.dynamic_slice(
-            vec_sum,
-            (z_index * vectors.shape[1], dp_index * vectors.shape[2]),
-            (vectors.shape[1], vectors.shape[2]),
-        )
+        vec_list[layer] = jnp.concatenate([shared[:4], placed[:2], shared[4:], placed[2:]], axis=0)
     input_grad = send_back(grad_hidden)
 
     grad_mats = jnp.stack(mat_list)
-    grad_vecs = jnp.stack(vec_list)
+    grad_vecs = lax.dynamic_slice_in_dim(
+        sum_vectors(jnp.stack(vec_list)), dp_index * vectors.shape[2], vectors.shape[2], axis=2
+    )
     moment_new = momentum_decay * mat_momentum + grad_mats
     update_in = grad_mats + momentum_decay * moment_new
     item_count = 3 * LAYERS

time: 934 us -> 659 us (0.71)
  waiting for transfers between devices: 427 us -> 255 us
  blocking collectives: 113 us -> 0 us
  starting transfers between devices: 67.9 us -> 162 us
  local copies, waits for them, and re-layouts: 151 us -> 65.3 us
  matrix products: 81.9 us -> 67 us
  other arithmetic: 66.5 us -> 78.4 us
    reduce_scatter x4 -> x0, waiting for transfers between devices: 171 us -> none  [scatter_mats(): return lax.psum_scatter(stack, REPLICAS, scatter_dimension=0, tiled=True)[0]]
    ppermute x2 -> x66, waiting for transfers between devices: 7.13 us -> 156 us  [the longest x30 65.7 us: rotate(): lax.ppermute(block, axis, [((i + step) % size, i) for i in range(size)])]
    psum x1 -> x0, waiting for transfers between devices: 131 us -> none  [local(): vec_sum = lax.psum(vec_term, EVERY)]
    ppermute x2 -> x66, starting transfers between devices: 1.17 us -> 113 us  [the longest x30 65.6 us: rotate(): lax.ppermute(block, axis, [((i + step) % size, i) for i in range(size)])]
    all_gather x1 -> x0, blocking collectives: 75.6 us -> none  [local(): vec_parts = lax.all_gather(vectors.astype(bf16), EVERY, axis=0, tiled=False)]
    all_gather x4 -> x0, waiting for transfers between devices: 43.4 us -> none  [gather_mats(): parts = lax.all_gather(mats, REPLICAS, axis=0, tiled=False)]
    all_to_all x3 -> x0, blocking collectives: 37.2 us -> none  [the longest x1 19.2 us: local(): lax.all_to_all(slots[:, None], DP, split_axis=0, concat_axis=1, tiled=True)]
    another operation x26 -> x11, local copies, waits for them, and re-layouts: 30.6 us -> 6.22 us  [the longest x2 2.56 us: from_group(): split = mats.reshape(count, TP, rows // TP, width)]
  transfers between devices with their start and end apart: 50 -> 104, of which waited for: 26 -> 42; matrix products, arithmetic and copies ran while one was open for 24% -> 25% of each run, Pallas kernels for 0% -> 0%
where the time goes in v2:
time: 659 us; the launch traced here: 647 us
  waiting for transfers between devices  255 us (39%)
  starting transfers between devices  162 us (25%)
  other arithmetic  78.4 us (12%)
  matrix products  67 us (10%)
  local copies, waits for them, and re-layouts  65.3 us (10%)
  between operations  18.2 us (3%)
    ppermute x30, waiting for transfers between devices, rotate(): lax.ppermute(block, axis, [((i + step) % size, i) for i in range(size)])  65.7 us
    ppermute x30, starting transfers between devices, rotate(): lax.ppermute(block, axis, [((i + step) % size, i) for i in range(size)])  65.6 us
    ppermute x8, waiting for transfers between devices, group_sum(): return mine + lax.ppermute(mine.astype(bf16), 'jx', SWAP).astype(f32)  50.7 us
    ppermute x4, waiting for transfers between devices, replica_sum(): lax.ppermute(give.astype(bf16), 'g', SWAP).astype(f32)  41.6 us
    dot_general x15, matrix products, dot(): return jnp.dot(operand, other, preferred_element_type=f32)  38 us
    ppermute x21, waiting for transfers between devices, pair_join(): other = lax.ppermute(block, axis, SWAP)  37.4 us
    ppermute x21, starting transfers between devices, pair_join(): other = lax.ppermute(block, axis, SWAP)  32.6 us
    all_gather x1, waiting for transfers between devices, local(): lax.all_gather(gram_part, 'ctx', axis=0, tiled=True).astype(f32)  18.1 us
  transfers between devices with their start and end apart: 104, of which 42 were waited for; matrix products, arithmetic and copies ran while one was open for 25% of the time, Pallas kernels for 0%

profile of v2, /device:TPU:0, one launch (start us, length us, event | category | flops | bytes accessed | tf_op | source)
XLA Modules:
  0.0 646.9 jit_solution(6221378467341570541)
XLA Ops:
  32.2 5.9 collective-permute-start.5
  40.5 16.8 %collective-permute-start.6 = (bf16[2,3,768]{2,0,1:T(2,128)(2,1)S(1)}, bf16[2,3,768]{2,0,1:T(2,128)(2,1)S(1)}, u32[]{:S(2)}, u32[]{:S(2)}) collective-permute-start(bf16[2,3,768]{2,0,1:T(2,128)(2,1)S(1)} %pad_maximum_fusion.41), channel_id=1, source_target_pairs={{2,0},{3,1},{0,2},{1,3},{6,4},{7,5},{4,6},{5,7},{10,8},{11,9},{8,1... | collective-permute-start | bytes 27656 | tf_op jit(solution)/shard_map/ppermute | solution.py:101
  85.8 7.1 %collective-permute-done.13 = bf16[192,384]{1,0:T(8,128)(2,1)} collective-permute-done((bf16[192,384]{1,0:T(8,128)(2,1)S(1)}, bf16[192,384]{1,0:T(8,128)(2,1)}, u32[]{:S(2)}, u32[]{:S(2)}) %collective-permute-start.13) | collective-permute-done | bytes 147488 | tf_op jit(solution)/shard_map/ppermute | solution.py:101
  135.1 8.4 %collective-permute-done.35 = bf16[192,384]{1,0:T(8,128)(2,1)S(1)} collective-permute-done((bf16[192,384]{1,0:T(8,128)(2,1)S(1)}, bf16[192,384]{1,0:T(8,128)(2,1)S(1)}, u32[]{:S(2)}, u32[]{:S(2)}) %collective-permute-start.35) | collective-permute-done | bytes 147488 | tf_op jit(solution)/shard_map/ppermute | solution.py:101
  147.3 14.3 %collective-permute-done.37 = bf16[192,384]{1,0:T(8,128)(2,1)S(1)} collective-permute-done((bf16[192,384]{1,0:T(8,128)(2,1)S(1)}, bf16[192,384]{1,0:T(8,128)(2,1)S(1)}, u32[]{:S(2)}, u32[]{:S(2)}) %collective-permute-start.37) | collective-permute-done | bytes 147488 | tf_op jit(solution)/shard_map/ppermute | solution.py:105
  181.1 8.3 %collective-permute-done.19 = bf16[256,768]{1,0:T(8,128)(2,1)S(1)} collective-permute-done((bf16[256,768]{1,0:T(8,128)(2,1)S(1)}, bf16[256,768]{1,0:T(8,128)(2,1)S(1)}, u32[]{:S(2)}, u32[]{:S(2)}) %collective-permute-start.19) | collective-permute-done | bytes 393248 | tf_op jit(solution)/shard_map/ppermute | solution.py:84
  197.2 10.7 %collective-permute-done.31 = bf16[256,768]{1,0:T(8,128)(2,1)S(1)} collective-permute-done((bf16[256,768]{1,0:T(8,128)(2,1)S(1)}, bf16[256,768]{1,0:T(8,128)(2,1)S(1)}, u32[]{:S(2)}, u32[]{:S(2)}) %collective-permute-start.31) | collective-permute-done | bytes 393248 | tf_op jit(solution)/shard_map/ppermute | solution.py:84
  219.5 6.2 collective-permute-done.47
  241.7 9.0 %fusion.205 = f32[512,768]{1,0:T(8,128)S(1)} fusion(bf16[512,768]{1,0:T(8,128)(2,1)S(1)} %get-tuple-element.202, bf16[768,768]{1,0:T(8,128)(2,1)S(1)} %bitcast.475), kind=kOutput, calls=%fused_computation.515 | convolution fusion | flops 603979776 | bytes 3538944 | tf_op jit(solution)/shard_map/dot_general | solution.py:52
  259.6 8.6 %collective-permute-done.57 = bf16[256,768]{1,0:T(8,128)(2,1)S(1)} collective-permute-done((bf16[256,768]{1,0:T(8,128)(2,1)S(1)}, bf16[256,768]{1,0:T(8,128)(2,1)S(1)}, u32[]{:S(2)}, u32[]{:S(2)}) %collective-permute-start.57) | collective-permute-done | bytes 393248 | tf_op jit(solution)/shard_map/ppermute | solution.py:84
  273.0 13.3 %collective-permute-done.84 = bf16[4,2,192,384]{3,2,1,0:T(8,128)(2,1)S(1)} collective-permute-done((bf16[4,2,192,384]{3,2,1,0:T(8,128)(2,1)S(1)}, bf16[4,2,192,384]{3,2,1,0:T(8,128)(2,1)S(1)}, u32[]{:S(2)}, u32[]{:S(2)}) %collective-permute-start.84) | collective-permute-done | bytes 1179680 | tf_op jit(solution)/shard_map/ppermute | solution.py:212
  313.6 17.9 %collective-permute-done.86 = bf16[2,192,384]{2,1,0:T(8,128)(2,1)} collective-permute-done((bf16[2,192,384]{2,1,0:T(8,128)(2,1)}, bf16[2,192,384]{2,1,0:T(8,128)(2,1)}, u32[]{:S(2)}, u32[]{:S(2)}) %collective-permute-start.86) | collective-permute-done | bytes 294944 | tf_op jit(solution)/shard_map/ppermute | solution.py:101
  358.2 6.1 collective-permute-done.80
  389.2 5.8 collective-permute-done.63
  410.3 19.6 %collective-permute-done.74 = bf16[4,2,192,384]{3,2,1,0:T(8,128)(2,1)S(1)} collective-permute-done((bf16[4,2,192,384]{3,2,1,0:T(8,128)(2,1)S(1)}, bf16[4,2,192,384]{3,2,1,0:T(8,128)(2,1)S(1)}, u32[]{:S(2)}, u32[]{:S(2)}) %collective-permute-start.74) | collective-permute-done | bytes 1179680 | tf_op jit(solution)/shard_map/ppermute | solution.py:212
  433.5 8.7 %collective-permute-done.68 = bf16[4,192,384]{2,1,0:T(8,128)(2,1)S(1)} collective-permute-done((bf16[4,192,384]{2,1,0:T(8,128)(2,1)S(1)}, bf16[4,192,384]{2,1,0:T(8,128)(2,1)S(1)}, u32[]{:S(2)}, u32[]{:S(2)}) %collective-permute-start.68) | collective-permute-done | bytes 589856 | tf_op jit(solution)/shard_map/ppermute | solution.py:212
  444.4 6.7 %collective-permute-start.69 = (bf16[192,384]{1,0:T(8,128)(2,1)}, bf16[192,384]{1,0:T(8,128)(2,1)}, u32[]{:S(2)}, u32[]{:S(2)}) collective-permute-start(bf16[192,384]{1,0:T(8,128)(2,1)} %get-tuple-element.124), channel_id=1, source_target_pairs={{3,0},{0,1},{1,2},{2,3},{7,4},{4,5},{5,6},{6,7},{11,8},{8,9},{9,10... | collective-permute-start | bytes 442376 | tf_op jit(solution)/shard_map/ppermute | solution.py:101
  451.1 13.6 %collective-permute-done.76 = bf16[2,192,384]{2,1,0:T(8,128)(2,1)S(1)} collective-permute-done((bf16[2,192,384]{2,1,0:T(8,128)(2,1)S(1)}, bf16[2,192,384]{2,1,0:T(8,128)(2,1)S(1)}, u32[]{:S(2)}, u32[]{:S(2)}) %collective-permute-start.76) | collective-permute-done | bytes 294944 | tf_op jit(solution)/shard_map/ppermute | solution.py:101
  498.6 12.7 %all-to-all-done.6 = bf16[8,1,96,768]{3,2,1,0:T(8,128)(2,1)S(1)} async-done(((bf16[8,1,96,768]{3,2,1,0:T(8,128)(2,1)}), bf16[8,1,96,768]{3,2,1,0:T(8,128)(2,1)S(1)}, u32[]{:S(2)}, u32[]{:S(2)}) %all-to-all-start.6) | async-done | bytes 1179680 | tf_op jit(solution)/shard_map/all_to_all | solution.py:432
  518.1 8.2 %collective-permute-done.51 = bf16[256,768]{1,0:T(8,128)(2,1)S(1)} collective-permute-done((bf16[256,768]{1,0:T(8,128)(2,1)}, bf16[256,768]{1,0:T(8,128)(2,1)S(1)}, u32[]{:S(2)}, u32[]{:S(2)}) %collective-permute-start.51) | collective-permute-done | bytes 393248 | tf_op jit(solution)/shard_map/ppermute | solution.py:84
  541.5 6.5 %reduce-scatter.2.cloned.1.call-done = bf16[192,768]{1,0:T(8,128)(2,1)} async-done(((bf16[768,768]{1,0:T(8,128)(2,1)}), bf16[192,768]{1,0:T(8,128)(2,1)}) %reduce-scatter.2.cloned.1.call-update) | async-done | bytes 294928 | tf_op jit(solution)/shard_map/reduce_scatter | solution.py:436
  563.6 18.1 %all-gather.2.cloned.1.call-done = bf16[768,768]{1,0:T(8,128)(2,1)} async-done(((bf16[192,768]{1,0:T(8,128)(2,1)}), bf16[768,768]{1,0:T(8,128)(2,1)}) %all-gather.2.cloned.1.call-update) | async-done | bytes 1179664 | tf_op jit(solution)/shard_map/all_gather | solution.py:437
  601.3 7.2 %add_convert_fusion = bf16[768,768]{1,0:T(8,128)(2,1)} fusion(bf16[768,768]{1,0:T(8,128)(2,1)} %multiply_convert_fusion.2, f32[768,768]{1,0:T(8,128)} %fusion.14), kind=kOutput, calls=%fused_computation.47 | convolution fusion | flops 1817247744 | bytes 4718592 | tf_op jit(solution)/shard_map/dot_general | solution.py:52
  625.3 9.7 %collective-permute-done.93 = f32[2,3,768]{2,0,1:T(2,128)S(1)} collective-permute-done((f32[2,3,768]{2,0,1:T(2,128)S(1)}, f32[2,3,768]{2,0,1:T(2,128)S(1)}, u32[]{:S(2)}, u32[]{:S(2)}) %collective-permute-start.93) | collective-permute-done | bytes 18464 | tf_op jit(solution)/shard_map/ppermute | solution.py:272
  (859 shorter events, 379.5 us)
Async XLA Ops:
  10.0 55.5 %collective-permute-start.22 = (bf16[96,384]{1,0:T(8,128)(2,1)S(1)}, bf16[96,384]{1,0:T(8,128)(2,1)S(1)}, u32[]{:S(2)}, u32[]{:S(2)}) collective-permute-start(bf16[96,384]{1,0:T(8,128)(2,1)S(1)} %dynamic-slice_bitcast_fusion.6), channel_id=1, source_target_pairs={{0,4},{4,0},{1,5},{5,1},{2,6},{6,2},{3,7},{7,3},{8,12},{12,8},{9,1... | collective-permute-start | bytes 221192 | tf_op jit(solution)/shard_map/ppermute | solution.py:141
  10.1 55.3 %collective-permute-start.9 = (bf16[96,384]{1,0:T(8,128)(2,1)S(1)}, bf16[96,384]{1,0:T(8,128)(2,1)S(1)}, u32[]{:S(2)}, u32[]{:S(2)}) collective-permute-start(bf16[96,384]{1,0:T(8,128)(2,1)S(1)} %dynamic-slice_bitcast_fusion.7), channel_id=1, source_target_pairs={{0,4},{4,0},{1,5},{5,1},{2,6},{6,2},{3,7},{7,3},{8,12},{12,8},{9,1... | collective-permute-start | bytes 221192 | tf_op jit(solution)/shard_map/ppermute | solution.py:141
  11.5 55.5 %all-to-all-start = ((bf16[1,96,4,192]{1,3,0,2:T(8,128)(2,1)}), bf16[1,96,4,192]{1,3,0,2:T(8,128)(2,1)S(1)}, u32[]{:S(2)}, u32[]{:S(2)}) async-start(bf16[1,96,4,192]{1,3,0,2:T(8,128)(2,1)} %bitcast.12), calls=%async_computation | async-start | bytes 393216 | tf_op jit(solution)/shard_map/all_to_all | solution.py:90
  16.1 64.8 %collective-permute-start = (f32[136,768]{1,0:T(8,128)}, f32[136,768]{1,0:T(8,128)S(1)}, u32[]{:S(2)}, u32[]{:S(2)}) collective-permute-start(f32[136,768]{1,0:T(8,128)} %select_maximum_fusion), channel_id=1, source_target_pairs={{0,0},{1,8},{2,4},{3,12},{4,1},{5,9},{6,5},{7,13},{8,2},{9,10},{10... | collective-permute-start | bytes 1253384 | tf_op jit(solution)/shard_map/ppermute | solution.py:299
  17.8 62.4 %collective-permute-start.53 = (f32[128,768]{1,0:T(8,128)}, f32[128,768]{1,0:T(8,128)}, u32[]{:S(2)}, u32[]{:S(2)}) collective-permute-start(f32[128,768]{1,0:T(8,128)} %bitcast.69), channel_id=1, source_target_pairs={{0,0},{1,8},{2,4},{3,12},{4,1},{5,9},{6,5},{7,13},{8,2},{9,10},{10... | collective-permute-start | bytes 1179656 | tf_op jit(solution)/shard_map/ppermute | solution.py:304
  80.9 39.9 %collective-permute-start.54 = (f32[128,768]{1,0:T(8,128)}, f32[128,768]{1,0:T(8,128)S(1)}, u32[]{:S(2)}, u32[]{:S(2)}) collective-permute-start(f32[128,768]{1,0:T(8,128)} %collective-permute-done.53), channel_id=1, source_target_pairs={{0,8},{8,0},{1,9},{9,1},{2,10},{10,2},{3,11},{11,3},{4,12},{12,4},... | collective-permute-start | bytes 1179656 | tf_op jit(solution)/shard_map/ppermute | solution.py:105
  84.9 39.9 %collective-permute-start.1 = (f32[128,768]{1,0:T(8,128)S(1)}, f32[128,768]{1,0:T(8,128)}, u32[]{:S(2)}, u32[]{:S(2)}) collective-permute-start(f32[128,768]{1,0:T(8,128)S(1)} %slice.405), channel_id=1, source_target_pairs={{0,8},{8,0},{1,9},{9,1},{2,10},{10,2},{3,11},{11,3},{4,12},{12,4},... | collective-permute-start | bytes 1179656 | tf_op jit(solution)/shard_map/ppermute | solution.py:105
  92.9 33.8 %collective-permute-start.24 = (bf16[2,192,384]{2,1,0:T(8,128)(2,1)S(1)}, bf16[2,192,384]{2,1,0:T(8,128)(2,1)}, u32[]{:S(2)}, u32[]{:S(2)}) collective-permute-start(bf16[2,192,384]{2,1,0:T(8,128)(2,1)S(1)} %bitcast.476), channel_id=1, source_target_pairs={{1,0},{2,1},{3,2},{0,3},{5,4},{6,5},{7,6},{4,7},{9,8},{10,9},{11,1... | collective-permute-start | bytes 884744 | tf_op jit(solution)/shard_map/ppermute | solution.py:101
  93.6 33.1 %collective-permute-start.25 = (bf16[2,192,384]{2,1,0:T(8,128)(2,1)S(1)}, bf16[2,192,384]{2,1,0:T(8,128)(2,1)}, u32[]{:S(2)}, u32[]{:S(2)}) collective-permute-start(bf16[2,192,384]{2,1,0:T(8,128)(2,1)S(1)} %bitcast.477), channel_id=1, source_target_pairs={{2,0},{3,1},{0,2},{1,3},{6,4},{7,5},{4,6},{5,7},{10,8},{11,9},{8,1... | collective-permute-start | bytes 884744 | tf_op jit(solution)/shard_map/ppermute | solution.py:101
  126.6 41.1 %collective-permute-start.8 = (bf16[256,768]{1,0:T(8,128)(2,1)S(1)}, bf16[256,768]{1,0:T(8,128)(2,1)S(1)}, u32[]{:S(2)}, u32[]{:S(2)}) collective-permute-start(bf16[256,768]{1,0:T(8,128)(2,1)S(1)} %add_convert_fusion.7), channel_id=1, source_target_pairs={{0,4},{4,0},{1,5},{5,1},{2,6},{6,2},{3,7},{7,3},{8,12},{12,8},{9,1... | collective-permute-start | bytes 1179656 | tf_op jit(solution)/shard_map/ppermute | solution.py:78
  133.3 40.4 %collective-permute-start.29 = (bf16[2,192,384]{2,1,0:T(8,128)(2,1)S(1)}, bf16[2,192,384]{2,1,0:T(8,128)(2,1)S(1)}, u32[]{:S(2)}, u32[]{:S(2)}) collective-permute-start(bf16[2,192,384]{2,1,0:T(8,128)(2,1)S(1)} %collective-permute-done.26), channel_id=1, source_target_pairs={{0,16},{16,0},{1,17},{17,1},{2,18},{18,2},{3,19},{19,3},{4,20},{20... | collective-permute-start | bytes 884744 | tf_op jit(solution)/shard_map/ppermute | solution.py:105
  145.2 33.1 %collective-permute-start.27 = (bf16[2,192,384]{2,1,0:T(8,128)(2,1)}, bf16[2,192,384]{2,1,0:T(8,128)(2,1)S(1)}, u32[]{:S(2)}, u32[]{:S(2)}) collective-permute-start(bf16[2,192,384]{2,1,0:T(8,128)(2,1)} %collective-permute-done.24), channel_id=1, source_target_pairs={{0,16},{16,0},{1,17},{17,1},{2,18},{18,2},{3,19},{19,3},{4,20},{20... | collective-permute-start | bytes 884744 | tf_op jit(solution)/shard_map/ppermute | solution.py:105
  166.7 42.3 %collective-permute-start.48 = (bf16[2,192,384]{2,1,0:T(8,128)(2,1)}, bf16[2,192,384]{2,1,0:T(8,128)(2,1)S(1)}, u32[]{:S(2)}, u32[]{:S(2)}) collective-permute-start(bf16[2,192,384]{2,1,0:T(8,128)(2,1)} %bitcast.46), channel_id=1, source_target_pairs={{3,0},{0,1},{1,2},{2,3},{7,4},{4,5},{5,6},{6,7},{11,8},{8,9},{9,10... | collective-permute-start | bytes 884744 | tf_op jit(solution)/shard_map/ppermute | solution.py:101
  167.7 41.8 %collective-permute-start.46 = (bf16[2,192,384]{2,1,0:T(8,128)(2,1)}, bf16[2,192,384]{2,1,0:T(8,128)(2,1)S(1)}, u32[]{:S(2)}, u32[]{:S(2)}) collective-permute-start(bf16[2,192,384]{2,1,0:T(8,128)(2,1)} %bitcast.46), channel_id=1, source_target_pairs={{2,0},{3,1},{0,2},{1,3},{6,4},{7,5},{4,6},{5,7},{10,8},{11,9},{8,1... | collective-permute-start | bytes 884744 | tf_op jit(solution)/shard_map/ppermute | solution.py:101
  173.9 37.1 %collective-permute-start.44 = (bf16[2,192,384]{2,1,0:T(8,128)(2,1)}, bf16[2,192,384]{2,1,0:T(8,128)(2,1)S(1)}, u32[]{:S(2)}, u32[]{:S(2)}) collective-permute-start(bf16[2,192,384]{2,1,0:T(8,128)(2,1)} %bitcast.46), channel_id=1, source_target_pairs={{1,0},{2,1},{3,2},{0,3},{5,4},{6,5},{7,6},{4,7},{9,8},{10,9},{11,1... | collective-permute-start | bytes 884744 | tf_op jit(solution)/shard_map/ppermute | solution.py:101
  209.0 30.5 %collective-permute-start.55 = (bf16[256,768]{1,0:T(8,128)(2,1)S(1)}, bf16[256,768]{1,0:T(8,128)(2,1)S(1)}, u32[]{:S(2)}, u32[]{:S(2)}) collective-permute-start(bf16[256,768]{1,0:T(8,128)(2,1)S(1)} %get-tuple-element.65), channel_id=1, source_target_pairs={{0,4},{4,0},{1,5},{5,1},{2,6},{6,2},{3,7},{7,3},{8,12},{12,8},{9,1... | collective-permute-start | bytes 1179656 | tf_op jit(solution)/shard_map/ppermute | solution.py:78
  301.1 40.7 %collective-permute-start.78 = (bf16[4,192,384]{2,1,0:T(8,128)(2,1)}, bf16[4,192,384]{2,1,0:T(8,128)(2,1)}, u32[]{:S(2)}, u32[]{:S(2)}) collective-permute-start(bf16[4,192,384]{2,1,0:T(8,128)(2,1)} %dynamic-slice_convert_fusion), channel_id=1, source_target_pairs={{0,16},{16,0},{1,17},{17,1},{2,18},{18,2},{3,19},{19,3},{4,20},{20... | collective-permute-start | bytes 1769480 | tf_op jit(solution)/shard_map/ppermute | solution.py:212
  308.9 34.7 %collective-permute-start.60 = (bf16[256,768]{1,0:T(8,128)(2,1)}, bf16[256,768]{1,0:T(8,128)(2,1)}, u32[]{:S(2)}, u32[]{:S(2)}) collective-permute-start(bf16[256,768]{1,0:T(8,128)(2,1)} %fusion.86), channel_id=1, source_target_pairs={{0,8},{8,0},{1,9},{9,1},{2,10},{10,2},{3,11},{11,3},{4,12},{12,4},... | collective-permute-start | bytes 1179656 | tf_op jit(solution)/shard_map/ppermute | solution.py:84
  408.9 33.3 %collective-permute-start.68 = (bf16[4,192,384]{2,1,0:T(8,128)(2,1)S(1)}, bf16[4,192,384]{2,1,0:T(8,128)(2,1)S(1)}, u32[]{:S(2)}, u32[]{:S(2)}) collective-permute-start(bf16[4,192,384]{2,1,0:T(8,128)(2,1)S(1)} %dynamic-slice_convert_fusion.1), channel_id=1, source_target_pairs={{0,16},{16,0},{1,17},{17,1},{2,18},{18,2},{3,19},{19,3},{4,20},{20... | collective-permute-start | bytes 1769480 | tf_op jit(solution)/shard_map/ppermute | solution.py:212
  430.9 33.8 %collective-permute-start.76 = (bf16[2,192,384]{2,1,0:T(8,128)(2,1)S(1)}, bf16[2,192,384]{2,1,0:T(8,128)(2,1)S(1)}, u32[]{:S(2)}, u32[]{:S(2)}) collective-permute-start(bf16[2,192,384]{2,1,0:T(8,128)(2,1)S(1)} %get-tuple-element.108), channel_id=1, source_target_pairs={{2,0},{3,1},{0,2},{1,3},{6,4},{7,5},{4,6},{5,7},{10,8},{11,9},{8,1... | collective-permute-start | bytes 884744 | tf_op jit(solution)/shard_map/ppermute | solution.py:101
  431.6 33.1 %collective-permute-start.75 = (bf16[2,192,384]{2,1,0:T(8,128)(2,1)S(1)}, bf16[2,192,384]{2,1,0:T(8,128)(2,1)S(1)}, u32[]{:S(2)}, u32[]{:S(2)}) collective-permute-start(bf16[2,192,384]{2,1,0:T(8,128)(2,1)S(1)} %get-tuple-element.106), channel_id=1, source_target_pairs={{3,0},{0,1},{1,2},{2,3},{7,4},{4,5},{5,6},{6,7},{11,8},{8,9},{9,10... | collective-permute-start | bytes 884744 | tf_op jit(solution)/shard_map/ppermute | solution.py:101
  494.5 53.5 %reduce-scatter.2.cloned.1.call-start = ((), (), s32[]{:S(2)}) async-start(), calls=%async_computation.9 | async-start | bytes 1474560 | tf_op jit(solution)/shard_map/reduce_scatter | solution.py:436
  514.2 67.5 %all-gather.2.cloned.1.call-start = ((), (), s32[]{:S(2)}) async-start(), calls=%async_computation.10 | async-start | bytes 1474560 | tf_op jit(solution)/shard_map/all_gather | solution.py:437
  527.0 98.2 %collective-permute-start.52 = (f32[128,768]{1,0:T(8,128)}, f32[128,768]{1,0:T(8,128)}, u32[]{:S(2)}, u32[]{:S(2)}) collective-permute-start(f32[128,768]{1,0:T(8,128)} %dynamic-slice_add_fusion.2), channel_id=1, source_target_pairs={{0,0},{8,1},{4,2},{12,3},{1,4},{9,5},{5,6},{13,7},{2,8},{10,9},{6,... | collective-permute-start | bytes 1179656 | tf_op jit(solution)/shard_map/ppermute | solution.py:349
  (251 other events, 2252.7 us)
Sparse Core Ops, SparseCore 0:
  514.3 33.6 reduce-scatter.1
  549.5 32.1 all-gather.1

commit v3 on v2

--- a/solution.py
+++ b/solution.py
@@ -3,6 +3,8 @@
 import jax
 import jax.numpy as jnp
 from jax import lax
+from jax.experimental import pallas as pl
+from jax.experimental.pallas import tpu as pltpu
 from jax.sharding import Mesh, PartitionSpec as P
 
 D = 768
@@ -109,15 +111,24 @@
     )
 
 
+def after(value, *others):
+    return lax.optimization_barrier((value, *others))[0]
+
+
+def roll_blocks(stack, sign):
+    place = lax.axis_index("ctx")
+    for bit in (1, 2):
+        moved = jnp.roll(stack, sign * bit, axis=0)
+        stack = jnp.where((place & bit) != 0, moved, stack)
+    return stack
+
+
 def from_own(stack):
-    double = jnp.concatenate([stack, stack], axis=0)
-    return lax.dynamic_slice_in_dim(double, lax.axis_index("ctx"), stack.shape[0], axis=0)
+    return roll_blocks(stack, -1)
 
 
 def to_absolute(stack):
-    count = stack.shape[0]
-    double = jnp.concatenate([stack, stack], axis=0)
-    return lax.dynamic_slice_in_dim(double, count - lax.axis_index("ctx"), count, axis=0)
+    return roll_blocks(stack, 1)
 
 
 def out_moves():
@@ -158,30 +169,40 @@
     )
 
 
-def gather_weights(low):
-    if lax.axis_size("g") != 2:
-        return gather_weights_wide(low)
-    layers = low.shape[0]
+def pack_pieces(low):
     first = to_group(low[0, 0:1])
-    rest = to_group(jnp.concatenate([low[0, 1:3], low[1:].reshape(-1, *low.shape[2:])]))
-    pieces = [attn_piece(low[0, 0], first[0].T), jnp.swapaxes(rest[0:2], 1, 2)]
-    for layer in range(1, layers):
+    rest = to_group(after(jnp.concatenate([low[0, 1:3], low[1:].reshape(-1, *low.shape[2:])]), first))
+    pieces = [(attn_piece(low[0, 0], first[0].T), jnp.swapaxes(rest[0:2], 1, 2))]
+    for layer in range(1, low.shape[0]):
         base = 3 * layer - 1
-        pieces.append(attn_piece(low[layer, 0], rest[base].T))
-        pieces.append(jnp.swapaxes(rest[base + 1 : base + 3], 1, 2))
-    full = []
-    for number, piece in enumerate(pieces):
-        if number:
-            piece, full[-1][1:] = lax.optimization_barrier((piece, full[-1][1:]))
-        full.append([piece] + [rotate(piece, "ctx", step) for step in range(1, 4)])
-    result = []
-    for layer in range(layers):
-        attn, mlp = [
-            jnp.stack([pair_join(block, "g", block.ndim - 1) for block in blocks])
-            for blocks in full[2 * layer : 2 * layer + 2]
-        ]
-        result.append((to_absolute(attn), mlp[:, 0].reshape(D, D), mlp[:, 1].reshape(D, D)))
-    return result
+        pieces.append(
+            (attn_piece(low[layer, 0], rest[base].T), jnp.swapaxes(rest[base + 1 : base + 3], 1, 2))
+        )
+    return pieces
+
+
+def ctx_gather(piece):
+    return [piece] + [rotate(piece, "ctx", step) for step in (1, 3, 2)]
+
+
+def group_join(blocks, pieces):
+    own, near, back, far = blocks
+    ordered = [own, near, far, back]
+    if pieces == 1:
+        other = lax.ppermute(jnp.stack(ordered), "g", SWAP)
+    else:
+        others = [lax.ppermute(block, "g", SWAP) for block in (own, near)]
+        others.append(lax.ppermute(jnp.stack([far, back]), "g", SWAP))
+        other = jnp.concatenate([others[0][None], others[1][None], others[2]])
+    mine = jnp.stack(ordered)
+    first = lax.axis_index("g") == 0
+    return jnp.concatenate(
+        [jnp.where(first, mine, other), jnp.where(first, other, mine)], axis=mine.ndim - 1
+    )
+
+
+def mlp_mats(stack):
+    return stack[:, 0].reshape(D, D), stack[:, 1].reshape(D, D)
 
 
 def gather_weights_wide(low):
@@ -203,38 +224,29 @@
     return result
 
 
-def replica_sum(blocks, ahead):
+def half_sum(blocks):
     half = D // 2
     group = lax.axis_index("g")
     last = blocks.ndim - 1
     mine = lax.dynamic_slice_in_dim(blocks, group * half, half, axis=last)
     give = lax.dynamic_slice_in_dim(blocks, (1 - group) * half, half, axis=last)
-    summed = mine.astype(f32) + lax.ppermute(give.astype(bf16), "g", SWAP).astype(f32)
-    if not ahead:
-        summed = from_own(summed)
-    total = summed[0]
-    for step in range(1, 4):
-        total = total + rotate(summed[step].astype(bf16), "ctx", -step).astype(f32)
+    return mine.astype(f32) + lax.ppermute(give.astype(bf16), "g", SWAP).astype(f32)
+
+
+def ctx_sum(blocks):
+    total = blocks[0]
+    for step in (1, 3, 2):
+        total = total + rotate(blocks[step].astype(bf16), "ctx", -step).astype(f32)
     return total
 
 
-def scatter_attn(grads):
-    if lax.axis_size("g") != 2:
-        g_wo = lax.all_to_all(
-            grads[3].reshape(COLS, TP, COLS), GROUP, split_axis=1, concat_axis=0, tiled=True
-        )[:, 0]
-        mats = jnp.concatenate([grads[:3], g_wo.T[None]], axis=0)
-        return scatter_wide(mats[:, None])[0]
-    part = replica_sum(grads, False).astype(bf16)
+def attn_rows(part):
     columns = from_group(part.T[None])[0]
     last = lax.axis_index("ctx") == lax.axis_size("ctx") - 1
     return jnp.where(last, out_back(part), columns).astype(f32)
 
 
-def scatter_mlp(grads):
-    if lax.axis_size("g") != 2:
-        return scatter_wide(grads)
-    part = replica_sum(grads, True).astype(bf16)
+def mlp_rows(part):
     return from_group(jnp.swapaxes(part, 1, 2)).astype(f32)
 
 
@@ -249,13 +261,13 @@
 
 def gather_vectors(vectors):
     low = vectors.astype(bf16)
-    low = pair_join(pair_join(low, "jc", 2), "jx", 2)
+    stack = jnp.stack([low] + [rotate(low, "ctx", step) for step in range(1, 4)])
+    stack = pair_join(pair_join(to_absolute(stack), "jc", 3), "jx", 3)
     if lax.axis_size("g") == 2:
-        low = pair_join(low, "g", 2)
+        stack = pair_join(stack, "g", 3)
     else:
-        low = lax.all_gather(low, "g", axis=2, tiled=True)
-    stack = jnp.stack([low] + [rotate(low, "ctx", step) for step in range(1, 4)])
-    return to_absolute(stack).transpose(1, 0, 2, 3).reshape(low.shape[0], -1, D).astype(f32)
+        stack = lax.all_gather(stack, "g", axis=3, tiled=True)
+    return stack.transpose(1, 0, 2, 3).reshape(low.shape[0], -1, D).astype(f32)
 
 
 def sum_vectors(terms):
@@ -272,6 +284,101 @@
     return total + lax.ppermute(total, "jx", SWAP)
 
 
+def orthogonalize_kernel(x_ref, gram_ref, out_ref, base_ref, work_ref, mat_ref, low_ref):
+    size = x_ref.shape[0]
+    rows = 256
+
+    def each(body):
+        for start in range(0, size, rows):
+            body(pl.ds(start, rows))
+
+    def polynomial():
+        low_ref[...] = base_ref[...].astype(bf16)
+
+        def body(block):
+            square = dot(low_ref[block, :], low_ref[...])
+            mat_ref[block, :] = (
+                quintic_two * base_ref[block, :] + quintic_three * square
+            ).astype(bf16)
+
+        each(body)
+
+    def two_part(left, right):
+        high = left.astype(bf16)
+        rest = (left - high.astype(f32)).astype(bf16)
+        return dot(high, right) + dot(rest, right)
+
+    trace = jnp.zeros((1, 1), f32)
+    for start in range(0, size, rows):
+        block = gram_ref[pl.ds(start, rows), pl.ds(start, rows)]
+        line = lax.broadcasted_iota(jnp.int32, (rows, rows), 0)
+        column = lax.broadcasted_iota(jnp.int32, (rows, rows), 1)
+        trace = trace + jnp.sum(jnp.where(line == column, block, 0.0), keepdims=True)
+    scale = 1.0 / (jnp.sqrt(trace) + 1e-07)
+    base_ref[...] = gram_ref[...] * (scale * scale)
+    polynomial()
+
+    def first_step(block):
+        value = quintic_one * x_ref[block, :].astype(f32) + dot(mat_ref[block, :], x_ref[...])
+        out_ref[block, :] = (scale * value).astype(bf16)
+        work_ref[block, :] = quintic_one * base_ref[block, :] + two_part(
+            base_ref[block, :], mat_ref[...]
+        )
+
+    each(first_step)
+    turned = work_ref[...].T
+    work_ref[...] = turned
+
+    def gram_step(block):
+        base_ref[block, :] = quintic_one * work_ref[block, :] + two_part(
+            work_ref[block, :], mat_ref[...]
+        )
+
+    each(gram_step)
+    polynomial()
+    low_ref[...] = out_ref[...]
+
+    def second_step(block):
+        value = quintic_one * low_ref[block, :].astype(f32) + dot(mat_ref[block, :], low_ref[...])
+        out_ref[block, :] = value.astype(bf16)
+
+    each(second_step)
+
+
+def orthogonalize(matrix, gram):
+    size = matrix.shape[0]
+    return pl.pallas_call(
+        orthogonalize_kernel,
+        out_shape=jax.ShapeDtypeStruct(matrix.shape, bf16),
+        in_specs=[pl.BlockSpec(memory_space=pltpu.VMEM)] * 2,
+        out_specs=pl.BlockSpec(memory_space=pltpu.VMEM),
+        scratch_shapes=[
+            pltpu.VMEM((size, size), f32),
+            pltpu.VMEM((size, size), f32),
+            pltpu.VMEM((size, size), bf16),
+            pltpu.VMEM((size, size), bf16),
+        ],
+        compiler_params=pltpu.CompilerParams(vmem_limit_bytes=48 * 1024 * 1024),
+    )(matrix, gram)
+
+
+def ctx_gram(gram):
+    size = lax.axis_size("ctx")
+
+    def shift(block, step):
+        moves = [((i + step) % size, i) for i in range(size)]
+        return lax.ppermute(block, ("jc", "ctx"), moves)
+
+    rows = gram.shape[0] // size
+    blocks = from_own(gram.astype(bf16).reshape(size, rows, -1))
+    total = blocks[0].astype(f32)
+    for step in (1, 3, 2):
+        total = total + shift(blocks[step], -step).astype(f32)
+    low = total.astype(bf16)
+    full = [low] + [shift(low, step) for step in range(1, size)]
+    return to_absolute(jnp.stack(full)).reshape(gram.shape).astype(f32)
+
+
 def local(hidden_in, segments, out_grad, weights, vectors, mat_momentum, vec_first, vec_second):
     tokens_dev = hidden_in.shape[1]
     seq_len = segments.shape[1]
@@ -295,14 +402,21 @@
     def x_join(block):
         return pair_join(block, "jx", 0)
 
+    vec_rows = gather_vectors(vectors)
     seg_row = jnp.pad(segments.astype(f32), ((0, 7), (0, D - seq_len)))
     moved = lax.ppermute(jnp.concatenate([hidden_in[0], seg_row], axis=0), axes, to_seq)
     hidden = x_join(moved[:tokens_dev])
     segment_row = moved[tokens_dev, :seq_len]
-    vec_rows = gather_vectors(vectors)
-    gathered = gather_weights(weights.astype(bf16))
-    grad_hidden = x_join(lax.ppermute(out_grad[0], axes, to_seq))
     relative = lax.axis_size("g") == 2
+    low = weights.astype(bf16)
+    gathered = [None] * LAYERS
+    if relative:
+        pieces = pack_pieces(low)
+        attn_blocks = ctx_gather(pieces[0][0])
+        mlp_blocks = ctx_gather(after(pieces[0][1], *attn_blocks[1:]))
+        gathered[0] = (to_absolute(group_join(attn_blocks, 3)), mlp_blocks)
+    else:
+        gathered = gather_weights_wide(low)
 
     order = [c_index * half, (1 - c_index) * half]
     pos = jnp.concatenate([start + jnp.arange(half) for start in order])
@@ -318,7 +432,7 @@
     stored = []
     for layer in range(LAYERS):
         vec = [vec_rows[layer, row : row + 1] for row in range(8)]
-        attn_w, w_up, w_down = gathered[layer]
+        attn_w = gathered[layer][0]
         w_qkv = attn_w[:3].reshape(3 * COLS, D)
         w_o = attn_w[3]
         b_up = mine(vec_rows[layer, 8:12])
@@ -335,10 +449,20 @@
         prob = (unnormed / total).astype(bf16)
         log_total = row_max + jnp.log(total)
         o = merge_heads(bdot(prob, v, 2, 1)).astype(bf16)
+        following = layer + 1 < LAYERS
+        if relative and following:
+            attn_blocks = ctx_gather(after(pieces[layer + 1][0], o))
         middle = hidden + (group_sum(dot(o, w_o)) + vec[6])
         c_all = core_gather(layer_norm(middle, vec[2], vec[3]).astype(bf16))
+        if relative:
+            w_up, w_down = mlp_mats(group_join(gathered[layer][1], 1))
+        else:
+            w_up, w_down = gathered[layer][1:]
         preact = dot_trans(c_all, w_up) + b_up
         act = smooth_unit(preact).astype(bf16)
+        if relative and following:
+            mlp_blocks = ctx_gather(after(pieces[layer + 1][1], act, *attn_blocks[1:]))
+            gathered[layer + 1] = (to_absolute(group_join(attn_blocks, 1)), mlp_blocks)
         stored.append(
             (hidden, middle, a_all, q, k, v, log_total, o, c_all, preact, act, w_qkv, w_o, w_up, w_down)
         )
@@ -349,10 +473,14 @@
         return lax.ppermute(block, axes, from_seq)
 
     hidden_out = send_back(hidden)
+    moved_grad = lax.ppermute(after(out_grad[0], stored[-1][7]), axes, to_seq)
+    grad_hidden = x_join(moved_grad)
 
     once = jnp.where(x_index == 0, 1.0, 0.0).astype(f32)
     mat_list = [None] * LAYERS
     vec_list = [None] * LAYERS
+    parts = [None] * LAYERS
+    attn_half = attn_part = up_part = down_part = None
     for layer in reversed(range(LAYERS)):
         (h_in, middle, a_all, q, k, v, log_total, o, c_all, preact, act, w_qkv, w_o, w_up, w_down) = stored[
             layer
@@ -360,14 +488,29 @@
         vec = [vec_rows[layer, row : row + 1] for row in range(8)]
         gy = grad_hidden.astype(bf16)
         gy_all = core_gather(gy)
+        down_grad = dot_tokens(act, gy_all).reshape(ctx_size, COLS, D)
+        if relative:
+            down_half = half_sum(down_grad)
         gu = dot_trans(gy_all, w_down)
         unused, gelu_pull = jax.vjp(smooth_unit, preact)
         gz = gelu_pull(gu)[0].astype(bf16)
+        if relative and attn_half is not None:
+            gz, attn_half, up_part = lax.optimization_barrier((gz, attn_half, up_part))
+            attn_part = ctx_sum(from_own(attn_half))
+        up_grad = dot_tokens(gz, c_all).reshape(ctx_size, COLS, D)
+        if relative:
+            up_half = half_sum(up_grad)
         gc = group_sum(dot(gz, w_up))
         unused, pull_two = jax.vjp(layer_norm, middle, vec[2], vec[3])
         g_mid, g_gain_two, g_shift_two = pull_two(gc)
         gm = grad_hidden + g_mid
         gb = gm.astype(bf16)
+        if relative:
+            if attn_part is not None:
+                gb, attn_part = lax.optimization_barrier((gb, attn_part))
+                parts[layer + 1] = (attn_part, down_part, up_part)
+            gb, down_half = lax.optimization_barrier((gb, down_half))
+            down_part = ctx_sum(down_half)
         gb_all = core_gather(gb)
         go = heads_of(dot_trans(gb_all, w_o).astype(bf16))
         prob = jnp.exp(scores_of(q, k) - log_total)
@@ -379,24 +522,26 @@
         gk = merge_heads(bdot(g_scores, q, 1, 1) * HEAD ** (-0.5)).astype(bf16)
         gv = merge_heads(bdot(prob_low, go, 1, 1)).astype(bf16)
         g_qkv = jnp.concatenate([gq, gk, gv], axis=1)
+        if relative:
+            g_qkv, up_half = lax.optimization_barrier((g_qkv, up_half))
+            up_part = ctx_sum(up_half)
+        attn_grad = jnp.concatenate([dot_tokens(g_qkv, a_all), dot_tokens(o, gb_all)])
+        attn_grad = attn_grad.reshape(4, COLS, D)
+        if relative:
+            attn_half = half_sum(attn_grad)
         ga = group_sum(dot(g_qkv, w_qkv))
+        if relative:
+            ga, down_part = lax.optimization_barrier((ga, down_part))
         unused, pull_one = jax.vjp(layer_norm, h_in, vec[0], vec[1])
         g_in, g_gain_one, g_shift_one = pull_one(ga)
         grad_hidden = gm + g_in
 
-        mlp_grad = scatter_mlp(
-            jnp.stack(
-                [
-                    dot_tokens(gz, c_all).reshape(ctx_size, COLS, D),
-                    dot_tokens(act, gy_all).reshape(ctx_size, COLS, D),
-                ],
-                axis=1,
-            )
-        )
-        attn_grad = scatter_attn(
-            jnp.concatenate([dot_tokens(g_qkv, a_all), dot_tokens(o, gb_all)]).reshape(4, COLS, D)
-        )
-        mat_list[layer] = jnp.concatenate([attn_grad[None], mlp_grad], axis=0)
+        if not relative:
+            g_wo = lax.all_to_all(
+                attn_grad[3].reshape(COLS, TP, COLS), GROUP, split_axis=1, concat_axis=0, tiled=True
+            )[:, 0]
+            attn_grad = jnp.concatenate([attn_grad[:3], g_wo.T[None]], axis=0)
+            mat_list[layer] = scatter_wide(jnp.stack([attn_grad, up_grad, down_grad], axis=1))
 
         def place(values):
             wide = jnp.zeros((values.shape[0], D), f32)
@@ -418,55 +563,51 @@
         vec_list[layer] = jnp.concatenate([shared[:4], placed[:2], shared[4:], placed[2:]], axis=0)
     input_grad = send_back(grad_hidden)
 
-    grad_mats = jnp.stack(mat_list)
+    if relative:
+        parts[0] = (ctx_sum(from_own(attn_half)), down_part, up_part)
+        for layer in range(LAYERS):
+            attn_part, down_part, up_part = [part.astype(bf16) for part in parts[layer]]
+            mat_list[layer] = jnp.concatenate(
+                [attn_rows(attn_part)[None], mlp_rows(jnp.stack([up_part, down_part]))]
+            )
     grad_vecs = lax.dynamic_slice_in_dim(
         sum_vectors(jnp.stack(vec_list)), dp_index * vectors.shape[2], vectors.shape[2], axis=2
     )
-    moment_new = momentum_decay * mat_momentum + grad_mats
-    update_in = grad_mats + momentum_decay * moment_new
-    item_count = 3 * LAYERS
-    cols_dev = update_in.shape[3]
-    items = update_in.astype(bf16).reshape(item_count, dp_rows, cols_dev)
-    copies = -(-dp_size // item_count)
-    slots = jnp.tile(items, (copies, 1, 1))[0:dp_size]
+    cols_dev = weights.shape[3]
+    grad_list, moment_list, low_list = [], [], []
+    for layer in range(LAYERS):
+        for item in range(3):
+            grad = mat_list[layer][item]
+            moment = momentum_decay * mat_momentum[layer, item] + grad
+            grad_list.append(grad)
+            moment_list.append(moment)
+            low_list.append((grad + momentum_decay * moment).astype(bf16))
+    wide = [item for item in range(3 * LAYERS) if item % 3]
+    squares = [item for item in range(3, 3 * LAYERS, 3)]
+    table = []
+    for number in range(4):
+        table += [wide[number], squares[number % len(squares)]]
+    table = (table * (-(-dp_size // 8)))[:dp_size]
+    slots = jnp.stack([low_list[item] for item in table])
     received = lax.all_to_all(slots[:, None], DP, split_axis=0, concat_axis=1, tiled=True)
     current = received.reshape(dp_size * dp_rows, cols_dev)
-    square = (dp_index % item_count) % 3 == 0
     gram_local = dot_trans(current, current)
-    gram_part = lax.psum_scatter(gram_local.astype(bf16), "ctx", scatter_dimension=0, tiled=True)
-    gram_total = lax.all_gather(gram_part, "ctx", axis=0, tiled=True).astype(f32)
-    gram = jnp.where(square, gram_local, gram_total)
-    scale = 1.0 / (jnp.sqrt(jnp.trace(gram)) + 1e-07)
-    base = gram * (scale * scale)
-    base_low = base.astype(bf16)
-    bmat = (quintic_two * base + quintic_three * dot(base_low, base_low)).astype(bf16)
-    current = (scale * (quintic_one * current.astype(f32) + dot(bmat, current))).astype(bf16)
-
-    def two_part(left, right):
-        high = right.astype(bf16)
-        rest = (right - high.astype(f32)).astype(bf16)
-        return dot(left, high) + dot(left, rest)
-
-    turned = two_part(bmat, base)
-    base = (
-        quintic_one * quintic_one * base
-        + quintic_one * (turned + turned.T)
-        + two_part(bmat, turned.T)
-    )
-    base_low = base.astype(bf16)
-    bmat = (quintic_two * base + quintic_three * dot(base_low, base_low)).astype(bf16)
-    current = (quintic_one * current.astype(f32) + dot(bmat, current)).astype(bf16)
+    gram = jnp.where(c_index == 0, ctx_gram(gram_local), gram_local)
+    ortho_mine = orthogonalize(current, gram)
     returned = lax.all_to_all(
-        current.reshape(dp_size, 1, dp_rows, cols_dev), DP, split_axis=0, concat_axis=1, tiled=True
+        ortho_mine.reshape(dp_size, 1, dp_rows, cols_dev),
+        DP,
+        split_axis=0,
+        concat_axis=1,
+        tiled=True,
     )[0]
-    spread = dp_size // item_count
-    chosen = [
-        lax.dynamic_index_in_dim(
-            returned, item + item_count * (dp_index % spread), 0, keepdims=False
-        )
-        for item in range(item_count)
-    ]
-    ortho = jnp.stack(chosen).reshape(LAYERS, 3, dp_rows, cols_dev).astype(f32)
+    first_full = lax.all_gather(low_list[0], DP, axis=0, tiled=True)
+    first_ortho = orthogonalize(first_full, dot_trans(first_full, first_full))
+    ortho_list = [lax.dynamic_slice_in_dim(first_ortho, dp_index * dp_rows, dp_rows, axis=0)]
+    ortho_list += [returned[table.index(item)] for item in range(1, 3 * LAYERS)]
+    ortho = jnp.stack(ortho_list).reshape(LAYERS, 3, dp_rows, cols_dev).astype(f32)
+    grad_mats = jnp.stack(grad_list).reshape(weights.shape)
+    moment_new = jnp.stack(moment_list).reshape(weights.shape)
     factor = jnp.array([0.2 * math.sqrt(D), 0.2 * math.sqrt(FF), 0.2 * math.sqrt(FF)], f32)
     weights_new = weights * (1.0 - matrix_rate * matrix_decay) - matrix_rate * (
         ortho * factor[None, :, None, None]

time: 659 us -> 682 us (1.035)
  waiting for transfers between devices: 255 us -> 171 us
  local copies, waits for them, and re-layouts: 65.3 us -> 123 us
  starting transfers between devices: 162 us -> 193 us
  other arithmetic: 78.4 us -> 103 us
  matrix products: 67 us -> 44.3 us
  Pallas kernels: 0 us -> 17.1 us
    ppermute x5 -> x19, waiting for transfers between devices: 41.6 us -> 83.3 us  [the longest x3 39.8 us: group_join(): other = lax.ppermute(jnp.stack(ordered), 'g', SWAP)]
    ppermute x8, waiting for transfers between devices: 50.7 us -> 12.1 us  [group_sum(): return mine + lax.ppermute(mine.astype(bf16), 'jx', SWAP).astype(f32)]
    ppermute x21 -> x5, waiting for transfers between devices: 37.4 us -> 7.64 us  [pair_join(): other = lax.ppermute(block, axis, SWAP)]
    dot_general x15 -> x8, matrix products: 38 us -> 9.81 us  [dot(): return jnp.dot(operand, other, preferred_element_type=f32)]
    ppermute x30 -> x36, waiting for transfers between devices: 65.7 us -> 40.6 us  [rotate(): lax.ppermute(block, axis, [((i + step) % size, i) for i in range(size)])]
    ppermute x5 -> x19, starting transfers between devices: 9.51 us -> 34 us  [the longest x6 19.7 us: shift(): return lax.ppermute(block, ('jc', 'ctx'), moves)]
    ppermute x21 -> x5, starting transfers between devices: 32.6 us -> 11.5 us  [pair_join(): other = lax.ppermute(block, axis, SWAP)]
    slice x13 -> x43, local copies, waits for them, and re-layouts: 3.29 us -> 23.1 us  [the longest x28 6.36 us: roll_blocks(): moved = jnp.roll(stack, sign * bit, axis=0)]
  transfers between devices with their start and end apart: 104 -> 107, of which waited for: 42 -> 35; matrix products, arithmetic and copies ran while one was open for 25% -> 31% of each run, Pallas kernels for 0% -> 3%
where the time goes in v3:
time: 682 us; the launch traced here: 669 us
  starting transfers between devices  193 us (28%)
  waiting for transfers between devices  171 us (25%)
  local copies, waits for them, and re-layouts  123 us (18%)
  other arithmetic  103 us (15%)
  matrix products  44.3 us (6%)
  between operations  17.6 us (3%)
  Pallas kernels  17.1 us (3%)
    ppermute x36, starting transfers between devices, rotate(): lax.ppermute(block, axis, [((i + step) % size, i) for i in range(size)])  74.9 us
    ppermute x36, waiting for transfers between devices, rotate(): lax.ppermute(block, axis, [((i + step) % size, i) for i in range(size)])  40.6 us
    ppermute x3, waiting for transfers between devices, group_join(): other = lax.ppermute(jnp.stack(ordered), 'g', SWAP)  39.8 us
    unnamed x367, local copies, waits for them, and re-layouts  30.7 us
    ppermute x6, waiting for transfers between devices, half_sum(): lax.ppermute(give.astype(bf16), 'g', SWAP).astype(f32)  24 us
    ppermute x6, starting transfers between devices, shift(): return lax.ppermute(block, ('jc', 'ctx'), moves)  19.7 us
    dot_general x10, matrix products, dot_trans(): lax.dot_general(operand, other, (((1,), (1,)), ((), ())), preferred_eleme...  19.3 us
    pallas_call x2, Pallas kernels, orthogonalize(): pl.pallas_call(orthogonalize_kernel, out_shape=jax.ShapeDtypeStruct(matri...  17.1 us
  transfers between devices with their start and end apart: 107, of which 35 were waited for; matrix products, arithmetic and copies ran while one was open for 31% of the time, Pallas kernels for 3%

profile of v3, /device:TPU:0, one launch (start us, length us, event | category | flops | bytes accessed | tf_op | source)
XLA Modules:
  0.0 668.6 jit_solution(6488752445883393392)
XLA Ops:
  40.2 9.2 %all-to-all-start.1 = ((bf16[5,96,4,192]{1,3,0,2:T(8,128)(2,1)}), bf16[5,96,4,192]{1,3,0,2:T(8,128)(2,1)}, u32[]{:S(2)}, u32[]{:S(2)}) async-start(bf16[5,96,4,192]{1,3,0,2:T(8,128)(2,1)} %copy.116), calls=%async_computation.1 | async-start | bytes 1966080 | tf_op jit(solution)/shard_map/all_to_all | solution.py:92
  58.5 4.7 collective-permute-done.12
  69.1 7.1 %collective-permute-done.15 = bf16[192,384]{1,0:T(8,128)(2,1)S(1)} collective-permute-done((bf16[192,384]{1,0:T(8,128)(2,1)S(1)}, bf16[192,384]{1,0:T(8,128)(2,1)S(1)}, u32[]{:S(2)}, u32[]{:S(2)}) %collective-permute-start.15) | collective-permute-done | bytes 147488 | tf_op jit(solution)/shard_map/ppermute | solution.py:194
  109.3 9.2 %collective-permute-done.21 = bf16[2,192,384]{2,1,0:T(8,128)(2,1)} collective-permute-done((bf16[2,192,384]{2,1,0:T(8,128)(2,1)}, bf16[2,192,384]{2,1,0:T(8,128)(2,1)}, u32[]{:S(2)}, u32[]{:S(2)}) %collective-permute-start.21) | collective-permute-done | bytes 294944 | tf_op jit(solution)/shard_map/ppermute | solution.py:103
  118.5 9.8 %collective-permute-start.29 = (bf16[192,384]{1,0:T(8,128)(2,1)}, bf16[192,384]{1,0:T(8,128)(2,1)}, u32[]{:S(2)}, u32[]{:S(2)}) collective-permute-start(bf16[192,384]{1,0:T(8,128)(2,1)} %bitcast_select_fusion), channel_id=1, source_target_pairs={{1,0},{2,1},{3,2},{0,3},{5,4},{6,5},{7,6},{4,7},{9,8},{10,9},{11,1... | collective-permute-start | bytes 442376 | tf_op jit(solution)/shard_map/ppermute | solution.py:103
  144.8 23.5 %collective-permute-done.23 = bf16[4,2,192,384]{3,2,1,0:T(8,128)(2,1)S(1)} collective-permute-done((bf16[4,2,192,384]{3,2,1,0:T(8,128)(2,1)S(1)}, bf16[4,2,192,384]{3,2,1,0:T(8,128)(2,1)S(1)}, u32[]{:S(2)}, u32[]{:S(2)}) %collective-permute-start.23) | collective-permute-done | bytes 1179680 | tf_op jit(solution)/shard_map/ppermute | solution.py:192
  173.7 5.4 collective-permute-done.32
  195.4 9.7 %collective-permute-done.37 = bf16[2,192,384]{2,1,0:T(8,128)(2,1)S(1)} collective-permute-done((bf16[2,192,384]{2,1,0:T(8,128)(2,1)S(1)}, bf16[2,192,384]{2,1,0:T(8,128)(2,1)S(1)}, u32[]{:S(2)}, u32[]{:S(2)}) %collective-permute-start.37) | collective-permute-done | bytes 294944 | tf_op jit(solution)/shard_map/ppermute | solution.py:103
  212.9 7.5 %collective-permute-start.34 = (bf16[256,768]{1,0:T(8,128)(2,1)S(1)}, bf16[256,768]{1,0:T(8,128)(2,1)S(1)}, u32[]{:S(2)}, u32[]{:S(2)}) collective-permute-start(bf16[256,768]{1,0:T(8,128)(2,1)S(1)} %fusion.62), channel_id=1, source_target_pairs={{0,8},{8,0},{1,9},{9,1},{2,10},{10,2},{3,11},{11,3},{4,12},{12,4},... | collective-permute-start | bytes 1179656 | tf_op jit(solution)/shard_map/ppermute | solution.py:86
  220.4 10.8 %collective-permute-done.39 = bf16[4,2,192,384]{3,2,1,0:T(8,128)(2,1)S(1)} collective-permute-done((bf16[4,2,192,384]{3,2,1,0:T(8,128)(2,1)S(1)}, bf16[4,2,192,384]{3,2,1,0:T(8,128)(2,1)S(1)}, u32[]{:S(2)}, u32[]{:S(2)}) %collective-permute-start.39) | collective-permute-done | bytes 1179680 | tf_op jit(solution)/shard_map/ppermute | solution.py:192
  237.2 4.9 collective-permute-done.44
  280.4 10.5 %collective-permute-done.50 = bf16[4,192,384]{2,1,0:T(8,128)(2,1)} collective-permute-done((bf16[4,192,384]{2,1,0:T(8,128)(2,1)}, bf16[4,192,384]{2,1,0:T(8,128)(2,1)}, u32[]{:S(2)}, u32[]{:S(2)}) %collective-permute-start.50) | collective-permute-done | bytes 589856 | tf_op jit(solution)/shard_map/ppermute | solution.py:233
  304.2 4.6 collective-permute-start.42
  323.6 6.5 collective-permute-start.60
  350.4 5.5 collective-permute-done.57
  421.9 4.9 collective-permute-done.62
  499.1 5.8 collective-permute-done.78
  530.4 6.8 %all-to-all-done.3 = bf16[2,4,96,192]{2,3,0,1:T(8,128)(2,1)S(1)} async-done(((bf16[2,4,96,192]{2,3,0,1:T(8,128)(2,1)}), bf16[2,4,96,192]{2,3,0,1:T(8,128)(2,1)S(1)}, u32[]{:S(2)}, u32[]{:S(2)}) %all-to-all-start.3) | async-done | bytes 294944 | tf_op jit(solution)/shard_map/all_to_all | solution.py:98
  560.1 13.5 %collective-permute-done.97 = f32[2,3,768]{2,0,1:T(2,128)S(1)} collective-permute-done((f32[2,3,768]{2,0,1:T(2,128)S(1)}, f32[2,3,768]{2,0,1:T(2,128)S(1)}, u32[]{:S(2)}, u32[]{:S(2)}) %collective-permute-start.97) | collective-permute-done | bytes 18464 | tf_op jit(solution)/shard_map/ppermute | solution.py:284
  582.1 7.4 %collective-permute-start.87 = (bf16[192,768]{1,0:T(8,128)(2,1)S(1)}, bf16[192,768]{1,0:T(8,128)(2,1)S(1)}, u32[]{:S(2)}, u32[]{:S(2)}) collective-permute-start(bf16[192,768]{1,0:T(8,128)(2,1)S(1)} %get-tuple-element.128), channel_id=1, source_target_pairs={{1,0},{2,1},{3,2},{0,3},{9,8},{10,9},{11,10},{8,11},{17,16},{18,17... | collective-permute-start | bytes 884744 | tf_op jit(solution)/shard_map/ppermute | solution.py:370
  594.1 5.8 collective-permute-done.86
  611.9 5.4 collective-permute-done.90
  622.0 9.1 %shard_map.153 = bf16[768,768]{1,0:T(8,128)(2,1)} custom-call(bf16[768,768]{1,0:T(8,128)(2,1)S(1)} %bitcast.464, f32[768,768]{1,0:T(8,128)S(1)} %convert_select_fusion.gram_ref), custom_call_target="tpu_custom_call" | custom-call | tf_op jit(solution)/shard_map/pallas_call | solution.py:350
  642.8 8.0 %shard_map.152 = bf16[768,768]{1,0:T(8,128)(2,1)S(1)} custom-call(bf16[768,768]{1,0:T(8,128)(2,1)S(1)} %copy-done, f32[768,768]{1,0:T(8,128)S(1)} %fusion.184.gram_ref), custom_call_target="tpu_custom_call" | custom-call | tf_op jit(solution)/shard_map/pallas_call | solution.py:350
  (928 shorter events, 455.2 us)
Async XLA Ops:
  21.5 43.9 %collective-permute-start = (f32[136,768]{1,0:T(8,128)S(1)}, f32[136,768]{1,0:T(8,128)S(1)}, u32[]{:S(2)}, u32[]{:S(2)}) collective-permute-start(f32[136,768]{1,0:T(8,128)S(1)} %select_maximum_fusion), channel_id=1, source_target_pairs={{0,0},{1,8},{2,4},{3,12},{4,1},{5,9},{6,5},{7,13},{8,2},{9,10},{10... | collective-permute-start | bytes 1253384 | tf_op jit(solution)/shard_map/ppermute | solution.py:407
  40.2 47.7 %all-to-all-start.1 = ((bf16[5,96,4,192]{1,3,0,2:T(8,128)(2,1)}), bf16[5,96,4,192]{1,3,0,2:T(8,128)(2,1)}, u32[]{:S(2)}, u32[]{:S(2)}) async-start(bf16[5,96,4,192]{1,3,0,2:T(8,128)(2,1)} %copy.116), calls=%async_computation.1 | async-start | bytes 1966080 | tf_op jit(solution)/shard_map/all_to_all | solution.py:92
  98.1 39.6 %collective-permute-start.20 = (bf16[2,192,384]{2,1,0:T(8,128)(2,1)}, bf16[2,192,384]{2,1,0:T(8,128)(2,1)}, u32[]{:S(2)}, u32[]{:S(2)}) collective-permute-start(bf16[2,192,384]{2,1,0:T(8,128)(2,1)} %bitcast.488), channel_id=1, source_target_pairs={{1,0},{2,1},{3,2},{0,3},{5,4},{6,5},{7,6},{4,7},{9,8},{10,9},{11,1... | collective-permute-start | bytes 884744 | tf_op jit(solution)/shard_map/ppermute | solution.py:103
  103.8 38.9 %collective-permute-start.18 = (bf16[256,768]{1,0:T(8,128)(2,1)}, bf16[256,768]{1,0:T(8,128)(2,1)}, u32[]{:S(2)}, u32[]{:S(2)}) collective-permute-start(bf16[256,768]{1,0:T(8,128)(2,1)} %fusion.60), channel_id=1, source_target_pairs={{0,8},{8,0},{1,9},{9,1},{2,10},{10,2},{3,11},{11,3},{4,12},{12,4},... | collective-permute-start | bytes 1179656 | tf_op jit(solution)/shard_map/ppermute | solution.py:86
  105.8 34.4 %collective-permute-start.31 = (bf16[192,384]{1,0:T(8,128)(2,1)}, bf16[192,384]{1,0:T(8,128)(2,1)}, u32[]{:S(2)}, u32[]{:S(2)}) collective-permute-start(bf16[192,384]{1,0:T(8,128)(2,1)} %bitcast_select_fusion), channel_id=1, source_target_pairs={{3,0},{0,1},{1,2},{2,3},{7,4},{4,5},{5,6},{6,7},{11,8},{8,9},{9,10... | collective-permute-start | bytes 442376 | tf_op jit(solution)/shard_map/ppermute | solution.py:103
  107.6 32.5 %collective-permute-start.30 = (bf16[192,384]{1,0:T(8,128)(2,1)}, bf16[192,384]{1,0:T(8,128)(2,1)}, u32[]{:S(2)}, u32[]{:S(2)}) collective-permute-start(bf16[192,384]{1,0:T(8,128)(2,1)} %bitcast_select_fusion), channel_id=1, source_target_pairs={{2,0},{3,1},{0,2},{1,3},{6,4},{7,5},{4,6},{5,7},{10,8},{11,9},{8,1... | collective-permute-start | bytes 442376 | tf_op jit(solution)/shard_map/ppermute | solution.py:103
  139.4 29.0 %collective-permute-start.23 = (bf16[4,2,192,384]{3,2,1,0:T(8,128)(2,1)S(1)}, bf16[4,2,192,384]{3,2,1,0:T(8,128)(2,1)S(1)}, u32[]{:S(2)}, u32[]{:S(2)}) collective-permute-start(bf16[4,2,192,384]{3,2,1,0:T(8,128)(2,1)S(1)} %pad_maximum_fusion.7), channel_id=1, source_target_pairs={{0,16},{16,0},{1,17},{17,1},{2,18},{18,2},{3,19},{19,3},{4,20},{20... | collective-permute-start | bytes 3538952 | tf_op jit(solution)/shard_map/ppermute | solution.py:192
  141.4 37.7 %collective-permute-start.32 = (bf16[4,192,384]{2,1,0:T(8,128)(2,1)S(1)}, bf16[4,192,384]{2,1,0:T(8,128)(2,1)S(1)}, u32[]{:S(2)}, u32[]{:S(2)}) collective-permute-start(bf16[4,192,384]{2,1,0:T(8,128)(2,1)S(1)} %pad_maximum_fusion.20), channel_id=1, source_target_pairs={{0,16},{16,0},{1,17},{17,1},{2,18},{18,2},{3,19},{19,3},{4,20},{20... | collective-permute-start | bytes 1769480 | tf_op jit(solution)/shard_map/ppermute | solution.py:192
  144.7 25.4 %collective-permute-start.19 = (bf16[256,768]{1,0:T(8,128)(2,1)S(1)}, bf16[256,768]{1,0:T(8,128)(2,1)S(1)}, u32[]{:S(2)}, u32[]{:S(2)}) collective-permute-start(bf16[256,768]{1,0:T(8,128)(2,1)S(1)} %add_convert_fusion.2), channel_id=1, source_target_pairs={{0,4},{4,0},{1,5},{5,1},{2,6},{6,2},{3,7},{7,3},{8,12},{12,8},{9,1... | collective-permute-start | bytes 1179656 | tf_op jit(solution)/shard_map/ppermute | solution.py:80
  205.3 25.9 %collective-permute-start.39 = (bf16[4,2,192,384]{3,2,1,0:T(8,128)(2,1)S(1)}, bf16[4,2,192,384]{3,2,1,0:T(8,128)(2,1)S(1)}, u32[]{:S(2)}, u32[]{:S(2)}) collective-permute-start(bf16[4,2,192,384]{3,2,1,0:T(8,128)(2,1)S(1)} %pad_maximum_fusion.8), channel_id=1, source_target_pairs={{0,16},{16,0},{1,17},{17,1},{2,18},{18,2},{3,19},{19,3},{4,20},{20... | collective-permute-start | bytes 3538952 | tf_op jit(solution)/shard_map/ppermute | solution.py:192
  267.4 23.5 %collective-permute-start.50 = (bf16[4,192,384]{2,1,0:T(8,128)(2,1)}, bf16[4,192,384]{2,1,0:T(8,128)(2,1)}, u32[]{:S(2)}, u32[]{:S(2)}) collective-permute-start(bf16[4,192,384]{2,1,0:T(8,128)(2,1)} %dynamic-slice_convert_fusion.4), channel_id=1, source_target_pairs={{0,16},{16,0},{1,17},{17,1},{2,18},{18,2},{3,19},{19,3},{4,20},{20... | collective-permute-start | bytes 1769480 | tf_op jit(solution)/shard_map/ppermute | solution.py:233
  271.9 31.4 %collective-permute-start.41 = (bf16[256,768]{1,0:T(8,128)(2,1)S(1)}, bf16[256,768]{1,0:T(8,128)(2,1)S(1)}, u32[]{:S(2)}, u32[]{:S(2)}) collective-permute-start(bf16[256,768]{1,0:T(8,128)(2,1)S(1)} %get-tuple-element.104), channel_id=1, source_target_pairs={{0,8},{8,0},{1,9},{9,1},{2,10},{10,2},{3,11},{11,3},{4,12},{12,4},... | collective-permute-start | bytes 1179656 | tf_op jit(solution)/shard_map/ppermute | solution.py:86
  304.2 35.2 %collective-permute-start.42 = (f32[128,768]{1,0:T(8,128)}, f32[128,768]{1,0:T(8,128)}, u32[]{:S(2)}, u32[]{:S(2)}) collective-permute-start(f32[128,768]{1,0:T(8,128)} %dynamic-slice_add_fusion.2), channel_id=1, source_target_pairs={{0,0},{8,1},{4,2},{12,3},{1,4},{9,5},{5,6},{13,7},{2,8},{10,9},{6,... | collective-permute-start | bytes 1179656 | tf_op jit(solution)/shard_map/ppermute | solution.py:473
  373.0 41.2 %collective-permute-start.61 = (bf16[256,768]{1,0:T(8,128)(2,1)}, bf16[256,768]{1,0:T(8,128)(2,1)}, u32[]{:S(2)}, u32[]{:S(2)}) collective-permute-start(bf16[256,768]{1,0:T(8,128)(2,1)} %slice.1190), channel_id=1, source_target_pairs={{0,4},{4,0},{1,5},{5,1},{2,6},{6,2},{3,7},{7,3},{8,12},{12,8},{9,1... | collective-permute-start | bytes 1179656 | tf_op jit(solution)/shard_map/ppermute | solution.py:85
  376.8 23.7 %collective-permute-start.65 = (bf16[192,384]{1,0:T(8,128)(2,1)}, bf16[192,384]{1,0:T(8,128)(2,1)}, u32[]{:S(2)}, u32[]{:S(2)}) collective-permute-start(bf16[192,384]{1,0:T(8,128)(2,1)} %get-tuple-element.169), channel_id=1, source_target_pairs={{2,0},{3,1},{0,2},{1,3},{6,4},{7,5},{4,6},{5,7},{10,8},{11,9},{8,1... | collective-permute-start | bytes 442376 | tf_op jit(solution)/shard_map/ppermute | solution.py:103
  377.1 23.8 %collective-permute-start.64 = (bf16[192,384]{1,0:T(8,128)(2,1)}, bf16[192,384]{1,0:T(8,128)(2,1)}, u32[]{:S(2)}, u32[]{:S(2)}) collective-permute-start(bf16[192,384]{1,0:T(8,128)(2,1)} %get-tuple-element.170), channel_id=1, source_target_pairs={{1,0},{2,1},{3,2},{0,3},{5,4},{6,5},{7,6},{4,7},{9,8},{10,9},{11,1... | collective-permute-start | bytes 442376 | tf_op jit(solution)/shard_map/ppermute | solution.py:103
  384.1 33.5 %collective-permute-start.66 = (bf16[4,192,384]{2,1,0:T(8,128)(2,1)}, bf16[4,192,384]{2,1,0:T(8,128)(2,1)}, u32[]{:S(2)}, u32[]{:S(2)}) collective-permute-start(bf16[4,192,384]{2,1,0:T(8,128)(2,1)} %dynamic-slice_convert_fusion.2), channel_id=1, source_target_pairs={{0,16},{16,0},{1,17},{17,1},{2,18},{18,2},{3,19},{19,3},{4,20},{20... | collective-permute-start | bytes 1769480 | tf_op jit(solution)/shard_map/ppermute | solution.py:233
  430.8 28.3 %collective-permute-start.67 = (bf16[256,768]{1,0:T(8,128)(2,1)}, bf16[256,768]{1,0:T(8,128)(2,1)}, u32[]{:S(2)}, u32[]{:S(2)}) collective-permute-start(bf16[256,768]{1,0:T(8,128)(2,1)} %get-tuple-element.41), channel_id=1, source_target_pairs={{0,4},{4,0},{1,5},{5,1},{2,6},{6,2},{3,7},{7,3},{8,12},{12,8},{9,1... | collective-permute-start | bytes 1179656 | tf_op jit(solution)/shard_map/ppermute | solution.py:80
  483.6 25.7 %collective-permute-start.70 = (bf16[256,768]{1,0:T(8,128)(2,1)}, bf16[256,768]{1,0:T(8,128)(2,1)}, u32[]{:S(2)}, u32[]{:S(2)}) collective-permute-start(bf16[256,768]{1,0:T(8,128)(2,1)} %fusion.66), channel_id=1, source_target_pairs={{0,8},{8,0},{1,9},{9,1},{2,10},{10,2},{3,11},{11,3},{4,12},{12,4},... | collective-permute-start | bytes 1179656 | tf_op jit(solution)/shard_map/ppermute | solution.py:86
  505.7 52.5 %collective-permute-start.79 = (bf16[192,384]{1,0:T(8,128)(2,1)}, bf16[192,384]{1,0:T(8,128)(2,1)}, u32[]{:S(2)}, u32[]{:S(2)}) collective-permute-start(bf16[192,384]{1,0:T(8,128)(2,1)} %fusion.79), channel_id=1, source_target_pairs={{3,3},{19,7},{7,11},{23,15},{11,19},{27,23},{15,27},{31,31}} | collective-permute-start | bytes 442376 | tf_op jit(solution)/shard_map/ppermute | solution.py:162
  529.9 28.2 %collective-permute-start.96 = (f32[2,3,768]{2,0,1:T(2,128)S(1)}, f32[2,3,768]{2,0,1:T(2,128)S(1)}, u32[]{:S(2)}, u32[]{:S(2)}) collective-permute-start(f32[2,3,768]{2,0,1:T(2,128)S(1)} %fusion.115), channel_id=1, source_target_pairs={{0,4},{4,0},{1,5},{5,1},{2,6},{6,2},{3,7},{7,3},{8,12},{12,8},{9,1... | collective-permute-start | bytes 55304 | tf_op jit(solution)/shard_map/ppermute | solution.py:283
  547.4 29.5 %all-to-all-start.6 = ((bf16[8,1,96,768]{3,2,1,0:T(8,128)(2,1)}), bf16[8,1,96,768]{3,2,1,0:T(8,128)(2,1)S(1)}, u32[]{:S(2)}, u32[]{:S(2)}) async-start(bf16[8,1,96,768]{3,2,1,0:T(8,128)(2,1)} %bitcast.506), calls=%async_computation.6 | async-start | bytes 2359296 | tf_op jit(solution)/shard_map/all_to_all | solution.py:592
  551.1 88.9 %all-gather.2.cloned.1.call-start = ((), (), s32[]{:S(2)}) async-start(), calls=%async_computation.8 | async-start | bytes 1327104 | tf_op jit(solution)/shard_map/all_gather | solution.py:604
  553.1 86.9 %collective-permute-start.74 = (f32[128,768]{1,0:T(8,128)}, f32[128,768]{1,0:T(8,128)}, u32[]{:S(2)}, u32[]{:S(2)}) collective-permute-start(f32[128,768]{1,0:T(8,128)} %dynamic-slice_add_fusion), channel_id=1, source_target_pairs={{0,0},{8,1},{4,2},{12,3},{1,4},{9,5},{5,6},{13,7},{2,8},{10,9},{6,... | collective-permute-start | bytes 1179656 | tf_op jit(solution)/shard_map/ppermute | solution.py:473
  (260 other events, 2409.3 us)
Sparse Core Ops, SparseCore 0:
  577.0 25.1 all-gather.1

commit v4 on v3

--- a/solution.py
+++ b/solution.py
@@ -40,16 +40,6 @@
 f32 = jnp.float32
 
 
-def layer_norm(hidden, gain_vec, bias_vec):
-    center = hidden - jnp.mean(hidden, axis=-1, keepdims=True)
-    variance = jnp.mean(center * center, axis=-1, keepdims=True)
-    return center * lax.rsqrt(variance + norm_epsilon) * gain_vec + bias_vec
-
-
-def smooth_unit(preact):
-    return jax.nn.gelu(preact, approximate=True)
-
-
 def dot(operand, other):
     return jnp.dot(operand, other, preferred_element_type=f32)
 
@@ -60,30 +50,6 @@
 
 def dot_trans(operand, other):
     return lax.dot_general(operand, other, (((1,), (1,)), ((), ())), preferred_element_type=f32)
-
-
-def bdot(operand, other, left, right):
-    return lax.dot_general(
-        operand, other, (((left,), (right,)), ((0,), (0,))), preferred_element_type=f32
-    )
-
-
-def heads_of(matrix):
-    return matrix.reshape(matrix.shape[0], TP_HEADS, HEAD).transpose(1, 0, 2)
-
-
-def merge_heads(stack):
-    return stack.transpose(1, 0, 2).reshape(stack.shape[1], TP_HEADS * HEAD)
-
-
-def core_gather(rows):
-    return jnp.concatenate([rows, lax.ppermute(rows, "jc", SWAP)], axis=0)
-
-
-def group_sum(partial):
-    half = partial.shape[0] // 2
-    mine = partial[:half] + lax.ppermute(partial[half:].astype(bf16), "jc", SWAP).astype(f32)
-    return mine + lax.ppermute(mine.astype(bf16), "jx", SWAP).astype(f32)
 
 
 def to_group(mats):
@@ -182,27 +148,8 @@
 
 
 def ctx_gather(piece):
-    return [piece] + [rotate(piece, "ctx", step) for step in (1, 3, 2)]
-
-
-def group_join(blocks, pieces):
-    own, near, back, far = blocks
-    ordered = [own, near, far, back]
-    if pieces == 1:
-        other = lax.ppermute(jnp.stack(ordered), "g", SWAP)
-    else:
-        others = [lax.ppermute(block, "g", SWAP) for block in (own, near)]
-        others.append(lax.ppermute(jnp.stack([far, back]), "g", SWAP))
-        other = jnp.concatenate([others[0][None], others[1][None], others[2]])
-    mine = jnp.stack(ordered)
-    first = lax.axis_index("g") == 0
-    return jnp.concatenate(
-        [jnp.where(first, mine, other), jnp.where(first, other, mine)], axis=mine.ndim - 1
-    )
-
-
-def mlp_mats(stack):
-    return stack[:, 0].reshape(D, D), stack[:, 1].reshape(D, D)
+    near, back, far = [rotate(piece, "ctx", step) for step in (1, 3, 2)]
+    return [piece, near, far, back]
 
 
 def gather_weights_wide(low):
@@ -220,17 +167,12 @@
             tiled=True,
         )
         attn = jnp.concatenate([full[0][: 3 * COLS].reshape(3, COLS, D), w_o], axis=0)
-        result.append((attn, full[1], full[2]))
+        result.append((attn.reshape(D, D), jnp.stack([full[1], full[2]])))
     return result
 
 
-def half_sum(blocks):
-    half = D // 2
-    group = lax.axis_index("g")
-    last = blocks.ndim - 1
-    mine = lax.dynamic_slice_in_dim(blocks, group * half, half, axis=last)
-    give = lax.dynamic_slice_in_dim(blocks, (1 - group) * half, half, axis=last)
-    return mine.astype(f32) + lax.ppermute(give.astype(bf16), "g", SWAP).astype(f32)
+def half_sum(mine, give):
+    return mine + lax.ppermute(give, "g", SWAP).astype(f32)
 
 
 def ctx_sum(blocks):
@@ -282,6 +224,369 @@
         total = total + rotate(blocks[step], "ctx", -step)
     total = total + lax.ppermute(total, "jc", SWAP)
     return total + lax.ppermute(total, "jx", SWAP)
+
+
+def call(kernel, outs, *args, scratch=()):
+    return pl.pallas_call(
+        kernel,
+        out_shape=[jax.ShapeDtypeStruct(shape, kind) for shape, kind in outs],
+        in_specs=[pl.BlockSpec(memory_space=pltpu.SMEM)]
+        + [pl.BlockSpec(memory_space=pltpu.VMEM)] * (len(args) - 1),
+        out_specs=[pl.BlockSpec(memory_space=pltpu.VMEM)] * len(outs),
+        scratch_shapes=list(scratch),
+        compiler_params=pltpu.CompilerParams(vmem_limit_bytes=52 * 1024 * 1024),
+    )(*args)
+
+
+def block_at(place_ref, step):
+    ahead = place_ref[0] + step
+    return jnp.where(ahead >= 4, ahead - 4, ahead)
+
+
+def put_blocks(place_ref, own_refs, other_refs, full_refs):
+    half = D // 2
+    mine = pl.multiple_of(place_ref[1] * half, half)
+    theirs = pl.multiple_of((1 - place_ref[1]) * half, half)
+    for step in range(4):
+        rows = pl.ds(pl.multiple_of(block_at(place_ref, step) * COLS, COLS), COLS)
+        for number, full_ref in enumerate(full_refs):
+            own, other = own_refs[step], other_refs[step]
+            if len(full_refs) > 1:
+                own, other = own.at[number], other.at[number]
+            full_ref[rows, pl.ds(mine, half)] = own[...]
+            full_ref[rows, pl.ds(theirs, half)] = other[...]
+
+
+def put_grads(place_ref, grad, mine_refs, give_refs, halves):
+    half = D // 2
+    for block in range(4):
+        rows = grad[block * COLS : (block + 1) * COLS]
+        if halves:
+            back = block - place_ref[0]
+            back = jnp.where(back < 0, back + 4, back)
+            low = place_ref[1] == 0
+            mine_refs(back)[...] = jnp.where(low, rows[:, :half], rows[:, half:])
+            give_refs(back)[...] = jnp.where(low, rows[:, half:], rows[:, :half]).astype(bf16)
+        else:
+            mine_refs(block)[...] = rows
+
+
+def norm_rows(hidden):
+    center = hidden - jnp.mean(hidden, axis=-1, keepdims=True)
+    variance = jnp.mean(center * center, axis=-1, keepdims=True)
+    inverse = lax.rsqrt(variance + norm_epsilon)
+    return center * inverse, inverse
+
+
+def norm_stage(vecs, layer, row, hidden, mine=None, recv=None, bias=None):
+    rows = hidden.shape[0]
+
+    def kernel(unused, vec_ref, hidden_ref, *refs):
+        total = hidden_ref[...]
+        if mine is not None:
+            mine_ref, recv_ref, total_ref, out_ref = refs
+            bias_row = vec_ref[bias[0], bias[1] : bias[1] + 1, :]
+            total = total + (mine_ref[...] + recv_ref[...].astype(f32) + bias_row)
+            total_ref[...] = total
+        else:
+            (out_ref,) = refs
+        normed, unused_scale = norm_rows(total)
+        gain = vec_ref[layer, row : row + 1, :]
+        shift = vec_ref[layer, row + 1 : row + 2, :]
+        out_ref[...] = (normed * gain + shift).astype(bf16)
+
+    outs = [((rows, D), bf16)]
+    args = [hidden]
+    if mine is not None:
+        outs = [((rows, D), f32)] + outs
+        args += [mine, recv]
+    return call(kernel, outs, jnp.zeros((1,), jnp.int32), vecs, *args)
+
+
+def norm_back_stage(vecs, layer, row, grad, mine, recv, hidden):
+    rows = hidden.shape[0]
+
+    def kernel(unused, vec_ref, grad_ref, mine_ref, recv_ref, hidden_ref, out_ref, low_ref, sum_ref):
+        through = mine_ref[...] + recv_ref[...].astype(f32)
+        normed, inverse = norm_rows(hidden_ref[...])
+        scaled = through * vec_ref[layer, row : row + 1, :]
+        part = jnp.mean(scaled, axis=-1, keepdims=True)
+        part = part + normed * jnp.mean(scaled * normed, axis=-1, keepdims=True)
+        total = grad_ref[...] + inverse * (scaled - part)
+        out_ref[...] = total
+        low = total.astype(bf16)
+        low_ref[...] = low
+        sum_ref[0:1, :] = jnp.sum(through * normed, axis=0, keepdims=True)
+        sum_ref[1:2, :] = jnp.sum(through, axis=0, keepdims=True)
+        sum_ref[2:3, :] = jnp.sum(low.astype(f32), axis=0, keepdims=True)
+
+    outs = [((rows, D), f32), ((rows, D), bf16), ((8, D), f32)]
+    return call(kernel, outs, jnp.zeros((1,), jnp.int32), vecs, grad, mine, recv, hidden)
+
+
+def both(first_ref, second_ref):
+    return jnp.concatenate([first_ref[...], second_ref[...]], axis=0)
+
+
+def allowed_of(row_ref, column_ref):
+    before = row_ref[0:1, :] <= column_ref[:, 0:1]
+    return before & (row_ref[1:2, :] == column_ref[:, 1:2])
+
+
+def attend_stage(place, row_info, column_info, bias, a_own, a_other, weights):
+    half = a_own.shape[0]
+    tokens = 2 * half
+    wide = 3 * COLS
+    own, other = weights if isinstance(weights, tuple) else ([], [])
+    stacked = bool(other) and other[0].ndim == 3
+
+    def kernel(place_ref, row_ref, column_ref, bias_ref, own_a_ref, other_a_ref, *refs):
+        if own:
+            own_refs, refs = refs[:4], refs[4:]
+            count = len(other)
+            others, refs = refs[:count], refs[count:]
+            if stacked:
+                others = [others[0].at[step] for step in range(4)]
+            w_ref, qkv_ref, lse_ref, o_ref, mine_ref, give_ref = refs
+            put_blocks(place_ref, own_refs, others, [w_ref])
+        else:
+            w_ref, qkv_ref, lse_ref, o_ref, mine_ref, give_ref = refs
+        for start, a_ref in ((0, own_a_ref), (half, other_a_ref)):
+            proj = dot_trans(a_ref[...], w_ref[0:wide, :]) + bias_ref[0:1, :]
+            qkv_ref[start : start + half, :] = proj.astype(bf16)
+        allowed = allowed_of(row_ref, column_ref)
+        for head in range(TP_HEADS):
+            lanes = head * HEAD
+            k = qkv_ref[:, COLS + lanes : COLS + lanes + HEAD]
+            v = qkv_ref[:, 2 * COLS + lanes : 2 * COLS + lanes + HEAD]
+            for start in (0, half):
+                rows = slice(start, start + half)
+                q = qkv_ref[rows, lanes : lanes + HEAD]
+                scores = jnp.where(allowed[rows], dot_trans(q, k) * HEAD ** (-0.5), masked_score)
+                top = jnp.max(scores, axis=-1, keepdims=True)
+                unnormed = jnp.exp(scores - top)
+                total = jnp.sum(unnormed, axis=-1, keepdims=True)
+                prob = (unnormed * (1.0 / total)).astype(bf16)
+                o_ref[rows, lanes : lanes + HEAD] = dot(prob, v).astype(bf16)
+                lse_ref[rows, head : head + 1] = top + jnp.log(total)
+        mine_ref[...] = dot(o_ref[0:half, :], w_ref[wide:, :])
+        give_ref[...] = dot(o_ref[half:, :], w_ref[wide:, :]).astype(bf16)
+
+    outs = [
+        ((tokens, wide), bf16),
+        ((tokens, 128), f32),
+        ((tokens, COLS), bf16),
+        ((half, D), f32),
+        ((half, D), bf16),
+    ]
+    if own:
+        outs = [((D, D), bf16)] + outs
+        return call(
+            kernel, outs, place, row_info, column_info, bias, a_own, a_other, *own, *other
+        )
+    result = call(kernel, outs, place, row_info, column_info, bias, a_own, a_other, weights)
+    return [weights] + list(result)
+
+
+def attend_back_stage(
+    place, row_info, column_info, gb_own, gb_other, a_own, a_other, qkv, lse, o, w_attn, halves
+):
+    half = a_own.shape[0]
+    tokens = 2 * half
+    wide = 3 * COLS
+
+    def kernel(
+        place_ref,
+        row_ref,
+        column_ref,
+        own_gb_ref,
+        other_gb_ref,
+        own_a_ref,
+        other_a_ref,
+        qkv_ref,
+        lse_ref,
+        o_ref,
+        w_ref,
+        mine_ref,
+        give_ref,
+        sum_ref,
+        *refs,
+    ):
+        *grad_refs, go_ref, all_ref = refs
+        w_o = w_ref[wide:, :]
+        for start, gb_ref in ((0, own_gb_ref), (half, other_gb_ref)):
+            go_ref[start : start + half, :] = dot_trans(gb_ref[...], w_o).astype(bf16)
+        allowed = allowed_of(row_ref, column_ref)
+        for head in range(TP_HEADS):
+            lanes = head * HEAD
+            q_lanes = slice(lanes, lanes + HEAD)
+            k_lanes = slice(COLS + lanes, COLS + lanes + HEAD)
+            v_lanes = slice(2 * COLS + lanes, 2 * COLS + lanes + HEAD)
+            k = qkv_ref[:, k_lanes]
+            v = qkv_ref[:, v_lanes]
+            gk = jnp.zeros((tokens, HEAD), f32)
+            gv = jnp.zeros((tokens, HEAD), f32)
+            for start in (0, half):
+                rows = slice(start, start + half)
+                q = qkv_ref[rows, q_lanes]
+                go = go_ref[rows, q_lanes]
+                scores = jnp.where(allowed[rows], dot_trans(q, k) * HEAD ** (-0.5), masked_score)
+                prob = jnp.exp(scores - lse_ref[rows, head : head + 1])
+                g_prob = dot_trans(go, v)
+                row_dot = jnp.sum(g_prob * prob, axis=-1, keepdims=True)
+                g_scores = (prob * (g_prob - row_dot)).astype(bf16)
+                all_ref[rows, q_lanes] = (dot(g_scores, k) * HEAD ** (-0.5)).astype(bf16)
+                gk = gk + dot_tokens(g_scores, q)
+                gv = gv + dot_tokens(prob.astype(bf16), go)
+            all_ref[:, k_lanes] = (gk * HEAD ** (-0.5)).astype(bf16)
+            all_ref[:, v_lanes] = gv.astype(bf16)
+        mine_ref[...] = dot(all_ref[0:half, :], w_ref[0:wide, :])
+        give_ref[...] = dot(all_ref[half:, :], w_ref[0:wide, :]).astype(bf16)
+        sum_ref[0:1, :] = jnp.sum(all_ref[...].astype(f32), axis=0, keepdims=True)
+        grad = jnp.concatenate(
+            [
+                dot_tokens(all_ref[...], both(own_a_ref, other_a_ref)),
+                dot_tokens(o_ref[...], both(own_gb_ref, other_gb_ref)),
+            ],
+            axis=0,
+        )
+        put_grads(
+            place_ref,
+            grad,
+            lambda block: grad_refs[0].at[block],
+            lambda block: grad_refs[1].at[block],
+            halves,
+        )
+
+    width = D // 2 if halves else D
+    outs = [((half, D), f32), ((half, D), bf16), ((8, wide), f32), ((4, COLS, width), f32)]
+    if halves:
+        outs.append(((4, COLS, width), bf16))
+    return call(
+        kernel,
+        outs,
+        place,
+        row_info,
+        column_info,
+        gb_own,
+        gb_other,
+        a_own,
+        a_other,
+        qkv,
+        lse,
+        o,
+        w_attn,
+        scratch=[pltpu.VMEM((tokens, COLS), bf16), pltpu.VMEM((tokens, wide), bf16)],
+    )
+
+
+def tanh_part(preact):
+    inner = math.sqrt(2.0 / math.pi) * (preact + 0.044715 * (preact * preact * preact))
+    return jnp.tanh(inner)
+
+
+def feed_stage(place, bias, c_own, c_other, weights):
+    half = c_own.shape[0]
+    own, other = weights if isinstance(weights, tuple) else ([], [])
+
+    def kernel(place_ref, bias_ref, own_c_ref, other_c_ref, *refs):
+        if own:
+            own_refs, other_ref, refs = refs[:4], refs[4], refs[5:]
+            others = [other_ref.at[step] for step in range(4)]
+            w_ref, preact_ref, act_ref, mine_ref, give_ref = refs
+            put_blocks(place_ref, own_refs, others, [w_ref.at[0], w_ref.at[1]])
+        else:
+            w_ref, preact_ref, act_ref, mine_ref, give_ref = refs
+        for start, c_ref, out_ref in ((0, own_c_ref, mine_ref), (half, other_c_ref, give_ref)):
+            rows = slice(start, start + half)
+            preact = dot_trans(c_ref[...], w_ref[0]) + bias_ref[...]
+            preact_ref[rows, :] = preact
+            act = (0.5 * preact * (1.0 + tanh_part(preact))).astype(bf16)
+            act_ref[rows, :] = act
+            out_ref[...] = dot(act, w_ref[1]).astype(out_ref.dtype)
+
+    outs = [
+        ((2 * half, D), f32),
+        ((2 * half, D), bf16),
+        ((half, D), f32),
+        ((half, D), bf16),
+    ]
+    if own:
+        outs = [((2, D, D), bf16)] + outs
+        return call(kernel, outs, place, bias, c_own, c_other, *own, *other)
+    return [weights] + list(call(kernel, outs, place, bias, c_own, c_other, weights))
+
+
+def feed_back_stage(place, gy_own, gy_other, c_own, c_other, preact, act, weights, halves):
+    half = c_own.shape[0]
+
+    def kernel(
+        place_ref,
+        own_gy_ref,
+        other_gy_ref,
+        own_c_ref,
+        other_c_ref,
+        preact_ref,
+        act_ref,
+        w_ref,
+        mine_ref,
+        give_ref,
+        sum_ref,
+        *refs,
+    ):
+        *grad_refs, gz_ref = refs
+        up_sum = jnp.zeros((1, D), f32)
+        for start, gy_ref, out_ref in ((0, own_gy_ref, mine_ref), (half, other_gy_ref, give_ref)):
+            rows = slice(start, start + half)
+            gu = dot_trans(gy_ref[...], w_ref[1])
+            x = preact_ref[rows, :]
+            tanh = tanh_part(x)
+            slope = math.sqrt(2.0 / math.pi) * (1.0 + 3.0 * 0.044715 * (x * x))
+            factor = 0.5 * (1.0 + tanh) + 0.5 * x * (1.0 - tanh * tanh) * slope
+            gz = (gu * factor).astype(bf16)
+            gz_ref[rows, :] = gz
+            up_sum = up_sum + jnp.sum(gz.astype(f32), axis=0, keepdims=True)
+            out_ref[...] = dot(gz, w_ref[0]).astype(out_ref.dtype)
+        sum_ref[0:1, :] = up_sum
+        sum_ref[1:2, :] = jnp.sum(own_gy_ref[...].astype(f32), axis=0, keepdims=True)
+        for number, left_ref, rights in (
+            (0, gz_ref, (own_c_ref, other_c_ref)),
+            (1, act_ref, (own_gy_ref, other_gy_ref)),
+        ):
+            put_grads(
+                place_ref,
+                dot_tokens(left_ref[...], both(*rights)),
+                lambda block: grad_refs[0].at[block, number],
+                lambda block: grad_refs[1].at[block, number],
+                halves,
+            )
+
+    width = D // 2 if halves else D
+    outs = [((half, D), f32), ((half, D), bf16), ((8, D), f32), ((4, 2, COLS, width), f32)]
+    if halves:
+        outs.append(((4, 2, COLS, width), bf16))
+    return call(
+        kernel,
+        outs,
+        place,
+        gy_own,
+        gy_other,
+        c_own,
+        c_other,
+        preact,
+        act,
+        weights,
+        scratch=[pltpu.VMEM((2 * half, D), bf16)],
+    )
+
+
+def core_swap(block):
+    return lax.ppermute(block, "jc", SWAP)
+
+
+def group_sum(mine, give):
+    mine = mine + core_swap(give).astype(f32)
+    return mine, lax.ppermute(mine.astype(bf16), "jx", SWAP)
 
 
 def orthogonalize_kernel(x_ref, gram_ref, out_ref, base_ref, work_ref, mat_ref, low_ref):
@@ -409,169 +714,152 @@
     segment_row = moved[tokens_dev, :seq_len]
     relative = lax.axis_size("g") == 2
     low = weights.astype(bf16)
-    gathered = [None] * LAYERS
+    place = jnp.stack([z_index, lax.axis_index("g")]).astype(jnp.int32)
     if relative:
         pieces = pack_pieces(low)
-        attn_blocks = ctx_gather(pieces[0][0])
-        mlp_blocks = ctx_gather(after(pieces[0][1], *attn_blocks[1:]))
-        gathered[0] = (to_absolute(group_join(attn_blocks, 3)), mlp_blocks)
+        own_attn = ctx_gather(pieces[0][0])
+        own_mlp = ctx_gather(after(pieces[0][1], *own_attn[1:]))
+        swap_attn = [lax.ppermute(block, "g", SWAP) for block in own_attn]
+        attn_weights = (own_attn, swap_attn)
     else:
-        gathered = gather_weights_wide(low)
-
-    order = [c_index * half, (1 - c_index) * half]
-    pos = jnp.concatenate([start + jnp.arange(half) for start in order])
-    seg = jnp.concatenate([lax.dynamic_slice_in_dim(segment_row, start, half) for start in order])
-    allowed = (pos[None, :] <= pos[:, None]) & (seg[None, :] == seg[:, None])
-
-    def mine(row):
-        return lax.dynamic_slice_in_dim(row, t_index * COLS, COLS, axis=-1)
-
-    def scores_of(q, k):
-        return jnp.where(allowed[None], bdot(q, k, 2, 2) * HEAD ** (-0.5), masked_score)
+        wide_weights = gather_weights_wide(low)
+
+    start = c_index * half
+    pos = jnp.concatenate([start + jnp.arange(half), half - start + jnp.arange(half)])
+    seg = jnp.roll(segment_row.reshape(2, half), -c_index, axis=0).reshape(-1)
+    info = jnp.stack([pos.astype(f32), seg])
+    row_info = jnp.pad(info, ((0, 6), (0, 0)))
+    column_info = jnp.pad(info.T, ((0, 0), (0, 126)))
+    vec_mine = lax.dynamic_slice_in_dim(vec_rows, t_index * COLS, COLS, axis=2)
+    no_bias = jnp.zeros((LAYERS, 1, COLS), f32)
+    qkv_bias = jnp.concatenate([vec_mine[:, 4:5], no_bias, vec_mine[:, 5:6]], axis=2)
+    up_bias = vec_mine[:, 8:12].reshape(LAYERS, 1, D)
 
     stored = []
+    (a_own,) = norm_stage(vec_rows, 0, 0, hidden)
     for layer in range(LAYERS):
-        vec = [vec_rows[layer, row : row + 1] for row in range(8)]
-        attn_w = gathered[layer][0]
-        w_qkv = attn_w[:3].reshape(3 * COLS, D)
-        w_o = attn_w[3]
-        b_up = mine(vec_rows[layer, 8:12])
-        b_up = (from_own(b_up) if relative else b_up).reshape(1, D)
-        a_all = core_gather(layer_norm(hidden, vec[0], vec[1]).astype(bf16))
-        proj = dot_trans(a_all, w_qkv)
-        q = heads_of((proj[:, :COLS] + mine(vec[4])).astype(bf16))
-        k = heads_of(proj[:, COLS : 2 * COLS].astype(bf16))
-        v = heads_of((proj[:, 2 * COLS :] + mine(vec[5])).astype(bf16))
-        scores = scores_of(q, k)
-        row_max = jnp.max(scores, axis=-1, keepdims=True)
-        unnormed = jnp.exp(scores - row_max)
-        total = jnp.sum(unnormed, axis=-1, keepdims=True)
-        prob = (unnormed / total).astype(bf16)
-        log_total = row_max + jnp.log(total)
-        o = merge_heads(bdot(prob, v, 2, 1)).astype(bf16)
         following = layer + 1 < LAYERS
+        a_other = core_swap(a_own)
+        if not relative:
+            attn_weights, mlp_weights = wide_weights[layer]
+        w_attn, qkv, lse, o, mine, give = attend_stage(
+            place, row_info, column_info, qkv_bias[layer], a_own, a_other, attn_weights
+        )
+        if relative:
+            mlp_weights = (own_mlp, [lax.ppermute(jnp.stack(own_mlp), "g", SWAP)])
+            if following:
+                own_attn = ctx_gather(after(pieces[layer + 1][0], o))
+        mine, recv = group_sum(mine, give)
+        middle, c_own = norm_stage(vec_rows, layer, 2, hidden, mine, recv, (layer, 6))
+        c_other = core_swap(c_own)
+        w_mlp, preact, act, mine, give = feed_stage(
+            place, up_bias[layer], c_own, c_other, mlp_weights
+        )
         if relative and following:
-            attn_blocks = ctx_gather(after(pieces[layer + 1][0], o))
-        middle = hidden + (group_sum(dot(o, w_o)) + vec[6])
-        c_all = core_gather(layer_norm(middle, vec[2], vec[3]).astype(bf16))
-        if relative:
-            w_up, w_down = mlp_mats(group_join(gathered[layer][1], 1))
+            own_mlp = ctx_gather(after(pieces[layer + 1][1], act, *own_attn[1:]))
+            attn_weights = (own_attn, [lax.ppermute(jnp.stack(own_attn), "g", SWAP)])
+        mine, recv = group_sum(mine, give)
+        stored.append(
+            (hidden, middle, a_own, a_other, qkv, lse, o, c_own, c_other, preact, act, w_attn, w_mlp)
+        )
+        if following:
+            hidden, a_own = norm_stage(vec_rows, layer + 1, 0, middle, mine, recv, (layer, 7))
         else:
-            w_up, w_down = gathered[layer][1:]
-        preact = dot_trans(c_all, w_up) + b_up
-        act = smooth_unit(preact).astype(bf16)
-        if relative and following:
-            mlp_blocks = ctx_gather(after(pieces[layer + 1][1], act, *attn_blocks[1:]))
-            gathered[layer + 1] = (to_absolute(group_join(attn_blocks, 1)), mlp_blocks)
-        stored.append(
-            (hidden, middle, a_all, q, k, v, log_total, o, c_all, preact, act, w_qkv, w_o, w_up, w_down)
-        )
-        hidden = middle + (group_sum(dot(act, w_down)) + vec[7])
+            hidden = middle + (mine + recv.astype(f32) + vec_rows[layer, 7:8])
 
     def send_back(rows):
         block = lax.dynamic_slice_in_dim(rows, x_index * tokens_dev, tokens_dev, axis=0)
         return lax.ppermute(block, axes, from_seq)
 
     hidden_out = send_back(hidden)
-    moved_grad = lax.ppermute(after(out_grad[0], stored[-1][7]), axes, to_seq)
-    grad_hidden = x_join(moved_grad)
-
-    once = jnp.where(x_index == 0, 1.0, 0.0).astype(f32)
+    grad_hidden = x_join(lax.ppermute(after(out_grad[0], stored[-1][6]), axes, to_seq))
+    gy_own = grad_hidden.astype(bf16)
+
     mat_list = [None] * LAYERS
-    vec_list = [None] * LAYERS
+    sum_list = [None] * LAYERS
     parts = [None] * LAYERS
-    attn_half = attn_part = up_part = down_part = None
+    attn_half = None
     for layer in reversed(range(LAYERS)):
-        (h_in, middle, a_all, q, k, v, log_total, o, c_all, preact, act, w_qkv, w_o, w_up, w_down) = stored[
+        h_in, middle, a_own, a_other, qkv, lse, o, c_own, c_other, preact, act, w_attn, w_mlp = stored[
             layer
         ]
-        vec = [vec_rows[layer, row : row + 1] for row in range(8)]
-        gy = grad_hidden.astype(bf16)
-        gy_all = core_gather(gy)
-        down_grad = dot_tokens(act, gy_all).reshape(ctx_size, COLS, D)
+        gy_other = core_swap(gy_own)
+        mine, give, up_sums, *mlp_grads = feed_back_stage(
+            place, gy_own, gy_other, c_own, c_other, preact, act, w_mlp, relative
+        )
         if relative:
-            down_half = half_sum(down_grad)
-        gu = dot_trans(gy_all, w_down)
-        unused, gelu_pull = jax.vjp(smooth_unit, preact)
-        gz = gelu_pull(gu)[0].astype(bf16)
+            if attn_half is not None:
+                mine, attn_half = lax.optimization_barrier((mine, attn_half))
+                attn_part = ctx_sum(attn_half)
+            mlp_half = half_sum(*mlp_grads)
+        mine, recv = group_sum(mine, give)
+        grad_middle, gb_own, mid_sums = norm_back_stage(
+            vec_rows, layer, 2, grad_hidden, mine, recv, middle
+        )
         if relative and attn_half is not None:
-            gz, attn_half, up_part = lax.optimization_barrier((gz, attn_half, up_part))
-            attn_part = ctx_sum(from_own(attn_half))
-        up_grad = dot_tokens(gz, c_all).reshape(ctx_size, COLS, D)
+            gb_own, mlp_part, attn_part = lax.optimization_barrier((gb_own, mlp_part, attn_part))
+            parts[layer + 1] = (attn_part, mlp_part)
+        gb_other = core_swap(gb_own)
+        mine, give, qkv_sums, *attn_grads = attend_back_stage(
+            place,
+            row_info,
+            column_info,
+            gb_own,
+            gb_other,
+            a_own,
+            a_other,
+            qkv,
+            lse,
+            o,
+            w_attn,
+            relative,
+        )
         if relative:
-            up_half = half_sum(up_grad)
-        gc = group_sum(dot(gz, w_up))
-        unused, pull_two = jax.vjp(layer_norm, middle, vec[2], vec[3])
-        g_mid, g_gain_two, g_shift_two = pull_two(gc)
-        gm = grad_hidden + g_mid
-        gb = gm.astype(bf16)
-        if relative:
-            if attn_part is not None:
-                gb, attn_part = lax.optimization_barrier((gb, attn_part))
-                parts[layer + 1] = (attn_part, down_part, up_part)
-            gb, down_half = lax.optimization_barrier((gb, down_half))
-            down_part = ctx_sum(down_half)
-        gb_all = core_gather(gb)
-        go = heads_of(dot_trans(gb_all, w_o).astype(bf16))
-        prob = jnp.exp(scores_of(q, k) - log_total)
-        prob_low = prob.astype(bf16)
-        g_prob = bdot(go, v, 2, 2)
-        row_dot = jnp.sum(g_prob * prob, axis=-1, keepdims=True)
-        g_scores = (prob * (g_prob - row_dot)).astype(bf16)
-        gq = merge_heads(bdot(g_scores, k, 2, 1) * HEAD ** (-0.5)).astype(bf16)
-        gk = merge_heads(bdot(g_scores, q, 1, 1) * HEAD ** (-0.5)).astype(bf16)
-        gv = merge_heads(bdot(prob_low, go, 1, 1)).astype(bf16)
-        g_qkv = jnp.concatenate([gq, gk, gv], axis=1)
-        if relative:
-            g_qkv, up_half = lax.optimization_barrier((g_qkv, up_half))
-            up_part = ctx_sum(up_half)
-        attn_grad = jnp.concatenate([dot_tokens(g_qkv, a_all), dot_tokens(o, gb_all)])
-        attn_grad = attn_grad.reshape(4, COLS, D)
-        if relative:
-            attn_half = half_sum(attn_grad)
-        ga = group_sum(dot(g_qkv, w_qkv))
-        if relative:
-            ga, down_part = lax.optimization_barrier((ga, down_part))
-        unused, pull_one = jax.vjp(layer_norm, h_in, vec[0], vec[1])
-        g_in, g_gain_one, g_shift_one = pull_one(ga)
-        grad_hidden = gm + g_in
-
-        if not relative:
+            mine, mlp_half = lax.optimization_barrier((mine, mlp_half))
+            mlp_part = ctx_sum(mlp_half)
+            attn_half = half_sum(*attn_grads)
+        else:
+            attn_grad = attn_grads[0]
             g_wo = lax.all_to_all(
                 attn_grad[3].reshape(COLS, TP, COLS), GROUP, split_axis=1, concat_axis=0, tiled=True
             )[:, 0]
             attn_grad = jnp.concatenate([attn_grad[:3], g_wo.T[None]], axis=0)
-            mat_list[layer] = scatter_wide(jnp.stack([attn_grad, up_grad, down_grad], axis=1))
-
-        def place(values):
-            wide = jnp.zeros((values.shape[0], D), f32)
-            return lax.dynamic_update_slice_in_dim(wide, values, t_index * COLS, axis=1)
-
-        def token_sum(values):
-            return jnp.sum(values, axis=0, keepdims=True, dtype=f32)
-
-        sum_qkv = token_sum(g_qkv)
-        sum_up = token_sum(gz).reshape(ctx_size, COLS)
-        placed = place(
-            jnp.concatenate(
-                [sum_qkv[:, :COLS], sum_qkv[:, 2 * COLS :], to_absolute(sum_up) if relative else sum_up]
+            mat_list[layer] = scatter_wide(
+                jnp.concatenate([attn_grad[:, None], mlp_grads[0]], axis=1)
             )
-        )
-        shared = once * jnp.concatenate(
-            [g_gain_one, g_shift_one, g_gain_two, g_shift_two, token_sum(gb), token_sum(gy)]
-        )
-        vec_list[layer] = jnp.concatenate([shared[:4], placed[:2], shared[4:], placed[2:]], axis=0)
+        mine, recv = group_sum(mine, give)
+        grad_hidden, gy_own, in_sums = norm_back_stage(
+            vec_rows, layer, 0, grad_middle, mine, recv, h_in
+        )
+        sum_list[layer] = (in_sums, mid_sums, up_sums, qkv_sums)
     input_grad = send_back(grad_hidden)
 
     if relative:
-        parts[0] = (ctx_sum(from_own(attn_half)), down_part, up_part)
+        parts[0] = (ctx_sum(attn_half), mlp_part)
         for layer in range(LAYERS):
-            attn_part, down_part, up_part = [part.astype(bf16) for part in parts[layer]]
-            mat_list[layer] = jnp.concatenate(
-                [attn_rows(attn_part)[None], mlp_rows(jnp.stack([up_part, down_part]))]
-            )
+            attn_part, mlp_part = [part.astype(bf16) for part in parts[layer]]
+            mat_list[layer] = jnp.concatenate([attn_rows(attn_part)[None], mlp_rows(mlp_part)])
+    once = jnp.where(x_index == 0, 1.0, 0.0).astype(f32)
+    in_sums, mid_sums, up_sums, qkv_sums = [jnp.stack(sums) for sums in zip(*sum_list)]
+    shared = once * jnp.concatenate(
+        [in_sums[:, 0:2], mid_sums[:, 0:3], up_sums[:, 1:2]], axis=1
+    )
+    placed = jnp.concatenate(
+        [
+            qkv_sums[:, 0:1, :COLS],
+            qkv_sums[:, 0:1, 2 * COLS :],
+            up_sums[:, 0].reshape(LAYERS, ctx_size, COLS),
+        ],
+        axis=1,
+    )
+    placed = lax.dynamic_update_slice_in_dim(
+        jnp.zeros((LAYERS, 6, D), f32), placed, t_index * COLS, axis=2
+    )
+    vec_terms = jnp.concatenate(
+        [shared[:, 0:4], placed[:, 0:2], shared[:, 4:6], placed[:, 2:6]], axis=1
+    )
     grad_vecs = lax.dynamic_slice_in_dim(
-        sum_vectors(jnp.stack(vec_list)), dp_index * vectors.shape[2], vectors.shape[2], axis=2
+        sum_vectors(vec_terms), dp_index * vectors.shape[2], vectors.shape[2], axis=2
     )
     cols_dev = weights.shape[3]
     grad_list, moment_list, low_list = [], [], []

time: 682 us -> 584 us (0.86)
  local copies, waits for them, and re-layouts: 123 us -> 48.4 us
  Pallas kernels: 17.1 us -> 86.2 us
  other arithmetic: 103 us -> 52.2 us
  waiting for transfers between devices: 171 us -> 215 us
  starting transfers between devices: 193 us -> 154 us
  matrix products: 44.3 us -> 5.4 us
    pallas_call x0 -> x16, Pallas kernels: none -> 69.2 us  [call(): pl.pallas_call(kernel, out_shape=[jax.ShapeDtypeStruct(shape, kind) for s...]
    ppermute x36 -> x30, waiting for transfers between devices: 40.6 us -> 94.8 us  [rotate(): lax.ppermute(block, axis, [((i + step) % size, i) for i in range(size)])]
    dot_general x28 -> x0, matrix products: 25 us -> none  [the longest x8 9.81 us: dot(): return jnp.dot(operand, other, preferred_element_type=f32)]
    ppermute x36 -> x30, starting transfers between devices: 74.9 us -> 54 us  [rotate(): lax.ppermute(block, axis, [((i + step) % size, i) for i in range(size)])]
    ppermute x37 -> x36, starting transfers between devices: 33.7 us -> 18 us  [the longest x8 5.92 us: group_sum(): return (mine, lax.ppermute(mine.astype(bf16), 'jx', SWAP))]
    reduce_sum x25 -> x0, other arithmetic: 14.9 us -> none  [the longest x8 4.92 us: layer_norm(): center = hidden - jnp.mean(hidden, axis=-1, keepdims=True)]
    ppermute x37 -> x36, waiting for transfers between devices: 84.4 us -> 70.2 us  [the longest x8 43.3 us: group_sum(): return (mine, lax.ppermute(mine.astype(bf16), 'jx', SWAP))]
    dot_general x10 -> x2, matrix products: 19.3 us -> 5.4 us  [dot_trans(): lax.dot_general(operand, other, (((1,), (1,)), ((), ())), preferred_eleme...]
  transfers between devices with their start and end apart: 107 -> 100, of which waited for: 35 -> 36; matrix products, arithmetic and copies ran while one was open for 31% -> 15% of each run, Pallas kernels for 3% -> 13%
where the time goes in v4:
time: 584 us; the launch traced here: 577 us
  waiting for transfers between devices  215 us (37%)
  starting transfers between devices  154 us (26%)
  Pallas kernels  86.2 us (15%)
  other arithmetic  52.2 us (9%)
  local copies, waits for them, and re-layouts  48.4 us (8%)
  between operations  16.3 us (3%)
    ppermute x30, waiting for transfers between devices, rotate(): lax.ppermute(block, axis, [((i + step) % size, i) for i in range(size)])  94.8 us
    pallas_call x16, Pallas kernels, call(): pl.pallas_call(kernel, out_shape=[jax.ShapeDtypeStruct(shape, kind) for s...  69.2 us
    ppermute x30, starting transfers between devices, rotate(): lax.ppermute(block, axis, [((i + step) % size, i) for i in range(size)])  54 us
    ppermute x8, waiting for transfers between devices, group_sum(): return (mine, lax.ppermute(mine.astype(bf16), 'jx', SWAP))  43.3 us
    ppermute x6, starting transfers between devices, shift(): return lax.ppermute(block, ('jc', 'ctx'), moves)  21.1 us
    ppermute x2, waiting for transfers between devices, local(): mlp_weights = (own_mlp, [lax.ppermute(jnp.stack(own_mlp), 'g', SWAP)])  18.3 us
    unnamed x160, local copies, waits for them, and re-layouts  18.2 us
    pallas_call x2, Pallas kernels, orthogonalize(): pl.pallas_call(orthogonalize_kernel, out_shape=jax.ShapeDtypeStruct(matri...  17.1 us
  transfers between devices with their start and end apart: 100, of which 36 were waited for; matrix products, arithmetic and copies ran while one was open for 15% of the time, Pallas kernels for 13%

profile of v4, /device:TPU:0, one launch (start us, length us, event | category | flops | bytes accessed | tf_op | source)
XLA Modules:
  0.0 577.1 jit_solution(10584945433124083949)
XLA Ops:
  55.6 6.7 %collective-permute-done.12.refs_2_ = bf16[192,384]{1,0:T(8,128)(2,1)S(1)} collective-permute-done((bf16[192,384]{1,0:T(8,128)(2,1)S(1)}, bf16[192,384]{1,0:T(8,128)(2,1)S(1)}, u32[]{:S(2)}, u32[]{:S(2)}) %collective-permute-start.12) | collective-permute-done | bytes 147488 | tf_op jit(solution)/shard_map/ppermute | solution.py:69
  74.2 6.1 %shard_map.153 = (bf16[768,768]{1,0:T(8,128)(2,1)}, bf16[512,576]{1,0:T(8,128)(2,1)}, f32[512,128]{1,0:T(8,128)S(1)}, bf16[512,192]{1,0:T(8,128)(2,1)S(1)}, f32[...) custom-call(s32[2]{0:T(128)S(1)} %pad_add_fusion.place_ref, f32[8,512]{1,0:T(8,128)S(1)} %pad.13.row_ref, ...), custom_call_target="tpu_custom_call" | custom-call | tf_op jit(solution)/shard_map/pallas_call | solution.py:230
  80.9 17.2 %collective-permute-done.22.refs_2_ = bf16[2,192,384]{2,1,0:T(8,128)(2,1)S(1)} collective-permute-done((bf16[2,192,384]{2,1,0:T(8,128)(2,1)S(1)}, bf16[2,192,384]{2,1,0:T(8,128)(2,1)S(1)}, u32[]{:S(2)}, u32[]{:S(2)}) %collective-permute-start.22) | collective-permute-done | bytes 294944 | tf_op jit(solution)/shard_map/ppermute | solution.py:69
  101.9 9.3 %collective-permute-done.19.refs_1_ = bf16[256,768]{1,0:T(8,128)(2,1)S(1)} collective-permute-done((bf16[256,768]{1,0:T(8,128)(2,1)S(1)}, bf16[256,768]{1,0:T(8,128)(2,1)S(1)}, u32[]{:S(2)}, u32[]{:S(2)}) %collective-permute-start.19) | collective-permute-done | bytes 393248 | tf_op jit(solution)/shard_map/ppermute | solution.py:589
  115.6 11.7 %collective-permute-done.24.refs_4_ = bf16[4,2,192,384]{3,2,1,0:T(8,128)(2,1)} collective-permute-done((bf16[4,2,192,384]{3,2,1,0:T(8,128)(2,1)}, bf16[4,2,192,384]{3,2,1,0:T(8,128)(2,1)}, u32[]{:S(2)}, u32[]{:S(2)}) %collective-permute-start.24) | collective-permute-done | bytes 1179680 | tf_op jit(solution)/shard_map/ppermute | solution.py:749
  142.1 10.1 %collective-permute-done.31.refs_2_ = bf16[192,384]{1,0:T(8,128)(2,1)S(1)} collective-permute-done((bf16[192,384]{1,0:T(8,128)(2,1)S(1)}, bf16[192,384]{1,0:T(8,128)(2,1)S(1)}, u32[]{:S(2)}, u32[]{:S(2)}) %collective-permute-start.31) | collective-permute-done | bytes 147488 | tf_op jit(solution)/shard_map/ppermute | solution.py:69
  168.4 6.2 %shard_map.157 = (bf16[768,768]{1,0:T(8,128)(2,1)}, bf16[512,576]{1,0:T(8,128)(2,1)}, f32[512,128]{1,0:T(8,128)S(1)}, bf16[512,192]{1,0:T(8,128)(2,1)S(1)}, f32[...) custom-call(s32[2]{0:T(128)S(1)} %pad_add_fusion.place_ref, f32[8,512]{1,0:T(8,128)S(1)} %pad.13.row_ref, ...), custom_call_target="tpu_custom_call" | custom-call | tf_op jit(solution)/shard_map/pallas_call | solution.py:230
  175.5 20.8 %collective-permute-done.38.refs_2_ = bf16[2,192,384]{2,1,0:T(8,128)(2,1)S(1)} collective-permute-done((bf16[2,192,384]{2,1,0:T(8,128)(2,1)S(1)}, bf16[2,192,384]{2,1,0:T(8,128)(2,1)S(1)}, u32[]{:S(2)}, u32[]{:S(2)}) %collective-permute-start.38) | collective-permute-done | bytes 294944 | tf_op jit(solution)/shard_map/ppermute | solution.py:69
  200.6 10.0 %collective-permute-done.35.refs_1_ = bf16[256,768]{1,0:T(8,128)(2,1)S(1)} collective-permute-done((bf16[256,768]{1,0:T(8,128)(2,1)S(1)}, bf16[256,768]{1,0:T(8,128)(2,1)S(1)}, u32[]{:S(2)}, u32[]{:S(2)}) %collective-permute-start.35) | collective-permute-done | bytes 393248 | tf_op jit(solution)/shard_map/ppermute | solution.py:589
  218.8 6.7 %collective-permute-done.40.refs_4_ = bf16[4,2,192,384]{3,2,1,0:T(8,128)(2,1)} collective-permute-done((bf16[4,2,192,384]{3,2,1,0:T(8,128)(2,1)}, bf16[4,2,192,384]{3,2,1,0:T(8,128)(2,1)}, u32[]{:S(2)}, u32[]{:S(2)}) %collective-permute-start.40) | collective-permute-done | bytes 1179680 | tf_op jit(solution)/shard_map/ppermute | solution.py:749
  231.6 7.5 %shard_map.160 = (f32[256,768]{1,0:T(8,128)}, bf16[256,768]{1,0:T(8,128)(2,1)S(1)}, f32[8,768]{1,0:T(8,128)S(1)}, f32[4,2,192,384]{3,2,1,0:T(8,128)}, bf16[4,2,192,384]{3,2,1,0:T(8,128)(2,1)}) custom-call(s32[2]{0:T(128)S(1)} %pad_add_fusion.place_ref, bf16[256,768]{1,0:T(8,128)(2,1)S(1)} %fusion.54.own_gy_ref, ...), custom_call_target="tpu_custom_call" | custom-call | tf_op jit(solution)/shard_map/pallas_call | solution.py:230
  243.9 10.2 %collective-permute-done.48.recv_ref = bf16[256,768]{1,0:T(8,128)(2,1)S(1)} collective-permute-done((bf16[256,768]{1,0:T(8,128)(2,1)S(1)}, bf16[256,768]{1,0:T(8,128)(2,1)S(1)}, u32[]{:S(2)}, u32[]{:S(2)}) %collective-permute-start.48) | collective-permute-done | bytes 393248 | tf_op jit(solution)/shard_map/ppermute | solution.py:589
  259.1 8.5 %shard_map.162 = (f32[256,768]{1,0:T(8,128)}, bf16[256,768]{1,0:T(8,128)(2,1)S(1)}, f32[8,576]{1,0:T(8,128)S(1)}, f32[4,192,384]{2,1,0:T(8,128)}, bf16[4,192,384]{2,1,0:T(8,128)(2,1)}) custom-call(s32[2]{0:T(128)S(1)} %pad_add_fusion.place_ref, f32[8,512]{1,0:T(8,128)S(1)} %pad.13.row_ref, f32[512,128]{1,0:T(8,128)S(1)} %pad.14.column_ref, ...), custom_call_target="tpu_custom_call" | custom-call | tf_op jit(solution)/shard_map/pallas_call | solution.py:230
  274.5 8.7 %collective-permute-done.52.recv_ref = bf16[256,768]{1,0:T(8,128)(2,1)S(1)} collective-permute-done((bf16[256,768]{1,0:T(8,128)(2,1)S(1)}, bf16[256,768]{1,0:T(8,128)(2,1)S(1)}, u32[]{:S(2)}, u32[]{:S(2)}) %collective-permute-start.52) | collective-permute-done | bytes 393248 | tf_op jit(solution)/shard_map/ppermute | solution.py:589
  295.1 7.5 %shard_map.164 = (f32[256,768]{1,0:T(8,128)}, bf16[256,768]{1,0:T(8,128)(2,1)S(1)}, f32[8,768]{1,0:T(8,128)S(1)}, f32[4,2,192,384]{3,2,1,0:T(8,128)}, bf16[4,2,192,384]{3,2,1,0:T(8,128)(2,1)}) custom-call(s32[2]{0:T(128)S(1)} %pad_add_fusion.place_ref, bf16[256,768]{1,0:T(8,128)(2,1)S(1)} %get-tuple-element.117.own_gy_ref, ...), custom_call_target="tpu_custom_call" | custom-call | tf_op jit(solution)/shard_map/pallas_call | solution.py:230
  316.1 10.9 %collective-permute-done.62 = bf16[192,384]{1,0:T(8,128)(2,1)S(1)} collective-permute-done((bf16[192,384]{1,0:T(8,128)(2,1)S(1)}, bf16[192,384]{1,0:T(8,128)(2,1)S(1)}, u32[]{:S(2)}, u32[]{:S(2)}) %collective-permute-start.62) | collective-permute-done | bytes 147488 | tf_op jit(solution)/shard_map/ppermute | solution.py:69
  359.2 9.2 %shard_map.166 = (f32[256,768]{1,0:T(8,128)}, bf16[256,768]{1,0:T(8,128)(2,1)S(1)}, f32[8,576]{1,0:T(8,128)S(1)}, f32[4,192,384]{2,1,0:T(8,128)}, bf16[4,192,384]{2,1,0:T(8,128)(2,1)}) custom-call(s32[2]{0:T(128)S(1)} %pad_add_fusion.place_ref, f32[8,512]{1,0:T(8,128)S(1)} %pad.13.row_ref, f32[512,128]{1,0:T(8,128)S(1)} %pad.14.column_ref, ...), custom_call_target="tpu_custom_call" | custom-call | tf_op jit(solution)/shard_map/pallas_call | solution.py:230
  369.4 8.4 %collective-permute-start.76 = (bf16[2,192,384]{2,1,0:T(8,128)(2,1)}, bf16[2,192,384]{2,1,0:T(8,128)(2,1)S(1)}, u32[]{:S(2)}, u32[]{:S(2)}) collective-permute-start(bf16[2,192,384]{2,1,0:T(8,128)(2,1)} %get-tuple-element.188), channel_id=1, source_target_pairs={{2,0},{3,1},{0,2},{1,3},{6,4},{7,5},{4,6},{5,7},{10,8},{11,9},{8,1... | collective-permute-start | bytes 884744 | tf_op jit(solution)/shard_map/ppermute | solution.py:69
  385.6 7.0 %collective-permute-done.76 = bf16[2,192,384]{2,1,0:T(8,128)(2,1)S(1)} collective-permute-done((bf16[2,192,384]{2,1,0:T(8,128)(2,1)}, bf16[2,192,384]{2,1,0:T(8,128)(2,1)S(1)}, u32[]{:S(2)}, u32[]{:S(2)}) %collective-permute-start.76) | collective-permute-done | bytes 294944 | tf_op jit(solution)/shard_map/ppermute | solution.py:69
  392.6 6.9 %collective-permute-done.75 = bf16[2,192,384]{2,1,0:T(8,128)(2,1)S(1)} collective-permute-done((bf16[2,192,384]{2,1,0:T(8,128)(2,1)}, bf16[2,192,384]{2,1,0:T(8,128)(2,1)S(1)}, u32[]{:S(2)}, u32[]{:S(2)}) %collective-permute-start.75) | collective-permute-done | bytes 294944 | tf_op jit(solution)/shard_map/ppermute | solution.py:69
  468.1 11.8 %collective-permute-done.90 = f32[2,3,768]{2,0,1:T(2,128)S(1)} collective-permute-done((f32[2,3,768]{2,0,1:T(2,128)S(1)}, f32[2,3,768]{2,0,1:T(2,128)S(1)}, u32[]{:S(2)}, u32[]{:S(2)}) %collective-permute-start.90) | collective-permute-done | bytes 18464 | tf_op jit(solution)/shard_map/ppermute | solution.py:226
  487.7 7.9 %collective-permute-start.80 = (bf16[192,768]{1,0:T(8,128)(2,1)S(1)}, bf16[192,768]{1,0:T(8,128)(2,1)S(1)}, u32[]{:S(2)}, u32[]{:S(2)}) collective-permute-start(bf16[192,768]{1,0:T(8,128)(2,1)S(1)} %get-tuple-element.184), channel_id=1, source_target_pairs={{1,0},{2,1},{3,2},{0,3},{9,8},{10,9},{11,10},{8,11},{17,16},{18,17... | collective-permute-start | bytes 884744 | tf_op jit(solution)/shard_map/ppermute | solution.py:675
  529.4 9.1 %shard_map.169 = bf16[768,768]{1,0:T(8,128)(2,1)} custom-call(bf16[768,768]{1,0:T(8,128)(2,1)S(1)} %bitcast.297, f32[768,768]{1,0:T(8,128)S(1)} %convert_select_fusion.gram_ref), custom_call_target="tpu_custom_call" | custom-call | tf_op jit(solution)/shard_map/pallas_call | solution.py:655
  549.3 8.0 %shard_map.168 = bf16[768,768]{1,0:T(8,128)(2,1)S(1)} custom-call(bf16[768,768]{1,0:T(8,128)(2,1)S(1)} %copy-done.11, f32[768,768]{1,0:T(8,128)S(1)} %fusion.77.gram_ref), custom_call_target="tpu_custom_call" | custom-call | tf_op jit(solution)/shard_map/pallas_call | solution.py:655
  (531 shorter events, 334.7 us)
Async XLA Ops:
  16.4 27.4 %collective-permute-start.6 = (f32[136,768]{1,0:T(8,128)}, f32[136,768]{1,0:T(8,128)S(1)}, u32[]{:S(2)}, u32[]{:S(2)}) collective-permute-start(f32[136,768]{1,0:T(8,128)} %select_maximum_fusion), channel_id=1, source_target_pairs={{0,0},{1,8},{2,4},{3,12},{4,1},{5,9},{6,5},{7,13},{8,2},{9,10},{10... | collective-permute-start | bytes 1253384 | tf_op jit(solution)/shard_map/ppermute | solution.py:712
  39.2 28.0 %all-to-all-start.1 = ((bf16[5,96,4,192]{1,3,0,2:T(8,128)(2,1)}), bf16[5,96,4,192]{1,3,0,2:T(8,128)(2,1)}, u32[]{:S(2)}, u32[]{:S(2)}) async-start(bf16[5,96,4,192]{1,3,0,2:T(8,128)(2,1)} %copy.92), calls=%async_computation.1 | async-start | bytes 1966080 | tf_op jit(solution)/shard_map/all_to_all | solution.py:58
  73.2 24.9 %collective-permute-start.22 = (bf16[2,192,384]{2,1,0:T(8,128)(2,1)S(1)}, bf16[2,192,384]{2,1,0:T(8,128)(2,1)S(1)}, u32[]{:S(2)}, u32[]{:S(2)}) collective-permute-start(bf16[2,192,384]{2,1,0:T(8,128)(2,1)S(1)} %bitcast.299), channel_id=1, source_target_pairs={{2,0},{3,1},{0,2},{1,3},{6,4},{7,5},{4,6},{5,7},{10,8},{11,9},{8,1... | collective-permute-start | bytes 884744 | tf_op jit(solution)/shard_map/ppermute | solution.py:69
  73.2 24.9 %collective-permute-start.23 = (bf16[2,192,384]{2,1,0:T(8,128)(2,1)S(1)}, bf16[2,192,384]{2,1,0:T(8,128)(2,1)S(1)}, u32[]{:S(2)}, u32[]{:S(2)}) collective-permute-start(bf16[2,192,384]{2,1,0:T(8,128)(2,1)S(1)} %bitcast.300), channel_id=1, source_target_pairs={{3,0},{0,1},{1,2},{2,3},{7,4},{4,5},{5,6},{6,7},{11,8},{8,9},{9,10... | collective-permute-start | bytes 884744 | tf_op jit(solution)/shard_map/ppermute | solution.py:69
  99.3 28.0 %collective-permute-start.24 = (bf16[4,2,192,384]{3,2,1,0:T(8,128)(2,1)}, bf16[4,2,192,384]{3,2,1,0:T(8,128)(2,1)}, u32[]{:S(2)}, u32[]{:S(2)}) collective-permute-start(bf16[4,2,192,384]{3,2,1,0:T(8,128)(2,1)} %pad_maximum_fusion.1), channel_id=1, source_target_pairs={{0,16},{16,0},{1,17},{17,1},{2,18},{18,2},{3,19},{19,3},{4,20},{20... | collective-permute-start | bytes 3538952 | tf_op jit(solution)/shard_map/ppermute | solution.py:749
  159.0 37.4 %collective-permute-start.38 = (bf16[2,192,384]{2,1,0:T(8,128)(2,1)S(1)}, bf16[2,192,384]{2,1,0:T(8,128)(2,1)S(1)}, u32[]{:S(2)}, u32[]{:S(2)}) collective-permute-start(bf16[2,192,384]{2,1,0:T(8,128)(2,1)S(1)} %bitcast.304), channel_id=1, source_target_pairs={{2,0},{3,1},{0,2},{1,3},{6,4},{7,5},{4,6},{5,7},{10,8},{11,9},{8,1... | collective-permute-start | bytes 884744 | tf_op jit(solution)/shard_map/ppermute | solution.py:69
  161.1 35.2 %collective-permute-start.39 = (bf16[2,192,384]{2,1,0:T(8,128)(2,1)S(1)}, bf16[2,192,384]{2,1,0:T(8,128)(2,1)S(1)}, u32[]{:S(2)}, u32[]{:S(2)}) collective-permute-start(bf16[2,192,384]{2,1,0:T(8,128)(2,1)S(1)} %bitcast.305), channel_id=1, source_target_pairs={{3,0},{0,1},{1,2},{2,3},{7,4},{4,5},{5,6},{6,7},{11,8},{8,9},{9,10... | collective-permute-start | bytes 884744 | tf_op jit(solution)/shard_map/ppermute | solution.py:69
  174.6 23.0 %collective-permute-start.34 = (bf16[256,768]{1,0:T(8,128)(2,1)S(1)}, bf16[256,768]{1,0:T(8,128)(2,1)S(1)}, u32[]{:S(2)}, u32[]{:S(2)}) collective-permute-start(bf16[256,768]{1,0:T(8,128)(2,1)S(1)} %get-tuple-element.92), channel_id=1, source_target_pairs={{0,4},{4,0},{1,5},{5,1},{2,6},{6,2},{3,7},{7,3},{8,12},{12,8},{9,1... | collective-permute-start | bytes 1179656 | tf_op jit(solution)/shard_map/ppermute | solution.py:584
  174.6 24.0 %collective-permute-start.44 = (f32[128,768]{1,0:T(8,128)S(1)}, f32[128,768]{1,0:T(8,128)S(1)}, u32[]{:S(2)}, u32[]{:S(2)}) collective-permute-start(f32[128,768]{1,0:T(8,128)S(1)} %bitcast.359), channel_id=1, source_target_pairs={{0,0},{1,8},{2,4},{3,12},{4,1},{5,9},{6,5},{7,13},{8,2},{9,10},{10... | collective-permute-start | bytes 1179656 | tf_op jit(solution)/shard_map/ppermute | solution.py:775
  197.5 27.9 %collective-permute-start.40 = (bf16[4,2,192,384]{3,2,1,0:T(8,128)(2,1)}, bf16[4,2,192,384]{3,2,1,0:T(8,128)(2,1)}, u32[]{:S(2)}, u32[]{:S(2)}) collective-permute-start(bf16[4,2,192,384]{3,2,1,0:T(8,128)(2,1)} %pad_maximum_fusion.2), channel_id=1, source_target_pairs={{0,16},{16,0},{1,17},{17,1},{2,18},{18,2},{3,19},{19,3},{4,20},{20... | collective-permute-start | bytes 3538952 | tf_op jit(solution)/shard_map/ppermute | solution.py:749
  239.0 29.1 %collective-permute-start.50 = (bf16[4,2,192,384]{3,2,1,0:T(8,128)(2,1)}, bf16[4,2,192,384]{3,2,1,0:T(8,128)(2,1)S(1)}, u32[]{:S(2)}, u32[]{:S(2)}) collective-permute-start(bf16[4,2,192,384]{3,2,1,0:T(8,128)(2,1)} %get-tuple-element.113), channel_id=1, source_target_pairs={{0,16},{16,0},{1,17},{17,1},{2,18},{18,2},{3,19},{19,3},{4,20},{20... | collective-permute-start | bytes 3538952 | tf_op jit(solution)/shard_map/ppermute | solution.py:175
  273.4 29.2 %collective-permute-start.54 = (bf16[4,192,384]{2,1,0:T(8,128)(2,1)}, bf16[4,192,384]{2,1,0:T(8,128)(2,1)S(1)}, u32[]{:S(2)}, u32[]{:S(2)}) collective-permute-start(bf16[4,192,384]{2,1,0:T(8,128)(2,1)} %get-tuple-element.122), channel_id=1, source_target_pairs={{0,16},{16,0},{1,17},{17,1},{2,18},{18,2},{3,19},{19,3},{4,20},{20... | collective-permute-start | bytes 1769480 | tf_op jit(solution)/shard_map/ppermute | solution.py:175
  293.1 22.8 %collective-permute-start.57 = (bf16[2,192,384]{2,1,0:T(8,128)(2,1)S(1)}, bf16[2,192,384]{2,1,0:T(8,128)(2,1)S(1)}, u32[]{:S(2)}, u32[]{:S(2)}) collective-permute-start(bf16[2,192,384]{2,1,0:T(8,128)(2,1)S(1)} %get-tuple-element.190), channel_id=1, source_target_pairs={{3,0},{0,1},{1,2},{2,3},{7,4},{4,5},{5,6},{6,7},{11,8},{8,9},{9,10... | collective-permute-start | bytes 884744 | tf_op jit(solution)/shard_map/ppermute | solution.py:69
  302.9 24.1 %collective-permute-start.62 = (bf16[192,384]{1,0:T(8,128)(2,1)S(1)}, bf16[192,384]{1,0:T(8,128)(2,1)S(1)}, u32[]{:S(2)}, u32[]{:S(2)}) collective-permute-start(bf16[192,384]{1,0:T(8,128)(2,1)S(1)} %get-tuple-element.209), channel_id=1, source_target_pairs={{2,0},{3,1},{0,2},{1,3},{6,4},{7,5},{4,6},{5,7},{10,8},{11,9},{8,1... | collective-permute-start | bytes 442376 | tf_op jit(solution)/shard_map/ppermute | solution.py:69
  305.8 25.6 %collective-permute-start.61 = (bf16[192,384]{1,0:T(8,128)(2,1)S(1)}, bf16[192,384]{1,0:T(8,128)(2,1)S(1)}, u32[]{:S(2)}, u32[]{:S(2)}) collective-permute-start(bf16[192,384]{1,0:T(8,128)(2,1)S(1)} %get-tuple-element.210), channel_id=1, source_target_pairs={{1,0},{2,1},{3,2},{0,3},{5,4},{6,5},{7,6},{4,7},{9,8},{10,9},{11,1... | collective-permute-start | bytes 442376 | tf_op jit(solution)/shard_map/ppermute | solution.py:69
  315.5 41.2 %collective-permute-start.64 = (bf16[4,2,192,384]{3,2,1,0:T(8,128)(2,1)}, bf16[4,2,192,384]{3,2,1,0:T(8,128)(2,1)}, u32[]{:S(2)}, u32[]{:S(2)}) collective-permute-start(bf16[4,2,192,384]{3,2,1,0:T(8,128)(2,1)} %get-tuple-element.135), channel_id=1, source_target_pairs={{0,16},{16,0},{1,17},{17,1},{2,18},{18,2},{3,19},{19,3},{4,20},{20... | collective-permute-start | bytes 3538952 | tf_op jit(solution)/shard_map/ppermute | solution.py:175
  350.5 29.4 %collective-permute-start.78 = (bf16[96,384]{1,0:T(8,128)(2,1)}, bf16[96,384]{1,0:T(8,128)(2,1)}, u32[]{:S(2)}, u32[]{:S(2)}) collective-permute-start(bf16[96,384]{1,0:T(8,128)(2,1)} %constant_dynamic-slice_fusion.5), channel_id=1, source_target_pairs={{0,4},{4,0},{1,5},{5,1},{2,6},{6,2},{3,7},{7,3},{8,12},{12,8},{9,1... | collective-permute-start | bytes 221192 | tf_op jit(solution)/shard_map/ppermute | solution.py:132
  368.4 38.0 %collective-permute-start.65 = (bf16[256,768]{1,0:T(8,128)(2,1)S(1)}, bf16[256,768]{1,0:T(8,128)(2,1)}, u32[]{:S(2)}, u32[]{:S(2)}) collective-permute-start(bf16[256,768]{1,0:T(8,128)(2,1)S(1)} %get-tuple-element.137), channel_id=1, source_target_pairs={{0,4},{4,0},{1,5},{5,1},{2,6},{6,2},{3,7},{7,3},{8,12},{12,8},{9,1... | collective-permute-start | bytes 1179656 | tf_op jit(solution)/shard_map/ppermute | solution.py:584
  369.4 23.2 %collective-permute-start.76 = (bf16[2,192,384]{2,1,0:T(8,128)(2,1)}, bf16[2,192,384]{2,1,0:T(8,128)(2,1)S(1)}, u32[]{:S(2)}, u32[]{:S(2)}) collective-permute-start(bf16[2,192,384]{2,1,0:T(8,128)(2,1)} %get-tuple-element.188), channel_id=1, source_target_pairs={{2,0},{3,1},{0,2},{1,3},{6,4},{7,5},{4,6},{5,7},{10,8},{11,9},{8,1... | collective-permute-start | bytes 884744 | tf_op jit(solution)/shard_map/ppermute | solution.py:69
  384.7 37.9 %collective-permute-start.68 = (bf16[4,192,384]{2,1,0:T(8,128)(2,1)}, bf16[4,192,384]{2,1,0:T(8,128)(2,1)}, u32[]{:S(2)}, u32[]{:S(2)}) collective-permute-start(bf16[4,192,384]{2,1,0:T(8,128)(2,1)} %get-tuple-element.140), channel_id=1, source_target_pairs={{0,16},{16,0},{1,17},{17,1},{2,18},{18,2},{3,19},{19,3},{4,20},{20... | collective-permute-start | bytes 1769480 | tf_op jit(solution)/shard_map/ppermute | solution.py:175
  408.5 23.9 %collective-permute-start.66 = (bf16[256,768]{1,0:T(8,128)(2,1)}, bf16[256,768]{1,0:T(8,128)(2,1)S(1)}, u32[]{:S(2)}, u32[]{:S(2)}) collective-permute-start(bf16[256,768]{1,0:T(8,128)(2,1)} %get-tuple-element.164), channel_id=1, source_target_pairs={{0,8},{8,0},{1,9},{9,1},{2,10},{10,2},{3,11},{11,3},{4,12},{12,4},... | collective-permute-start | bytes 1179656 | tf_op jit(solution)/shard_map/ppermute | solution.py:589
  453.8 28.7 %all-to-all-start.6 = ((bf16[8,1,96,768]{3,2,1,0:T(8,128)(2,1)}), bf16[8,1,96,768]{3,2,1,0:T(8,128)(2,1)S(1)}, u32[]{:S(2)}, u32[]{:S(2)}) async-start(bf16[8,1,96,768]{3,2,1,0:T(8,128)(2,1)} %bitcast.94), calls=%async_computation.6 | async-start | bytes 2359296 | tf_op jit(solution)/shard_map/all_to_all | solution.py:880
  457.4 89.1 %all-gather.2.cloned.1.call-start = ((), (), s32[]{:S(2)}) async-start(), calls=%async_computation.8 | async-start | bytes 1327104 | tf_op jit(solution)/shard_map/all_gather | solution.py:892
  458.8 87.7 %collective-permute-start.67 = (f32[128,768]{1,0:T(8,128)}, f32[128,768]{1,0:T(8,128)}, u32[]{:S(2)}, u32[]{:S(2)}) collective-permute-start(f32[128,768]{1,0:T(8,128)} %constant_dynamic-slice_fusion.7), channel_id=1, source_target_pairs={{0,0},{8,1},{4,2},{12,3},{1,4},{9,5},{5,6},{13,7},{2,8},{10,9},{6,... | collective-permute-start | bytes 1179656 | tf_op jit(solution)/shard_map/ppermute | solution.py:772
  (151 other events, 1494.6 us)
Sparse Core Ops, SparseCore 0:
  516.5 25.1 all-gather.1

commit v5 on v4

--- a/solution.py
+++ b/solution.py
@@ -110,17 +110,16 @@
     return moves
 
 
-def attn_piece(mat, piece):
-    half = mat.shape[1] // 2
+def out_pieces(mats):
+    half = mats.shape[2] // 2
     core = lax.axis_index("jc")
-    mine = lax.dynamic_slice_in_dim(mat, core * half, half, axis=1)
-    give = lax.dynamic_slice_in_dim(mat, (1 - core) * half, half, axis=1)
+    mine = lax.dynamic_slice_in_dim(mats, core * half, half, axis=2)
+    give = lax.dynamic_slice_in_dim(mats, (1 - core) * half, half, axis=2)
     got = lax.ppermute(give, "jc", SWAP)
     rows = jnp.concatenate(
-        [jnp.where(core == 0, mine, got), jnp.where(core == 0, got, mine)], axis=0
-    )
-    rows = lax.ppermute(rows, EVERY, out_moves())
-    return jnp.where(lax.axis_index("ctx") == lax.axis_size("ctx") - 1, rows, piece)
+        [jnp.where(core == 0, mine, got), jnp.where(core == 0, got, mine)], axis=1
+    )
+    return lax.ppermute(rows, EVERY, out_moves())
 
 
 def out_back(piece):
@@ -135,14 +134,21 @@
     )
 
 
-def pack_pieces(low):
-    first = to_group(low[0, 0:1])
-    rest = to_group(after(jnp.concatenate([low[0, 1:3], low[1:].reshape(-1, *low.shape[2:])]), first))
-    pieces = [(attn_piece(low[0, 0], first[0].T), jnp.swapaxes(rest[0:2], 1, 2))]
-    for layer in range(1, low.shape[0]):
+def pack_pieces(mats):
+    attn = mats[:, 0].astype(bf16)
+    outs = out_pieces(attn)
+    first = to_group(attn[0:1])
+    rest = [mats[0, 1:3]] + [mats[layer] for layer in range(1, mats.shape[0])]
+    rest = to_group(after(jnp.concatenate(rest), first).astype(bf16))
+    last = lax.axis_index("ctx") == lax.axis_size("ctx") - 1
+    pieces = [(jnp.where(last, outs[0], first[0].T), jnp.swapaxes(rest[0:2], 1, 2))]
+    for layer in range(1, mats.shape[0]):
         base = 3 * layer - 1
         pieces.append(
-            (attn_piece(low[layer, 0], rest[base].T), jnp.swapaxes(rest[base + 1 : base + 3], 1, 2))
+            (
+                jnp.where(last, outs[layer], rest[base].T),
+                jnp.swapaxes(rest[base + 1 : base + 3], 1, 2),
+            )
         )
     return pieces
 
@@ -150,6 +156,10 @@
 def ctx_gather(piece):
     near, back, far = [rotate(piece, "ctx", step) for step in (1, 3, 2)]
     return [piece, near, far, back]
+
+
+def group_swap(blocks):
+    return [lax.ppermute(block, "g", SWAP) for block in blocks]
 
 
 def gather_weights_wide(low):
@@ -338,15 +348,11 @@
     tokens = 2 * half
     wide = 3 * COLS
     own, other = weights if isinstance(weights, tuple) else ([], [])
-    stacked = bool(other) and other[0].ndim == 3
 
     def kernel(place_ref, row_ref, column_ref, bias_ref, own_a_ref, other_a_ref, *refs):
         if own:
             own_refs, refs = refs[:4], refs[4:]
-            count = len(other)
-            others, refs = refs[:count], refs[count:]
-            if stacked:
-                others = [others[0].at[step] for step in range(4)]
+            others, refs = refs[:4], refs[4:]
             w_ref, qkv_ref, lse_ref, o_ref, mine_ref, give_ref = refs
             put_blocks(place_ref, own_refs, others, [w_ref])
         else:
@@ -491,8 +497,7 @@
 
     def kernel(place_ref, bias_ref, own_c_ref, other_c_ref, *refs):
         if own:
-            own_refs, other_ref, refs = refs[:4], refs[4], refs[5:]
-            others = [other_ref.at[step] for step in range(4)]
+            own_refs, others, refs = refs[:4], refs[4:8], refs[8:]
             w_ref, preact_ref, act_ref, mine_ref, give_ref = refs
             put_blocks(place_ref, own_refs, others, [w_ref.at[0], w_ref.at[1]])
         else:
@@ -713,16 +718,15 @@
     hidden = x_join(moved[:tokens_dev])
     segment_row = moved[tokens_dev, :seq_len]
     relative = lax.axis_size("g") == 2
-    low = weights.astype(bf16)
     place = jnp.stack([z_index, lax.axis_index("g")]).astype(jnp.int32)
     if relative:
-        pieces = pack_pieces(low)
+        pieces = pack_pieces(weights)
         own_attn = ctx_gather(pieces[0][0])
         own_mlp = ctx_gather(after(pieces[0][1], *own_attn[1:]))
-        swap_attn = [lax.ppermute(block, "g", SWAP) for block in own_attn]
-        attn_weights = (own_attn, swap_attn)
+        attn_weights = (own_attn, group_swap(own_attn))
+        mlp_weights = (own_mlp, group_swap(own_mlp))
     else:
-        wide_weights = gather_weights_wide(low)
+        wide_weights = gather_weights_wide(weights.astype(bf16))
 
     start = c_index * half
     pos = jnp.concatenate([start + jnp.arange(half), half - start + jnp.arange(half)])
@@ -745,19 +749,23 @@
         w_attn, qkv, lse, o, mine, give = attend_stage(
             place, row_info, column_info, qkv_bias[layer], a_own, a_other, attn_weights
         )
-        if relative:
-            mlp_weights = (own_mlp, [lax.ppermute(jnp.stack(own_mlp), "g", SWAP)])
-            if following:
-                own_attn = ctx_gather(after(pieces[layer + 1][0], o))
+        if relative and layer:
+            mine, own_mlp = lax.optimization_barrier((mine, own_mlp))
+            mlp_weights = (own_mlp, group_swap(own_mlp))
+        if relative and following:
+            next_attn = ctx_gather(after(pieces[layer + 1][0], *own_mlp[1:]))
+            next_mlp = ctx_gather(after(pieces[layer + 1][1], *next_attn[1:]))
         mine, recv = group_sum(mine, give)
         middle, c_own = norm_stage(vec_rows, layer, 2, hidden, mine, recv, (layer, 6))
+        if relative and following:
+            c_own, next_attn = lax.optimization_barrier((c_own, next_attn))
         c_other = core_swap(c_own)
         w_mlp, preact, act, mine, give = feed_stage(
             place, up_bias[layer], c_own, c_other, mlp_weights
         )
         if relative and following:
-            own_mlp = ctx_gather(after(pieces[layer + 1][1], act, *own_attn[1:]))
-            attn_weights = (own_attn, [lax.ppermute(jnp.stack(own_attn), "g", SWAP)])
+            attn_weights = (next_attn, group_swap(next_attn))
+            own_mlp = next_mlp
         mine, recv = group_sum(mine, give)
         stored.append(
             (hidden, middle, a_own, a_other, qkv, lse, o, c_own, c_other, preact, act, w_attn, w_mlp)
@@ -774,31 +782,33 @@
     hidden_out = send_back(hidden)
     grad_hidden = x_join(lax.ppermute(after(out_grad[0], stored[-1][6]), axes, to_seq))
     gy_own = grad_hidden.astype(bf16)
+    attn_half = mlp_part = None
 
     mat_list = [None] * LAYERS
     sum_list = [None] * LAYERS
     parts = [None] * LAYERS
-    attn_half = None
     for layer in reversed(range(LAYERS)):
         h_in, middle, a_own, a_other, qkv, lse, o, c_own, c_other, preact, act, w_attn, w_mlp = stored[
             layer
         ]
+        if relative and attn_half is not None:
+            gy_own, attn_half, mlp_part = lax.optimization_barrier((gy_own, attn_half, mlp_part))
+            attn_part = ctx_sum(attn_half)
         gy_other = core_swap(gy_own)
         mine, give, up_sums, *mlp_grads = feed_back_stage(
             place, gy_own, gy_other, c_own, c_other, preact, act, w_mlp, relative
         )
         if relative:
-            if attn_half is not None:
-                mine, attn_half = lax.optimization_barrier((mine, attn_half))
-                attn_part = ctx_sum(attn_half)
             mlp_half = half_sum(*mlp_grads)
         mine, recv = group_sum(mine, give)
         grad_middle, gb_own, mid_sums = norm_back_stage(
             vec_rows, layer, 2, grad_hidden, mine, recv, middle
         )
         if relative and attn_half is not None:
-            gb_own, mlp_part, attn_part = lax.optimization_barrier((gb_own, mlp_part, attn_part))
+            gb_own, attn_part = lax.optimization_barrier((gb_own, attn_part))
             parts[layer + 1] = (attn_part, mlp_part)
+        if layer == LAYERS - 1:
+            gb_own, hidden_out = lax.optimization_barrier((gb_own, hidden_out))
         gb_other = core_swap(gb_own)
         mine, give, qkv_sums, *attn_grads = attend_back_stage(
             place,
@@ -837,7 +847,9 @@
     if relative:
         parts[0] = (ctx_sum(attn_half), mlp_part)
         for layer in range(LAYERS):
-            attn_part, mlp_part = [part.astype(bf16) for part in parts[layer]]
+            attn_part, mlp_part = [
+                after(part, grad_hidden).astype(bf16) for part in parts[layer]
+            ]
             mat_list[layer] = jnp.concatenate([attn_rows(attn_part)[None], mlp_rows(mlp_part)])
     once = jnp.where(x_index == 0, 1.0, 0.0).astype(f32)
     in_sums, mid_sums, up_sums, qkv_sums = [jnp.stack(sums) for sums in zip(*sum_list)]

time: 584 us -> 679 us (1.16)
  starting transfers between devices: 154 us -> 198 us
  waiting for transfers between devices: 215 us -> 250 us
  local copies, waits for them, and re-layouts: 48.4 us -> 64 us
    ppermute x11 -> x18, waiting for transfers between devices: 24 us -> 65.5 us  [the longest x16 65.5 us: group_swap(): return [lax.ppermute(block, 'g', SWAP) for block in blocks]]
    ppermute x30, starting transfers between devices: 54 us -> 77.7 us  [rotate(): lax.ppermute(block, axis, [((i + step) % size, i) for i in range(size)])]
    ppermute x16, starting transfers between devices: 1.33 us -> 11.3 us  [core_swap(): return lax.ppermute(block, 'jc', SWAP)]
    all_to_all x2, waiting for transfers between devices: 0.01 us -> 9.46 us  [to_group(): lax.all_to_all(split, GROUP, split_axis=2, concat_axis=1, tiled=True)]
    slice x10, local copies, waits for them, and re-layouts: 3.06 us -> 9.98 us  [local(): grad = mat_list[layer][item]]
    ppermute x11 -> x18, starting transfers between devices: 12 us -> 18.4 us  [the longest x16 16.3 us: group_swap(): return [lax.ppermute(block, 'g', SWAP) for block in blocks]]
    unnamed x160 -> x172, local copies, waits for them, and re-layouts: 18.2 us -> 22.1 us
  transfers between devices with their start and end apart: 100 -> 107, of which waited for: 36 -> 48; matrix products, arithmetic and copies ran while one was open for 15% -> 14% of each run, Pallas kernels for 13% -> 7%
where the time goes in v5:
time: 679 us; the launch traced here: 669 us
  waiting for transfers between devices  250 us (37%)
  starting transfers between devices  198 us (29%)
  Pallas kernels  85.5 us (13%)
  local copies, waits for them, and re-layouts  64 us (9%)
  other arithmetic  51.3 us (8%)
  between operations  15.8 us (2%)
    ppermute x30, waiting for transfers between devices, rotate(): lax.ppermute(block, axis, [((i + step) % size, i) for i in range(size)])  90.2 us
    ppermute x30, starting transfers between devices, rotate(): lax.ppermute(block, axis, [((i + step) % size, i) for i in range(size)])  77.7 us
    pallas_call x16, Pallas kernels, call(): pl.pallas_call(kernel, out_shape=[jax.ShapeDtypeStruct(shape, kind) for s...  68.4 us
    ppermute x16, waiting for transfers between devices, group_swap(): return [lax.ppermute(block, 'g', SWAP) for block in blocks]  65.5 us
    ppermute x8, waiting for transfers between devices, group_sum(): return (mine, lax.ppermute(mine.astype(bf16), 'jx', SWAP))  42.7 us
    unnamed x172, local copies, waits for them, and re-layouts  22.1 us
    ppermute x6, starting transfers between devices, shift(): return lax.ppermute(block, ('jc', 'ctx'), moves)  21.9 us
    pallas_call x2, Pallas kernels, orthogonalize(): pl.pallas_call(orthogonalize_kernel, out_shape=jax.ShapeDtypeStruct(matri...  17.1 us
  transfers between devices with their start and end apart: 107, of which 48 were waited for; matrix products, arithmetic and copies ran while one was open for 14% of the time, Pallas kernels for 7%

profile of v5, /device:TPU:0, one launch (start us, length us, event | category | flops | bytes accessed | tf_op | source)
XLA Modules:
  0.0 669.4 jit_solution(3552083862504643959)
XLA Ops:
  18.7 6.5 all-to-all-start
  47.1 9.5 %all-to-all-done.1 = bf16[5,96,4,192]{1,3,0,2:T(8,128)(2,1)S(1)} async-done(((bf16[5,96,4,192]{1,3,0,2:T(8,128)(2,1)}), bf16[5,96,4,192]{1,3,0,2:T(8,128)(2,1)S(1)}, u32[]{:S(2)}, u32[]{:S(2)}) %all-to-all-start.1) | async-done | bytes 737312 | tf_op jit(solution)/shard_map/all_to_all | solution.py:58
  105.5 12.4 %collective-permute-done.21.refs_2_ = bf16[2,192,384]{2,1,0:T(8,128)(2,1)S(1)} collective-permute-done((bf16[2,192,384]{2,1,0:T(8,128)(2,1)S(1)}, bf16[2,192,384]{2,1,0:T(8,128)(2,1)S(1)}, u32[]{:S(2)}, u32[]{:S(2)}) %collective-permute-start.21) | collective-permute-done | bytes 294944 | tf_op jit(solution)/shard_map/ppermute | solution.py:69
  117.8 10.0 %collective-permute-start.25 = (bf16[192,384]{1,0:T(8,128)(2,1)S(1)}, bf16[192,384]{1,0:T(8,128)(2,1)S(1)}, u32[]{:S(2)}, u32[]{:S(2)}) collective-permute-start(bf16[192,384]{1,0:T(8,128)(2,1)S(1)} %get-tuple-element.106.refs_0_), channel_id=1, source_target_pairs={{3,0},{0,1},{1,2},{2,3},{7,4},{4,5},{5,6},{6,7},{11,8},{8,9},{9,10... | collective-permute-start | bytes 442376 | tf_op jit(solution)/shard_map/ppermute | solution.py:69
  175.1 11.2 %collective-permute-done.32.refs_1_ = bf16[256,768]{1,0:T(8,128)(2,1)S(1)} collective-permute-done((bf16[256,768]{1,0:T(8,128)(2,1)S(1)}, bf16[256,768]{1,0:T(8,128)(2,1)S(1)}, u32[]{:S(2)}, u32[]{:S(2)}) %collective-permute-start.32) | collective-permute-done | bytes 393248 | tf_op jit(solution)/shard_map/ppermute | solution.py:594
  221.0 6.7 %collective-permute-done.43.refs_3_ = bf16[2,192,384]{2,1,0:T(8,128)(2,1)S(1)} collective-permute-done((bf16[2,192,384]{2,1,0:T(8,128)(2,1)S(1)}, bf16[2,192,384]{2,1,0:T(8,128)(2,1)S(1)}, u32[]{:S(2)}, u32[]{:S(2)}) %collective-permute-start.43) | collective-permute-done | bytes 294944 | tf_op jit(solution)/shard_map/ppermute | solution.py:69
  227.8 12.7 %collective-permute-done.42.refs_2_ = bf16[2,192,384]{2,1,0:T(8,128)(2,1)} collective-permute-done((bf16[2,192,384]{2,1,0:T(8,128)(2,1)S(1)}, bf16[2,192,384]{2,1,0:T(8,128)(2,1)}, u32[]{:S(2)}, u32[]{:S(2)}) %collective-permute-start.42) | collective-permute-done | bytes 294944 | tf_op jit(solution)/shard_map/ppermute | solution.py:69
  241.6 8.2 %collective-permute-start.39 = (f32[128,768]{1,0:T(8,128)S(1)}, f32[128,768]{1,0:T(8,128)S(1)}, u32[]{:S(2)}, u32[]{:S(2)}) collective-permute-start(f32[128,768]{1,0:T(8,128)S(1)} %collective-permute-done.38), channel_id=1, source_target_pairs={{0,8},{8,0},{1,9},{9,1},{2,10},{10,2},{3,11},{11,3},{4,12},{12,4},... | collective-permute-start | bytes 1179656 | tf_op jit(solution)/shard_map/ppermute | solution.py:73
  257.6 7.3 %collective-permute-start.46 = (bf16[256,768]{1,0:T(8,128)(2,1)S(1)}, bf16[256,768]{1,0:T(8,128)(2,1)S(1)}, u32[]{:S(2)}, u32[]{:S(2)}) collective-permute-start(bf16[256,768]{1,0:T(8,128)(2,1)S(1)} %get-tuple-element.117.own_c_ref), channel_id=1, source_target_pairs={{0,4},{4,0},{1,5},{5,1},{2,6},{6,2},{3,7},{7,3},{8,12},{12,8},{9,1... | collective-permute-start | bytes 1179656 | tf_op jit(solution)/shard_map/ppermute | solution.py:589
  300.9 7.5 %shard_map.160 = (f32[256,768]{1,0:T(8,128)}, bf16[256,768]{1,0:T(8,128)(2,1)S(1)}, f32[8,768]{1,0:T(8,128)S(1)}, f32[4,2,192,384]{3,2,1,0:T(8,128)}, bf16[4,2,192,384]{3,2,1,0:T(8,128)(2,1)}) custom-call(s32[2]{0:T(128)S(1)} %pad_add_fusion.place_ref, bf16[256,768]{1,0:T(8,128)(2,1)S(1)} %fusion.53.own_gy_ref, ...), custom_call_target="tpu_custom_call" | custom-call | tf_op jit(solution)/shard_map/pallas_call | solution.py:240
  314.4 7.9 %collective-permute-done.54 = bf16[256,768]{1,0:T(8,128)(2,1)S(1)} collective-permute-done((bf16[256,768]{1,0:T(8,128)(2,1)S(1)}, bf16[256,768]{1,0:T(8,128)(2,1)S(1)}, u32[]{:S(2)}, u32[]{:S(2)}) %collective-permute-start.54) | collective-permute-done | bytes 393248 | tf_op jit(solution)/shard_map/ppermute | solution.py:594
  324.4 13.1 %collective-permute-done.52.recv_ref = bf16[256,768]{1,0:T(8,128)(2,1)S(1)} collective-permute-done((bf16[256,768]{1,0:T(8,128)(2,1)S(1)}, bf16[256,768]{1,0:T(8,128)(2,1)S(1)}, u32[]{:S(2)}, u32[]{:S(2)}) %collective-permute-start.52) | collective-permute-done | bytes 393248 | tf_op jit(solution)/shard_map/ppermute | solution.py:594
  343.5 8.5 %shard_map.162 = (f32[256,768]{1,0:T(8,128)}, bf16[256,768]{1,0:T(8,128)(2,1)S(1)}, f32[8,576]{1,0:T(8,128)S(1)}, f32[4,192,384]{2,1,0:T(8,128)}, bf16[4,192,384]{2,1,0:T(8,128)(2,1)}) custom-call(s32[2]{0:T(128)S(1)} %pad_add_fusion.place_ref, f32[8,512]{1,0:T(8,128)S(1)} %pad.13.row_ref, f32[512,128]{1,0:T(8,128)S(1)} %pad.14.column_ref, ...), custom_call_target="tpu_custom_call" | custom-call | tf_op jit(solution)/shard_map/pallas_call | solution.py:240
  366.2 11.5 %collective-permute-done.63 = bf16[2,192,384]{2,1,0:T(8,128)(2,1)S(1)} collective-permute-done((bf16[2,192,384]{2,1,0:T(8,128)(2,1)S(1)}, bf16[2,192,384]{2,1,0:T(8,128)(2,1)S(1)}, u32[]{:S(2)}, u32[]{:S(2)}) %collective-permute-start.63) | collective-permute-done | bytes 294944 | tf_op jit(solution)/shard_map/ppermute | solution.py:69
  383.1 7.4 %shard_map.164 = (f32[256,768]{1,0:T(8,128)}, bf16[256,768]{1,0:T(8,128)(2,1)S(1)}, f32[8,768]{1,0:T(8,128)S(1)}, f32[4,2,192,384]{3,2,1,0:T(8,128)}, bf16[4,2,192,384]{3,2,1,0:T(8,128)(2,1)}) custom-call(s32[2]{0:T(128)S(1)} %pad_add_fusion.place_ref, bf16[256,768]{1,0:T(8,128)(2,1)S(1)} %get-tuple-element.147.own_gy_ref, ...), custom_call_target="tpu_custom_call" | custom-call | tf_op jit(solution)/shard_map/pallas_call | solution.py:240
  392.0 6.8 %collective-permute-start.67 = (bf16[192,384]{1,0:T(8,128)(2,1)S(1)}, bf16[192,384]{1,0:T(8,128)(2,1)S(1)}, u32[]{:S(2)}, u32[]{:S(2)}) collective-permute-start(bf16[192,384]{1,0:T(8,128)(2,1)S(1)} %get-tuple-element.238), channel_id=1, source_target_pairs={{3,0},{0,1},{1,2},{2,3},{7,4},{4,5},{5,6},{6,7},{11,8},{8,9},{9,10... | collective-permute-start | bytes 442376 | tf_op jit(solution)/shard_map/ppermute | solution.py:69
  419.7 8.4 %shard_map.166 = (f32[256,768]{1,0:T(8,128)}, bf16[256,768]{1,0:T(8,128)(2,1)S(1)}, f32[8,576]{1,0:T(8,128)S(1)}, f32[4,192,384]{2,1,0:T(8,128)}, bf16[4,192,384]{2,1,0:T(8,128)(2,1)}) custom-call(s32[2]{0:T(128)S(1)} %pad_add_fusion.place_ref, f32[8,512]{1,0:T(8,128)S(1)} %pad.13.row_ref, f32[512,128]{1,0:T(8,128)S(1)} %pad.14.column_ref, ...), custom_call_target="tpu_custom_call" | custom-call | tf_op jit(solution)/shard_map/pallas_call | solution.py:240
  429.2 6.8 %collective-permute-start.81 = (bf16[2,192,384]{2,1,0:T(8,128)(2,1)}, bf16[2,192,384]{2,1,0:T(8,128)(2,1)S(1)}, u32[]{:S(2)}, u32[]{:S(2)}) collective-permute-start(bf16[2,192,384]{2,1,0:T(8,128)(2,1)} %get-tuple-element.219), channel_id=1, source_target_pairs={{3,0},{0,1},{1,2},{2,3},{7,4},{4,5},{5,6},{6,7},{11,8},{8,9},{9,10... | collective-permute-start | bytes 884744 | tf_op jit(solution)/shard_map/ppermute | solution.py:69
  444.2 11.3 %collective-permute-done.83 = bf16[2,192,384]{2,1,0:T(8,128)(2,1)} collective-permute-done((bf16[2,192,384]{2,1,0:T(8,128)(2,1)}, bf16[2,192,384]{2,1,0:T(8,128)(2,1)}, u32[]{:S(2)}, u32[]{:S(2)}) %collective-permute-start.83) | collective-permute-done | bytes 294944 | tf_op jit(solution)/shard_map/ppermute | solution.py:69
  459.3 6.8 %collective-permute-start.76 = (bf16[192,384]{1,0:T(8,128)(2,1)S(1)}, bf16[192,384]{1,0:T(8,128)(2,1)S(1)}, u32[]{:S(2)}, u32[]{:S(2)}) collective-permute-start(bf16[192,384]{1,0:T(8,128)(2,1)S(1)} %get-tuple-element.235), channel_id=1, source_target_pairs={{3,0},{0,1},{1,2},{2,3},{7,4},{4,5},{5,6},{6,7},{11,8},{8,9},{9,10... | collective-permute-start | bytes 442376 | tf_op jit(solution)/shard_map/ppermute | solution.py:69
  511.1 6.5 all-to-all-done.3
  561.7 9.5 %collective-permute-done.97 = f32[2,3,768]{2,0,1:T(2,128)S(1)} collective-permute-done((f32[2,3,768]{2,0,1:T(2,128)S(1)}, f32[2,3,768]{2,0,1:T(2,128)S(1)}, u32[]{:S(2)}, u32[]{:S(2)}) %collective-permute-start.97) | collective-permute-done | bytes 18464 | tf_op jit(solution)/shard_map/ppermute | solution.py:236
  624.1 9.1 %shard_map.169 = bf16[768,768]{1,0:T(8,128)(2,1)} custom-call(bf16[768,768]{1,0:T(8,128)(2,1)S(1)} %bitcast.283, f32[768,768]{1,0:T(8,128)S(1)} %convert_select_fusion.gram_ref), custom_call_target="tpu_custom_call" | custom-call | tf_op jit(solution)/shard_map/pallas_call | solution.py:660
  644.9 8.0 %shard_map.168 = bf16[768,768]{1,0:T(8,128)(2,1)S(1)} custom-call(bf16[768,768]{1,0:T(8,128)(2,1)S(1)} %copy-done.14, f32[768,768]{1,0:T(8,128)S(1)} %fusion.75.gram_ref), custom_call_target="tpu_custom_call" | custom-call | tf_op jit(solution)/shard_map/pallas_call | solution.py:660
  (551 shorter events, 439.8 us)
Async XLA Ops:
  15.6 29.0 %collective-permute-start.6 = (f32[136,768]{1,0:T(8,128)S(1)}, f32[136,768]{1,0:T(8,128)S(1)}, u32[]{:S(2)}, u32[]{:S(2)}) collective-permute-start(f32[136,768]{1,0:T(8,128)S(1)} %select_maximum_fusion), channel_id=1, source_target_pairs={{0,0},{1,8},{2,4},{3,12},{4,1},{5,9},{6,5},{7,13},{8,2},{9,10},{10... | collective-permute-start | bytes 1253384 | tf_op jit(solution)/shard_map/ppermute | solution.py:717
  92.0 25.9 %collective-permute-start.21 = (bf16[2,192,384]{2,1,0:T(8,128)(2,1)S(1)}, bf16[2,192,384]{2,1,0:T(8,128)(2,1)S(1)}, u32[]{:S(2)}, u32[]{:S(2)}) collective-permute-start(bf16[2,192,384]{2,1,0:T(8,128)(2,1)S(1)} %bitcast.285), channel_id=1, source_target_pairs={{2,0},{3,1},{0,2},{1,3},{6,4},{7,5},{4,6},{5,7},{10,8},{11,9},{8,1... | collective-permute-start | bytes 884744 | tf_op jit(solution)/shard_map/ppermute | solution.py:69
  99.0 31.4 %collective-permute-start.19 = (bf16[256,768]{1,0:T(8,128)(2,1)S(1)}, bf16[256,768]{1,0:T(8,128)(2,1)S(1)}, u32[]{:S(2)}, u32[]{:S(2)}) collective-permute-start(bf16[256,768]{1,0:T(8,128)(2,1)S(1)} %get-tuple-element.210), channel_id=1, source_target_pairs={{0,8},{8,0},{1,9},{9,1},{2,10},{10,2},{3,11},{11,3},{4,12},{12,4},... | collective-permute-start | bytes 1179656 | tf_op jit(solution)/shard_map/ppermute | solution.py:594
  137.5 28.4 %collective-permute-start.26 = (bf16[256,768]{1,0:T(8,128)(2,1)S(1)}, bf16[256,768]{1,0:T(8,128)(2,1)S(1)}, u32[]{:S(2)}, u32[]{:S(2)}) collective-permute-start(bf16[256,768]{1,0:T(8,128)(2,1)S(1)} %get-tuple-element.102.own_c_ref), channel_id=1, source_target_pairs={{0,4},{4,0},{1,5},{5,1},{2,6},{6,2},{3,7},{7,3},{8,12},{12,8},{9,1... | collective-permute-start | bytes 1179656 | tf_op jit(solution)/shard_map/ppermute | solution.py:589
  139.9 26.1 %collective-permute-start.28 = (bf16[2,192,384]{2,1,0:T(8,128)(2,1)S(1)}, bf16[2,192,384]{2,1,0:T(8,128)(2,1)S(1)}, u32[]{:S(2)}, u32[]{:S(2)}) collective-permute-start(bf16[2,192,384]{2,1,0:T(8,128)(2,1)S(1)} %collective-permute-done.20.refs_1_), channel_id=1, source_target_pairs={{0,16},{16,0},{1,17},{17,1},{2,18},{18,2},{3,19},{19,3},{4,20},{20... | collective-permute-start | bytes 884744 | tf_op jit(solution)/shard_map/ppermute | solution.py:162
  212.9 27.6 %collective-permute-start.44 = (bf16[256,768]{1,0:T(8,128)(2,1)}, bf16[256,768]{1,0:T(8,128)(2,1)S(1)}, u32[]{:S(2)}, u32[]{:S(2)}) collective-permute-start(bf16[256,768]{1,0:T(8,128)(2,1)} %get-tuple-element.116), channel_id=1, source_target_pairs={{0,4},{4,0},{1,5},{5,1},{2,6},{6,2},{3,7},{7,3},{8,12},{12,8},{9,1... | collective-permute-start | bytes 1179656 | tf_op jit(solution)/shard_map/ppermute | solution.py:589
  217.0 23.6 %collective-permute-start.42 = (bf16[2,192,384]{2,1,0:T(8,128)(2,1)S(1)}, bf16[2,192,384]{2,1,0:T(8,128)(2,1)}, u32[]{:S(2)}, u32[]{:S(2)}) collective-permute-start(bf16[2,192,384]{2,1,0:T(8,128)(2,1)S(1)} %bitcast.290), channel_id=1, source_target_pairs={{2,0},{3,1},{0,2},{1,3},{6,4},{7,5},{4,6},{5,7},{10,8},{11,9},{8,1... | collective-permute-start | bytes 884744 | tf_op jit(solution)/shard_map/ppermute | solution.py:69
  241.6 25.8 %collective-permute-start.39 = (f32[128,768]{1,0:T(8,128)S(1)}, f32[128,768]{1,0:T(8,128)S(1)}, u32[]{:S(2)}, u32[]{:S(2)}) collective-permute-start(f32[128,768]{1,0:T(8,128)S(1)} %collective-permute-done.38), channel_id=1, source_target_pairs={{0,8},{8,0},{1,9},{9,1},{2,10},{10,2},{3,11},{11,3},{4,12},{12,4},... | collective-permute-start | bytes 1179656 | tf_op jit(solution)/shard_map/ppermute | solution.py:73
  257.6 35.3 %collective-permute-start.46 = (bf16[256,768]{1,0:T(8,128)(2,1)S(1)}, bf16[256,768]{1,0:T(8,128)(2,1)S(1)}, u32[]{:S(2)}, u32[]{:S(2)}) collective-permute-start(bf16[256,768]{1,0:T(8,128)(2,1)S(1)} %get-tuple-element.117.own_c_ref), channel_id=1, source_target_pairs={{0,4},{4,0},{1,5},{5,1},{2,6},{6,2},{3,7},{7,3},{8,12},{12,8},{9,1... | collective-permute-start | bytes 1179656 | tf_op jit(solution)/shard_map/ppermute | solution.py:589
  267.4 25.6 %collective-permute-start.50 = (bf16[2,192,384]{2,1,0:T(8,128)(2,1)S(1)}, bf16[2,192,384]{2,1,0:T(8,128)(2,1)S(1)}, u32[]{:S(2)}, u32[]{:S(2)}) collective-permute-start(bf16[2,192,384]{2,1,0:T(8,128)(2,1)S(1)} %collective-permute-done.43.refs_3_), channel_id=1, source_target_pairs={{0,16},{16,0},{1,17},{17,1},{2,18},{18,2},{3,19},{19,3},{4,20},{20... | collective-permute-start | bytes 884744 | tf_op jit(solution)/shard_map/ppermute | solution.py:162
  274.9 24.0 %collective-permute-start.40 = (bf16[256,768]{1,0:T(8,128)(2,1)S(1)}, bf16[256,768]{1,0:T(8,128)(2,1)S(1)}, u32[]{:S(2)}, u32[]{:S(2)}) collective-permute-start(bf16[256,768]{1,0:T(8,128)(2,1)S(1)} %fusion.53.own_gy_ref), channel_id=1, source_target_pairs={{0,4},{4,0},{1,5},{5,1},{2,6},{6,2},{3,7},{7,3},{8,12},{12,8},{9,1... | collective-permute-start | bytes 1179656 | tf_op jit(solution)/shard_map/ppermute | solution.py:589
  312.7 39.6 %collective-permute-start.57 = (bf16[4,2,192,384]{3,2,1,0:T(8,128)(2,1)S(1)}, bf16[4,2,192,384]{3,2,1,0:T(8,128)(2,1)S(1)}, u32[]{:S(2)}, u32[]{:S(2)}) collective-permute-start(bf16[4,2,192,384]{3,2,1,0:T(8,128)(2,1)S(1)} %copy-done.78), channel_id=1, source_target_pairs={{0,16},{16,0},{1,17},{17,1},{2,18},{18,2},{3,19},{19,3},{4,20},{20... | collective-permute-start | bytes 3538952 | tf_op jit(solution)/shard_map/ppermute | solution.py:185
  353.4 24.5 %collective-permute-start.60 = (bf16[4,192,384]{2,1,0:T(8,128)(2,1)S(1)}, bf16[4,192,384]{2,1,0:T(8,128)(2,1)S(1)}, u32[]{:S(2)}, u32[]{:S(2)}) collective-permute-start(bf16[4,192,384]{2,1,0:T(8,128)(2,1)S(1)} %copy-done.79), channel_id=1, source_target_pairs={{0,16},{16,0},{1,17},{17,1},{2,18},{18,2},{3,19},{19,3},{4,20},{20... | collective-permute-start | bytes 1769480 | tf_op jit(solution)/shard_map/ppermute | solution.py:185
  390.5 28.2 %collective-permute-start.71 = (bf16[4,2,192,384]{3,2,1,0:T(8,128)(2,1)}, bf16[4,2,192,384]{3,2,1,0:T(8,128)(2,1)S(1)}, u32[]{:S(2)}, u32[]{:S(2)}) collective-permute-start(bf16[4,2,192,384]{3,2,1,0:T(8,128)(2,1)} %get-tuple-element.163), channel_id=1, source_target_pairs={{0,16},{16,0},{1,17},{17,1},{2,18},{18,2},{3,19},{19,3},{4,20},{20... | collective-permute-start | bytes 3538952 | tf_op jit(solution)/shard_map/ppermute | solution.py:185
  479.2 79.3 %collective-permute-start.79 = (bf16[192,384]{1,0:T(8,128)(2,1)}, bf16[192,384]{1,0:T(8,128)(2,1)}, u32[]{:S(2)}, u32[]{:S(2)}) collective-permute-start(bf16[192,384]{1,0:T(8,128)(2,1)} %fusion.14), channel_id=1, source_target_pairs={{3,3},{19,7},{7,11},{23,15},{11,19},{27,23},{15,27},{31,31}} | collective-permute-start | bytes 442376 | tf_op jit(solution)/shard_map/ppermute | solution.py:127
  480.6 25.6 %collective-permute-start.84 = (bf16[192,384]{1,0:T(8,128)(2,1)S(1)}, bf16[192,384]{1,0:T(8,128)(2,1)S(1)}, u32[]{:S(2)}, u32[]{:S(2)}) collective-permute-start(bf16[192,384]{1,0:T(8,128)(2,1)S(1)} %fusion.17), channel_id=1, source_target_pairs={{3,3},{19,7},{7,11},{23,15},{11,19},{27,23},{15,27},{31,31}} | collective-permute-start | bytes 442376 | tf_op jit(solution)/shard_map/ppermute | solution.py:127
  496.5 52.2 %collective-permute-start.93 = (f32[2,3,768]{2,0,1:T(2,128)}, f32[2,3,768]{2,0,1:T(2,128)}, u32[]{:S(2)}, u32[]{:S(2)}) collective-permute-start(f32[2,3,768]{2,0,1:T(2,128)} %get-tuple-element.249), channel_id=1, source_target_pairs={{3,0},{0,1},{1,2},{2,3},{7,4},{4,5},{5,6},{6,7},{11,8},{8,9},{9,10... | collective-permute-start | bytes 55304 | tf_op jit(solution)/shard_map/ppermute | solution.py:69
  501.1 47.6 %collective-permute-start.95 = (f32[2,3,768]{2,0,1:T(2,128)S(1)}, f32[2,3,768]{2,0,1:T(2,128)}, u32[]{:S(2)}, u32[]{:S(2)}) collective-permute-start(f32[2,3,768]{2,0,1:T(2,128)S(1)} %get-tuple-element.250), channel_id=1, source_target_pairs={{1,0},{2,1},{3,2},{0,3},{5,4},{6,5},{7,6},{4,7},{9,8},{10,9},{11,1... | collective-permute-start | bytes 55304 | tf_op jit(solution)/shard_map/ppermute | solution.py:69
  504.6 44.2 %collective-permute-start.94 = (f32[2,3,768]{2,0,1:T(2,128)S(1)}, f32[2,3,768]{2,0,1:T(2,128)}, u32[]{:S(2)}, u32[]{:S(2)}) collective-permute-start(f32[2,3,768]{2,0,1:T(2,128)S(1)} %get-tuple-element.251), channel_id=1, source_target_pairs={{2,0},{3,1},{0,2},{1,3},{6,4},{7,5},{4,6},{5,7},{10,8},{11,9},{8,1... | collective-permute-start | bytes 55304 | tf_op jit(solution)/shard_map/ppermute | solution.py:69
  506.2 28.8 %collective-permute-start.85 = (bf16[96,384]{1,0:T(8,128)(2,1)S(1)}, bf16[96,384]{1,0:T(8,128)(2,1)S(1)}, u32[]{:S(2)}, u32[]{:S(2)}) collective-permute-start(bf16[96,384]{1,0:T(8,128)(2,1)S(1)} %constant_dynamic-slice_fusion.5), channel_id=1, source_target_pairs={{0,4},{4,0},{1,5},{5,1},{2,6},{6,2},{3,7},{7,3},{8,12},{12,8},{9,1... | collective-permute-start | bytes 221192 | tf_op jit(solution)/shard_map/ppermute | solution.py:131
  518.4 25.4 %all-to-all-start.2 = ((bf16[1,4,96,192]{3,2,0,1:T(8,128)(2,1)}), bf16[1,4,96,192]{3,2,0,1:T(8,128)(2,1)}, u32[]{:S(2)}, u32[]{:S(2)}) async-start(bf16[1,4,96,192]{3,2,0,1:T(8,128)(2,1)} %bitcast.49), calls=%async_computation.2 | async-start | bytes 393216 | tf_op jit(solution)/shard_map/all_to_all | solution.py:64
  543.9 30.8 %all-to-all-start.6 = ((bf16[8,1,96,768]{3,2,1,0:T(8,128)(2,1)}), bf16[8,1,96,768]{3,2,1,0:T(8,128)(2,1)S(1)}, u32[]{:S(2)}, u32[]{:S(2)}) async-start(bf16[8,1,96,768]{3,2,1,0:T(8,128)(2,1)} %bitcast.309), calls=%async_computation.6 | async-start | bytes 2359296 | tf_op jit(solution)/shard_map/all_to_all | solution.py:892
  548.6 93.4 %all-gather.2.cloned.1.call-start = ((), (), s32[]{:S(2)}) async-start(), calls=%async_computation.8 | async-start | bytes 1327104 | tf_op jit(solution)/shard_map/all_gather | solution.py:904
  550.9 91.2 %collective-permute-start.74 = (f32[128,768]{1,0:T(8,128)}, f32[128,768]{1,0:T(8,128)}, u32[]{:S(2)}, u32[]{:S(2)}) collective-permute-start(f32[128,768]{1,0:T(8,128)} %constant_dynamic-slice_fusion.7), channel_id=1, source_target_pairs={{0,0},{8,1},{4,2},{12,3},{1,4},{9,5},{5,6},{13,7},{2,8},{10,9},{6,... | collective-permute-start | bytes 1179656 | tf_op jit(solution)/shard_map/ppermute | solution.py:780
  (164 other events, 1780.3 us)
Sparse Core Ops, SparseCore 0:
  574.7 27.3 all-gather.1

commit v6 on v5

--- a/solution.py
+++ b/solution.py
@@ -153,13 +153,19 @@
     return pieces
 
 
-def ctx_gather(piece):
-    near, back, far = [rotate(piece, "ctx", step) for step in (1, 3, 2)]
+def ctx_gather(piece, *earlier):
+    near = rotate(after(piece, *earlier), "ctx", 1)
+    back = rotate(after(piece, near), "ctx", 3)
+    far = rotate(after(piece, back), "ctx", 2)
     return [piece, near, far, back]
 
 
-def group_swap(blocks):
-    return [lax.ppermute(block, "g", SWAP) for block in blocks]
+def group_swap(blocks, *earlier):
+    others = []
+    for block in blocks:
+        others.append(lax.ppermute(after(block, *earlier), "g", SWAP))
+        earlier = others[-1:]
+    return others
 
 
 def gather_weights_wide(low):
@@ -185,10 +191,13 @@
     return mine + lax.ppermute(give, "g", SWAP).astype(f32)
 
 
-def ctx_sum(blocks):
+def ctx_sum(blocks, *earlier):
+    low = after(blocks, *earlier).astype(bf16)
     total = blocks[0]
     for step in (1, 3, 2):
-        total = total + rotate(blocks[step].astype(bf16), "ctx", -step).astype(f32)
+        got = rotate(low[step], "ctx", -step)
+        total = total + got.astype(f32)
+        low = after(low, got)
     return total
 
 
@@ -722,9 +731,9 @@
     if relative:
         pieces = pack_pieces(weights)
         own_attn = ctx_gather(pieces[0][0])
-        own_mlp = ctx_gather(after(pieces[0][1], *own_attn[1:]))
+        own_mlp = ctx_gather(pieces[0][1], own_attn[2])
         attn_weights = (own_attn, group_swap(own_attn))
-        mlp_weights = (own_mlp, group_swap(own_mlp))
+        mlp_weights = (own_mlp, group_swap(own_mlp, attn_weights[1][3]))
     else:
         wide_weights = gather_weights_wide(weights.astype(bf16))
 
@@ -749,23 +758,19 @@
         w_attn, qkv, lse, o, mine, give = attend_stage(
             place, row_info, column_info, qkv_bias[layer], a_own, a_other, attn_weights
         )
-        if relative and layer:
-            mine, own_mlp = lax.optimization_barrier((mine, own_mlp))
-            mlp_weights = (own_mlp, group_swap(own_mlp))
         if relative and following:
-            next_attn = ctx_gather(after(pieces[layer + 1][0], *own_mlp[1:]))
-            next_mlp = ctx_gather(after(pieces[layer + 1][1], *next_attn[1:]))
+            next_attn = ctx_gather(pieces[layer + 1][0], own_mlp[2])
+            next_mlp = ctx_gather(pieces[layer + 1][1], next_attn[2])
         mine, recv = group_sum(mine, give)
         middle, c_own = norm_stage(vec_rows, layer, 2, hidden, mine, recv, (layer, 6))
-        if relative and following:
-            c_own, next_attn = lax.optimization_barrier((c_own, next_attn))
         c_other = core_swap(c_own)
         w_mlp, preact, act, mine, give = feed_stage(
             place, up_bias[layer], c_own, c_other, mlp_weights
         )
         if relative and following:
-            attn_weights = (next_attn, group_swap(next_attn))
+            attn_weights = (next_attn, group_swap(next_attn, mlp_weights[1][3]))
             own_mlp = next_mlp
+            mlp_weights = (own_mlp, group_swap(own_mlp, attn_weights[1][3]))
         mine, recv = group_sum(mine, give)
         stored.append(
             (hidden, middle, a_own, a_other, qkv, lse, o, c_own, c_other, preact, act, w_attn, w_mlp)
@@ -780,7 +785,7 @@
         return lax.ppermute(block, axes, from_seq)
 
     hidden_out = send_back(hidden)
-    grad_hidden = x_join(lax.ppermute(after(out_grad[0], stored[-1][6]), axes, to_seq))
+    grad_hidden = x_join(lax.ppermute(after(out_grad[0], next_mlp[2] if relative else stored[-1][6]), axes, to_seq))
     gy_own = grad_hidden.astype(bf16)
     attn_half = mlp_part = None
 
@@ -792,8 +797,7 @@
             layer
         ]
         if relative and attn_half is not None:
-            gy_own, attn_half, mlp_part = lax.optimization_barrier((gy_own, attn_half, mlp_part))
-            attn_part = ctx_sum(attn_half)
+            attn_part = ctx_sum(attn_half, mlp_part)
         gy_other = core_swap(gy_own)
         mine, give, up_sums, *mlp_grads = feed_back_stage(
             place, gy_own, gy_other, c_own, c_other, preact, act, w_mlp, relative
@@ -826,7 +830,7 @@
         )
         if relative:
             mine, mlp_half = lax.optimization_barrier((mine, mlp_half))
-            mlp_part = ctx_sum(mlp_half)
+            mlp_part = ctx_sum(mlp_half, *([] if parts[-1] is None else parts[-1]))
             attn_half = half_sum(*attn_grads)
         else:
             attn_grad = attn_grads[0]
@@ -845,7 +849,7 @@
     input_grad = send_back(grad_hidden)
 
     if relative:
-        parts[0] = (ctx_sum(attn_half), mlp_part)
+        parts[0] = (ctx_sum(attn_half, mlp_part), mlp_part)
         for layer in range(LAYERS):
             attn_part, mlp_part = [
                 after(part, grad_hidden).astype(bf16) for part in parts[layer]

time: 679 us -> 618 us (0.910)
  starting transfers between devices: 198 us -> 147 us
  other arithmetic: 51.3 us -> 43.5 us
    ppermute x30, starting transfers between devices: 77.7 us -> 20.9 us  [rotate(): lax.ppermute(block, axis, [((i + step) % size, i) for i in range(size)])]
    ppermute x30, waiting for transfers between devices: 90.2 us -> 109 us  [rotate(): lax.ppermute(block, axis, [((i + step) % size, i) for i in range(size)])]
    ppermute x17, waiting for transfers between devices: 65.5 us -> 53.6 us  [the longest x16 53.6 us: group_swap(): others.append(lax.ppermute(after(block, *earlier), 'g', SWAP))]
    ppermute x8, waiting for transfers between devices: 42.7 us -> 31.7 us  [group_sum(): return (mine, lax.ppermute(mine.astype(bf16), 'jx', SWAP))]
    unnamed x172 -> x182, local copies, waits for them, and re-layouts: 22.1 us -> 22.4 us
  transfers between devices with their start and end apart: 107 -> 107, of which waited for: 48 -> 54; matrix products, arithmetic and copies ran while one was open for 14% -> 14% of each run, Pallas kernels for 7% -> 9%
where the time goes in v6:
time: 618 us; the launch traced here: 608 us
  waiting for transfers between devices  249 us (40%)
  starting transfers between devices  147 us (24%)
  Pallas kernels  85.3 us (14%)
  local copies, waits for them, and re-layouts  63.4 us (10%)
  other arithmetic  43.5 us (7%)
  between operations  16.1 us (3%)
    ppermute x30, waiting for transfers between devices, rotate(): lax.ppermute(block, axis, [((i + step) % size, i) for i in range(size)])  109 us
    pallas_call x16, Pallas kernels, call(): pl.pallas_call(kernel, out_shape=[jax.ShapeDtypeStruct(shape, kind) for s...  68.2 us
    ppermute x16, waiting for transfers between devices, group_swap(): others.append(lax.ppermute(after(block, *earlier), 'g', SWAP))  53.6 us
    ppermute x8, waiting for transfers between devices, group_sum(): return (mine, lax.ppermute(mine.astype(bf16), 'jx', SWAP))  31.7 us
    unnamed x182, local copies, waits for them, and re-layouts  22.4 us
    ppermute x16, starting transfers between devices, group_swap(): others.append(lax.ppermute(after(block, *earlier), 'g', SWAP))  22 us
    ppermute x30, starting transfers between devices, rotate(): lax.ppermute(block, axis, [((i + step) % size, i) for i in range(size)])  20.9 us
    ppermute x6, starting transfers between devices, shift(): return lax.ppermute(block, ('jc', 'ctx'), moves)  20.6 us
  transfers between devices with their start and end apart: 107, of which 54 were waited for; matrix products, arithmetic and copies ran while one was open for 14% of the time, Pallas kernels for 9%

profile of v6, /device:TPU:0, one launch (start us, length us, event | category | flops | bytes accessed | tf_op | source)
XLA Modules:
  0.0 607.9 jit_solution(4964768841556398337)
XLA Ops:
  18.7 6.5 %all-to-all-start.1 = ((bf16[1,96,4,192]{1,3,0,2:T(8,128)(2,1)}), bf16[1,96,4,192]{1,3,0,2:T(8,128)(2,1)S(1)}, u32[]{:S(2)}, u32[]{:S(2)}) async-start(bf16[1,96,4,192]{1,3,0,2:T(8,128)(2,1)} %bitcast.19), calls=%async_computation.1 | async-start | bytes 393216 | tf_op jit(solution)/shard_map/all_to_all | solution.py:58
  45.9 10.1 %all-to-all-done = bf16[5,96,4,192]{1,3,0,2:T(8,128)(2,1)S(1)} async-done(((bf16[5,96,4,192]{1,3,0,2:T(8,128)(2,1)}), bf16[5,96,4,192]{1,3,0,2:T(8,128)(2,1)S(1)}, u32[]{:S(2)}, u32[]{:S(2)}) %all-to-all-start) | async-done | bytes 737312 | tf_op jit(solution)/shard_map/all_to_all | solution.py:58
  100.7 7.2 %collective-permute-done.33.refs_4_ = bf16[2,192,384]{2,1,0:T(8,128)(2,1)S(1)} collective-permute-done((bf16[2,192,384]{2,1,0:T(8,128)(2,1)S(1)}, bf16[2,192,384]{2,1,0:T(8,128)(2,1)S(1)}, u32[]{:S(2)}, u32[]{:S(2)}) %collective-permute-start.33) | collective-permute-done | bytes 294944 | tf_op jit(solution)/shard_map/ppermute | solution.py:166
  116.5 8.8 %collective-permute-done.13.refs_2_ = bf16[2,192,384]{2,1,0:T(8,128)(2,1)S(1)} collective-permute-done((bf16[2,192,384]{2,1,0:T(8,128)(2,1)S(1)}, bf16[2,192,384]{2,1,0:T(8,128)(2,1)S(1)}, u32[]{:S(2)}, u32[]{:S(2)}) %collective-permute-start.13) | collective-permute-done | bytes 294944 | tf_op jit(solution)/shard_map/ppermute | solution.py:69
  135.4 7.0 %collective-permute-done.36.refs_7_ = bf16[2,192,384]{2,1,0:T(8,128)(2,1)} collective-permute-done((bf16[2,192,384]{2,1,0:T(8,128)(2,1)S(1)}, bf16[2,192,384]{2,1,0:T(8,128)(2,1)}, u32[]{:S(2)}, u32[]{:S(2)}) %collective-permute-start.36) | collective-permute-done | bytes 294944 | tf_op jit(solution)/shard_map/ppermute | solution.py:166
  147.5 6.3 %collective-permute-done.14.refs_1_ = bf16[192,384]{1,0:T(8,128)(2,1)S(1)} collective-permute-done((bf16[192,384]{1,0:T(8,128)(2,1)S(1)}, bf16[192,384]{1,0:T(8,128)(2,1)S(1)}, u32[]{:S(2)}, u32[]{:S(2)}) %collective-permute-start.14) | collective-permute-done | bytes 147488 | tf_op jit(solution)/shard_map/ppermute | solution.py:69
  161.6 6.5 %collective-permute-done.16.refs_2_ = bf16[192,384]{1,0:T(8,128)(2,1)S(1)} collective-permute-done((bf16[192,384]{1,0:T(8,128)(2,1)S(1)}, bf16[192,384]{1,0:T(8,128)(2,1)S(1)}, u32[]{:S(2)}, u32[]{:S(2)}) %collective-permute-start.16) | collective-permute-done | bytes 147488 | tf_op jit(solution)/shard_map/ppermute | solution.py:69
  191.7 6.1 %shard_map.157 = (bf16[768,768]{1,0:T(8,128)(2,1)}, bf16[512,576]{1,0:T(8,128)(2,1)}, f32[512,128]{1,0:T(8,128)S(1)}, bf16[512,192]{1,0:T(8,128)(2,1)S(1)}, f32[...) custom-call(s32[2]{0:T(128)S(1)} %pad_add_fusion.place_ref, f32[8,512]{1,0:T(8,128)S(1)} %pad.13.row_ref, ...), custom_call_target="tpu_custom_call" | custom-call | tf_op jit(solution)/shard_map/pallas_call | solution.py:249
  212.0 11.4 %collective-permute-start.21 = (f32[128,768]{1,0:T(8,128)S(1)}, f32[128,768]{1,0:T(8,128)S(1)}, u32[]{:S(2)}, u32[]{:S(2)}) collective-permute-start(f32[128,768]{1,0:T(8,128)S(1)} %collective-permute-done.20), channel_id=1, source_target_pairs={{0,8},{8,0},{1,9},{9,1},{2,10},{10,2},{3,11},{11,3},{4,12},{12,4},... | collective-permute-start | bytes 1179656 | tf_op jit(solution)/shard_map/ppermute | solution.py:73
  251.7 7.5 %shard_map.160 = (f32[256,768]{1,0:T(8,128)}, bf16[256,768]{1,0:T(8,128)(2,1)S(1)}, f32[8,768]{1,0:T(8,128)S(1)}, f32[4,2,192,384]{3,2,1,0:T(8,128)}, bf16[4,2,192,384]{3,2,1,0:T(8,128)(2,1)}) custom-call(s32[2]{0:T(128)S(1)} %pad_add_fusion.place_ref, bf16[256,768]{1,0:T(8,128)(2,1)S(1)} %fusion.54.own_gy_ref, ...), custom_call_target="tpu_custom_call" | custom-call | tf_op jit(solution)/shard_map/pallas_call | solution.py:249
  264.8 8.9 %collective-permute-done.54 = bf16[256,768]{1,0:T(8,128)(2,1)S(1)} collective-permute-done((bf16[256,768]{1,0:T(8,128)(2,1)S(1)}, bf16[256,768]{1,0:T(8,128)(2,1)S(1)}, u32[]{:S(2)}, u32[]{:S(2)}) %collective-permute-start.54) | collective-permute-done | bytes 393248 | tf_op jit(solution)/shard_map/ppermute | solution.py:603
  275.6 11.5 %collective-permute-done.52.recv_ref = bf16[256,768]{1,0:T(8,128)(2,1)S(1)} collective-permute-done((bf16[256,768]{1,0:T(8,128)(2,1)S(1)}, bf16[256,768]{1,0:T(8,128)(2,1)S(1)}, u32[]{:S(2)}, u32[]{:S(2)}) %collective-permute-start.52) | collective-permute-done | bytes 393248 | tf_op jit(solution)/shard_map/ppermute | solution.py:603
  291.9 8.4 %shard_map.162 = (f32[256,768]{1,0:T(8,128)}, bf16[256,768]{1,0:T(8,128)(2,1)S(1)}, f32[8,576]{1,0:T(8,128)S(1)}, f32[4,192,384]{2,1,0:T(8,128)}, bf16[4,192,384]{2,1,0:T(8,128)(2,1)}) custom-call(s32[2]{0:T(128)S(1)} %pad_add_fusion.place_ref, f32[8,512]{1,0:T(8,128)S(1)} %pad.13.row_ref, f32[512,128]{1,0:T(8,128)S(1)} %pad.14.column_ref, ...), custom_call_target="tpu_custom_call" | custom-call | tf_op jit(solution)/shard_map/pallas_call | solution.py:249
  303.1 8.6 %collective-permute-done.64 = bf16[2,192,384]{2,1,0:T(8,128)(2,1)S(1)} collective-permute-done((bf16[2,192,384]{2,1,0:T(8,128)(2,1)S(1)}, bf16[2,192,384]{2,1,0:T(8,128)(2,1)S(1)}, u32[]{:S(2)}, u32[]{:S(2)}) %collective-permute-start.64) | collective-permute-done | bytes 294944 | tf_op jit(solution)/shard_map/ppermute | solution.py:69
  326.7 8.1 %collective-permute-done.66 = bf16[2,192,384]{2,1,0:T(8,128)(2,1)S(1)} collective-permute-done((bf16[2,192,384]{2,1,0:T(8,128)(2,1)S(1)}, bf16[2,192,384]{2,1,0:T(8,128)(2,1)S(1)}, u32[]{:S(2)}, u32[]{:S(2)}) %collective-permute-start.66) | collective-permute-done | bytes 294944 | tf_op jit(solution)/shard_map/ppermute | solution.py:69
  335.2 7.6 %collective-permute-done.67 = bf16[192,384]{1,0:T(8,128)(2,1)S(1)} collective-permute-done((bf16[192,384]{1,0:T(8,128)(2,1)S(1)}, bf16[192,384]{1,0:T(8,128)(2,1)S(1)}, u32[]{:S(2)}, u32[]{:S(2)}) %collective-permute-start.67) | collective-permute-done | bytes 147488 | tf_op jit(solution)/shard_map/ppermute | solution.py:69
  342.7 7.4 %shard_map.164 = (f32[256,768]{1,0:T(8,128)}, bf16[256,768]{1,0:T(8,128)(2,1)S(1)}, f32[8,768]{1,0:T(8,128)S(1)}, f32[4,2,192,384]{3,2,1,0:T(8,128)}, bf16[4,2,192,384]{3,2,1,0:T(8,128)(2,1)}) custom-call(s32[2]{0:T(128)S(1)} %pad_add_fusion.place_ref, bf16[256,768]{1,0:T(8,128)(2,1)S(1)} %get-tuple-element.177.own_gy_ref, ...), custom_call_target="tpu_custom_call" | custom-call | tf_op jit(solution)/shard_map/pallas_call | solution.py:249
  379.7 8.4 %shard_map.166 = (f32[256,768]{1,0:T(8,128)}, bf16[256,768]{1,0:T(8,128)(2,1)S(1)}, f32[8,576]{1,0:T(8,128)S(1)}, f32[4,192,384]{2,1,0:T(8,128)}, bf16[4,192,384]{2,1,0:T(8,128)(2,1)}) custom-call(s32[2]{0:T(128)S(1)} %pad_add_fusion.place_ref, f32[8,512]{1,0:T(8,128)S(1)} %pad.13.row_ref, f32[512,128]{1,0:T(8,128)S(1)} %pad.14.column_ref, ...), custom_call_target="tpu_custom_call" | custom-call | tf_op jit(solution)/shard_map/pallas_call | solution.py:249
  390.9 8.8 %collective-permute-done.76 = bf16[2,192,384]{2,1,0:T(8,128)(2,1)S(1)} collective-permute-done((bf16[2,192,384]{2,1,0:T(8,128)(2,1)}, bf16[2,192,384]{2,1,0:T(8,128)(2,1)S(1)}, u32[]{:S(2)}, u32[]{:S(2)}) %collective-permute-start.76) | collective-permute-done | bytes 294944 | tf_op jit(solution)/shard_map/ppermute | solution.py:69
  472.6 8.1 %collective-permute-done.81 = bf16[192,384]{1,0:T(8,128)(2,1)S(1)} collective-permute-done((bf16[192,384]{1,0:T(8,128)(2,1)S(1)}, bf16[192,384]{1,0:T(8,128)(2,1)S(1)}, u32[]{:S(2)}, u32[]{:S(2)}) %collective-permute-start.81) | collective-permute-done | bytes 147488 | tf_op jit(solution)/shard_map/ppermute | solution.py:69
  500.3 11.4 %collective-permute-done.97 = f32[2,3,768]{2,0,1:T(2,128)S(1)} collective-permute-done((f32[2,3,768]{2,0,1:T(2,128)S(1)}, f32[2,3,768]{2,0,1:T(2,128)S(1)}, u32[]{:S(2)}, u32[]{:S(2)}) %collective-permute-start.97) | collective-permute-done | bytes 18464 | tf_op jit(solution)/shard_map/ppermute | solution.py:245
  554.2 6.1 %collective-permute-done.89 = bf16[192,768]{1,0:T(8,128)(2,1)S(1)} collective-permute-done((bf16[192,768]{1,0:T(8,128)(2,1)S(1)}, bf16[192,768]{1,0:T(8,128)(2,1)S(1)}, u32[]{:S(2)}, u32[]{:S(2)}) %collective-permute-start.89) | collective-permute-done | bytes 294944 | tf_op jit(solution)/shard_map/ppermute | solution.py:689
  561.5 9.1 %shard_map.169 = bf16[768,768]{1,0:T(8,128)(2,1)} custom-call(bf16[768,768]{1,0:T(8,128)(2,1)S(1)} %bitcast.285, f32[768,768]{1,0:T(8,128)S(1)} %convert_select_fusion.gram_ref), custom_call_target="tpu_custom_call" | custom-call | tf_op jit(solution)/shard_map/pallas_call | solution.py:669
  581.0 8.0 %shard_map.168 = bf16[768,768]{1,0:T(8,128)(2,1)S(1)} custom-call(bf16[768,768]{1,0:T(8,128)(2,1)S(1)} %copy-done.14, f32[768,768]{1,0:T(8,128)S(1)} %fusion.75.gram_ref), custom_call_target="tpu_custom_call" | custom-call | tf_op jit(solution)/shard_map/pallas_call | solution.py:669
  (570 shorter events, 394.0 us)
Async XLA Ops:
  7.9 21.2 %collective-permute-start.1 = (bf16[2,3,96]{2,0,1:T(2,128)(2,1)S(1)}, bf16[2,3,96]{2,0,1:T(2,128)(2,1)S(1)}, u32[]{:S(2)}, u32[]{:S(2)}) collective-permute-start(bf16[2,3,96]{2,0,1:T(2,128)(2,1)S(1)} %convert_element_type.280), channel_id=1, source_target_pairs={{1,0},{2,1},{3,2},{0,3},{5,4},{6,5},{7,6},{4,7},{9,8},{10,9},{11,1... | collective-permute-start | bytes 3464 | tf_op jit(solution)/shard_map/ppermute | solution.py:69
  12.9 16.2 %collective-permute-start = (bf16[2,3,96]{2,0,1:T(2,128)(2,1)S(1)}, bf16[2,3,96]{2,0,1:T(2,128)(2,1)S(1)}, u32[]{:S(2)}, u32[]{:S(2)}) collective-permute-start(bf16[2,3,96]{2,0,1:T(2,128)(2,1)S(1)} %convert_element_type.280), channel_id=1, source_target_pairs={{3,0},{0,1},{1,2},{2,3},{7,4},{4,5},{5,6},{6,7},{11,8},{8,9},{9,10... | collective-permute-start | bytes 3464 | tf_op jit(solution)/shard_map/ppermute | solution.py:69
  15.6 28.2 %collective-permute-start.23 = (f32[136,768]{1,0:T(8,128)S(1)}, f32[136,768]{1,0:T(8,128)S(1)}, u32[]{:S(2)}, u32[]{:S(2)}) collective-permute-start(f32[136,768]{1,0:T(8,128)S(1)} %select_maximum_fusion), channel_id=1, source_target_pairs={{0,0},{1,8},{2,4},{3,12},{4,1},{5,9},{6,5},{7,13},{8,2},{9,10},{10... | collective-permute-start | bytes 1253384 | tf_op jit(solution)/shard_map/ppermute | solution.py:726
  18.7 19.6 %all-to-all-start.1 = ((bf16[1,96,4,192]{1,3,0,2:T(8,128)(2,1)}), bf16[1,96,4,192]{1,3,0,2:T(8,128)(2,1)S(1)}, u32[]{:S(2)}, u32[]{:S(2)}) async-start(bf16[1,96,4,192]{1,3,0,2:T(8,128)(2,1)} %bitcast.19), calls=%async_computation.1 | async-start | bytes 393216 | tf_op jit(solution)/shard_map/all_to_all | solution.py:58
  38.3 17.7 %all-to-all-start = ((bf16[5,96,4,192]{1,3,0,2:T(8,128)(2,1)}), bf16[5,96,4,192]{1,3,0,2:T(8,128)(2,1)S(1)}, u32[]{:S(2)}, u32[]{:S(2)}) async-start(bf16[5,96,4,192]{1,3,0,2:T(8,128)(2,1)} %copy.87), calls=%async_computation | async-start | bytes 1966080 | tf_op jit(solution)/shard_map/all_to_all | solution.py:58
  43.9 26.0 %collective-permute-start.24 = (f32[128,768]{1,0:T(8,128)S(1)}, f32[128,768]{1,0:T(8,128)}, u32[]{:S(2)}, u32[]{:S(2)}) collective-permute-start(f32[128,768]{1,0:T(8,128)S(1)} %slice.411), channel_id=1, source_target_pairs={{0,8},{8,0},{1,9},{9,1},{2,10},{10,2},{3,11},{11,3},{4,12},{12,4},... | collective-permute-start | bytes 1179656 | tf_op jit(solution)/shard_map/ppermute | solution.py:73
  71.3 19.5 %collective-permute-start.25 = (bf16[256,768]{1,0:T(8,128)(2,1)S(1)}, bf16[256,768]{1,0:T(8,128)(2,1)S(1)}, u32[]{:S(2)}, u32[]{:S(2)}) collective-permute-start(bf16[256,768]{1,0:T(8,128)(2,1)S(1)} %shard_map.152.own_a_ref), channel_id=1, source_target_pairs={{0,4},{4,0},{1,5},{5,1},{2,6},{6,2},{3,7},{7,3},{8,12},{12,8},{9,1... | collective-permute-start | bytes 1179656 | tf_op jit(solution)/shard_map/ppermute | solution.py:598
  155.9 20.0 %collective-permute-start.38 = (bf16[256,768]{1,0:T(8,128)(2,1)S(1)}, bf16[256,768]{1,0:T(8,128)(2,1)S(1)}, u32[]{:S(2)}, u32[]{:S(2)}) collective-permute-start(bf16[256,768]{1,0:T(8,128)(2,1)S(1)} %get-tuple-element.248), channel_id=1, source_target_pairs={{0,8},{8,0},{1,9},{9,1},{2,10},{10,2},{3,11},{11,3},{4,12},{12,4},... | collective-permute-start | bytes 1179656 | tf_op jit(solution)/shard_map/ppermute | solution.py:603
  212.0 22.8 %collective-permute-start.21 = (f32[128,768]{1,0:T(8,128)S(1)}, f32[128,768]{1,0:T(8,128)S(1)}, u32[]{:S(2)}, u32[]{:S(2)}) collective-permute-start(f32[128,768]{1,0:T(8,128)S(1)} %collective-permute-done.20), channel_id=1, source_target_pairs={{0,8},{8,0},{1,9},{9,1},{2,10},{10,2},{3,11},{11,3},{4,12},{12,4},... | collective-permute-start | bytes 1179656 | tf_op jit(solution)/shard_map/ppermute | solution.py:73
  259.8 30.8 %collective-permute-start.57 = (bf16[4,2,192,384]{3,2,1,0:T(8,128)(2,1)}, bf16[4,2,192,384]{3,2,1,0:T(8,128)(2,1)S(1)}, u32[]{:S(2)}, u32[]{:S(2)}) collective-permute-start(bf16[4,2,192,384]{3,2,1,0:T(8,128)(2,1)} %get-tuple-element.173), channel_id=1, source_target_pairs={{0,16},{16,0},{1,17},{17,1},{2,18},{18,2},{3,19},{19,3},{4,20},{20... | collective-permute-start | bytes 3538952 | tf_op jit(solution)/shard_map/ppermute | solution.py:191
  263.7 23.5 %collective-permute-start.52 = (bf16[256,768]{1,0:T(8,128)(2,1)S(1)}, bf16[256,768]{1,0:T(8,128)(2,1)S(1)}, u32[]{:S(2)}, u32[]{:S(2)}) collective-permute-start(bf16[256,768]{1,0:T(8,128)(2,1)S(1)} %get-tuple-element.244), channel_id=1, source_target_pairs={{0,8},{8,0},{1,9},{9,1},{2,10},{10,2},{3,11},{11,3},{4,12},{12,4},... | collective-permute-start | bytes 1179656 | tf_op jit(solution)/shard_map/ppermute | solution.py:603
  301.4 19.1 %collective-permute-start.63 = (bf16[4,192,384]{2,1,0:T(8,128)(2,1)S(1)}, bf16[4,192,384]{2,1,0:T(8,128)(2,1)S(1)}, u32[]{:S(2)}, u32[]{:S(2)}) collective-permute-start(bf16[4,192,384]{2,1,0:T(8,128)(2,1)S(1)} %copy-done.84), channel_id=1, source_target_pairs={{0,16},{16,0},{1,17},{17,1},{2,18},{18,2},{3,19},{19,3},{4,20},{20... | collective-permute-start | bytes 1769480 | tf_op jit(solution)/shard_map/ppermute | solution.py:191
  350.1 28.6 %collective-permute-start.71 = (bf16[4,2,192,384]{3,2,1,0:T(8,128)(2,1)}, bf16[4,2,192,384]{3,2,1,0:T(8,128)(2,1)S(1)}, u32[]{:S(2)}, u32[]{:S(2)}) collective-permute-start(bf16[4,2,192,384]{3,2,1,0:T(8,128)(2,1)} %get-tuple-element.200), channel_id=1, source_target_pairs={{0,16},{16,0},{1,17},{17,1},{2,18},{18,2},{3,19},{19,3},{4,20},{20... | collective-permute-start | bytes 3538952 | tf_op jit(solution)/shard_map/ppermute | solution.py:191
  389.2 20.1 %collective-permute-start.75 = (bf16[4,192,384]{2,1,0:T(8,128)(2,1)}, bf16[4,192,384]{2,1,0:T(8,128)(2,1)}, u32[]{:S(2)}, u32[]{:S(2)}) collective-permute-start(bf16[4,192,384]{2,1,0:T(8,128)(2,1)} %get-tuple-element.205), channel_id=1, source_target_pairs={{0,16},{16,0},{1,17},{17,1},{2,18},{18,2},{3,19},{19,3},{4,20},{20... | collective-permute-start | bytes 1769480 | tf_op jit(solution)/shard_map/ppermute | solution.py:191
  409.2 24.9 %collective-permute-start.78 = (bf16[2,192,384]{2,1,0:T(8,128)(2,1)}, bf16[2,192,384]{2,1,0:T(8,128)(2,1)}, u32[]{:S(2)}, u32[]{:S(2)}) collective-permute-start(bf16[2,192,384]{2,1,0:T(8,128)(2,1)} %slice_bitcast_fusion.11), channel_id=1, source_target_pairs={{2,0},{3,1},{0,2},{1,3},{6,4},{7,5},{4,6},{5,7},{10,8},{11,9},{8,1... | collective-permute-start | bytes 884744 | tf_op jit(solution)/shard_map/ppermute | solution.py:69
  419.3 22.8 %collective-permute-start.84 = (bf16[192,384]{1,0:T(8,128)(2,1)S(1)}, bf16[192,384]{1,0:T(8,128)(2,1)S(1)}, u32[]{:S(2)}, u32[]{:S(2)}) collective-permute-start(bf16[192,384]{1,0:T(8,128)(2,1)S(1)} %fusion.17), channel_id=1, source_target_pairs={{3,3},{19,7},{7,11},{23,15},{11,19},{27,23},{15,27},{31,31}} | collective-permute-start | bytes 442376 | tf_op jit(solution)/shard_map/ppermute | solution.py:127
  424.9 93.3 %collective-permute-start.74 = (f32[128,768]{1,0:T(8,128)}, f32[128,768]{1,0:T(8,128)}, u32[]{:S(2)}, u32[]{:S(2)}) collective-permute-start(f32[128,768]{1,0:T(8,128)} %constant_dynamic-slice_fusion.7), channel_id=1, source_target_pairs={{0,0},{8,1},{4,2},{12,3},{1,4},{9,5},{5,6},{13,7},{2,8},{10,9},{6,... | collective-permute-start | bytes 1179656 | tf_op jit(solution)/shard_map/ppermute | solution.py:785
  430.3 65.2 %collective-permute-start.93 = (f32[2,3,768]{2,0,1:T(2,128)}, f32[2,3,768]{2,0,1:T(2,128)}, u32[]{:S(2)}, u32[]{:S(2)}) collective-permute-start(f32[2,3,768]{2,0,1:T(2,128)} %get-tuple-element.277), channel_id=1, source_target_pairs={{3,0},{0,1},{1,2},{2,3},{7,4},{4,5},{5,6},{6,7},{11,8},{8,9},{9,10... | collective-permute-start | bytes 55304 | tf_op jit(solution)/shard_map/ppermute | solution.py:69
  430.3 65.2 %collective-permute-start.95 = (f32[2,3,768]{2,0,1:T(2,128)}, f32[2,3,768]{2,0,1:T(2,128)}, u32[]{:S(2)}, u32[]{:S(2)}) collective-permute-start(f32[2,3,768]{2,0,1:T(2,128)} %get-tuple-element.278), channel_id=1, source_target_pairs={{1,0},{2,1},{3,2},{0,3},{5,4},{6,5},{7,6},{4,7},{9,8},{10,9},{11,1... | collective-permute-start | bytes 55304 | tf_op jit(solution)/shard_map/ppermute | solution.py:69
  434.2 61.4 %collective-permute-start.94 = (f32[2,3,768]{2,0,1:T(2,128)}, f32[2,3,768]{2,0,1:T(2,128)}, u32[]{:S(2)}, u32[]{:S(2)}) collective-permute-start(f32[2,3,768]{2,0,1:T(2,128)} %get-tuple-element.279), channel_id=1, source_target_pairs={{2,0},{3,1},{0,2},{1,3},{6,4},{7,5},{4,6},{5,7},{10,8},{11,9},{8,1... | collective-permute-start | bytes 55304 | tf_op jit(solution)/shard_map/ppermute | solution.py:69
  491.9 29.2 %all-to-all-start.6 = ((bf16[8,1,96,768]{3,2,1,0:T(8,128)(2,1)}), bf16[8,1,96,768]{3,2,1,0:T(8,128)(2,1)S(1)}, u32[]{:S(2)}, u32[]{:S(2)}) async-start(bf16[8,1,96,768]{3,2,1,0:T(8,128)(2,1)} %bitcast.313), calls=%async_computation.6 | async-start | bytes 2359296 | tf_op jit(solution)/shard_map/all_to_all | solution.py:896
  495.5 82.6 %all-gather.2.cloned.1.call-start = ((), (), s32[]{:S(2)}) async-start(), calls=%async_computation.8 | async-start | bytes 1327104 | tf_op jit(solution)/shard_map/all_gather | solution.py:908
  500.3 19.2 %collective-permute-start.83 = (bf16[96,384]{1,0:T(8,128)(2,1)}, bf16[96,384]{1,0:T(8,128)(2,1)}, u32[]{:S(2)}, u32[]{:S(2)}) collective-permute-start(bf16[96,384]{1,0:T(8,128)(2,1)} %constant_dynamic-slice_fusion.6), channel_id=1, source_target_pairs={{0,4},{4,0},{1,5},{5,1},{2,6},{6,2},{3,7},{7,3},{8,12},{12,8},{9,1... | collective-permute-start | bytes 221192 | tf_op jit(solution)/shard_map/ppermute | solution.py:131
  570.6 21.5 %all-to-all-start.7 = ((bf16[8,1,96,768]{3,2,1,0:T(8,128)(2,1)}), bf16[8,1,96,768]{3,2,1,0:T(8,128)(2,1)}, u32[]{:S(2)}, u32[]{:S(2)}) async-start(bf16[8,1,96,768]{3,2,1,0:T(8,128)(2,1)} %bitcast.97), calls=%async_computation.7 | async-start | bytes 2359296 | tf_op jit(solution)/shard_map/all_to_all | solution.py:901
  (169 other events, 1472.4 us)
Sparse Core Ops, SparseCore 0:
  521.3 22.0 all-gather.1

commit v7 on v5

--- a/solution.py
+++ b/solution.py
@@ -16,6 +16,7 @@
 TP = 4
 COLS = D // TP
 TP_HEADS = HEADS // TP
+ROWS = 256
 
 norm_epsilon = 1e-05
 quintic_one = 3.4445
@@ -122,44 +123,59 @@
     return lax.ppermute(rows, EVERY, out_moves())
 
 
-def out_back(piece):
+def out_back(pieces):
     core = lax.axis_index("jc")
-    rows = lax.ppermute(piece, EVERY, [(b, a) for a, b in out_moves()])
-    half = rows.shape[0] // 2
-    mine = lax.dynamic_slice_in_dim(rows, core * half, half, axis=0)
-    give = lax.dynamic_slice_in_dim(rows, (1 - core) * half, half, axis=0)
+    rows = lax.ppermute(pieces, EVERY, [(b, a) for a, b in out_moves()])
+    half = rows.shape[1] // 2
+    mine = lax.dynamic_slice_in_dim(rows, core * half, half, axis=1)
+    give = lax.dynamic_slice_in_dim(rows, (1 - core) * half, half, axis=1)
     got = lax.ppermute(give, "jc", SWAP)
     return jnp.concatenate(
-        [jnp.where(core == 0, mine, got), jnp.where(core == 0, got, mine)], axis=1
-    )
-
-
-def pack_pieces(mats):
+        [jnp.where(core == 0, mine, got), jnp.where(core == 0, got, mine)], axis=2
+    )
+
+
+def last_block():
+    return lax.axis_index("ctx") == lax.axis_size("ctx") - 1
+
+
+def first_piece(mats):
     attn = mats[:, 0].astype(bf16)
     outs = out_pieces(attn)
-    first = to_group(attn[0:1])
+    return jnp.where(last_block(), outs[0], to_group(attn[0:1])[0].T), outs
+
+
+def other_pieces(mats, outs, *earlier):
     rest = [mats[0, 1:3]] + [mats[layer] for layer in range(1, mats.shape[0])]
-    rest = to_group(after(jnp.concatenate(rest), first).astype(bf16))
-    last = lax.axis_index("ctx") == lax.axis_size("ctx") - 1
-    pieces = [(jnp.where(last, outs[0], first[0].T), jnp.swapaxes(rest[0:2], 1, 2))]
+    rest = to_group(after(jnp.concatenate(rest), *earlier).astype(bf16))
+    rest = jnp.swapaxes(rest, 1, 2)
+    pieces = [rest[0:2]]
     for layer in range(1, mats.shape[0]):
-        base = 3 * layer - 1
-        pieces.append(
-            (
-                jnp.where(last, outs[layer], rest[base].T),
-                jnp.swapaxes(rest[base + 1 : base + 3], 1, 2),
-            )
-        )
+        attn = jnp.where(last_block(), outs[layer], rest[3 * layer - 1])
+        pieces.append((attn, rest[3 * layer : 3 * layer + 2]))
     return pieces
 
 
-def ctx_gather(piece):
+def momentum_pieces(mats):
+    layers, count, rows, width = mats.shape
+    columns = jnp.swapaxes(to_group(mats.reshape(layers * count, rows, width)), 1, 2)
+    columns = columns.reshape(layers, count, *columns.shape[1:])
+    attn = jnp.where(last_block(), out_pieces(mats[:, 0]), columns[:, 0])
+    return jnp.concatenate([attn[:, None], columns[:, 1:]], axis=1)
+
+
+def ctx_gather(piece, *earlier):
+    piece = after(piece, *earlier)
     near, back, far = [rotate(piece, "ctx", step) for step in (1, 3, 2)]
     return [piece, near, far, back]
 
 
 def group_swap(blocks):
     return [lax.ppermute(block, "g", SWAP) for block in blocks]
+
+
+def group_swap_all(blocks):
+    return [lax.ppermute(jnp.stack(blocks), "g", SWAP)]
 
 
 def gather_weights_wide(low):
@@ -185,21 +201,20 @@
     return mine + lax.ppermute(give, "g", SWAP).astype(f32)
 
 
-def ctx_sum(blocks):
+def ctx_sum(blocks, *earlier):
+    low = after(blocks, *earlier).astype(bf16)
     total = blocks[0]
     for step in (1, 3, 2):
-        total = total + rotate(blocks[step].astype(bf16), "ctx", -step).astype(f32)
+        total = total + rotate(low[step], "ctx", -step).astype(f32)
     return total
 
 
-def attn_rows(part):
-    columns = from_group(part.T[None])[0]
-    last = lax.axis_index("ctx") == lax.axis_size("ctx") - 1
-    return jnp.where(last, out_back(part), columns).astype(f32)
-
-
-def mlp_rows(part):
-    return from_group(jnp.swapaxes(part, 1, 2)).astype(f32)
+def grad_rows(parts):
+    layers, count, width, half = parts.shape
+    flat = jnp.swapaxes(parts.reshape(layers * count, width, half), 1, 2)
+    rows = from_group(flat).reshape(layers, count, -1, D)
+    attn = jnp.where(last_block(), out_back(parts[:, 0]), rows[:, 0])
+    return jnp.concatenate([attn[:, None], rows[:, 1:]], axis=1).astype(f32)
 
 
 def scatter_wide(mats):
@@ -352,7 +367,9 @@
     def kernel(place_ref, row_ref, column_ref, bias_ref, own_a_ref, other_a_ref, *refs):
         if own:
             own_refs, refs = refs[:4], refs[4:]
-            others, refs = refs[:4], refs[4:]
+            others, refs = refs[: len(other)], refs[len(other) :]
+            if len(other) == 1:
+                others = [others[0].at[step] for step in range(4)]
             w_ref, qkv_ref, lse_ref, o_ref, mine_ref, give_ref = refs
             put_blocks(place_ref, own_refs, others, [w_ref])
         else:
@@ -497,7 +514,8 @@
 
     def kernel(place_ref, bias_ref, own_c_ref, other_c_ref, *refs):
         if own:
-            own_refs, others, refs = refs[:4], refs[4:8], refs[8:]
+            own_refs, other_ref, refs = refs[:4], refs[4], refs[5:]
+            others = [other_ref.at[step] for step in range(4)]
             w_ref, preact_ref, act_ref, mine_ref, give_ref = refs
             put_blocks(place_ref, own_refs, others, [w_ref.at[0], w_ref.at[1]])
         else:
@@ -594,98 +612,157 @@
     return mine, lax.ppermute(mine.astype(bf16), "jx", SWAP)
 
 
-def orthogonalize_kernel(x_ref, gram_ref, out_ref, base_ref, work_ref, mat_ref, low_ref):
+def polynomial(base_ref, low_ref, mat_ref):
+    low_ref[...] = base_ref[...].astype(bf16)
+    for start in range(0, base_ref.shape[0], ROWS):
+        block = pl.ds(start, ROWS)
+        square = dot(low_ref[block, :], low_ref[...])
+        mat_ref[block, :] = (quintic_two * base_ref[block, :] + quintic_three * square).astype(bf16)
+
+
+def two_part(left, right):
+    high = left.astype(bf16)
+    rest = (left - high.astype(f32)).astype(bf16)
+    return dot(high, right) + dot(rest, right)
+
+
+def iterate(x_ref, out_ref, base_ref, work_ref, mat_ref, low_ref):
     size = x_ref.shape[0]
-    rows = 256
-
-    def each(body):
-        for start in range(0, size, rows):
-            body(pl.ds(start, rows))
-
-    def polynomial():
-        low_ref[...] = base_ref[...].astype(bf16)
-
-        def body(block):
-            square = dot(low_ref[block, :], low_ref[...])
-            mat_ref[block, :] = (
-                quintic_two * base_ref[block, :] + quintic_three * square
-            ).astype(bf16)
-
-        each(body)
-
-    def two_part(left, right):
-        high = left.astype(bf16)
-        rest = (left - high.astype(f32)).astype(bf16)
-        return dot(high, right) + dot(rest, right)
-
+    blocks = [pl.ds(start, ROWS) for start in range(0, size, ROWS)]
     trace = jnp.zeros((1, 1), f32)
-    for start in range(0, size, rows):
-        block = gram_ref[pl.ds(start, rows), pl.ds(start, rows)]
-        line = lax.broadcasted_iota(jnp.int32, (rows, rows), 0)
-        column = lax.broadcasted_iota(jnp.int32, (rows, rows), 1)
-        trace = trace + jnp.sum(jnp.where(line == column, block, 0.0), keepdims=True)
+    line = lax.broadcasted_iota(jnp.int32, (ROWS, ROWS), 0)
+    column = lax.broadcasted_iota(jnp.int32, (ROWS, ROWS), 1)
+    for block in blocks:
+        part = jnp.where(line == column, base_ref[block, block], 0.0)
+        trace = trace + jnp.sum(part, keepdims=True)
     scale = 1.0 / (jnp.sqrt(trace) + 1e-07)
-    base_ref[...] = gram_ref[...] * (scale * scale)
-    polynomial()
-
-    def first_step(block):
-        value = quintic_one * x_ref[block, :].astype(f32) + dot(mat_ref[block, :], x_ref[...])
+    base_ref[...] = base_ref[...] * (scale * scale)
+    polynomial(base_ref, low_ref, mat_ref)
+
+    for block in blocks:
+        value = quintic_one * x_ref[block, :].astype(f32) + dot(x_ref[block, :], mat_ref[...])
         out_ref[block, :] = (scale * value).astype(bf16)
         work_ref[block, :] = quintic_one * base_ref[block, :] + two_part(
             base_ref[block, :], mat_ref[...]
         )
-
-    each(first_step)
     turned = work_ref[...].T
     work_ref[...] = turned
-
-    def gram_step(block):
+    for block in blocks:
         base_ref[block, :] = quintic_one * work_ref[block, :] + two_part(
             work_ref[block, :], mat_ref[...]
         )
-
-    each(gram_step)
-    polynomial()
-    low_ref[...] = out_ref[...]
-
-    def second_step(block):
-        value = quintic_one * low_ref[block, :].astype(f32) + dot(mat_ref[block, :], low_ref[...])
-        out_ref[block, :] = value.astype(bf16)
-
-    each(second_step)
+    polynomial(base_ref, low_ref, mat_ref)
+    for block in blocks:
+        x = out_ref[block, :]
+        out_ref[block, :] = (quintic_one * x.astype(f32) + dot(x, mat_ref[...])).astype(bf16)
 
 
 def orthogonalize(matrix, gram):
     size = matrix.shape[0]
-    return pl.pallas_call(
-        orthogonalize_kernel,
-        out_shape=jax.ShapeDtypeStruct(matrix.shape, bf16),
-        in_specs=[pl.BlockSpec(memory_space=pltpu.VMEM)] * 2,
-        out_specs=pl.BlockSpec(memory_space=pltpu.VMEM),
-        scratch_shapes=[
-            pltpu.VMEM((size, size), f32),
-            pltpu.VMEM((size, size), f32),
-            pltpu.VMEM((size, size), bf16),
-            pltpu.VMEM((size, size), bf16),
-        ],
-        compiler_params=pltpu.CompilerParams(vmem_limit_bytes=48 * 1024 * 1024),
-    )(matrix, gram)
+
+    def kernel(unused, x_ref, gram_ref, out_ref, in_ref, base_ref, work_ref, mat_ref, low_ref):
+        in_ref[...] = x_ref[...].T
+        base_ref[...] = gram_ref[...]
+        iterate(in_ref, out_ref, base_ref, work_ref, mat_ref, low_ref)
+        out_ref[...] = out_ref[...].T
+
+    return call(
+        kernel,
+        [((size, size), bf16)],
+        jnp.zeros((1,), jnp.int32),
+        matrix,
+        gram,
+        scratch=[pltpu.VMEM((size, size), kind) for kind in (bf16, f32, f32, bf16, bf16)],
+    )[0]
+
+
+def put_slots(slot_ref, x_ref):
+    half = D // 2
+    for source in range(8):
+        group, number = source // TP, source % TP
+        x_ref[number * COLS : (number + 1) * COLS, group * half : (group + 1) * half] = slot_ref[
+            source
+        ]
+
+
+def slot_gram(place, slots):
+    def kernel(place_ref, slot_ref, x_ref, gram_ref):
+        put_slots(slot_ref, x_ref)
+        half = D // 2
+        for part in range(2):
+            rows = dot_tokens(x_ref[:, part * half : (part + 1) * half], x_ref[...]).astype(bf16)
+            for number in range(2):
+                back = 2 * part + number - place_ref[0]
+                back = jnp.where(back < 0, back + 4, back)
+                gram_ref[back] = rows[number * COLS : (number + 1) * COLS]
+
+    return call(kernel, [((D, D), bf16), ((4, COLS, D), bf16)], place, slots)
+
+
+def slot_orthogonalize(place, x_wide, grams, square_slots):
+    def kernel(
+        place_ref,
+        wide_ref,
+        gram0_ref,
+        gram1_ref,
+        gram2_ref,
+        gram3_ref,
+        slot_ref,
+        out_ref,
+        x_ref,
+        base_ref,
+        work_ref,
+        mat_ref,
+        low_ref,
+    ):
+        core = place_ref[2]
+
+        @pl.when(core == 0)
+        def wide():
+            x_ref[...] = wide_ref[...]
+            for step, gram_ref in enumerate((gram0_ref, gram1_ref, gram2_ref, gram3_ref)):
+                rows = pl.ds(pl.multiple_of(block_at(place_ref, step) * COLS, COLS), COLS)
+                base_ref[rows, :] = gram_ref[...].astype(f32)
+
+        @pl.when(core == 1)
+        def square():
+            put_slots(slot_ref, x_ref)
+            base_ref[...] = dot_tokens(x_ref[...], x_ref[...])
+
+        iterate(x_ref, out_ref, base_ref, work_ref, mat_ref, low_ref)
+
+        @pl.when((core == 0) | (place_ref[0] < 3))
+        def turn():
+            out_ref[...] = out_ref[...].T
+
+    return call(
+        kernel,
+        [((D, D), bf16)],
+        place,
+        x_wide,
+        *grams,
+        square_slots,
+        scratch=[pltpu.VMEM((D, D), kind) for kind in (bf16, f32, f32, bf16, bf16)],
+    )[0]
+
+
+def slot_exchange(blocks):
+    return lax.all_to_all(blocks, DP, split_axis=0, concat_axis=0, tiled=True)
+
+
+def core_shift(block, step):
+    size = lax.axis_size("ctx")
+    return lax.ppermute(block, ("jc", "ctx"), [((i + step) % size, i) for i in range(size)])
 
 
 def ctx_gram(gram):
     size = lax.axis_size("ctx")
-
-    def shift(block, step):
-        moves = [((i + step) % size, i) for i in range(size)]
-        return lax.ppermute(block, ("jc", "ctx"), moves)
-
-    rows = gram.shape[0] // size
-    blocks = from_own(gram.astype(bf16).reshape(size, rows, -1))
+    blocks = from_own(gram.astype(bf16).reshape(size, gram.shape[0] // size, -1))
     total = blocks[0].astype(f32)
     for step in (1, 3, 2):
-        total = total + shift(blocks[step], -step).astype(f32)
+        total = total + core_shift(blocks[step], -step).astype(f32)
     low = total.astype(bf16)
-    full = [low] + [shift(low, step) for step in range(1, size)]
+    full = [low] + [core_shift(low, step) for step in range(1, size)]
     return to_absolute(jnp.stack(full)).reshape(gram.shape).astype(f32)
 
 
@@ -718,13 +795,14 @@
     hidden = x_join(moved[:tokens_dev])
     segment_row = moved[tokens_dev, :seq_len]
     relative = lax.axis_size("g") == 2
-    place = jnp.stack([z_index, lax.axis_index("g")]).astype(jnp.int32)
+    place = jnp.stack([z_index, lax.axis_index("g"), c_index]).astype(jnp.int32)
     if relative:
-        pieces = pack_pieces(weights)
-        own_attn = ctx_gather(pieces[0][0])
-        own_mlp = ctx_gather(after(pieces[0][1], *own_attn[1:]))
+        piece, outs = first_piece(weights)
+        own_attn = ctx_gather(piece)
         attn_weights = (own_attn, group_swap(own_attn))
-        mlp_weights = (own_mlp, group_swap(own_mlp))
+        pieces = other_pieces(weights, outs, own_attn[1])
+        own_mlp = ctx_gather(pieces[0], *own_attn[1:])
+        mlp_weights = (own_mlp, group_swap_all(own_mlp))
     else:
         wide_weights = gather_weights_wide(weights.astype(bf16))
 
@@ -749,23 +827,18 @@
         w_attn, qkv, lse, o, mine, give = attend_stage(
             place, row_info, column_info, qkv_bias[layer], a_own, a_other, attn_weights
         )
-        if relative and layer:
-            mine, own_mlp = lax.optimization_barrier((mine, own_mlp))
-            mlp_weights = (own_mlp, group_swap(own_mlp))
         if relative and following:
-            next_attn = ctx_gather(after(pieces[layer + 1][0], *own_mlp[1:]))
-            next_mlp = ctx_gather(after(pieces[layer + 1][1], *next_attn[1:]))
+            own_attn = ctx_gather(pieces[layer + 1][0], *own_mlp[1:])
+            own_mlp = ctx_gather(pieces[layer + 1][1], *own_attn[1:])
         mine, recv = group_sum(mine, give)
         middle, c_own = norm_stage(vec_rows, layer, 2, hidden, mine, recv, (layer, 6))
-        if relative and following:
-            c_own, next_attn = lax.optimization_barrier((c_own, next_attn))
         c_other = core_swap(c_own)
         w_mlp, preact, act, mine, give = feed_stage(
             place, up_bias[layer], c_own, c_other, mlp_weights
         )
         if relative and following:
-            attn_weights = (next_attn, group_swap(next_attn))
-            own_mlp = next_mlp
+            attn_weights = (own_attn, group_swap_all(own_attn))
+            mlp_weights = (own_mlp, group_swap_all(own_mlp))
         mine, recv = group_sum(mine, give)
         stored.append(
             (hidden, middle, a_own, a_other, qkv, lse, o, c_own, c_other, preact, act, w_attn, w_mlp)
@@ -780,9 +853,12 @@
         return lax.ppermute(block, axes, from_seq)
 
     hidden_out = send_back(hidden)
-    grad_hidden = x_join(lax.ppermute(after(out_grad[0], stored[-1][6]), axes, to_seq))
+    if relative:
+        scaled = after(mat_momentum, stored[0][6]) * (momentum_decay * momentum_decay)
+        moments = momentum_pieces(scaled.astype(bf16))
+    grad_hidden = x_join(lax.ppermute(after(out_grad[0], own_mlp[2] if relative else stored[-1][6]), axes, to_seq))
     gy_own = grad_hidden.astype(bf16)
-    attn_half = mlp_part = None
+    attn_half = mlp_half = None
 
     mat_list = [None] * LAYERS
     sum_list = [None] * LAYERS
@@ -792,8 +868,8 @@
             layer
         ]
         if relative and attn_half is not None:
-            gy_own, attn_half, mlp_part = lax.optimization_barrier((gy_own, attn_half, mlp_part))
-            attn_part = ctx_sum(attn_half)
+            gy_own, attn_half, mlp_half = lax.optimization_barrier((gy_own, attn_half, mlp_half))
+            part = ctx_sum(jnp.concatenate([attn_half[:, None], mlp_half], axis=1))
         gy_other = core_swap(gy_own)
         mine, give, up_sums, *mlp_grads = feed_back_stage(
             place, gy_own, gy_other, c_own, c_other, preact, act, w_mlp, relative
@@ -805,8 +881,8 @@
             vec_rows, layer, 2, grad_hidden, mine, recv, middle
         )
         if relative and attn_half is not None:
-            gb_own, attn_part = lax.optimization_barrier((gb_own, attn_part))
-            parts[layer + 1] = (attn_part, mlp_part)
+            gb_own, part = lax.optimization_barrier((gb_own, part))
+            parts[layer + 1] = part
         if layer == LAYERS - 1:
             gb_own, hidden_out = lax.optimization_barrier((gb_own, hidden_out))
         gb_other = core_swap(gb_own)
@@ -826,7 +902,8 @@
         )
         if relative:
             mine, mlp_half = lax.optimization_barrier((mine, mlp_half))
-            mlp_part = ctx_sum(mlp_half)
+            if layer == 0:
+                mlp_part = ctx_sum(mlp_half)
             attn_half = half_sum(*attn_grads)
         else:
             attn_grad = attn_grads[0]
@@ -844,13 +921,6 @@
         sum_list[layer] = (in_sums, mid_sums, up_sums, qkv_sums)
     input_grad = send_back(grad_hidden)
 
-    if relative:
-        parts[0] = (ctx_sum(attn_half), mlp_part)
-        for layer in range(LAYERS):
-            attn_part, mlp_part = [
-                after(part, grad_hidden).astype(bf16) for part in parts[layer]
-            ]
-            mat_list[layer] = jnp.concatenate([attn_rows(attn_part)[None], mlp_rows(mlp_part)])
     once = jnp.where(x_index == 0, 1.0, 0.0).astype(f32)
     in_sums, mid_sums, up_sums, qkv_sums = [jnp.stack(sums) for sums in zip(*sum_list)]
     shared = once * jnp.concatenate(
@@ -873,41 +943,67 @@
     grad_vecs = lax.dynamic_slice_in_dim(
         sum_vectors(vec_terms), dp_index * vectors.shape[2], vectors.shape[2], axis=2
     )
-    cols_dev = weights.shape[3]
-    grad_list, moment_list, low_list = [], [], []
-    for layer in range(LAYERS):
-        for item in range(3):
-            grad = mat_list[layer][item]
-            moment = momentum_decay * mat_momentum[layer, item] + grad
-            grad_list.append(grad)
-            moment_list.append(moment)
-            low_list.append((grad + momentum_decay * moment).astype(bf16))
-    wide = [item for item in range(3 * LAYERS) if item % 3]
-    squares = [item for item in range(3, 3 * LAYERS, 3)]
-    table = []
-    for number in range(4):
-        table += [wide[number], squares[number % len(squares)]]
-    table = (table * (-(-dp_size // 8)))[:dp_size]
-    slots = jnp.stack([low_list[item] for item in table])
-    received = lax.all_to_all(slots[:, None], DP, split_axis=0, concat_axis=1, tiled=True)
-    current = received.reshape(dp_size * dp_rows, cols_dev)
-    gram_local = dot_trans(current, current)
-    gram = jnp.where(c_index == 0, ctx_gram(gram_local), gram_local)
-    ortho_mine = orthogonalize(current, gram)
-    returned = lax.all_to_all(
-        ortho_mine.reshape(dp_size, 1, dp_rows, cols_dev),
-        DP,
-        split_axis=0,
-        concat_axis=1,
-        tiled=True,
-    )[0]
-    first_full = lax.all_gather(low_list[0], DP, axis=0, tiled=True)
-    first_ortho = orthogonalize(first_full, dot_trans(first_full, first_full))
-    ortho_list = [lax.dynamic_slice_in_dim(first_ortho, dp_index * dp_rows, dp_rows, axis=0)]
-    ortho_list += [returned[table.index(item)] for item in range(1, 3 * LAYERS)]
-    ortho = jnp.stack(ortho_list).reshape(LAYERS, 3, dp_rows, cols_dev).astype(f32)
-    grad_mats = jnp.stack(grad_list).reshape(weights.shape)
-    moment_new = jnp.stack(moment_list).reshape(weights.shape)
+    if relative:
+        wide_low = [parts[layer][1:] * (1.0 + momentum_decay) for layer in range(1, LAYERS)]
+        wide_low = jnp.concatenate(wide_low + [mlp_part * (1.0 + momentum_decay)])
+        moment_wide = jnp.concatenate([moments[layer, 1:] for layer in (*range(1, LAYERS), 0)])
+        wide_low = (wide_low + moment_wide.astype(f32)).astype(bf16)
+        received = slot_exchange(jnp.repeat(wide_low, 2, axis=0))
+        x_wide, gram_blocks = slot_gram(place, received)
+        attn_part = ctx_sum(attn_half)
+        square_low = [parts[layer][0] for layer in range(1, LAYERS)] + [attn_part]
+        square_low = jnp.stack(square_low) * (1.0 + momentum_decay)
+        moment_square = jnp.stack([moments[layer, 0] for layer in (*range(1, LAYERS), 0)])
+        square_low = (square_low + moment_square.astype(f32)).astype(bf16)
+        square_slots = slot_exchange(jnp.tile(jnp.repeat(square_low, 2, axis=0), (2, 1, 1)))
+        total = gram_blocks[0].astype(f32)
+        for step in (1, 3, 2):
+            total = total + core_shift(gram_blocks[step], -step).astype(f32)
+        low = total.astype(bf16)
+        near, back, far = [core_shift(low, step) for step in (1, 3, 2)]
+        ortho_mine = slot_orthogonalize(place, x_wide, (low, near, far, back), square_slots)
+        returned = slot_exchange(ortho_mine.reshape(dp_size, dp_rows, D))
+        ortho = jnp.stack([returned[3], returned[4], returned[6], returned[1], returned[0], returned[2]])
+        ortho = ortho.reshape(weights.shape).astype(f32)
+        first = jnp.concatenate([attn_part[None], mlp_part])
+        grad_mats = grad_rows(jnp.stack([first, *parts[1:]]).astype(bf16))
+        moment_new = momentum_decay * mat_momentum + grad_mats
+    else:
+        cols_dev = weights.shape[3]
+        grad_list, moment_list, low_list = [], [], []
+        for layer in range(LAYERS):
+            for item in range(3):
+                grad = mat_list[layer][item]
+                moment = momentum_decay * mat_momentum[layer, item] + grad
+                grad_list.append(grad)
+                moment_list.append(moment)
+                low_list.append((grad + momentum_decay * moment).astype(bf16))
+        wide = [item for item in range(3 * LAYERS) if item % 3]
+        squares = [item for item in range(3, 3 * LAYERS, 3)]
+        table = []
+        for number in range(4):
+            table += [wide[number], squares[number % len(squares)]]
+        table = (table * (-(-dp_size // 8)))[:dp_size]
+        slots = jnp.stack([low_list[item] for item in table])
+        received = lax.all_to_all(slots[:, None], DP, split_axis=0, concat_axis=1, tiled=True)
+        current = received.reshape(dp_size * dp_rows, cols_dev)
+        gram_local = dot_trans(current, current)
+        gram = jnp.where(c_index == 0, ctx_gram(gram_local), gram_local)
+        ortho_mine = orthogonalize(current, gram)
+        returned = lax.all_to_all(
+            ortho_mine.reshape(dp_size, 1, dp_rows, cols_dev),
+            DP,
+            split_axis=0,
+            concat_axis=1,
+            tiled=True,
+        )[0]
+        first_full = lax.all_gather(low_list[0], DP, axis=0, tiled=True)
+        first_ortho = orthogonalize(first_full, dot_trans(first_full, first_full))
+        ortho_list = [lax.dynamic_slice_in_dim(first_ortho, dp_index * dp_rows, dp_rows, axis=0)]
+        ortho_list += [returned[table.index(item)] for item in range(1, 3 * LAYERS)]
+        ortho = jnp.stack(ortho_list).reshape(LAYERS, 3, dp_rows, cols_dev).astype(f32)
+        grad_mats = jnp.stack(grad_list).reshape(weights.shape)
+        moment_new = jnp.stack(moment_list).reshape(weights.shape)
     factor = jnp.array([0.2 * math.sqrt(D), 0.2 * math.sqrt(FF), 0.2 * math.sqrt(FF)], f32)
     weights_new = weights * (1.0 - matrix_rate * matrix_decay) - matrix_rate * (
         ortho * factor[None, :, None, None]

time: 679 us -> 569 us (0.84)
  waiting for transfers between devices: 250 us -> 201 us
  starting transfers between devices: 198 us -> 167 us
  between operations: 15.8 us -> 2.66 us
  other arithmetic: 51.3 us -> 40.6 us
    ppermute x16 -> x4, waiting for transfers between devices: 65.5 us -> 0.01 us  [group_swap(): return [lax.ppermute(block, 'g', SWAP) for block in blocks]]
    ppermute x30 -> x27, starting transfers between devices: 77.7 us -> 43.9 us  [rotate(): lax.ppermute(block, axis, [((i + step) % size, i) for i in range(size)])]
    pallas_call x2 -> x0, Pallas kernels: 17.1 us -> none  [orthogonalize(): pl.pallas_call(orthogonalize_kernel, out_shape=jax.ShapeDtypeStruct(matri...]
    pallas_call x16 -> x18, Pallas kernels: 68.4 us -> 84.4 us  [call(): pl.pallas_call(kernel, out_shape=[jax.ShapeDtypeStruct(shape, kind) for s...]
    ppermute x9 -> x11, waiting for transfers between devices: 9.12 us -> 22.5 us  [the longest x3 19.1 us: group_swap_all(): return [lax.ppermute(jnp.stack(blocks), 'g', SWAP)]]
    unnamed x11 -> x1, other arithmetic: 12 us -> 0.01 us
    ppermute x16 -> x4, starting transfers between devices: 16.3 us -> 5.22 us  [group_swap(): return [lax.ppermute(block, 'g', SWAP) for block in blocks]]
    ppermute x8, starting transfers between devices: 3.06 us -> 13.9 us  [group_sum(): return (mine, lax.ppermute(mine.astype(bf16), 'jx', SWAP))]
  transfers between devices with their start and end apart: 107 -> 93, of which waited for: 48 -> 33; matrix products, arithmetic and copies ran while one was open for 14% -> 15% of each run, Pallas kernels for 7% -> 13%
where the time goes in v7:
time: 569 us; the launch traced here: 559 us
  waiting for transfers between devices  201 us (35%)
  starting transfers between devices  167 us (29%)
  Pallas kernels  84.4 us (15%)
  local copies, waits for them, and re-layouts  63.5 us (11%)
  other arithmetic  40.6 us (7%)
    ppermute x27, waiting for transfers between devices, rotate(): lax.ppermute(block, axis, [((i + step) % size, i) for i in range(size)])  97.5 us
    pallas_call x18, Pallas kernels, call(): pl.pallas_call(kernel, out_shape=[jax.ShapeDtypeStruct(shape, kind) for s...  84.4 us
    ppermute x8, waiting for transfers between devices, group_sum(): return (mine, lax.ppermute(mine.astype(bf16), 'jx', SWAP))  44.8 us
    ppermute x27, starting transfers between devices, rotate(): lax.ppermute(block, axis, [((i + step) % size, i) for i in range(size)])  43.9 us
    ppermute x5, starting transfers between devices, pair_join(): other = lax.ppermute(block, axis, SWAP)  22.4 us
    ppermute x3, waiting for transfers between devices, group_swap_all(): return [lax.ppermute(jnp.stack(blocks), 'g', SWAP)]  19.1 us
    ppermute x6, starting transfers between devices, core_shift(): lax.ppermute(block, ('jc', 'ctx'), [((i + step) % size, i) for i in range...  18.6 us
    all_to_all x3, starting transfers between devices, slot_exchange(): return lax.all_to_all(blocks, DP, split_axis=0, concat_axis=0, tiled=True)  15.4 us
  transfers between devices with their start and end apart: 93, of which 33 were waited for; matrix products, arithmetic and copies ran while one was open for 15% of the time, Pallas kernels for 13%

profile of v7, /device:TPU:0, one launch (start us, length us, event | category | flops | bytes accessed | tf_op | source)
XLA Modules:
  0.0 558.9 jit_solution(18429849823160690967)
XLA Ops:
  46.6 7.4 %all-to-all-start.1 = ((bf16[5,96,4,192]{1,3,0,2:T(8,128)(2,1)}), bf16[5,96,4,192]{1,3,0,2:T(8,128)(2,1)}, u32[]{:S(2)}, u32[]{:S(2)}) async-start(bf16[5,96,4,192]{1,3,0,2:T(8,128)(2,1)} %copy.100), calls=%async_computation.1 | async-start | bytes 1966080 | tf_op jit(solution)/shard_map/all_to_all | solution.py:59
  60.9 6.9 %all-to-all-done.1 = bf16[5,96,4,192]{1,3,0,2:T(8,128)(2,1)} async-done(((bf16[5,96,4,192]{1,3,0,2:T(8,128)(2,1)}), bf16[5,96,4,192]{1,3,0,2:T(8,128)(2,1)}, u32[]{:S(2)}, u32[]{:S(2)}) %all-to-all-start.1) | async-done | bytes 737312 | tf_op jit(solution)/shard_map/all_to_all | solution.py:59
  87.7 13.0 %collective-permute-done.12.refs_2_ = bf16[2,192,384]{2,1,0:T(8,128)(2,1)S(1)} collective-permute-done((bf16[2,192,384]{2,1,0:T(8,128)(2,1)S(1)}, bf16[2,192,384]{2,1,0:T(8,128)(2,1)S(1)}, u32[]{:S(2)}, u32[]{:S(2)}) %collective-permute-start.12) | collective-permute-done | bytes 294944 | tf_op jit(solution)/shard_map/ppermute | solution.py:70
  107.6 9.4 %collective-permute-done.29.refs_1_ = bf16[256,768]{1,0:T(8,128)(2,1)S(1)} collective-permute-done((bf16[256,768]{1,0:T(8,128)(2,1)S(1)}, bf16[256,768]{1,0:T(8,128)(2,1)S(1)}, u32[]{:S(2)}, u32[]{:S(2)}) %collective-permute-start.29) | collective-permute-done | bytes 393248 | tf_op jit(solution)/shard_map/ppermute | solution.py:612
  121.3 10.4 %collective-permute-done.31.refs_4_ = bf16[4,2,192,384]{3,2,1,0:T(8,128)(2,1)} collective-permute-done((bf16[4,2,192,384]{3,2,1,0:T(8,128)(2,1)}, bf16[4,2,192,384]{3,2,1,0:T(8,128)(2,1)}, u32[]{:S(2)}, u32[]{:S(2)}) %collective-permute-start.31) | collective-permute-done | bytes 1179680 | tf_op jit(solution)/shard_map/ppermute | solution.py:178
  146.6 9.2 %collective-permute-done.15.refs_2_ = bf16[192,384]{1,0:T(8,128)(2,1)S(1)} collective-permute-done((bf16[192,384]{1,0:T(8,128)(2,1)S(1)}, bf16[192,384]{1,0:T(8,128)(2,1)S(1)}, u32[]{:S(2)}, u32[]{:S(2)}) %collective-permute-start.15) | collective-permute-done | bytes 147488 | tf_op jit(solution)/shard_map/ppermute | solution.py:70
  162.3 8.8 %collective-permute-done.35.refs_4_ = bf16[4,192,384]{2,1,0:T(8,128)(2,1)S(1)} collective-permute-done((bf16[4,192,384]{2,1,0:T(8,128)(2,1)S(1)}, bf16[4,192,384]{2,1,0:T(8,128)(2,1)S(1)}, u32[]{:S(2)}, u32[]{:S(2)}) %collective-permute-start.35) | collective-permute-done | bytes 589856 | tf_op jit(solution)/shard_map/ppermute | solution.py:178
  178.2 9.1 %collective-permute-done.17.refs_2_ = bf16[2,192,384]{2,1,0:T(8,128)(2,1)S(1)} collective-permute-done((bf16[2,192,384]{2,1,0:T(8,128)(2,1)S(1)}, bf16[2,192,384]{2,1,0:T(8,128)(2,1)S(1)}, u32[]{:S(2)}, u32[]{:S(2)}) %collective-permute-start.17) | collective-permute-done | bytes 294944 | tf_op jit(solution)/shard_map/ppermute | solution.py:70
  197.4 9.0 %collective-permute-start.19 = (f32[128,768]{1,0:T(8,128)S(1)}, f32[128,768]{1,0:T(8,128)S(1)}, u32[]{:S(2)}, u32[]{:S(2)}) collective-permute-start(f32[128,768]{1,0:T(8,128)S(1)} %collective-permute-done.18), channel_id=1, source_target_pairs={{0,8},{8,0},{1,9},{9,1},{2,10},{10,2},{3,11},{11,3},{4,12},{12,4},... | collective-permute-start | bytes 1179656 | tf_op jit(solution)/shard_map/ppermute | solution.py:74
  229.1 7.6 %shard_map.160 = (f32[256,768]{1,0:T(8,128)}, bf16[256,768]{1,0:T(8,128)(2,1)S(1)}, f32[8,768]{1,0:T(8,128)S(1)}, f32[4,2,192,384]{3,2,1,0:T(8,128)}, bf16[4,2,192,384]{3,2,1,0:T(8,128)(2,1)}) custom-call(s32[3]{0:T(128)S(1)} %pad_add_fusion.place_ref, bf16[256,768]{1,0:T(8,128)(2,1)S(1)} %fusion.42.own_gy_ref, ...), custom_call_target="tpu_custom_call" | custom-call | tf_op jit(solution)/shard_map/pallas_call | solution.py:255
  241.7 7.4 %collective-permute-done.45 = bf16[256,768]{1,0:T(8,128)(2,1)S(1)} collective-permute-done((bf16[256,768]{1,0:T(8,128)(2,1)S(1)}, bf16[256,768]{1,0:T(8,128)(2,1)S(1)}, u32[]{:S(2)}, u32[]{:S(2)}) %collective-permute-start.45) | collective-permute-done | bytes 393248 | tf_op jit(solution)/shard_map/ppermute | solution.py:612
  251.3 13.7 %collective-permute-done.43.recv_ref = bf16[256,768]{1,0:T(8,128)(2,1)S(1)} collective-permute-done((bf16[256,768]{1,0:T(8,128)(2,1)S(1)}, bf16[256,768]{1,0:T(8,128)(2,1)S(1)}, u32[]{:S(2)}, u32[]{:S(2)}) %collective-permute-start.43) | collective-permute-done | bytes 393248 | tf_op jit(solution)/shard_map/ppermute | solution.py:612
  270.8 8.5 %shard_map.162 = (f32[256,768]{1,0:T(8,128)}, bf16[256,768]{1,0:T(8,128)(2,1)S(1)}, f32[8,576]{1,0:T(8,128)S(1)}, f32[4,192,384]{2,1,0:T(8,128)}, bf16[4,192,384]{2,1,0:T(8,128)(2,1)}) custom-call(s32[3]{0:T(128)S(1)} %pad_add_fusion.place_ref, f32[8,512]{1,0:T(8,128)S(1)} %pad.13.row_ref, f32[512,128]{1,0:T(8,128)S(1)} %pad.14.column_ref, ...), custom_call_target="tpu_custom_call" | custom-call | tf_op jit(solution)/shard_map/pallas_call | solution.py:255
  297.3 8.0 %collective-permute-done.51 = bf16[4,192,384]{2,1,0:T(8,128)(2,1)S(1)} collective-permute-done((bf16[4,192,384]{2,1,0:T(8,128)(2,1)}, bf16[4,192,384]{2,1,0:T(8,128)(2,1)S(1)}, u32[]{:S(2)}, u32[]{:S(2)}) %collective-permute-start.51) | collective-permute-done | bytes 589856 | tf_op jit(solution)/shard_map/ppermute | solution.py:201
  305.4 8.9 %collective-permute-done.50.recv_ref = bf16[256,768]{1,0:T(8,128)(2,1)S(1)} collective-permute-done((bf16[256,768]{1,0:T(8,128)(2,1)S(1)}, bf16[256,768]{1,0:T(8,128)(2,1)S(1)}, u32[]{:S(2)}, u32[]{:S(2)}) %collective-permute-start.50) | collective-permute-done | bytes 393248 | tf_op jit(solution)/shard_map/ppermute | solution.py:612
  327.9 7.6 %shard_map.164 = (f32[256,768]{1,0:T(8,128)}, bf16[256,768]{1,0:T(8,128)(2,1)S(1)}, f32[8,768]{1,0:T(8,128)S(1)}, f32[4,2,192,384]{3,2,1,0:T(8,128)}, bf16[4,2,192,384]{3,2,1,0:T(8,128)(2,1)}) custom-call(s32[3]{0:T(128)S(1)} %pad_add_fusion.place_ref, bf16[256,768]{1,0:T(8,128)(2,1)S(1)} %get-tuple-element.128.own_gy_ref, ...), custom_call_target="tpu_custom_call" | custom-call | tf_op jit(solution)/shard_map/pallas_call | solution.py:255
  343.8 8.1 %collective-permute-done.55 = bf16[3,192,384]{2,1,0:T(8,128)(2,1)S(1)} collective-permute-done((bf16[3,192,384]{2,1,0:T(8,128)(2,1)S(1)}, bf16[3,192,384]{2,1,0:T(8,128)(2,1)S(1)}, u32[]{:S(2)}, u32[]{:S(2)}) %collective-permute-start.55) | collective-permute-done | bytes 442400 | tf_op jit(solution)/shard_map/ppermute | solution.py:70
  352.0 6.6 %collective-permute-done.56 = bf16[3,192,384]{2,1,0:T(8,128)(2,1)S(1)} collective-permute-done((bf16[3,192,384]{2,1,0:T(8,128)(2,1)S(1)}, bf16[3,192,384]{2,1,0:T(8,128)(2,1)S(1)}, u32[]{:S(2)}, u32[]{:S(2)}) %collective-permute-start.56) | collective-permute-done | bytes 442400 | tf_op jit(solution)/shard_map/ppermute | solution.py:70
  358.6 20.5 %collective-permute-done.57 = bf16[3,192,384]{2,1,0:T(8,128)(2,1)S(1)} collective-permute-done((bf16[3,192,384]{2,1,0:T(8,128)(2,1)S(1)}, bf16[3,192,384]{2,1,0:T(8,128)(2,1)S(1)}, u32[]{:S(2)}, u32[]{:S(2)}) %collective-permute-start.57) | collective-permute-done | bytes 442400 | tf_op jit(solution)/shard_map/ppermute | solution.py:70
  386.6 9.2 %shard_map.166 = (f32[256,768]{1,0:T(8,128)}, bf16[256,768]{1,0:T(8,128)(2,1)S(1)}, f32[8,576]{1,0:T(8,128)S(1)}, f32[4,192,384]{2,1,0:T(8,128)}, bf16[4,192,384]{2,1,0:T(8,128)(2,1)}) custom-call(s32[3]{0:T(128)S(1)} %pad_add_fusion.place_ref, f32[8,512]{1,0:T(8,128)S(1)} %pad.13.row_ref, f32[512,128]{1,0:T(8,128)S(1)} %pad.14.column_ref, ...), custom_call_target="tpu_custom_call" | custom-call | tf_op jit(solution)/shard_map/pallas_call | solution.py:255
  403.7 6.8 %collective-permute-done.67 = bf16[2,192,384]{2,1,0:T(8,128)(2,1)S(1)} collective-permute-done((bf16[2,192,384]{2,1,0:T(8,128)(2,1)}, bf16[2,192,384]{2,1,0:T(8,128)(2,1)S(1)}, u32[]{:S(2)}, u32[]{:S(2)}) %collective-permute-start.67) | collective-permute-done | bytes 294944 | tf_op jit(solution)/shard_map/ppermute | solution.py:70
  416.8 9.4 %collective-permute-done.69 = bf16[2,192,384]{2,1,0:T(8,128)(2,1)} collective-permute-done((bf16[2,192,384]{2,1,0:T(8,128)(2,1)}, bf16[2,192,384]{2,1,0:T(8,128)(2,1)}, u32[]{:S(2)}, u32[]{:S(2)}) %collective-permute-start.69) | collective-permute-done | bytes 294944 | tf_op jit(solution)/shard_map/ppermute | solution.py:70
  518.9 11.4 %shard_map.169 = bf16[768,768]{1,0:T(8,128)(2,1)} custom-call(s32[3]{0:T(128)S(1)} %pad_add_fusion.place_ref, bf16[768,768]{1,0:T(8,128)(2,1)} %copy-done.10, bf16[192,768]{1,0:T(8,128)(2,1)S(1)} %fusion.12.gram0_ref, bf16[192,768]{1,0:T(8,128)(2,1)S(1)} %collective-permute-done.75.gram1_ref, bf16[192,768]{1,0:T(8,128)(2,1)S(1)} %collective-permute-done.76.gram2_ref, ...), custom_call_target="tpu_custom_call" | custom-call | tf_op jit(solution)/shard_map/pallas_call | solution.py:255
  530.3 8.0 %all-to-all-start.6 = ((bf16[8,96,768]{2,1,0:T(8,128)(2,1)}), bf16[8,96,768]{2,1,0:T(8,128)(2,1)S(1)}, u32[]{:S(2)}, u32[]{:S(2)}) async-start(bf16[8,96,768]{2,1,0:T(8,128)(2,1)} %bitcast.232), calls=%async_computation.6 | async-start | bytes 2359296 | tf_op jit(solution)/shard_map/all_to_all | solution.py:750
  (466 shorter events, 331.1 us)
Async XLA Ops:
  29.8 29.5 %collective-permute-start.22 = (f32[128,768]{1,0:T(8,128)}, f32[128,768]{1,0:T(8,128)}, u32[]{:S(2)}, u32[]{:S(2)}) collective-permute-start(f32[128,768]{1,0:T(8,128)} %slice.315), channel_id=1, source_target_pairs={{0,8},{8,0},{1,9},{9,1},{2,10},{10,2},{3,11},{11,3},{4,12},{12,4},... | collective-permute-start | bytes 1179656 | tf_op jit(solution)/shard_map/ppermute | solution.py:74
  57.2 21.8 %collective-permute-start.25 = (bf16[192,384]{1,0:T(8,128)(2,1)S(1)}, bf16[192,384]{1,0:T(8,128)(2,1)S(1)}, u32[]{:S(2)}, u32[]{:S(2)}) collective-permute-start(bf16[192,384]{1,0:T(8,128)(2,1)S(1)} %collective-permute-done.8.refs_1_), channel_id=1, source_target_pairs={{0,16},{16,0},{1,17},{17,1},{2,18},{18,2},{3,19},{19,3},{4,20},{20... | collective-permute-start | bytes 442376 | tf_op jit(solution)/shard_map/ppermute | solution.py:174
  78.9 21.8 %collective-permute-start.12 = (bf16[2,192,384]{2,1,0:T(8,128)(2,1)S(1)}, bf16[2,192,384]{2,1,0:T(8,128)(2,1)S(1)}, u32[]{:S(2)}, u32[]{:S(2)}) collective-permute-start(bf16[2,192,384]{2,1,0:T(8,128)(2,1)S(1)} %get-tuple-element.87.refs_0_), channel_id=1, source_target_pairs={{2,0},{3,1},{0,2},{1,3},{6,4},{7,5},{4,6},{5,7},{10,8},{11,9},{8,1... | collective-permute-start | bytes 884744 | tf_op jit(solution)/shard_map/ppermute | solution.py:70
  101.9 29.7 %collective-permute-start.31 = (bf16[4,2,192,384]{3,2,1,0:T(8,128)(2,1)}, bf16[4,2,192,384]{3,2,1,0:T(8,128)(2,1)}, u32[]{:S(2)}, u32[]{:S(2)}) collective-permute-start(bf16[4,2,192,384]{3,2,1,0:T(8,128)(2,1)} %pad_maximum_fusion.2), channel_id=1, source_target_pairs={{0,16},{16,0},{1,17},{17,1},{2,18},{18,2},{3,19},{19,3},{4,20},{20... | collective-permute-start | bytes 3538952 | tf_op jit(solution)/shard_map/ppermute | solution.py:178
  161.4 25.9 %collective-permute-start.17 = (bf16[2,192,384]{2,1,0:T(8,128)(2,1)S(1)}, bf16[2,192,384]{2,1,0:T(8,128)(2,1)S(1)}, u32[]{:S(2)}, u32[]{:S(2)}) collective-permute-start(bf16[2,192,384]{2,1,0:T(8,128)(2,1)S(1)} %get-tuple-element.89.refs_0_), channel_id=1, source_target_pairs={{2,0},{3,1},{0,2},{1,3},{6,4},{7,5},{4,6},{5,7},{10,8},{11,9},{8,1... | collective-permute-start | bytes 884744 | tf_op jit(solution)/shard_map/ppermute | solution.py:70
  161.4 25.9 %collective-permute-start.40 = (bf16[2,192,384]{2,1,0:T(8,128)(2,1)S(1)}, bf16[2,192,384]{2,1,0:T(8,128)(2,1)S(1)}, u32[]{:S(2)}, u32[]{:S(2)}) collective-permute-start(bf16[2,192,384]{2,1,0:T(8,128)(2,1)S(1)} %get-tuple-element.89.refs_0_), channel_id=1, source_target_pairs={{3,0},{0,1},{1,2},{2,3},{7,4},{4,5},{5,6},{6,7},{11,8},{8,9},{9,10... | collective-permute-start | bytes 884744 | tf_op jit(solution)/shard_map/ppermute | solution.py:70
  188.6 31.7 %collective-permute-start.41 = (bf16[4,2,192,384]{3,2,1,0:T(8,128)(2,1)}, bf16[4,2,192,384]{3,2,1,0:T(8,128)(2,1)}, u32[]{:S(2)}, u32[]{:S(2)}) collective-permute-start(bf16[4,2,192,384]{3,2,1,0:T(8,128)(2,1)} %pad_maximum_fusion.3), channel_id=1, source_target_pairs={{0,16},{16,0},{1,17},{17,1},{2,18},{18,2},{3,19},{19,3},{4,20},{20... | collective-permute-start | bytes 3538952 | tf_op jit(solution)/shard_map/ppermute | solution.py:178
  239.9 50.2 %collective-permute-start.48 = (bf16[4,2,192,384]{3,2,1,0:T(8,128)(2,1)}, bf16[4,2,192,384]{3,2,1,0:T(8,128)(2,1)}, u32[]{:S(2)}, u32[]{:S(2)}) collective-permute-start(bf16[4,2,192,384]{3,2,1,0:T(8,128)(2,1)} %get-tuple-element.120), channel_id=1, source_target_pairs={{0,16},{16,0},{1,17},{17,1},{2,18},{18,2},{3,19},{19,3},{4,20},{20... | collective-permute-start | bytes 3538952 | tf_op jit(solution)/shard_map/ppermute | solution.py:201
  241.6 23.5 %collective-permute-start.43 = (bf16[256,768]{1,0:T(8,128)(2,1)S(1)}, bf16[256,768]{1,0:T(8,128)(2,1)S(1)}, u32[]{:S(2)}, u32[]{:S(2)}) collective-permute-start(bf16[256,768]{1,0:T(8,128)(2,1)S(1)} %get-tuple-element.189), channel_id=1, source_target_pairs={{0,8},{8,0},{1,9},{9,1},{2,10},{10,2},{3,11},{11,3},{4,12},{12,4},... | collective-permute-start | bytes 1179656 | tf_op jit(solution)/shard_map/ppermute | solution.py:612
  285.1 34.8 %all-to-all-start.3 = ((bf16[6,96,4,192]{1,3,0,2:T(8,128)(2,1)}), bf16[6,96,4,192]{1,3,0,2:T(8,128)(2,1)}, u32[]{:S(2)}, u32[]{:S(2)}) async-start(bf16[6,96,4,192]{1,3,0,2:T(8,128)(2,1)} %copy.117), calls=%async_computation.3 | async-start | bytes 2359296 | tf_op jit(solution)/shard_map/all_to_all | solution.py:59
  318.4 23.7 %collective-permute-start.79 = (bf16[2,192,384]{2,1,0:T(8,128)(2,1)}, bf16[2,192,384]{2,1,0:T(8,128)(2,1)}, u32[]{:S(2)}, u32[]{:S(2)}) collective-permute-start(bf16[2,192,384]{2,1,0:T(8,128)(2,1)} %pad_maximum_fusion.8), channel_id=1, source_target_pairs={{3,3},{7,19},{11,7},{15,23},{19,11},{23,27},{27,15},{31,31}} | collective-permute-start | bytes 884744 | tf_op jit(solution)/shard_map/ppermute | solution.py:123
  336.2 48.3 %collective-permute-start.59 = (bf16[4,2,192,384]{3,2,1,0:T(8,128)(2,1)}, bf16[4,2,192,384]{3,2,1,0:T(8,128)(2,1)S(1)}, u32[]{:S(2)}, u32[]{:S(2)}) collective-permute-start(bf16[4,2,192,384]{3,2,1,0:T(8,128)(2,1)} %get-tuple-element.145), channel_id=1, source_target_pairs={{0,16},{16,0},{1,17},{17,1},{2,18},{18,2},{3,19},{19,3},{4,20},{20... | collective-permute-start | bytes 3538952 | tf_op jit(solution)/shard_map/ppermute | solution.py:201
  341.1 38.0 %collective-permute-start.57 = (bf16[3,192,384]{2,1,0:T(8,128)(2,1)S(1)}, bf16[3,192,384]{2,1,0:T(8,128)(2,1)S(1)}, u32[]{:S(2)}, u32[]{:S(2)}) collective-permute-start(bf16[3,192,384]{2,1,0:T(8,128)(2,1)S(1)} %get-tuple-element.199), channel_id=1, source_target_pairs={{2,0},{3,1},{0,2},{1,3},{6,4},{7,5},{4,6},{5,7},{10,8},{11,9},{8,1... | collective-permute-start | bytes 1327112 | tf_op jit(solution)/shard_map/ppermute | solution.py:70
  342.1 38.3 %collective-permute-start.54 = (bf16[256,768]{1,0:T(8,128)(2,1)S(1)}, bf16[256,768]{1,0:T(8,128)(2,1)S(1)}, u32[]{:S(2)}, u32[]{:S(2)}) collective-permute-start(bf16[256,768]{1,0:T(8,128)(2,1)S(1)} %get-tuple-element.183), channel_id=1, source_target_pairs={{0,8},{8,0},{1,9},{9,1},{2,10},{10,2},{3,11},{11,3},{4,12},{12,4},... | collective-permute-start | bytes 1179656 | tf_op jit(solution)/shard_map/ppermute | solution.py:612
  395.8 37.4 %collective-permute-start.63 = (bf16[4,192,384]{2,1,0:T(8,128)(2,1)}, bf16[4,192,384]{2,1,0:T(8,128)(2,1)}, u32[]{:S(2)}, u32[]{:S(2)}) collective-permute-start(bf16[4,192,384]{2,1,0:T(8,128)(2,1)} %get-tuple-element.150), channel_id=1, source_target_pairs={{0,16},{16,0},{1,17},{17,1},{2,18},{18,2},{3,19},{19,3},{4,20},{20... | collective-permute-start | bytes 1769480 | tf_op jit(solution)/shard_map/ppermute | solution.py:201
  402.4 23.8 %collective-permute-start.69 = (bf16[2,192,384]{2,1,0:T(8,128)(2,1)}, bf16[2,192,384]{2,1,0:T(8,128)(2,1)}, u32[]{:S(2)}, u32[]{:S(2)}) collective-permute-start(bf16[2,192,384]{2,1,0:T(8,128)(2,1)} %get-tuple-element.204), channel_id=1, source_target_pairs={{2,0},{3,1},{0,2},{1,3},{6,4},{7,5},{4,6},{5,7},{10,8},{11,9},{8,1... | collective-permute-start | bytes 884744 | tf_op jit(solution)/shard_map/ppermute | solution.py:70
  403.6 35.2 %collective-permute-start.60 = (bf16[256,768]{1,0:T(8,128)(2,1)S(1)}, bf16[256,768]{1,0:T(8,128)(2,1)}, u32[]{:S(2)}, u32[]{:S(2)}) collective-permute-start(bf16[256,768]{1,0:T(8,128)(2,1)S(1)} %get-tuple-element.147), channel_id=1, source_target_pairs={{0,4},{4,0},{1,5},{5,1},{2,6},{6,2},{3,7},{7,3},{8,12},{12,8},{9,1... | collective-permute-start | bytes 1179656 | tf_op jit(solution)/shard_map/ppermute | solution.py:607
  429.6 35.8 %all-to-all-start.4 = ((bf16[8,192,384]{2,1,0:T(8,128)(2,1)}), bf16[8,192,384]{2,1,0:T(8,128)(2,1)S(1)}, u32[]{:S(2)}, u32[]{:S(2)}) async-start(bf16[8,192,384]{2,1,0:T(8,128)(2,1)} %bitcast.233), calls=%async_computation.4 | async-start | bytes 2359296 | tf_op jit(solution)/shard_map/all_to_all | solution.py:750
  451.4 58.1 %collective-permute-start.70 = (bf16[2,192,384]{2,1,0:T(8,128)(2,1)}, bf16[2,192,384]{2,1,0:T(8,128)(2,1)}, u32[]{:S(2)}, u32[]{:S(2)}) collective-permute-start(bf16[2,192,384]{2,1,0:T(8,128)(2,1)} %slice_bitcast_fusion.9), channel_id=1, source_target_pairs={{3,3},{19,7},{7,11},{23,15},{11,19},{27,23},{15,27},{31,31}} | collective-permute-start | bytes 884744 | tf_op jit(solution)/shard_map/ppermute | solution.py:128
  489.5 40.8 %all-to-all-start.2 = ((bf16[6,4,96,192]{2,3,0,1:T(8,128)(2,1)}), bf16[6,4,96,192]{2,3,0,1:T(8,128)(2,1)}, u32[]{:S(2)}, u32[]{:S(2)}) async-start(bf16[6,4,96,192]{2,3,0,1:T(8,128)(2,1)} %copy.113), calls=%async_computation.2 | async-start | bytes 2359296 | tf_op jit(solution)/shard_map/all_to_all | solution.py:65
  508.8 31.2 %collective-permute-start.62 = (f32[128,768]{1,0:T(8,128)S(1)}, f32[128,768]{1,0:T(8,128)S(1)}, u32[]{:S(2)}, u32[]{:S(2)}) collective-permute-start(f32[128,768]{1,0:T(8,128)S(1)} %constant_dynamic-slice_fusion.6), channel_id=1, source_target_pairs={{0,0},{8,1},{4,2},{12,3},{1,4},{9,5},{5,6},{13,7},{2,8},{10,9},{6,... | collective-permute-start | bytes 1179656 | tf_op jit(solution)/shard_map/ppermute | solution.py:853
  509.6 28.8 %collective-permute-start.85 = (f32[2,3,768]{2,0,1:T(2,128)S(1)}, f32[2,3,768]{2,0,1:T(2,128)S(1)}, u32[]{:S(2)}, u32[]{:S(2)}) collective-permute-start(f32[2,3,768]{2,0,1:T(2,128)S(1)} %add.248), channel_id=1, source_target_pairs={{0,8},{8,0},{1,9},{9,1},{2,10},{10,2},{3,11},{11,3},{4,12},{12,4},... | collective-permute-start | bytes 55304 | tf_op jit(solution)/shard_map/ppermute | solution.py:251
  515.3 23.8 %collective-permute-start.71 = (bf16[2,96,384]{2,1,0:T(8,128)(2,1)S(1)}, bf16[2,96,384]{2,1,0:T(8,128)(2,1)S(1)}, u32[]{:S(2)}, u32[]{:S(2)}) collective-permute-start(bf16[2,96,384]{2,1,0:T(8,128)(2,1)S(1)} %constant_dynamic-slice_fusion.5), channel_id=1, source_target_pairs={{0,4},{4,0},{1,5},{5,1},{2,6},{6,2},{3,7},{7,3},{8,12},{12,8},{9,1... | collective-permute-start | bytes 442376 | tf_op jit(solution)/shard_map/ppermute | solution.py:132
  530.3 24.8 %all-to-all-start.6 = ((bf16[8,96,768]{2,1,0:T(8,128)(2,1)}), bf16[8,96,768]{2,1,0:T(8,128)(2,1)S(1)}, u32[]{:S(2)}, u32[]{:S(2)}) async-start(bf16[8,96,768]{2,1,0:T(8,128)(2,1)} %bitcast.232), calls=%async_computation.6 | async-start | bytes 2359296 | tf_op jit(solution)/shard_map/all_to_all | solution.py:750
  (137 other events, 1347.3 us)

commit v8 on v7

--- a/solution.py
+++ b/solution.py
@@ -139,29 +139,51 @@
     return lax.axis_index("ctx") == lax.axis_size("ctx") - 1
 
 
-def first_piece(mats):
-    attn = mats[:, 0].astype(bf16)
-    outs = out_pieces(attn)
-    return jnp.where(last_block(), outs[0], to_group(attn[0:1])[0].T), outs
-
-
-def other_pieces(mats, outs, *earlier):
-    rest = [mats[0, 1:3]] + [mats[layer] for layer in range(1, mats.shape[0])]
-    rest = to_group(after(jnp.concatenate(rest), *earlier).astype(bf16))
-    rest = jnp.swapaxes(rest, 1, 2)
-    pieces = [rest[0:2]]
-    for layer in range(1, mats.shape[0]):
-        attn = jnp.where(last_block(), outs[layer], rest[3 * layer - 1])
-        pieces.append((attn, rest[3 * layer : 3 * layer + 2]))
-    return pieces
-
-
-def momentum_pieces(mats):
-    layers, count, rows, width = mats.shape
-    columns = jnp.swapaxes(to_group(mats.reshape(layers * count, rows, width)), 1, 2)
-    columns = columns.reshape(layers, count, *columns.shape[1:])
-    attn = jnp.where(last_block(), out_pieces(mats[:, 0]), columns[:, 0])
-    return jnp.concatenate([attn[:, None], columns[:, 1:]], axis=1)
+def split_columns(mats, items):
+    rows = mats.shape[2]
+
+    def kernel(unused, mats_ref, out_ref):
+        for number, (layer, item) in enumerate(items):
+            turned = mats_ref[layer, item].T.astype(bf16)
+            for quarter in range(TP):
+                out_ref[quarter, number] = turned[quarter * COLS : (quarter + 1) * COLS]
+
+    outs = [((TP, len(items), COLS, rows), bf16)]
+    return call(kernel, outs, jnp.zeros((1,), jnp.int32), mats)[0]
+
+
+def join_columns(place, blocks, outs, items):
+    rows = blocks.shape[3]
+
+    def kernel(place_ref, blocks_ref, outs_ref, *out_refs):
+        for number, (layer, item) in enumerate(items):
+            for source in range(TP):
+                lanes = slice(source * rows, (source + 1) * rows)
+                out_refs[number][:, lanes] = blocks_ref[source, number]
+            if item == 0:
+
+                @pl.when(place_ref[0] == 3)
+                def last(number=number, layer=layer):
+                    out_refs[number][...] = outs_ref[layer]
+
+    shapes = [((COLS, TP * rows), bf16)] * len(items)
+    return call(kernel, shapes, place, blocks, outs)
+
+
+def group_exchange(blocks):
+    return lax.all_to_all(blocks, GROUP, split_axis=0, concat_axis=0, tiled=True)
+
+
+def first_piece(place, mats):
+    outs = out_pieces(mats[:, 0].astype(bf16))
+    blocks = group_exchange(split_columns(mats, [(0, 0)]))
+    return join_columns(place, blocks, outs, [(0, 0)])[0], outs
+
+
+def other_pieces(place, mats, outs, *earlier):
+    items = [(layer, item) for layer in range(mats.shape[0]) for item in range(3)][1:]
+    blocks = group_exchange(split_columns(after(mats, *earlier), items))
+    return join_columns(place, blocks, outs, items)
 
 
 def ctx_gather(piece, *earlier):
@@ -174,8 +196,12 @@
     return [lax.ppermute(block, "g", SWAP) for block in blocks]
 
 
-def group_swap_all(blocks):
-    return [lax.ppermute(jnp.stack(blocks), "g", SWAP)]
+def ctx_group_gather(pieces, *earlier):
+    piece = after(jnp.stack(pieces), *earlier)
+    near, back = [rotate(piece, "ctx", step) for step in (1, 3)]
+    far = rotate(after(piece, near, back), "ctx", 2)
+    first = lax.ppermute(jnp.stack([piece, near, back]), "g", SWAP)
+    return [piece, near, far, back], [first, lax.ppermute(after(far, first), "g", SWAP)]
 
 
 def gather_weights_wide(low):
@@ -201,20 +227,57 @@
     return mine + lax.ppermute(give, "g", SWAP).astype(f32)
 
 
-def ctx_sum(blocks, *earlier):
-    low = after(blocks, *earlier).astype(bf16)
-    total = blocks[0]
-    for step in (1, 3, 2):
-        total = total + rotate(low[step], "ctx", -step).astype(f32)
-    return total
-
-
-def grad_rows(parts):
-    layers, count, width, half = parts.shape
-    flat = jnp.swapaxes(parts.reshape(layers * count, width, half), 1, 2)
-    rows = from_group(flat).reshape(layers, count, -1, D)
-    attn = jnp.where(last_block(), out_back(parts[:, 0]), rows[:, 0])
-    return jnp.concatenate([attn[:, None], rows[:, 1:]], axis=1).astype(f32)
+def ctx_sum(blocks):
+    return ctx_sum_last(blocks, ctx_sum_first(blocks))
+
+
+def ctx_sum_first(blocks):
+    low = blocks.astype(bf16)
+    near, back = [rotate(low[step], "ctx", -step) for step in (1, 3)]
+    return blocks[0] + near.astype(f32) + back.astype(f32)
+
+
+def ctx_sum_last(blocks, total):
+    far = rotate(after(blocks[2], total).astype(bf16), "ctx", -2)
+    return total + far.astype(f32)
+
+
+def grad_rows(place, attn_parts, mlp_parts, momentum):
+    layers, count, rows, width = momentum.shape
+    half = width // 2
+    zero = jnp.zeros((1,), jnp.int32)
+
+    def split(unused, *refs):
+        *part_refs, out_ref = refs
+        for layer in range(layers):
+            for item in range(3):
+                if item:
+                    part = part_refs[layers + layer][item - 1]
+                else:
+                    part = part_refs[layer][...]
+                turned = part.T.astype(bf16)
+                for target in range(TP):
+                    out_ref[target, 3 * layer + item] = turned[target * rows : (target + 1) * rows]
+
+    blocks = call(split, [((TP, 3 * layers, rows, COLS), bf16)], zero, *attn_parts, *mlp_parts)[0]
+    blocks = group_exchange(blocks)
+    outs = out_back(jnp.stack(attn_parts).astype(bf16))
+
+    def join(place_ref, blocks_ref, outs_ref, momentum_ref, grad_ref, new_ref):
+        for layer in range(layers):
+            for item in range(3):
+                for source in range(TP):
+                    lanes = slice(source * COLS, (source + 1) * COLS)
+                    grad_ref[layer, item, :, lanes] = blocks_ref[source, 3 * layer + item].astype(f32)
+
+            @pl.when(place_ref[0] == 3)
+            def last(layer=layer):
+                grad_ref[layer, 0] = outs_ref[layer].astype(f32)
+
+        new_ref[...] = momentum_decay * momentum_ref[...] + grad_ref[...]
+
+    shape = (momentum.shape, f32)
+    return call(join, [shape, shape], place, blocks, outs, momentum)
 
 
 def scatter_wide(mats):
@@ -368,8 +431,10 @@
         if own:
             own_refs, refs = refs[:4], refs[4:]
             others, refs = refs[: len(other)], refs[len(other) :]
-            if len(other) == 1:
-                others = [others[0].at[step] for step in range(4)]
+            if len(other) == 2:
+                own_refs = [ref.at[0] for ref in own_refs]
+                first, last = others
+                others = [first.at[0, 0], first.at[1, 0], last.at[0], first.at[2, 0]]
             w_ref, qkv_ref, lse_ref, o_ref, mine_ref, give_ref = refs
             put_blocks(place_ref, own_refs, others, [w_ref])
         else:
@@ -514,8 +579,8 @@
 
     def kernel(place_ref, bias_ref, own_c_ref, other_c_ref, *refs):
         if own:
-            own_refs, other_ref, refs = refs[:4], refs[4], refs[5:]
-            others = [other_ref.at[step] for step in range(4)]
+            own_refs, (first, last), refs = refs[:4], refs[4:6], refs[6:]
+            others = [first.at[0], first.at[1], last, first.at[2]]
             w_ref, preact_ref, act_ref, mine_ref, give_ref = refs
             put_blocks(place_ref, own_refs, others, [w_ref.at[0], w_ref.at[1]])
         else:
@@ -685,9 +750,17 @@
         ]
 
 
-def slot_gram(place, slots):
-    def kernel(place_ref, slot_ref, x_ref, gram_ref):
-        put_slots(slot_ref, x_ref)
+def slot_input(place_ref, slot_ref, moment_ref, sum_ref, x_ref, turned):
+    put_slots(slot_ref, sum_ref)
+    moment = moment_ref[...].astype(f32) * (momentum_decay * momentum_decay)
+    if turned:
+        moment = moment.T
+    x_ref[...] = (sum_ref[...].astype(f32) * (1.0 + momentum_decay) + moment).astype(bf16)
+
+
+def slot_gram(place, slots, moments):
+    def kernel(place_ref, slot_ref, moment_ref, x_ref, gram_ref, sum_ref):
+        slot_input(place_ref, slot_ref, moment_ref, sum_ref, x_ref, True)
         half = D // 2
         for part in range(2):
             rows = dot_tokens(x_ref[:, part * half : (part + 1) * half], x_ref[...]).astype(bf16)
@@ -696,10 +769,17 @@
                 back = jnp.where(back < 0, back + 4, back)
                 gram_ref[back] = rows[number * COLS : (number + 1) * COLS]
 
-    return call(kernel, [((D, D), bf16), ((4, COLS, D), bf16)], place, slots)
-
-
-def slot_orthogonalize(place, x_wide, grams, square_slots):
+    return call(
+        kernel,
+        [((D, D), bf16), ((4, COLS, D), bf16)],
+        place,
+        slots,
+        moments,
+        scratch=[pltpu.VMEM((D, D), bf16)],
+    )
+
+
+def slot_orthogonalize(place, x_wide, grams, square_slots, moments):
     def kernel(
         place_ref,
         wide_ref,
@@ -708,6 +788,7 @@
         gram2_ref,
         gram3_ref,
         slot_ref,
+        moment_ref,
         out_ref,
         x_ref,
         base_ref,
@@ -716,6 +797,7 @@
         low_ref,
     ):
         core = place_ref[2]
+        plain = (core == 1) & (place_ref[0] == 3)
 
         @pl.when(core == 0)
         def wide():
@@ -724,14 +806,21 @@
                 rows = pl.ds(pl.multiple_of(block_at(place_ref, step) * COLS, COLS), COLS)
                 base_ref[rows, :] = gram_ref[...].astype(f32)
 
+        @pl.when(plain)
+        def square_plain():
+            slot_input(place_ref, slot_ref, moment_ref, low_ref, x_ref, False)
+
+        @pl.when((core == 1) & jnp.logical_not(plain))
+        def square_turned():
+            slot_input(place_ref, slot_ref, moment_ref, low_ref, x_ref, True)
+
         @pl.when(core == 1)
         def square():
-            put_slots(slot_ref, x_ref)
             base_ref[...] = dot_tokens(x_ref[...], x_ref[...])
 
         iterate(x_ref, out_ref, base_ref, work_ref, mat_ref, low_ref)
 
-        @pl.when((core == 0) | (place_ref[0] < 3))
+        @pl.when(jnp.logical_not(plain))
         def turn():
             out_ref[...] = out_ref[...].T
 
@@ -742,6 +831,7 @@
         x_wide,
         *grams,
         square_slots,
+        moments,
         scratch=[pltpu.VMEM((D, D), kind) for kind in (bf16, f32, f32, bf16, bf16)],
     )[0]
 
@@ -797,12 +887,11 @@
     relative = lax.axis_size("g") == 2
     place = jnp.stack([z_index, lax.axis_index("g"), c_index]).astype(jnp.int32)
     if relative:
-        piece, outs = first_piece(weights)
+        piece, outs = first_piece(place, weights)
         own_attn = ctx_gather(piece)
         attn_weights = (own_attn, group_swap(own_attn))
-        pieces = other_pieces(weights, outs, own_attn[1])
-        own_mlp = ctx_gather(pieces[0], *own_attn[1:])
-        mlp_weights = (own_mlp, group_swap_all(own_mlp))
+        pieces = other_pieces(place, weights, outs, own_attn[1])
+        mlp_weights = ctx_group_gather(pieces[0:2], *own_attn[1:])
     else:
         wide_weights = gather_weights_wide(weights.astype(bf16))
 
@@ -827,36 +916,45 @@
         w_attn, qkv, lse, o, mine, give = attend_stage(
             place, row_info, column_info, qkv_bias[layer], a_own, a_other, attn_weights
         )
-        if relative and following:
-            own_attn = ctx_gather(pieces[layer + 1][0], *own_mlp[1:])
-            own_mlp = ctx_gather(pieces[layer + 1][1], *own_attn[1:])
         mine, recv = group_sum(mine, give)
         middle, c_own = norm_stage(vec_rows, layer, 2, hidden, mine, recv, (layer, 6))
+        if relative and layer == 0:
+            moved_grad = lax.ppermute(after(out_grad[0], *mlp_weights[0][2:3]), axes, to_seq)
+            c_own, moved_grad = lax.optimization_barrier((c_own, moved_grad))
+            grad_hidden = x_join(moved_grad)
         c_other = core_swap(c_own)
         w_mlp, preact, act, mine, give = feed_stage(
             place, up_bias[layer], c_own, c_other, mlp_weights
         )
         if relative and following:
-            attn_weights = (own_attn, group_swap_all(own_attn))
-            mlp_weights = (own_mlp, group_swap_all(own_mlp))
-        mine, recv = group_sum(mine, give)
+            base = 3 * layer + 2
+            attn_weights = ctx_group_gather(pieces[base : base + 1], *mlp_weights[0][2:3])
+            mine, grad_hidden, ready = lax.optimization_barrier(
+                (mine, grad_hidden, attn_weights[0][1])
+            )
+            attn_weights[0][1] = ready
+            mlp_weights = ctx_group_gather(pieces[base + 1 : base + 3], *attn_weights[0][2:3])
+        if following:
+            mine, recv = group_sum(mine, give)
         stored.append(
             (hidden, middle, a_own, a_other, qkv, lse, o, c_own, c_other, preact, act, w_attn, w_mlp)
         )
         if following:
             hidden, a_own = norm_stage(vec_rows, layer + 1, 0, middle, mine, recv, (layer, 7))
-        else:
-            hidden = middle + (mine + recv.astype(f32) + vec_rows[layer, 7:8])
 
     def send_back(rows):
         block = lax.dynamic_slice_in_dim(rows, x_index * tokens_dev, tokens_dev, axis=0)
         return lax.ppermute(block, axes, from_seq)
 
-    hidden_out = send_back(hidden)
-    if relative:
-        scaled = after(mat_momentum, stored[0][6]) * (momentum_decay * momentum_decay)
-        moments = momentum_pieces(scaled.astype(bf16))
-    grad_hidden = x_join(lax.ppermute(after(out_grad[0], own_mlp[2] if relative else stored[-1][6]), axes, to_seq))
+    last_sum = (mine, give)
+
+    def last_hidden(*earlier):
+        mine, recv = group_sum(last_sum[0], after(last_sum[1], *earlier))
+        return stored[-1][1] + (mine + recv.astype(f32) + vec_rows[LAYERS - 1, 7:8])
+
+    if not relative:
+        grad_hidden = x_join(lax.ppermute(out_grad[0], axes, to_seq))
+        hidden_out = send_back(last_hidden())
     gy_own = grad_hidden.astype(bf16)
     attn_half = mlp_half = None
 
@@ -868,23 +966,33 @@
             layer
         ]
         if relative and attn_half is not None:
-            gy_own, attn_half, mlp_half = lax.optimization_barrier((gy_own, attn_half, mlp_half))
-            part = ctx_sum(jnp.concatenate([attn_half[:, None], mlp_half], axis=1))
+            gy_own, mlp_first = lax.optimization_barrier((gy_own, mlp_first))
+            mlp_part = ctx_sum_last(mlp_half, mlp_first)
+            hidden = last_hidden(gy_own)
         gy_other = core_swap(gy_own)
         mine, give, up_sums, *mlp_grads = feed_back_stage(
             place, gy_own, gy_other, c_own, c_other, preact, act, w_mlp, relative
         )
         if relative:
+            if attn_half is not None:
+                mine, mlp_part, hidden, attn_half = lax.optimization_barrier(
+                    (mine, mlp_part, hidden, attn_half)
+                )
+                attn_part = ctx_sum(attn_half)
             mlp_half = half_sum(*mlp_grads)
         mine, recv = group_sum(mine, give)
         grad_middle, gb_own, mid_sums = norm_back_stage(
             vec_rows, layer, 2, grad_hidden, mine, recv, middle
         )
-        if relative and attn_half is not None:
-            gb_own, part = lax.optimization_barrier((gb_own, part))
-            parts[layer + 1] = part
-        if layer == LAYERS - 1:
-            gb_own, hidden_out = lax.optimization_barrier((gb_own, hidden_out))
+        if relative and layer == LAYERS - 1:
+            moment_low = mat_momentum.astype(bf16)
+            table = [(1, 1), (1, 0), (1, 2), (0, 0), (0, 1), (1, 0), (0, 2), (0, 0)]
+            moment_slots = slot_exchange(
+                after(jnp.stack([moment_low[slot] for slot in table]), gb_own)
+            ).reshape(D, D)
+        elif relative:
+            gb_own, attn_part = lax.optimization_barrier((gb_own, attn_part))
+            parts[layer + 1] = (attn_part, mlp_part)
         gb_other = core_swap(gb_own)
         mine, give, qkv_sums, *attn_grads = attend_back_stage(
             place,
@@ -902,7 +1010,10 @@
         )
         if relative:
             mine, mlp_half = lax.optimization_barrier((mine, mlp_half))
-            if layer == 0:
+            if layer == LAYERS - 1:
+                mine, moment_slots = lax.optimization_barrier((mine, moment_slots))
+                mlp_first = ctx_sum_first(mlp_half)
+            else:
                 mlp_part = ctx_sum(mlp_half)
             attn_half = half_sum(*attn_grads)
         else:
@@ -914,12 +1025,19 @@
             mat_list[layer] = scatter_wide(
                 jnp.concatenate([attn_grad[:, None], mlp_grads[0]], axis=1)
             )
+        if relative and layer == 0:
+            wide_low = jnp.concatenate([parts[1][1], mlp_part]).astype(bf16)
+            x_wide, gram_blocks = slot_gram(
+                place, slot_exchange(jnp.repeat(wide_low, 2, axis=0)), moment_slots
+            )
+            mine = after(mine, gram_blocks)
         mine, recv = group_sum(mine, give)
         grad_hidden, gy_own, in_sums = norm_back_stage(
             vec_rows, layer, 0, grad_middle, mine, recv, h_in
         )
         sum_list[layer] = (in_sums, mid_sums, up_sums, qkv_sums)
-    input_grad = send_back(grad_hidden)
+    if not relative:
+        input_grad = send_back(grad_hidden)
 
     once = jnp.where(x_index == 0, 1.0, 0.0).astype(f32)
     in_sums, mid_sums, up_sums, qkv_sums = [jnp.stack(sums) for sums in zip(*sum_list)]
@@ -944,30 +1062,26 @@
         sum_vectors(vec_terms), dp_index * vectors.shape[2], vectors.shape[2], axis=2
     )
     if relative:
-        wide_low = [parts[layer][1:] * (1.0 + momentum_decay) for layer in range(1, LAYERS)]
-        wide_low = jnp.concatenate(wide_low + [mlp_part * (1.0 + momentum_decay)])
-        moment_wide = jnp.concatenate([moments[layer, 1:] for layer in (*range(1, LAYERS), 0)])
-        wide_low = (wide_low + moment_wide.astype(f32)).astype(bf16)
-        received = slot_exchange(jnp.repeat(wide_low, 2, axis=0))
-        x_wide, gram_blocks = slot_gram(place, received)
         attn_part = ctx_sum(attn_half)
-        square_low = [parts[layer][0] for layer in range(1, LAYERS)] + [attn_part]
-        square_low = jnp.stack(square_low) * (1.0 + momentum_decay)
-        moment_square = jnp.stack([moments[layer, 0] for layer in (*range(1, LAYERS), 0)])
-        square_low = (square_low + moment_square.astype(f32)).astype(bf16)
+        square_low = jnp.stack([parts[1][0], attn_part]).astype(bf16)
         square_slots = slot_exchange(jnp.tile(jnp.repeat(square_low, 2, axis=0), (2, 1, 1)))
         total = gram_blocks[0].astype(f32)
         for step in (1, 3, 2):
             total = total + core_shift(gram_blocks[step], -step).astype(f32)
         low = total.astype(bf16)
         near, back, far = [core_shift(low, step) for step in (1, 3, 2)]
-        ortho_mine = slot_orthogonalize(place, x_wide, (low, near, far, back), square_slots)
+        ortho_mine = slot_orthogonalize(
+            place, x_wide, (low, near, far, back), square_slots, moment_slots
+        )
         returned = slot_exchange(ortho_mine.reshape(dp_size, dp_rows, D))
-        ortho = jnp.stack([returned[3], returned[4], returned[6], returned[1], returned[0], returned[2]])
+        ends = jnp.stack([hidden, grad_hidden])
+        ends = lax.dynamic_slice_in_dim(ends, x_index * tokens_dev, tokens_dev, axis=1)
+        hidden_out, input_grad = lax.ppermute(after(ends, ortho_mine), axes, from_seq)
+        ortho = jnp.stack([returned[slot] for slot in (3, 4, 6, 1, 0, 2)])
         ortho = ortho.reshape(weights.shape).astype(f32)
-        first = jnp.concatenate([attn_part[None], mlp_part])
-        grad_mats = grad_rows(jnp.stack([first, *parts[1:]]).astype(bf16))
-        moment_new = momentum_decay * mat_momentum + grad_mats
+        grad_mats, moment_new = grad_rows(
+            place, [attn_part, parts[1][0]], [mlp_part, parts[1][1]], mat_momentum
+        )
     else:
         cols_dev = weights.shape[3]
         grad_list, moment_list, low_list = [], [], []

time: 569 us -> 530 us (0.931)
  local copies, waits for them, and re-layouts: 63.5 us -> 33 us
  waiting for transfers between devices: 201 us -> 181 us
  starting transfers between devices: 167 us -> 180 us
  Pallas kernels: 84.4 us -> 95.2 us
  other arithmetic: 40.6 us -> 29.9 us
    ppermute x8, waiting for transfers between devices: 44.8 us -> 19 us  [group_sum(): return (mine, lax.ppermute(mine.astype(bf16), 'jx', SWAP))]
    ppermute x1, waiting for transfers between devices: 0.01 us -> 19 us  [sum_vectors(): return total + lax.ppermute(total, 'jx', SWAP)]
    ppermute x27 -> x30, starting transfers between devices: 43.9 us -> 60 us  [rotate(): lax.ppermute(block, axis, [((i + step) % size, i) for i in range(size)])]
    ppermute x16, starting transfers between devices: 2.72 us -> 16.7 us  [core_swap(): return lax.ppermute(block, 'jc', SWAP)]
    pallas_call x18 -> x24, Pallas kernels: 84.4 us -> 95.2 us  [call(): pl.pallas_call(kernel, out_shape=[jax.ShapeDtypeStruct(shape, kind) for s...]
    all_to_all x4 -> x0, local copies, waits for them, and re-layouts: 8.8 us -> none  [the longest x3 6.26 us: to_group(): lax.all_to_all(split, GROUP, split_axis=2, concat_axis=1, tiled=True)]
    squeeze x9 -> x8, local copies, waits for them, and re-layouts: 11.6 us -> 2.89 us  [the longest x4 1.88 us: ctx_sum_last(): far = rotate(after(blocks[2], total).astype(bf16), 'ctx', -2)]
    reshape x4 -> x0, local copies, waits for them, and re-layouts: 7.23 us -> none  [the longest x2 4.25 us: from_group(): split = mats.reshape(count, TP, rows // TP, width)]
  transfers between devices with their start and end apart: 93 -> 96, of which waited for: 33 -> 39; matrix products, arithmetic and copies ran while one was open for 15% -> 9% of each run, Pallas kernels for 13% -> 15%
where the time goes in v8:
time: 530 us; the launch traced here: 521 us
  waiting for transfers between devices  181 us (34%)
  starting transfers between devices  180 us (34%)
  Pallas kernels  95.2 us (18%)
  local copies, waits for them, and re-layouts  33 us (6%)
  other arithmetic  29.9 us (6%)
    ppermute x30, waiting for transfers between devices, rotate(): lax.ppermute(block, axis, [((i + step) % size, i) for i in range(size)])  102 us
    pallas_call x24, Pallas kernels, call(): pl.pallas_call(kernel, out_shape=[jax.ShapeDtypeStruct(shape, kind) for s...  95.2 us
    ppermute x30, starting transfers between devices, rotate(): lax.ppermute(block, axis, [((i + step) % size, i) for i in range(size)])  60 us
    ppermute x6, starting transfers between devices, core_shift(): lax.ppermute(block, ('jc', 'ctx'), [((i + step) % size, i) for i in range...  20 us
    ppermute x8, waiting for transfers between devices, group_sum(): return (mine, lax.ppermute(mine.astype(bf16), 'jx', SWAP))  19 us
    ppermute x1, waiting for transfers between devices, sum_vectors(): return total + lax.ppermute(total, 'jx', SWAP)  19 us
    unnamed x144, local copies, waits for them, and re-layouts  17.8 us
    ppermute x16, starting transfers between devices, core_swap(): return lax.ppermute(block, 'jc', SWAP)  16.7 us
  transfers between devices with their start and end apart: 96, of which 39 were waited for; matrix products, arithmetic and copies ran while one was open for 9% of the time, Pallas kernels for 15%

profile of v8, /device:TPU:0, one launch (start us, length us, event | category | flops | bytes accessed | tf_op | source)
XLA Modules:
  0.0 521.0 jit_solution(7320769066574584906)
XLA Ops:
  27.2 8.9 %collective-permute-start.7 = (f32[128,768]{1,0:T(8,128)S(1)}, f32[128,768]{1,0:T(8,128)}, u32[]{:S(2)}, u32[]{:S(2)}) collective-permute-start(f32[128,768]{1,0:T(8,128)S(1)} %slice.267), channel_id=1, source_target_pairs={{0,8},{8,0},{1,9},{9,1},{2,10},{10,2},{3,11},{11,3},{4,12},{12,4},... | collective-permute-start | bytes 1179656 | tf_op jit(solution)/shard_map/ppermute | solution.py:74
  47.2 5.7 %all-to-all-start.1 = ((bf16[4,5,192,96]{3,2,1,0:T(8,128)(2,1)}), bf16[4,5,192,96]{3,2,1,0:T(8,128)(2,1)S(1)}, u32[]{:S(2)}, u32[]{:S(2)}) async-start(bf16[4,5,192,96]{3,2,1,0:T(8,128)(2,1)} %shard_map.157), calls=%async_computation.1 | async-start | bytes 1966080 | tf_op jit(solution)/shard_map/all_to_all | solution.py:174
  75.6 6.2 %shard_map.155 = (bf16[768,768]{1,0:T(8,128)(2,1)}, bf16[512,576]{1,0:T(8,128)(2,1)}, f32[512,128]{1,0:T(8,128)S(1)}, bf16[512,192]{1,0:T(8,128)(2,1)S(1)}, f32[...) custom-call(s32[3]{0:T(128)S(1)} %pad_add_fusion.place_ref, f32[8,512]{1,0:T(8,128)S(1)} %pad.13.row_ref, ...), custom_call_target="tpu_custom_call" | custom-call | tf_op jit(solution)/shard_map/pallas_call | solution.py:318
  90.2 12.6 %collective-permute-done.22.refs_2_ = bf16[2,192,384]{2,1,0:T(8,128)(2,1)S(1)} collective-permute-done((bf16[2,192,384]{2,1,0:T(8,128)(2,1)S(1)}, bf16[2,192,384]{2,1,0:T(8,128)(2,1)S(1)}, u32[]{:S(2)}, u32[]{:S(2)}) %collective-permute-start.22) | collective-permute-done | bytes 294944 | tf_op jit(solution)/shard_map/ppermute | solution.py:70
  106.8 15.1 %collective-permute-start.24 = (bf16[256,768]{1,0:T(8,128)(2,1)S(1)}, bf16[256,768]{1,0:T(8,128)(2,1)S(1)}, u32[]{:S(2)}, u32[]{:S(2)}) collective-permute-start(bf16[256,768]{1,0:T(8,128)(2,1)S(1)} %get-tuple-element.123.own_c_ref), channel_id=1, source_target_pairs={{0,4},{4,0},{1,5},{5,1},{2,6},{6,2},{3,7},{7,3},{8,12},{12,8},{9,1... | collective-permute-start | bytes 1179656 | tf_op jit(solution)/shard_map/ppermute | solution.py:672
  141.3 9.0 %collective-permute-done.31.refs_1_ = bf16[256,768]{1,0:T(8,128)(2,1)S(1)} collective-permute-done((bf16[256,768]{1,0:T(8,128)(2,1)S(1)}, bf16[256,768]{1,0:T(8,128)(2,1)S(1)}, u32[]{:S(2)}, u32[]{:S(2)}) %collective-permute-start.31) | collective-permute-done | bytes 393248 | tf_op jit(solution)/shard_map/ppermute | solution.py:677
  155.3 7.9 %collective-permute-done.34.refs_2_ = bf16[1,192,384]{2,1,0:T(8,128)(2,1)S(1)} collective-permute-done((bf16[1,192,384]{2,1,0:T(8,128)(2,1)S(1)}, bf16[1,192,384]{2,1,0:T(8,128)(2,1)S(1)}, u32[]{:S(2)}, u32[]{:S(2)}) %collective-permute-start.34) | collective-permute-done | bytes 147488 | tf_op jit(solution)/shard_map/ppermute | solution.py:70
  167.1 5.0 collective-permute-done.36.refs_5_
  172.9 6.1 %shard_map.161 = (bf16[768,768]{1,0:T(8,128)(2,1)}, bf16[512,576]{1,0:T(8,128)(2,1)}, f32[512,128]{1,0:T(8,128)S(1)}, bf16[512,192]{1,0:T(8,128)(2,1)S(1)}, f32[...) custom-call(s32[3]{0:T(128)S(1)} %pad_add_fusion.place_ref, f32[8,512]{1,0:T(8,128)S(1)} %pad.13.row_ref, ...), custom_call_target="tpu_custom_call" | custom-call | tf_op jit(solution)/shard_map/pallas_call | solution.py:318
  183.5 12.9 %collective-permute-done.42.refs_2_ = bf16[2,192,384]{2,1,0:T(8,128)(2,1)S(1)} collective-permute-done((bf16[2,192,384]{2,1,0:T(8,128)(2,1)S(1)}, bf16[2,192,384]{2,1,0:T(8,128)(2,1)S(1)}, u32[]{:S(2)}, u32[]{:S(2)}) %collective-permute-start.42) | collective-permute-done | bytes 294944 | tf_op jit(solution)/shard_map/ppermute | solution.py:70
  216.9 7.5 %shard_map.164 = (f32[256,768]{1,0:T(8,128)}, bf16[256,768]{1,0:T(8,128)(2,1)S(1)}, f32[8,768]{1,0:T(8,128)S(1)}, f32[4,2,192,384]{3,2,1,0:T(8,128)}, bf16[4,2,192,384]{3,2,1,0:T(8,128)(2,1)}) custom-call(s32[3]{0:T(128)S(1)} %pad_add_fusion.place_ref, bf16[256,768]{1,0:T(8,128)(2,1)S(1)} %convert_element_type.195.own_gy_ref, ...), custom_call_target="tpu_custom_call" | custom-call | tf_op jit(solution)/shard_map/pallas_call | solution.py:318
  230.0 9.6 %collective-permute-done.46.recv_ref = bf16[256,768]{1,0:T(8,128)(2,1)S(1)} collective-permute-done((bf16[256,768]{1,0:T(8,128)(2,1)S(1)}, bf16[256,768]{1,0:T(8,128)(2,1)S(1)}, u32[]{:S(2)}, u32[]{:S(2)}) %collective-permute-start.46) | collective-permute-done | bytes 393248 | tf_op jit(solution)/shard_map/ppermute | solution.py:677
  248.6 8.5 %shard_map.166 = (f32[256,768]{1,0:T(8,128)}, bf16[256,768]{1,0:T(8,128)(2,1)S(1)}, f32[8,576]{1,0:T(8,128)S(1)}, f32[4,192,384]{2,1,0:T(8,128)}, bf16[4,192,384]{2,1,0:T(8,128)(2,1)}) custom-call(s32[3]{0:T(128)S(1)} %pad_add_fusion.place_ref, f32[8,512]{1,0:T(8,128)S(1)} %pad.13.row_ref, f32[512,128]{1,0:T(8,128)S(1)} %pad.14.column_ref, ...), custom_call_target="tpu_custom_call" | custom-call | tf_op jit(solution)/shard_map/pallas_call | solution.py:318
  290.0 7.9 %collective-permute-done.57 = bf16[4,192,384]{2,1,0:T(8,128)(2,1)S(1)} collective-permute-done((bf16[4,192,384]{2,1,0:T(8,128)(2,1)S(1)}, bf16[4,192,384]{2,1,0:T(8,128)(2,1)S(1)}, u32[]{:S(2)}, u32[]{:S(2)}) %collective-permute-start.57) | collective-permute-done | bytes 589856 | tf_op jit(solution)/shard_map/ppermute | solution.py:227
  302.4 7.5 %shard_map.168 = (f32[256,768]{1,0:T(8,128)}, bf16[256,768]{1,0:T(8,128)(2,1)S(1)}, f32[8,768]{1,0:T(8,128)S(1)}, f32[4,2,192,384]{3,2,1,0:T(8,128)}, bf16[4,2,192,384]{3,2,1,0:T(8,128)(2,1)}) custom-call(s32[3]{0:T(128)S(1)} %pad_add_fusion.place_ref, bf16[256,768]{1,0:T(8,128)(2,1)S(1)} %get-tuple-element.167.own_gy_ref, ...), custom_call_target="tpu_custom_call" | custom-call | tf_op jit(solution)/shard_map/pallas_call | solution.py:318
  323.6 7.6 %collective-permute-done.62 = bf16[192,384]{1,0:T(8,128)(2,1)S(1)} collective-permute-done((bf16[192,384]{1,0:T(8,128)(2,1)S(1)}, bf16[192,384]{1,0:T(8,128)(2,1)S(1)}, u32[]{:S(2)}, u32[]{:S(2)}) %collective-permute-start.62) | collective-permute-done | bytes 147488 | tf_op jit(solution)/shard_map/ppermute | solution.py:70
  338.6 8.4 %shard_map.170 = (f32[256,768]{1,0:T(8,128)}, bf16[256,768]{1,0:T(8,128)(2,1)S(1)}, f32[8,576]{1,0:T(8,128)S(1)}, f32[4,192,384]{2,1,0:T(8,128)}, bf16[4,192,384]{2,1,0:T(8,128)(2,1)}) custom-call(s32[3]{0:T(128)S(1)} %pad_add_fusion.place_ref, f32[8,512]{1,0:T(8,128)S(1)} %pad.13.row_ref, f32[512,128]{1,0:T(8,128)S(1)} %pad.14.column_ref, ...), custom_call_target="tpu_custom_call" | custom-call | tf_op jit(solution)/shard_map/pallas_call | solution.py:318
  351.9 7.2 %collective-permute-done.65 = bf16[2,192,384]{2,1,0:T(8,128)(2,1)S(1)} collective-permute-done((bf16[2,192,384]{2,1,0:T(8,128)(2,1)S(1)}, bf16[2,192,384]{2,1,0:T(8,128)(2,1)S(1)}, u32[]{:S(2)}, u32[]{:S(2)}) %collective-permute-start.65) | collective-permute-done | bytes 294944 | tf_op jit(solution)/shard_map/ppermute | solution.py:70
  365.3 12.3 %collective-permute-done.67 = bf16[2,192,384]{2,1,0:T(8,128)(2,1)} collective-permute-done((bf16[2,192,384]{2,1,0:T(8,128)(2,1)}, bf16[2,192,384]{2,1,0:T(8,128)(2,1)}, u32[]{:S(2)}, u32[]{:S(2)}) %collective-permute-start.67) | collective-permute-done | bytes 294944 | tf_op jit(solution)/shard_map/ppermute | solution.py:70
  397.7 6.8 %collective-permute-done.79 = bf16[192,384]{1,0:T(8,128)(2,1)S(1)} collective-permute-done((bf16[192,384]{1,0:T(8,128)(2,1)S(1)}, bf16[192,384]{1,0:T(8,128)(2,1)S(1)}, u32[]{:S(2)}, u32[]{:S(2)}) %collective-permute-start.79) | collective-permute-done | bytes 147488 | tf_op jit(solution)/shard_map/ppermute | solution.py:70
  426.2 6.8 %collective-permute-start.71 = (bf16[192,768]{1,0:T(8,128)(2,1)S(1)}, bf16[192,768]{1,0:T(8,128)(2,1)S(1)}, u32[]{:S(2)}, u32[]{:S(2)}) collective-permute-start(bf16[192,768]{1,0:T(8,128)(2,1)S(1)} %get-tuple-element.247), channel_id=1, source_target_pairs={{1,0},{2,1},{3,2},{0,3},{9,8},{10,9},{11,10},{8,11},{17,16},{18,17... | collective-permute-start | bytes 884744 | tf_op jit(solution)/shard_map/ppermute | solution.py:845
  466.2 11.9 %shard_map.173 = bf16[768,768]{1,0:T(8,128)(2,1)} custom-call(s32[3]{0:T(128)S(1)} %pad_add_fusion.place_ref, bf16[768,768]{1,0:T(8,128)(2,1)} %copy-done.17, bf16[192,768]{1,0:T(8,128)(2,1)S(1)} %fusion.5.gram0_ref, bf16[192,768]{1,0:T(8,128)(2,1)S(1)} %collective-permute-done.73.gram1_ref, bf16[192,768]{1,0:T(8,128)(2,1)S(1)} %collective-permute-done.74.gram2_ref, ...), custom_call_target="tpu_custom_call" | custom-call | tf_op jit(solution)/shard_map/pallas_call | solution.py:318
  478.1 7.4 %collective-permute-start.80 = (f32[2,128,768]{2,1,0:T(8,128)}, f32[2,128,768]{2,1,0:T(8,128)}, u32[]{:S(2)}, u32[]{:S(2)}) collective-permute-start(f32[2,128,768]{2,1,0:T(8,128)} %fusion.2), channel_id=1, source_target_pairs={{0,0},{8,1},{4,2},{12,3},{1,4},{9,5},{5,6},{13,7},{2,8},{10,9},{6,... | collective-permute-start | bytes 2359304 | tf_op jit(solution)/shard_map/ppermute | solution.py:1079
  496.0 19.0 %collective-permute-done.88 = f32[2,3,768]{2,0,1:T(2,128)S(1)} collective-permute-done((f32[2,3,768]{2,0,1:T(2,128)S(1)}, f32[2,3,768]{2,0,1:T(2,128)S(1)}, u32[]{:S(2)}, u32[]{:S(2)}) %collective-permute-start.88) | collective-permute-done | bytes 18464 | tf_op jit(solution)/shard_map/ppermute | solution.py:314
  (457 shorter events, 301.0 us)
Async XLA Ops:
  10.9 25.2 %all-to-all-start = ((bf16[4,1,192,96]{3,2,1,0:T(8,128)(2,1)}), bf16[4,1,192,96]{3,2,1,0:T(8,128)(2,1)S(1)}, u32[]{:S(2)}, u32[]{:S(2)}) async-start(bf16[4,1,192,96]{3,2,1,0:T(8,128)(2,1)} %shard_map.153), calls=%async_computation | async-start | bytes 393216 | tf_op jit(solution)/shard_map/all_to_all | solution.py:174
  27.2 32.9 %collective-permute-start.7 = (f32[128,768]{1,0:T(8,128)S(1)}, f32[128,768]{1,0:T(8,128)}, u32[]{:S(2)}, u32[]{:S(2)}) collective-permute-start(f32[128,768]{1,0:T(8,128)S(1)} %slice.267), channel_id=1, source_target_pairs={{0,8},{8,0},{1,9},{9,1},{2,10},{10,2},{3,11},{11,3},{4,12},{12,4},... | collective-permute-start | bytes 1179656 | tf_op jit(solution)/shard_map/ppermute | solution.py:74
  47.2 21.6 %all-to-all-start.1 = ((bf16[4,5,192,96]{3,2,1,0:T(8,128)(2,1)}), bf16[4,5,192,96]{3,2,1,0:T(8,128)(2,1)S(1)}, u32[]{:S(2)}, u32[]{:S(2)}) async-start(bf16[4,5,192,96]{3,2,1,0:T(8,128)(2,1)} %shard_map.157), calls=%async_computation.1 | async-start | bytes 1966080 | tf_op jit(solution)/shard_map/all_to_all | solution.py:174
  85.7 36.1 %collective-permute-start.25 = (bf16[3,2,192,384]{3,2,1,0:T(8,128)(2,1)S(1)}, bf16[3,2,192,384]{3,2,1,0:T(8,128)(2,1)}, u32[]{:S(2)}, u32[]{:S(2)}) collective-permute-start(bf16[3,2,192,384]{3,2,1,0:T(8,128)(2,1)S(1)} %pad_maximum_fusion), channel_id=1, source_target_pairs={{0,16},{16,0},{1,17},{17,1},{2,18},{18,2},{3,19},{19,3},{4,20},{20... | collective-permute-start | bytes 2654216 | tf_op jit(solution)/shard_map/ppermute | solution.py:203
  106.8 21.4 %collective-permute-start.24 = (bf16[256,768]{1,0:T(8,128)(2,1)S(1)}, bf16[256,768]{1,0:T(8,128)(2,1)S(1)}, u32[]{:S(2)}, u32[]{:S(2)}) collective-permute-start(bf16[256,768]{1,0:T(8,128)(2,1)S(1)} %get-tuple-element.123.own_c_ref), channel_id=1, source_target_pairs={{0,4},{4,0},{1,5},{5,1},{2,6},{6,2},{3,7},{7,3},{8,12},{12,8},{9,1... | collective-permute-start | bytes 1179656 | tf_op jit(solution)/shard_map/ppermute | solution.py:672
  140.5 26.0 %collective-permute-start.35 = (bf16[3,1,192,384]{3,2,1,0:T(8,128)(2,1)S(1)}, bf16[3,1,192,384]{3,2,1,0:T(8,128)(2,1)S(1)}, u32[]{:S(2)}, u32[]{:S(2)}) collective-permute-start(bf16[3,1,192,384]{3,2,1,0:T(8,128)(2,1)S(1)} %pad_maximum_fusion.5), channel_id=1, source_target_pairs={{0,16},{16,0},{1,17},{17,1},{2,18},{18,2},{3,19},{19,3},{4,20},{20... | collective-permute-start | bytes 1327112 | tf_op jit(solution)/shard_map/ppermute | solution.py:203
  183.4 31.5 %collective-permute-start.29 = (bf16[256,768]{1,0:T(8,128)(2,1)S(1)}, bf16[256,768]{1,0:T(8,128)(2,1)S(1)}, u32[]{:S(2)}, u32[]{:S(2)}) collective-permute-start(bf16[256,768]{1,0:T(8,128)(2,1)S(1)} %convert_element_type.195.own_gy_ref), channel_id=1, source_target_pairs={{0,4},{4,0},{1,5},{5,1},{2,6},{6,2},{3,7},{7,3},{8,12},{12,8},{9,1... | collective-permute-start | bytes 1179656 | tf_op jit(solution)/shard_map/ppermute | solution.py:672
  225.1 32.4 %collective-permute-start.48 = (bf16[4,2,192,384]{3,2,1,0:T(8,128)(2,1)}, bf16[4,2,192,384]{3,2,1,0:T(8,128)(2,1)}, u32[]{:S(2)}, u32[]{:S(2)}) collective-permute-start(bf16[4,2,192,384]{3,2,1,0:T(8,128)(2,1)} %get-tuple-element.160), channel_id=1, source_target_pairs={{0,16},{16,0},{1,17},{17,1},{2,18},{18,2},{3,19},{19,3},{4,20},{20... | collective-permute-start | bytes 3538952 | tf_op jit(solution)/shard_map/ppermute | solution.py:227
  242.8 23.5 %all-to-all-start.2 = ((bf16[8,96,768]{2,1,0:T(8,128)(2,1)}), bf16[8,96,768]{2,1,0:T(8,128)(2,1)S(1)}, u32[]{:S(2)}, u32[]{:S(2)}) async-start(bf16[8,96,768]{2,1,0:T(8,128)(2,1)} %fusion.19), calls=%async_computation.2 | async-start | bytes 2359296 | tf_op jit(solution)/shard_map/all_to_all | solution.py:840
  288.4 22.0 %collective-permute-start.56 = (bf16[256,768]{1,0:T(8,128)(2,1)S(1)}, bf16[256,768]{1,0:T(8,128)(2,1)S(1)}, u32[]{:S(2)}, u32[]{:S(2)}) collective-permute-start(bf16[256,768]{1,0:T(8,128)(2,1)S(1)} %fusion.8), channel_id=1, source_target_pairs={{0,8},{8,0},{1,9},{9,1},{2,10},{10,2},{3,11},{11,3},{4,12},{12,4},... | collective-permute-start | bytes 1179656 | tf_op jit(solution)/shard_map/ppermute | solution.py:677
  309.9 27.6 %collective-permute-start.64 = (bf16[4,2,192,384]{3,2,1,0:T(8,128)(2,1)}, bf16[4,2,192,384]{3,2,1,0:T(8,128)(2,1)S(1)}, u32[]{:S(2)}, u32[]{:S(2)}) collective-permute-start(bf16[4,2,192,384]{3,2,1,0:T(8,128)(2,1)} %get-tuple-element.194), channel_id=1, source_target_pairs={{0,16},{16,0},{1,17},{17,1},{2,18},{18,2},{3,19},{19,3},{4,20},{20... | collective-permute-start | bytes 3538952 | tf_op jit(solution)/shard_map/ppermute | solution.py:227
  365.3 46.0 %collective-permute-start.68 = (bf16[256,768]{1,0:T(8,128)(2,1)S(1)}, bf16[256,768]{1,0:T(8,128)(2,1)}, u32[]{:S(2)}, u32[]{:S(2)}) collective-permute-start(bf16[256,768]{1,0:T(8,128)(2,1)S(1)} %get-tuple-element.202), channel_id=1, source_target_pairs={{0,4},{4,0},{1,5},{5,1},{2,6},{6,2},{3,7},{7,3},{8,12},{12,8},{9,1... | collective-permute-start | bytes 1179656 | tf_op jit(solution)/shard_map/ppermute | solution.py:672
  379.9 26.9 %all-to-all-start.3 = ((bf16[8,192,384]{2,1,0:T(8,128)(2,1)}), bf16[8,192,384]{2,1,0:T(8,128)(2,1)}, u32[]{:S(2)}, u32[]{:S(2)}) async-start(bf16[8,192,384]{2,1,0:T(8,128)(2,1)} %bitcast.191), calls=%async_computation.3 | async-start | bytes 2359296 | tf_op jit(solution)/shard_map/all_to_all | solution.py:840
  405.4 30.2 %collective-permute-start.81 = (bf16[2,192,384]{2,1,0:T(8,128)(2,1)}, bf16[2,192,384]{2,1,0:T(8,128)(2,1)}, u32[]{:S(2)}, u32[]{:S(2)}) collective-permute-start(bf16[2,192,384]{2,1,0:T(8,128)(2,1)} %get-tuple-element.266), channel_id=1, source_target_pairs={{3,3},{19,7},{7,11},{23,15},{11,19},{27,23},{15,27},{31,31}} | collective-permute-start | bytes 884744 | tf_op jit(solution)/shard_map/ppermute | solution.py:128
  414.0 23.2 %collective-permute-start.69 = (bf16[256,768]{1,0:T(8,128)(2,1)}, bf16[256,768]{1,0:T(8,128)(2,1)S(1)}, u32[]{:S(2)}, u32[]{:S(2)}) collective-permute-start(bf16[256,768]{1,0:T(8,128)(2,1)} %get-tuple-element.229), channel_id=1, source_target_pairs={{0,8},{8,0},{1,9},{9,1},{2,10},{10,2},{3,11},{11,3},{4,12},{12,4},... | collective-permute-start | bytes 1179656 | tf_op jit(solution)/shard_map/ppermute | solution.py:677
  418.2 36.2 %all-to-all-start.4 = ((bf16[8,192,384]{2,1,0:T(8,128)(2,1)}), bf16[8,192,384]{2,1,0:T(8,128)(2,1)}, u32[]{:S(2)}, u32[]{:S(2)}) async-start(bf16[8,192,384]{2,1,0:T(8,128)(2,1)} %bitcast.190), calls=%async_computation.4 | async-start | bytes 2359296 | tf_op jit(solution)/shard_map/all_to_all | solution.py:840
  454.4 31.0 %all-to-all-start.5 = ((bf16[4,6,96,192]{3,2,1,0:T(8,128)(2,1)}), bf16[4,6,96,192]{3,2,1,0:T(8,128)(2,1)S(1)}, u32[]{:S(2)}, u32[]{:S(2)}) async-start(bf16[4,6,96,192]{3,2,1,0:T(8,128)(2,1)} %shard_map.174), calls=%async_computation.5 | async-start | bytes 2359296 | tf_op jit(solution)/shard_map/all_to_all | solution.py:174
  458.1 31.0 %collective-permute-start.84 = (f32[2,3,768]{2,0,1:T(2,128)S(1)}, f32[2,3,768]{2,0,1:T(2,128)S(1)}, u32[]{:S(2)}, u32[]{:S(2)}) collective-permute-start(f32[2,3,768]{2,0,1:T(2,128)S(1)} %get-tuple-element.268), channel_id=1, source_target_pairs={{3,0},{0,1},{1,2},{2,3},{7,4},{4,5},{5,6},{6,7},{11,8},{8,9},{9,10... | collective-permute-start | bytes 55304 | tf_op jit(solution)/shard_map/ppermute | solution.py:70
  461.1 28.0 %collective-permute-start.85 = (f32[2,3,768]{2,0,1:T(2,128)S(1)}, f32[2,3,768]{2,0,1:T(2,128)S(1)}, u32[]{:S(2)}, u32[]{:S(2)}) collective-permute-start(f32[2,3,768]{2,0,1:T(2,128)S(1)} %get-tuple-element.270), channel_id=1, source_target_pairs={{2,0},{3,1},{0,2},{1,3},{6,4},{7,5},{4,6},{5,7},{10,8},{11,9},{8,1... | collective-permute-start | bytes 55304 | tf_op jit(solution)/shard_map/ppermute | solution.py:70
  462.0 27.1 %collective-permute-start.86 = (f32[2,3,768]{2,0,1:T(2,128)S(1)}, f32[2,3,768]{2,0,1:T(2,128)S(1)}, u32[]{:S(2)}, u32[]{:S(2)}) collective-permute-start(f32[2,3,768]{2,0,1:T(2,128)S(1)} %get-tuple-element.269), channel_id=1, source_target_pairs={{1,0},{2,1},{3,2},{0,3},{5,4},{6,5},{7,6},{4,7},{9,8},{10,9},{11,1... | collective-permute-start | bytes 55304 | tf_op jit(solution)/shard_map/ppermute | solution.py:70
  466.2 23.4 %collective-permute-start.82 = (bf16[2,96,384]{2,1,0:T(8,128)(2,1)S(1)}, bf16[2,96,384]{2,1,0:T(8,128)(2,1)S(1)}, u32[]{:S(2)}, u32[]{:S(2)}) collective-permute-start(bf16[2,96,384]{2,1,0:T(8,128)(2,1)S(1)} %copy-done.58), channel_id=1, source_target_pairs={{0,4},{4,0},{1,5},{5,1},{2,6},{6,2},{3,7},{7,3},{8,12},{12,8},{9,1... | collective-permute-start | bytes 442376 | tf_op jit(solution)/shard_map/ppermute | solution.py:132
  478.1 37.6 %collective-permute-start.80 = (f32[2,128,768]{2,1,0:T(8,128)}, f32[2,128,768]{2,1,0:T(8,128)}, u32[]{:S(2)}, u32[]{:S(2)}) collective-permute-start(f32[2,128,768]{2,1,0:T(8,128)} %fusion.2), channel_id=1, source_target_pairs={{0,0},{8,1},{4,2},{12,3},{1,4},{9,5},{5,6},{13,7},{2,8},{10,9},{6,... | collective-permute-start | bytes 2359304 | tf_op jit(solution)/shard_map/ppermute | solution.py:1079
  485.5 32.2 %all-to-all-start.6 = ((bf16[8,96,768]{2,1,0:T(8,128)(2,1)}), bf16[8,96,768]{2,1,0:T(8,128)(2,1)S(1)}, u32[]{:S(2)}, u32[]{:S(2)}) async-start(bf16[8,96,768]{2,1,0:T(8,128)(2,1)} %bitcast.192), calls=%async_computation.6 | async-start | bytes 2359296 | tf_op jit(solution)/shard_map/all_to_all | solution.py:840
  490.6 24.4 %collective-permute-start.88 = (f32[2,3,768]{2,0,1:T(2,128)S(1)}, f32[2,3,768]{2,0,1:T(2,128)S(1)}, u32[]{:S(2)}, u32[]{:S(2)}) collective-permute-start(f32[2,3,768]{2,0,1:T(2,128)S(1)} %add.245), channel_id=1, source_target_pairs={{0,8},{8,0},{1,9},{9,1},{2,10},{10,2},{3,11},{11,3},{4,12},{12,4},... | collective-permute-start | bytes 55304 | tf_op jit(solution)/shard_map/ppermute | solution.py:314
  (138 other events, 1277.8 us)

commit v9 on v8

--- a/solution.py
+++ b/solution.py
@@ -196,12 +196,17 @@
     return [lax.ppermute(block, "g", SWAP) for block in blocks]
 
 
-def ctx_group_gather(pieces, *earlier):
+def ctx_near(pieces, *earlier):
     piece = after(jnp.stack(pieces), *earlier)
-    near, back = [rotate(piece, "ctx", step) for step in (1, 3)]
-    far = rotate(after(piece, near, back), "ctx", 2)
-    first = lax.ppermute(jnp.stack([piece, near, back]), "g", SWAP)
-    return [piece, near, far, back], [first, lax.ppermute(after(far, first), "g", SWAP)]
+    return piece, rotate(piece, "ctx", 1), rotate(piece, "ctx", 3)
+
+
+def ctx_far(piece, near, back):
+    return rotate(after(piece, near, back), "ctx", 2)
+
+
+def group_first(piece, near, back):
+    return lax.ppermute(jnp.stack([piece, near, back]), "g", SWAP)
 
 
 def gather_weights_wide(low):
@@ -228,7 +233,9 @@
 
 
 def ctx_sum(blocks):
-    return ctx_sum_last(blocks, ctx_sum_first(blocks))
+    low = blocks.astype(bf16)
+    near, back, far = [rotate(low[step], "ctx", -step) for step in (1, 3, 2)]
+    return blocks[0] + near.astype(f32) + back.astype(f32) + far.astype(f32)
 
 
 def ctx_sum_first(blocks):
@@ -242,9 +249,8 @@
     return total + far.astype(f32)
 
 
-def grad_rows(place, attn_parts, mlp_parts, momentum):
-    layers, count, rows, width = momentum.shape
-    half = width // 2
+def grad_blocks(attn_parts, mlp_parts, rows, *earlier):
+    layers = len(attn_parts)
     zero = jnp.zeros((1,), jnp.int32)
 
     def split(unused, *refs):
@@ -260,8 +266,11 @@
                     out_ref[target, 3 * layer + item] = turned[target * rows : (target + 1) * rows]
 
     blocks = call(split, [((TP, 3 * layers, rows, COLS), bf16)], zero, *attn_parts, *mlp_parts)[0]
-    blocks = group_exchange(blocks)
-    outs = out_back(jnp.stack(attn_parts).astype(bf16))
+    return group_exchange(after(blocks, *earlier)), out_back(jnp.stack(attn_parts).astype(bf16))
+
+
+def grad_rows(place, blocks, outs, momentum):
+    layers = momentum.shape[0]
 
     def join(place_ref, blocks_ref, outs_ref, momentum_ref, grad_ref, new_ref):
         for layer in range(layers):
@@ -289,10 +298,10 @@
     return from_group(part).astype(f32)
 
 
-def gather_vectors(vectors):
+def gather_vectors(vectors, *earlier):
     low = vectors.astype(bf16)
     stack = jnp.stack([low] + [rotate(low, "ctx", step) for step in range(1, 4)])
-    stack = pair_join(pair_join(to_absolute(stack), "jc", 3), "jx", 3)
+    stack = pair_join(pair_join(after(to_absolute(stack), *earlier), "jc", 3), "jx", 3)
     if lax.axis_size("g") == 2:
         stack = pair_join(stack, "g", 3)
     else:
@@ -431,10 +440,8 @@
         if own:
             own_refs, refs = refs[:4], refs[4:]
             others, refs = refs[: len(other)], refs[len(other) :]
-            if len(other) == 2:
-                own_refs = [ref.at[0] for ref in own_refs]
-                first, last = others
-                others = [first.at[0, 0], first.at[1, 0], last.at[0], first.at[2, 0]]
+            if len(other) == 1:
+                others = [others[0].at[step] for step in range(4)]
             w_ref, qkv_ref, lse_ref, o_ref, mine_ref, give_ref = refs
             put_blocks(place_ref, own_refs, others, [w_ref])
         else:
@@ -879,10 +886,8 @@
     def x_join(block):
         return pair_join(block, "jx", 0)
 
-    vec_rows = gather_vectors(vectors)
     seg_row = jnp.pad(segments.astype(f32), ((0, 7), (0, D - seq_len)))
     moved = lax.ppermute(jnp.concatenate([hidden_in[0], seg_row], axis=0), axes, to_seq)
-    hidden = x_join(moved[:tokens_dev])
     segment_row = moved[tokens_dev, :seq_len]
     relative = lax.axis_size("g") == 2
     place = jnp.stack([z_index, lax.axis_index("g"), c_index]).astype(jnp.int32)
@@ -891,9 +896,14 @@
         own_attn = ctx_gather(piece)
         attn_weights = (own_attn, group_swap(own_attn))
         pieces = other_pieces(place, weights, outs, own_attn[1])
-        mlp_weights = ctx_group_gather(pieces[0:2], *own_attn[1:])
+        near_blocks = ctx_near(pieces[0:2], *own_attn[1:])
+        far = ctx_far(*near_blocks)
+        first = group_first(*near_blocks)
     else:
         wide_weights = gather_weights_wide(weights.astype(bf16))
+        outs = piece = place
+    vec_rows = gather_vectors(vectors, outs)
+    hidden = x_join(after(moved[:tokens_dev], piece))
 
     start = c_index * half
     pos = jnp.concatenate([start + jnp.arange(half), half - start + jnp.arange(half)])
@@ -916,24 +926,26 @@
         w_attn, qkv, lse, o, mine, give = attend_stage(
             place, row_info, column_info, qkv_bias[layer], a_own, a_other, attn_weights
         )
+        if relative and not following:
+            mine, gy_own = lax.optimization_barrier((mine, gy_own))
+            moved_grad = lax.ppermute(after(out_grad[0], far), axes, to_seq)
         mine, recv = group_sum(mine, give)
         middle, c_own = norm_stage(vec_rows, layer, 2, hidden, mine, recv, (layer, 6))
-        if relative and layer == 0:
-            moved_grad = lax.ppermute(after(out_grad[0], *mlp_weights[0][2:3]), axes, to_seq)
-            c_own, moved_grad = lax.optimization_barrier((c_own, moved_grad))
-            grad_hidden = x_join(moved_grad)
+        if relative:
+            last = lax.ppermute(after(far, first), "g", SWAP)
+            mlp_weights = ([near_blocks[0], near_blocks[1], far, near_blocks[2]], [first, last])
         c_other = core_swap(c_own)
+        if relative and following:
+            base = 3 * layer + 2
+            own_attn = ctx_gather(pieces[base], far)
+            c_other, own_attn = lax.optimization_barrier((c_other, own_attn))
         w_mlp, preact, act, mine, give = feed_stage(
             place, up_bias[layer], c_own, c_other, mlp_weights
         )
         if relative and following:
-            base = 3 * layer + 2
-            attn_weights = ctx_group_gather(pieces[base : base + 1], *mlp_weights[0][2:3])
-            mine, grad_hidden, ready = lax.optimization_barrier(
-                (mine, grad_hidden, attn_weights[0][1])
-            )
-            attn_weights[0][1] = ready
-            mlp_weights = ctx_group_gather(pieces[base + 1 : base + 3], *attn_weights[0][2:3])
+            attn_weights = (own_attn, [lax.ppermute(jnp.stack(own_attn), "g", SWAP)])
+            near_blocks = ctx_near(pieces[base + 1 : base + 3], *own_attn[1:])
+            moved_low = lax.ppermute(after(out_grad[0].astype(bf16), own_attn[2]), axes, to_seq)
         if following:
             mine, recv = group_sum(mine, give)
         stored.append(
@@ -941,6 +953,13 @@
         )
         if following:
             hidden, a_own = norm_stage(vec_rows, layer + 1, 0, middle, mine, recv, (layer, 7))
+            if relative:
+                a_own, near_blocks, moved_low = lax.optimization_barrier(
+                    (a_own, near_blocks, moved_low)
+                )
+                far = ctx_far(*near_blocks)
+                first = group_first(*near_blocks)
+                gy_own = x_join(moved_low)
 
     def send_back(rows):
         block = lax.dynamic_slice_in_dim(rows, x_index * tokens_dev, tokens_dev, axis=0)
@@ -955,7 +974,7 @@
     if not relative:
         grad_hidden = x_join(lax.ppermute(out_grad[0], axes, to_seq))
         hidden_out = send_back(last_hidden())
-    gy_own = grad_hidden.astype(bf16)
+        gy_own = grad_hidden.astype(bf16)
     attn_half = mlp_half = None
 
     mat_list = [None] * LAYERS
@@ -970,13 +989,18 @@
             mlp_part = ctx_sum_last(mlp_half, mlp_first)
             hidden = last_hidden(gy_own)
         gy_other = core_swap(gy_own)
+        if relative and attn_half is None:
+            gy_other, moved_grad = lax.optimization_barrier((gy_other, moved_grad))
+            grad_hidden = x_join(moved_grad)
         mine, give, up_sums, *mlp_grads = feed_back_stage(
             place, gy_own, gy_other, c_own, c_other, preact, act, w_mlp, relative
         )
         if relative:
-            if attn_half is not None:
-                mine, mlp_part, hidden, attn_half = lax.optimization_barrier(
-                    (mine, mlp_part, hidden, attn_half)
+            if attn_half is None:
+                mine, grad_hidden = lax.optimization_barrier((mine, grad_hidden))
+            else:
+                mine, hidden, attn_half, wide_part = lax.optimization_barrier(
+                    (mine, hidden, attn_half, mlp_part)
                 )
                 attn_part = ctx_sum(attn_half)
             mlp_half = half_sum(*mlp_grads)
@@ -990,10 +1014,13 @@
             moment_slots = slot_exchange(
                 after(jnp.stack([moment_low[slot] for slot in table]), gb_own)
             ).reshape(D, D)
-        elif relative:
-            gb_own, attn_part = lax.optimization_barrier((gb_own, attn_part))
-            parts[layer + 1] = (attn_part, mlp_part)
         gb_other = core_swap(gb_own)
+        if relative and layer < LAYERS - 1:
+            gb_other, attn_part, mlp_half = lax.optimization_barrier(
+                (gb_other, attn_part, mlp_half)
+            )
+            parts[layer + 1] = (attn_part, wide_part)
+            mlp_part = ctx_sum(mlp_half)
         mine, give, qkv_sums, *attn_grads = attend_back_stage(
             place,
             row_info,
@@ -1009,12 +1036,11 @@
             relative,
         )
         if relative:
-            mine, mlp_half = lax.optimization_barrier((mine, mlp_half))
             if layer == LAYERS - 1:
-                mine, moment_slots = lax.optimization_barrier((mine, moment_slots))
+                mine, mlp_half, moment_slots = lax.optimization_barrier(
+                    (mine, mlp_half, moment_slots)
+                )
                 mlp_first = ctx_sum_first(mlp_half)
-            else:
-                mlp_part = ctx_sum(mlp_half)
             attn_half = half_sum(*attn_grads)
         else:
             attn_grad = attn_grads[0]
@@ -1025,12 +1051,6 @@
             mat_list[layer] = scatter_wide(
                 jnp.concatenate([attn_grad[:, None], mlp_grads[0]], axis=1)
             )
-        if relative and layer == 0:
-            wide_low = jnp.concatenate([parts[1][1], mlp_part]).astype(bf16)
-            x_wide, gram_blocks = slot_gram(
-                place, slot_exchange(jnp.repeat(wide_low, 2, axis=0)), moment_slots
-            )
-            mine = after(mine, gram_blocks)
         mine, recv = group_sum(mine, give)
         grad_hidden, gy_own, in_sums = norm_back_stage(
             vec_rows, layer, 0, grad_middle, mine, recv, h_in
@@ -1063,25 +1083,34 @@
     )
     if relative:
         attn_part = ctx_sum(attn_half)
-        square_low = jnp.stack([parts[1][0], attn_part]).astype(bf16)
-        square_slots = slot_exchange(jnp.tile(jnp.repeat(square_low, 2, axis=0), (2, 1, 1)))
+        wide_low = jnp.concatenate([parts[1][1], mlp_part]).astype(bf16)
+        wide_slots = slot_exchange(jnp.repeat(after(wide_low, give), 2, axis=0))
+        wide_slots, attn_part, grad_hidden = lax.optimization_barrier(
+            (wide_slots, attn_part, grad_hidden)
+        )
+        x_wide, gram_blocks = slot_gram(place, wide_slots, moment_slots)
         total = gram_blocks[0].astype(f32)
         for step in (1, 3, 2):
             total = total + core_shift(gram_blocks[step], -step).astype(f32)
-        low = total.astype(bf16)
-        near, back, far = [core_shift(low, step) for step in (1, 3, 2)]
+        gram_low = total.astype(bf16)
+        square_low = after(jnp.stack([parts[1][0], attn_part]).astype(bf16), gram_low)
+        square_slots = slot_exchange(jnp.tile(jnp.repeat(square_low, 2, axis=0), (2, 1, 1)))
+        near, back, far = [core_shift(gram_low, step) for step in (1, 3, 2)]
+        near, grad_vecs = lax.optimization_barrier((near, grad_vecs))
         ortho_mine = slot_orthogonalize(
-            place, x_wide, (low, near, far, back), square_slots, moment_slots
-        )
+            place, x_wide, (gram_low, near, far, back), square_slots, moment_slots
+        )
+        blocks, outs = grad_blocks(
+            [attn_part, parts[1][0]], [mlp_part, parts[1][1]], dp_rows, square_slots
+        )
+        ortho_mine, blocks = lax.optimization_barrier((ortho_mine, blocks))
         returned = slot_exchange(ortho_mine.reshape(dp_size, dp_rows, D))
         ends = jnp.stack([hidden, grad_hidden])
         ends = lax.dynamic_slice_in_dim(ends, x_index * tokens_dev, tokens_dev, axis=1)
-        hidden_out, input_grad = lax.ppermute(after(ends, ortho_mine), axes, from_seq)
+        hidden_out, input_grad = lax.ppermute(after(ends, near, back, far), axes, from_seq)
         ortho = jnp.stack([returned[slot] for slot in (3, 4, 6, 1, 0, 2)])
         ortho = ortho.reshape(weights.shape).astype(f32)
-        grad_mats, moment_new = grad_rows(
-            place, [attn_part, parts[1][0]], [mlp_part, parts[1][1]], mat_momentum
-        )
+        grad_mats, moment_new = grad_rows(place, blocks, outs, mat_momentum)
     else:
         cols_dev = weights.shape[3]
         grad_list, moment_list, low_list = [], [], []

time: 530 us -> 530 us (level)
    ppermute x30, waiting for transfers between devices: 102 us -> 55.2 us  [rotate(): lax.ppermute(block, axis, [((i + step) % size, i) for i in range(size)])]
    ppermute x8, waiting for transfers between devices: 19 us -> 35.7 us  [group_sum(): return (mine, lax.ppermute(mine.astype(bf16), 'jx', SWAP))]
    ppermute x1, waiting for transfers between devices: 0.01 us -> 15.8 us  [sum_vectors(): terms = terms + lax.ppermute(terms, 'g', SWAP)]
    ppermute x1, waiting for transfers between devices: 19 us -> 3.44 us  [sum_vectors(): return total + lax.ppermute(total, 'jx', SWAP)]
    all_to_all x4, waiting for transfers between devices: 0.48 us -> 13.7 us  [slot_exchange(): return lax.all_to_all(blocks, DP, split_axis=0, concat_axis=0, tiled=True)]
    ppermute x8, waiting for transfers between devices: 15.8 us -> 3.89 us  [the longest x2 3.87 us: group_first(): return lax.ppermute(jnp.stack([piece, near, back]), 'g', SWAP)]
    ppermute x4, waiting for transfers between devices: 11.7 us -> 21.8 us  [half_sum(): return mine + lax.ppermute(give, 'g', SWAP).astype(f32)]
    all_to_all x3, waiting for transfers between devices: 0.01 us -> 9.66 us  [group_exchange(): lax.all_to_all(blocks, GROUP, split_axis=0, concat_axis=0, tiled=True)]
  transfers between devices with their start and end apart: 96 -> 97, of which waited for: 39 -> 39; matrix products, arithmetic and copies ran while one was open for 9% -> 8% of each run, Pallas kernels for 15% -> 16%
where the time goes in v9:
time: 530 us; the launch traced here: 519 us
  waiting for transfers between devices  178 us (34%)
  starting transfers between devices  175 us (33%)
  Pallas kernels  95.6 us (18%)
  local copies, waits for them, and re-layouts  35.7 us (7%)
  other arithmetic  32.7 us (6%)
    pallas_call x24, Pallas kernels, call(): pl.pallas_call(kernel, out_shape=[jax.ShapeDtypeStruct(shape, kind) for s...  95.6 us
    ppermute x30, waiting for transfers between devices, rotate(): lax.ppermute(block, axis, [((i + step) % size, i) for i in range(size)])  55.2 us
    ppermute x30, starting transfers between devices, rotate(): lax.ppermute(block, axis, [((i + step) % size, i) for i in range(size)])  54.9 us
    ppermute x8, waiting for transfers between devices, group_sum(): return (mine, lax.ppermute(mine.astype(bf16), 'jx', SWAP))  35.7 us
    ppermute x6, starting transfers between devices, core_shift(): lax.ppermute(block, ('jc', 'ctx'), [((i + step) % size, i) for i in range...  25 us
    ppermute x4, waiting for transfers between devices, half_sum(): return mine + lax.ppermute(give, 'g', SWAP).astype(f32)  21.8 us
    unnamed x156, local copies, waits for them, and re-layouts  21.1 us
    all_to_all x4, starting transfers between devices, slot_exchange(): return lax.all_to_all(blocks, DP, split_axis=0, concat_axis=0, tiled=True)  18.6 us
  transfers between devices with their start and end apart: 97, of which 39 were waited for; matrix products, arithmetic and copies ran while one was open for 8% of the time, Pallas kernels for 16%

profile of v9, /device:TPU:0, one launch (start us, length us, event | category | flops | bytes accessed | tf_op | source)
XLA Modules:
  0.0 519.3 jit_solution(18273549694506962845)
XLA Ops:
  12.4 6.8 %all-to-all-start = ((bf16[4,1,192,96]{3,2,1,0:T(8,128)(2,1)}), bf16[4,1,192,96]{3,2,1,0:T(8,128)(2,1)S(1)}, u32[]{:S(2)}, u32[]{:S(2)}) async-start(bf16[4,1,192,96]{3,2,1,0:T(8,128)(2,1)} %shard_map.152), calls=%async_computation | async-start | bytes 393216 | tf_op jit(solution)/shard_map/all_to_all | solution.py:174
  30.5 12.4 %collective-permute-start.11 = (bf16[192,384]{1,0:T(8,128)(2,1)S(1)}, bf16[192,384]{1,0:T(8,128)(2,1)S(1)}, u32[]{:S(2)}, u32[]{:S(2)}) collective-permute-start(bf16[192,384]{1,0:T(8,128)(2,1)S(1)} %shard_map.153.refs_0_), channel_id=1, source_target_pairs={{1,0},{2,1},{3,2},{0,3},{5,4},{6,5},{7,6},{4,7},{9,8},{10,9},{11,1... | collective-permute-start | bytes 442376 | tf_op jit(solution)/shard_map/ppermute | solution.py:70
  57.7 9.7 %all-to-all-done.1.blocks_ref = bf16[4,5,192,96]{3,2,1,0:T(8,128)(2,1)S(1)} async-done(((bf16[4,5,192,96]{3,2,1,0:T(8,128)(2,1)}), bf16[4,5,192,96]{3,2,1,0:T(8,128)(2,1)S(1)}, u32[]{:S(2)}, u32[]{:S(2)}) %all-to-all-start.1) | async-done | bytes 737312 | tf_op jit(solution)/shard_map/all_to_all | solution.py:174
  74.8 6.5 %shard_map.155 = (bf16[768,768]{1,0:T(8,128)(2,1)}, bf16[512,576]{1,0:T(8,128)(2,1)}, f32[512,128]{1,0:T(8,128)S(1)}, bf16[512,192]{1,0:T(8,128)(2,1)S(1)}, f32[...) custom-call(s32[3]{0:T(128)S(1)} %pad_add_fusion.place_ref, f32[8,512]{1,0:T(8,128)S(1)} %pad.13.row_ref, ...), custom_call_target="tpu_custom_call" | custom-call | tf_op jit(solution)/shard_map/pallas_call | solution.py:327
  88.5 9.1 %collective-permute-done.19.refs_1_ = bf16[256,768]{1,0:T(8,128)(2,1)S(1)} collective-permute-done((bf16[256,768]{1,0:T(8,128)(2,1)S(1)}, bf16[256,768]{1,0:T(8,128)(2,1)S(1)}, u32[]{:S(2)}, u32[]{:S(2)}) %collective-permute-start.19) | collective-permute-done | bytes 393248 | tf_op jit(solution)/shard_map/ppermute | solution.py:684
  114.1 7.1 %collective-permute-done.25.refs_2_ = bf16[192,384]{1,0:T(8,128)(2,1)S(1)} collective-permute-done((bf16[192,384]{1,0:T(8,128)(2,1)S(1)}, bf16[192,384]{1,0:T(8,128)(2,1)S(1)}, u32[]{:S(2)}, u32[]{:S(2)}) %collective-permute-start.25) | collective-permute-done | bytes 147488 | tf_op jit(solution)/shard_map/ppermute | solution.py:70
  134.7 6.9 %collective-permute-done.30.refs_1_ = bf16[256,768]{1,0:T(8,128)(2,1)S(1)} collective-permute-done((bf16[256,768]{1,0:T(8,128)(2,1)S(1)}, bf16[256,768]{1,0:T(8,128)(2,1)S(1)}, u32[]{:S(2)}, u32[]{:S(2)}) %collective-permute-start.30) | collective-permute-done | bytes 393248 | tf_op jit(solution)/shard_map/ppermute | solution.py:684
  144.2 6.3 %collective-permute-start.34 = (bf16[256,768]{1,0:T(8,128)(2,1)S(1)}, bf16[256,768]{1,0:T(8,128)(2,1)S(1)}, u32[]{:S(2)}, u32[]{:S(2)}) collective-permute-start(bf16[256,768]{1,0:T(8,128)(2,1)S(1)} %get-tuple-element.155.own_a_ref), channel_id=1, source_target_pairs={{0,4},{4,0},{1,5},{5,1},{2,6},{6,2},{3,7},{7,3},{8,12},{12,8},{9,1... | collective-permute-start | bytes 1179656 | tf_op jit(solution)/shard_map/ppermute | solution.py:679
  154.4 6.1 %shard_map.161 = (bf16[768,768]{1,0:T(8,128)(2,1)}, bf16[512,576]{1,0:T(8,128)(2,1)}, f32[512,128]{1,0:T(8,128)S(1)}, bf16[512,192]{1,0:T(8,128)(2,1)S(1)}, f32[...) custom-call(s32[3]{0:T(128)S(1)} %pad_add_fusion.place_ref, f32[8,512]{1,0:T(8,128)S(1)} %pad.13.row_ref, ...), custom_call_target="tpu_custom_call" | custom-call | tf_op jit(solution)/shard_map/pallas_call | solution.py:327
  175.3 6.9 %collective-permute-start.45 = (f32[128,768]{1,0:T(8,128)}, f32[128,768]{1,0:T(8,128)}, u32[]{:S(2)}, u32[]{:S(2)}) collective-permute-start(f32[128,768]{1,0:T(8,128)} %collective-permute-done.39), channel_id=1, source_target_pairs={{0,8},{8,0},{1,9},{9,1},{2,10},{10,2},{3,11},{11,3},{4,12},{12,4},... | collective-permute-start | bytes 1179656 | tf_op jit(solution)/shard_map/ppermute | solution.py:74
  201.6 7.5 %shard_map.164 = (f32[256,768]{1,0:T(8,128)}, bf16[256,768]{1,0:T(8,128)(2,1)S(1)}, f32[8,768]{1,0:T(8,128)S(1)}, f32[4,2,192,384]{3,2,1,0:T(8,128)}, bf16[4,2,192,384]{3,2,1,0:T(8,128)(2,1)}) custom-call(s32[3]{0:T(128)S(1)} %pad_add_fusion.place_ref, bf16[256,768]{1,0:T(8,128)(2,1)S(1)} %pad_maximum_fusion.6.own_gy_ref, ...), custom_call_target="tpu_custom_call" | custom-call | tf_op jit(solution)/shard_map/pallas_call | solution.py:327
  219.4 6.2 %collective-permute-done.47.recv_ref = bf16[256,768]{1,0:T(8,128)(2,1)S(1)} collective-permute-done((bf16[256,768]{1,0:T(8,128)(2,1)S(1)}, bf16[256,768]{1,0:T(8,128)(2,1)S(1)}, u32[]{:S(2)}, u32[]{:S(2)}) %collective-permute-start.47) | collective-permute-done | bytes 393248 | tf_op jit(solution)/shard_map/ppermute | solution.py:684
  234.7 8.5 %shard_map.166 = (f32[256,768]{1,0:T(8,128)}, bf16[256,768]{1,0:T(8,128)(2,1)S(1)}, f32[8,576]{1,0:T(8,128)S(1)}, f32[4,192,384]{2,1,0:T(8,128)}, bf16[4,192,384]{2,1,0:T(8,128)(2,1)}) custom-call(s32[3]{0:T(128)S(1)} %pad_add_fusion.place_ref, f32[8,512]{1,0:T(8,128)S(1)} %pad.13.row_ref, f32[512,128]{1,0:T(8,128)S(1)} %pad.14.column_ref, ...), custom_call_target="tpu_custom_call" | custom-call | tf_op jit(solution)/shard_map/pallas_call | solution.py:327
  260.3 6.3 %collective-permute-done.53 = bf16[2,192,384]{2,1,0:T(8,128)(2,1)S(1)} collective-permute-done((bf16[2,192,384]{2,1,0:T(8,128)(2,1)S(1)}, bf16[2,192,384]{2,1,0:T(8,128)(2,1)S(1)}, u32[]{:S(2)}, u32[]{:S(2)}) %collective-permute-start.53) | collective-permute-done | bytes 294944 | tf_op jit(solution)/shard_map/ppermute | solution.py:70
  280.9 11.0 %collective-permute-done.57 = bf16[4,192,384]{2,1,0:T(8,128)(2,1)S(1)} collective-permute-done((bf16[4,192,384]{2,1,0:T(8,128)(2,1)S(1)}, bf16[4,192,384]{2,1,0:T(8,128)(2,1)S(1)}, u32[]{:S(2)}, u32[]{:S(2)}) %collective-permute-start.57) | collective-permute-done | bytes 589856 | tf_op jit(solution)/shard_map/ppermute | solution.py:232
  293.0 7.4 %shard_map.168 = (f32[256,768]{1,0:T(8,128)}, bf16[256,768]{1,0:T(8,128)(2,1)S(1)}, f32[8,768]{1,0:T(8,128)S(1)}, f32[4,2,192,384]{3,2,1,0:T(8,128)}, bf16[4,2,192,384]{3,2,1,0:T(8,128)(2,1)}) custom-call(s32[3]{0:T(128)S(1)} %pad_add_fusion.place_ref, bf16[256,768]{1,0:T(8,128)(2,1)S(1)} %get-tuple-element.194.own_gy_ref, ...), custom_call_target="tpu_custom_call" | custom-call | tf_op jit(solution)/shard_map/pallas_call | solution.py:327
  308.6 6.7 %collective-permute-done.60.recv_ref = bf16[256,768]{1,0:T(8,128)(2,1)S(1)} collective-permute-done((bf16[256,768]{1,0:T(8,128)(2,1)S(1)}, bf16[256,768]{1,0:T(8,128)(2,1)S(1)}, u32[]{:S(2)}, u32[]{:S(2)}) %collective-permute-start.60) | collective-permute-done | bytes 393248 | tf_op jit(solution)/shard_map/ppermute | solution.py:684
  318.9 10.3 %collective-permute-done.65 = bf16[4,2,192,384]{3,2,1,0:T(8,128)(2,1)S(1)} collective-permute-done((bf16[4,2,192,384]{3,2,1,0:T(8,128)(2,1)}, bf16[4,2,192,384]{3,2,1,0:T(8,128)(2,1)S(1)}, u32[]{:S(2)}, u32[]{:S(2)}) %collective-permute-start.65) | collective-permute-done | bytes 1179680 | tf_op jit(solution)/shard_map/ppermute | solution.py:232
  336.8 8.4 %shard_map.170 = (f32[256,768]{1,0:T(8,128)}, bf16[256,768]{1,0:T(8,128)(2,1)S(1)}, f32[8,576]{1,0:T(8,128)S(1)}, f32[4,192,384]{2,1,0:T(8,128)}, bf16[4,192,384]{2,1,0:T(8,128)(2,1)}) custom-call(s32[3]{0:T(128)S(1)} %pad_add_fusion.place_ref, f32[8,512]{1,0:T(8,128)S(1)} %pad.13.row_ref, f32[512,128]{1,0:T(8,128)S(1)} %pad.14.column_ref, ...), custom_call_target="tpu_custom_call" | custom-call | tf_op jit(solution)/shard_map/pallas_call | solution.py:327
  396.2 7.4 %collective-permute-start.77 = (bf16[192,768]{1,0:T(8,128)(2,1)S(1)}, bf16[192,768]{1,0:T(8,128)(2,1)S(1)}, u32[]{:S(2)}, u32[]{:S(2)}) collective-permute-start(bf16[192,768]{1,0:T(8,128)(2,1)S(1)} %get-tuple-element.275), channel_id=1, source_target_pairs={{2,0},{3,1},{0,2},{1,3},{10,8},{11,9},{8,10},{9,11},{18,16},{19,17... | collective-permute-start | bytes 884744 | tf_op jit(solution)/shard_map/ppermute | solution.py:852
  427.4 15.8 %collective-permute-done.79 = f32[2,12,768]{2,1,0:T(8,128)S(1)} collective-permute-done((f32[2,12,768]{2,1,0:T(8,128)S(1)}, f32[2,12,768]{2,1,0:T(8,128)S(1)}, u32[]{:S(2)}, u32[]{:S(2)}) %collective-permute-start.79) | collective-permute-done | bytes 73760 | tf_op jit(solution)/shard_map/ppermute | solution.py:314
  452.8 6.9 %collective-permute-start.78 = (bf16[192,768]{1,0:T(8,128)(2,1)S(1)}, bf16[192,768]{1,0:T(8,128)(2,1)S(1)}, u32[]{:S(2)}, u32[]{:S(2)}) collective-permute-start(bf16[192,768]{1,0:T(8,128)(2,1)S(1)} %fusion.5.gram0_ref), channel_id=1, source_target_pairs={{1,0},{2,1},{3,2},{0,3},{9,8},{10,9},{11,10},{8,11},{17,16},{18,17... | collective-permute-start | bytes 884744 | tf_op jit(solution)/shard_map/ppermute | solution.py:852
  478.3 11.9 %shard_map.173 = bf16[768,768]{1,0:T(8,128)(2,1)} custom-call(s32[3]{0:T(128)S(1)} %pad_add_fusion.place_ref, bf16[768,768]{1,0:T(8,128)(2,1)} %copy-done.17, bf16[192,768]{1,0:T(8,128)(2,1)S(1)} %fusion.5.gram0_ref, bf16[192,768]{1,0:T(8,128)(2,1)S(1)} %collective-permute-done.78.gram1_ref, bf16[192,768]{1,0:T(8,128)(2,1)S(1)} %collective-permute-done.86.gram2_ref, ...), custom_call_target="tpu_custom_call" | custom-call | tf_op jit(solution)/shard_map/pallas_call | solution.py:327
  504.4 8.2 %all-to-all-done.6 = bf16[8,96,768]{2,1,0:T(8,128)(2,1)} async-done(((bf16[8,96,768]{2,1,0:T(8,128)(2,1)}), bf16[8,96,768]{2,1,0:T(8,128)(2,1)}, u32[]{:S(2)}, u32[]{:S(2)}) %all-to-all-start.6) | async-done | bytes 1179680 | tf_op jit(solution)/shard_map/all_to_all | solution.py:847
  (469 shorter events, 316.5 us)
Async XLA Ops:
  1.4 18.6 %collective-permute-start.2 = (bf16[2,3,96]{2,0,1:T(2,128)(2,1)S(1)}, bf16[2,3,96]{2,0,1:T(2,128)(2,1)S(1)}, u32[]{:S(2)}, u32[]{:S(2)}) collective-permute-start(bf16[2,3,96]{2,0,1:T(2,128)(2,1)S(1)} %convert_element_type.178), channel_id=1, source_target_pairs={{2,0},{3,1},{0,2},{1,3},{6,4},{7,5},{4,6},{5,7},{10,8},{11,9},{8,1... | collective-permute-start | bytes 3464 | tf_op jit(solution)/shard_map/ppermute | solution.py:70
  43.6 24.9 %collective-permute-start.14 = (bf16[192,384]{1,0:T(8,128)(2,1)S(1)}, bf16[192,384]{1,0:T(8,128)(2,1)}, u32[]{:S(2)}, u32[]{:S(2)}) collective-permute-start(bf16[192,384]{1,0:T(8,128)(2,1)S(1)} %shard_map.153.refs_0_), channel_id=1, source_target_pairs={{0,16},{16,0},{1,17},{17,1},{2,18},{18,2},{3,19},{19,3},{4,20},{20... | collective-permute-start | bytes 442376 | tf_op jit(solution)/shard_map/ppermute | solution.py:196
  53.6 19.2 %collective-permute-start.15 = (bf16[192,384]{1,0:T(8,128)(2,1)S(1)}, bf16[192,384]{1,0:T(8,128)(2,1)}, u32[]{:S(2)}, u32[]{:S(2)}) collective-permute-start(bf16[192,384]{1,0:T(8,128)(2,1)S(1)} %collective-permute-done.11.refs_1_), channel_id=1, source_target_pairs={{0,16},{16,0},{1,17},{17,1},{2,18},{18,2},{3,19},{19,3},{4,20},{20... | collective-permute-start | bytes 442376 | tf_op jit(solution)/shard_map/ppermute | solution.py:196
  86.1 20.7 %collective-permute-start.27 = (bf16[3,2,192,384]{3,2,1,0:T(8,128)(2,1)S(1)}, bf16[3,2,192,384]{3,2,1,0:T(8,128)(2,1)S(1)}, u32[]{:S(2)}, u32[]{:S(2)}) collective-permute-start(bf16[3,2,192,384]{3,2,1,0:T(8,128)(2,1)S(1)} %pad_maximum_fusion), channel_id=1, source_target_pairs={{0,16},{16,0},{1,17},{17,1},{2,18},{18,2},{3,19},{19,3},{4,20},{20... | collective-permute-start | bytes 2654216 | tf_op jit(solution)/shard_map/ppermute | solution.py:209
  100.2 21.0 %collective-permute-start.20 = (bf16[256,768]{1,0:T(8,128)(2,1)S(1)}, bf16[256,768]{1,0:T(8,128)(2,1)S(1)}, u32[]{:S(2)}, u32[]{:S(2)}) collective-permute-start(bf16[256,768]{1,0:T(8,128)(2,1)S(1)} %get-tuple-element.135.own_c_ref), channel_id=1, source_target_pairs={{0,4},{4,0},{1,5},{5,1},{2,6},{6,2},{3,7},{7,3},{8,12},{12,8},{9,1... | collective-permute-start | bytes 1179656 | tf_op jit(solution)/shard_map/ppermute | solution.py:679
  133.1 20.3 %collective-permute-start.35 = (bf16[4,192,384]{2,1,0:T(8,128)(2,1)S(1)}, bf16[4,192,384]{2,1,0:T(8,128)(2,1)S(1)}, u32[]{:S(2)}, u32[]{:S(2)}) collective-permute-start(bf16[4,192,384]{2,1,0:T(8,128)(2,1)S(1)} %pad_maximum_fusion.4), channel_id=1, source_target_pairs={{0,16},{16,0},{1,17},{17,1},{2,18},{18,2},{3,19},{19,3},{4,20},{20... | collective-permute-start | bytes 1769480 | tf_op jit(solution)/shard_map/ppermute | solution.py:946
  160.7 22.1 %collective-permute-start.43 = (bf16[3,2,192,384]{3,2,1,0:T(8,128)(2,1)S(1)}, bf16[3,2,192,384]{3,2,1,0:T(8,128)(2,1)S(1)}, u32[]{:S(2)}, u32[]{:S(2)}) collective-permute-start(bf16[3,2,192,384]{3,2,1,0:T(8,128)(2,1)S(1)} %pad_maximum_fusion.1), channel_id=1, source_target_pairs={{0,16},{16,0},{1,17},{17,1},{2,18},{18,2},{3,19},{19,3},{4,20},{20... | collective-permute-start | bytes 2654216 | tf_op jit(solution)/shard_map/ppermute | solution.py:209
  175.3 34.4 %collective-permute-start.45 = (f32[128,768]{1,0:T(8,128)}, f32[128,768]{1,0:T(8,128)}, u32[]{:S(2)}, u32[]{:S(2)}) collective-permute-start(f32[128,768]{1,0:T(8,128)} %collective-permute-done.39), channel_id=1, source_target_pairs={{0,8},{8,0},{1,9},{9,1},{2,10},{10,2},{3,11},{11,3},{4,12},{12,4},... | collective-permute-start | bytes 1179656 | tf_op jit(solution)/shard_map/ppermute | solution.py:74
  211.8 32.3 %collective-permute-start.49 = (bf16[4,2,192,384]{3,2,1,0:T(8,128)(2,1)}, bf16[4,2,192,384]{3,2,1,0:T(8,128)(2,1)}, u32[]{:S(2)}, u32[]{:S(2)}) collective-permute-start(bf16[4,2,192,384]{3,2,1,0:T(8,128)(2,1)} %get-tuple-element.188), channel_id=1, source_target_pairs={{0,16},{16,0},{1,17},{17,1},{2,18},{18,2},{3,19},{19,3},{4,20},{20... | collective-permute-start | bytes 3538952 | tf_op jit(solution)/shard_map/ppermute | solution.py:232
  228.8 23.8 %all-to-all-start.2 = ((bf16[8,96,768]{2,1,0:T(8,128)(2,1)}), bf16[8,96,768]{2,1,0:T(8,128)(2,1)S(1)}, u32[]{:S(2)}, u32[]{:S(2)}) async-start(bf16[8,96,768]{2,1,0:T(8,128)(2,1)} %fusion.22), calls=%async_computation.2 | async-start | bytes 2359296 | tf_op jit(solution)/shard_map/all_to_all | solution.py:847
  279.0 21.5 %collective-permute-start.58 = (bf16[2,192,384]{2,1,0:T(8,128)(2,1)S(1)}, bf16[2,192,384]{2,1,0:T(8,128)(2,1)S(1)}, u32[]{:S(2)}, u32[]{:S(2)}) collective-permute-start(bf16[2,192,384]{2,1,0:T(8,128)(2,1)S(1)} %slice_bitcast_fusion), channel_id=1, source_target_pairs={{2,0},{3,1},{0,2},{1,3},{6,4},{7,5},{4,6},{5,7},{10,8},{11,9},{8,1... | collective-permute-start | bytes 884744 | tf_op jit(solution)/shard_map/ppermute | solution.py:70
  279.9 22.1 %collective-permute-start.56 = (bf16[256,768]{1,0:T(8,128)(2,1)S(1)}, bf16[256,768]{1,0:T(8,128)(2,1)S(1)}, u32[]{:S(2)}, u32[]{:S(2)}) collective-permute-start(bf16[256,768]{1,0:T(8,128)(2,1)S(1)} %fusion.9), channel_id=1, source_target_pairs={{0,8},{8,0},{1,9},{9,1},{2,10},{10,2},{3,11},{11,3},{4,12},{12,4},... | collective-permute-start | bytes 1179656 | tf_op jit(solution)/shard_map/ppermute | solution.py:684
  300.5 28.6 %collective-permute-start.65 = (bf16[4,2,192,384]{3,2,1,0:T(8,128)(2,1)}, bf16[4,2,192,384]{3,2,1,0:T(8,128)(2,1)S(1)}, u32[]{:S(2)}, u32[]{:S(2)}) collective-permute-start(bf16[4,2,192,384]{3,2,1,0:T(8,128)(2,1)} %get-tuple-element.214), channel_id=1, source_target_pairs={{0,16},{16,0},{1,17},{17,1},{2,18},{18,2},{3,19},{19,3},{4,20},{20... | collective-permute-start | bytes 3538952 | tf_op jit(solution)/shard_map/ppermute | solution.py:232
  331.8 18.7 %collective-permute-start.68 = (bf16[2,192,384]{2,1,0:T(8,128)(2,1)}, bf16[2,192,384]{2,1,0:T(8,128)(2,1)}, u32[]{:S(2)}, u32[]{:S(2)}) collective-permute-start(bf16[2,192,384]{2,1,0:T(8,128)(2,1)} %get-tuple-element.278), channel_id=1, source_target_pairs={{2,0},{3,1},{0,2},{1,3},{6,4},{7,5},{4,6},{5,7},{10,8},{11,9},{8,1... | collective-permute-start | bytes 884744 | tf_op jit(solution)/shard_map/ppermute | solution.py:70
  335.9 19.7 %collective-permute-start.66 = (bf16[2,192,384]{2,1,0:T(8,128)(2,1)}, bf16[2,192,384]{2,1,0:T(8,128)(2,1)}, u32[]{:S(2)}, u32[]{:S(2)}) collective-permute-start(bf16[2,192,384]{2,1,0:T(8,128)(2,1)} %get-tuple-element.277), channel_id=1, source_target_pairs={{3,0},{0,1},{1,2},{2,3},{7,4},{4,5},{5,6},{6,7},{11,8},{8,9},{9,10... | collective-permute-start | bytes 884744 | tf_op jit(solution)/shard_map/ppermute | solution.py:70
  346.7 18.9 %collective-permute-start.69 = (bf16[4,192,384]{2,1,0:T(8,128)(2,1)}, bf16[4,192,384]{2,1,0:T(8,128)(2,1)}, u32[]{:S(2)}, u32[]{:S(2)}) collective-permute-start(bf16[4,192,384]{2,1,0:T(8,128)(2,1)} %get-tuple-element.224), channel_id=1, source_target_pairs={{0,16},{16,0},{1,17},{17,1},{2,18},{18,2},{3,19},{19,3},{4,20},{20... | collective-permute-start | bytes 1769480 | tf_op jit(solution)/shard_map/ppermute | solution.py:232
  358.3 31.7 %all-to-all-start.3 = ((bf16[8,192,384]{2,1,0:T(8,128)(2,1)}), bf16[8,192,384]{2,1,0:T(8,128)(2,1)}, u32[]{:S(2)}, u32[]{:S(2)}) async-start(bf16[8,192,384]{2,1,0:T(8,128)(2,1)} %bitcast.195), calls=%async_computation.3 | async-start | bytes 2359296 | tf_op jit(solution)/shard_map/all_to_all | solution.py:847
  363.8 23.2 %collective-permute-start.74 = (bf16[256,768]{1,0:T(8,128)(2,1)S(1)}, bf16[256,768]{1,0:T(8,128)(2,1)S(1)}, u32[]{:S(2)}, u32[]{:S(2)}) collective-permute-start(bf16[256,768]{1,0:T(8,128)(2,1)S(1)} %get-tuple-element.256), channel_id=1, source_target_pairs={{0,8},{8,0},{1,9},{9,1},{2,10},{10,2},{3,11},{11,3},{4,12},{12,4},... | collective-permute-start | bytes 1179656 | tf_op jit(solution)/shard_map/ppermute | solution.py:684
  420.6 24.2 %all-to-all-start.4 = ((bf16[8,192,384]{2,1,0:T(8,128)(2,1)}), bf16[8,192,384]{2,1,0:T(8,128)(2,1)}, u32[]{:S(2)}, u32[]{:S(2)}) async-start(bf16[8,192,384]{2,1,0:T(8,128)(2,1)} %bitcast.196), calls=%async_computation.4 | async-start | bytes 2359296 | tf_op jit(solution)/shard_map/all_to_all | solution.py:847
  444.8 45.4 %all-to-all-start.5 = ((bf16[4,6,96,192]{3,2,1,0:T(8,128)(2,1)}), bf16[4,6,96,192]{3,2,1,0:T(8,128)(2,1)S(1)}, u32[]{:S(2)}, u32[]{:S(2)}) async-start(bf16[4,6,96,192]{3,2,1,0:T(8,128)(2,1)} %shard_map.174), calls=%async_computation.5 | async-start | bytes 2359296 | tf_op jit(solution)/shard_map/all_to_all | solution.py:174
  451.4 44.3 %collective-permute-start.88 = (bf16[2,192,384]{2,1,0:T(8,128)(2,1)}, bf16[2,192,384]{2,1,0:T(8,128)(2,1)}, u32[]{:S(2)}, u32[]{:S(2)}) collective-permute-start(bf16[2,192,384]{2,1,0:T(8,128)(2,1)} %get-tuple-element.300), channel_id=1, source_target_pairs={{3,3},{19,7},{7,11},{23,15},{11,19},{27,23},{15,27},{31,31}} | collective-permute-start | bytes 884744 | tf_op jit(solution)/shard_map/ppermute | solution.py:128
  452.8 18.6 %collective-permute-start.78 = (bf16[192,768]{1,0:T(8,128)(2,1)S(1)}, bf16[192,768]{1,0:T(8,128)(2,1)S(1)}, u32[]{:S(2)}, u32[]{:S(2)}) collective-permute-start(bf16[192,768]{1,0:T(8,128)(2,1)S(1)} %fusion.5.gram0_ref), channel_id=1, source_target_pairs={{1,0},{2,1},{3,2},{0,3},{9,8},{10,9},{11,10},{8,11},{17,16},{18,17... | collective-permute-start | bytes 884744 | tf_op jit(solution)/shard_map/ppermute | solution.py:852
  476.5 23.4 %collective-permute-start.87 = (f32[2,128,768]{2,1,0:T(8,128)}, f32[2,128,768]{2,1,0:T(8,128)S(1)}, u32[]{:S(2)}, u32[]{:S(2)}) collective-permute-start(f32[2,128,768]{2,1,0:T(8,128)} %fusion.2), channel_id=1, source_target_pairs={{0,0},{8,1},{4,2},{12,3},{1,4},{9,5},{5,6},{13,7},{2,8},{10,9},{6,... | collective-permute-start | bytes 2359304 | tf_op jit(solution)/shard_map/ppermute | solution.py:1110
  490.2 22.4 %all-to-all-start.6 = ((bf16[8,96,768]{2,1,0:T(8,128)(2,1)}), bf16[8,96,768]{2,1,0:T(8,128)(2,1)}, u32[]{:S(2)}, u32[]{:S(2)}) async-start(bf16[8,96,768]{2,1,0:T(8,128)(2,1)} %bitcast.197), calls=%async_computation.6 | async-start | bytes 2359296 | tf_op jit(solution)/shard_map/all_to_all | solution.py:847
  (145 other events, 1323.9 us)

commit v10 on v9

--- a/solution.py
+++ b/solution.py
@@ -238,17 +238,6 @@
     return blocks[0] + near.astype(f32) + back.astype(f32) + far.astype(f32)
 
 
-def ctx_sum_first(blocks):
-    low = blocks.astype(bf16)
-    near, back = [rotate(low[step], "ctx", -step) for step in (1, 3)]
-    return blocks[0] + near.astype(f32) + back.astype(f32)
-
-
-def ctx_sum_last(blocks, total):
-    far = rotate(after(blocks[2], total).astype(bf16), "ctx", -2)
-    return total + far.astype(f32)
-
-
 def grad_blocks(attn_parts, mlp_parts, rows, *earlier):
     layers = len(attn_parts)
     zero = jnp.zeros((1,), jnp.int32)
@@ -319,6 +308,10 @@
     total = blocks[0]
     for step in range(1, 4):
         total = total + rotate(blocks[step], "ctx", -step)
+    return total
+
+
+def sum_group(total):
     total = total + lax.ppermute(total, "jc", SWAP)
     return total + lax.ppermute(total, "jx", SWAP)
 
@@ -985,8 +978,7 @@
             layer
         ]
         if relative and attn_half is not None:
-            gy_own, mlp_first = lax.optimization_barrier((gy_own, mlp_first))
-            mlp_part = ctx_sum_last(mlp_half, mlp_first)
+            gy_own, attn_half = lax.optimization_barrier((gy_own, attn_half))
             hidden = last_hidden(gy_own)
         gy_other = core_swap(gy_own)
         if relative and attn_half is None:
@@ -999,9 +991,7 @@
             if attn_half is None:
                 mine, grad_hidden = lax.optimization_barrier((mine, grad_hidden))
             else:
-                mine, hidden, attn_half, wide_part = lax.optimization_barrier(
-                    (mine, hidden, attn_half, mlp_part)
-                )
+                mine, hidden, wide_part = lax.optimization_barrier((mine, hidden, mlp_part))
                 attn_part = ctx_sum(attn_half)
             mlp_half = half_sum(*mlp_grads)
         mine, recv = group_sum(mine, give)
@@ -1040,7 +1030,7 @@
                 mine, mlp_half, moment_slots = lax.optimization_barrier(
                     (mine, mlp_half, moment_slots)
                 )
-                mlp_first = ctx_sum_first(mlp_half)
+                mlp_part = ctx_sum(mlp_half)
             attn_half = half_sum(*attn_grads)
         else:
             attn_grad = attn_grads[0]
@@ -1078,30 +1068,30 @@
     vec_terms = jnp.concatenate(
         [shared[:, 0:4], placed[:, 0:2], shared[:, 4:6], placed[:, 2:6]], axis=1
     )
-    grad_vecs = lax.dynamic_slice_in_dim(
-        sum_vectors(vec_terms), dp_index * vectors.shape[2], vectors.shape[2], axis=2
-    )
+    vec_sums = sum_vectors(vec_terms)
     if relative:
-        attn_part = ctx_sum(attn_half)
+        attn_low = attn_half.astype(bf16)
+        attn_sums = [rotate(attn_low[step], "ctx", -step) for step in (1, 3, 2)]
         wide_low = jnp.concatenate([parts[1][1], mlp_part]).astype(bf16)
         wide_slots = slot_exchange(jnp.repeat(after(wide_low, give), 2, axis=0))
-        wide_slots, attn_part, grad_hidden = lax.optimization_barrier(
-            (wide_slots, attn_part, grad_hidden)
-        )
+        wide_slots, grad_hidden = lax.optimization_barrier((wide_slots, grad_hidden))
         x_wide, gram_blocks = slot_gram(place, wide_slots, moment_slots)
+        attn_sums, unused = lax.optimization_barrier((attn_sums, gram_blocks))
+        attn_part = attn_half[0] + sum(block.astype(f32) for block in attn_sums)
         total = gram_blocks[0].astype(f32)
         for step in (1, 3, 2):
             total = total + core_shift(gram_blocks[step], -step).astype(f32)
         gram_low = total.astype(bf16)
-        square_low = after(jnp.stack([parts[1][0], attn_part]).astype(bf16), gram_low)
+        square_low, vec_sums, unused = lax.optimization_barrier(
+            (jnp.stack([parts[1][0], attn_part]).astype(bf16), vec_sums, gram_low)
+        )
         square_slots = slot_exchange(jnp.tile(jnp.repeat(square_low, 2, axis=0), (2, 1, 1)))
         near, back, far = [core_shift(gram_low, step) for step in (1, 3, 2)]
-        near, grad_vecs = lax.optimization_barrier((near, grad_vecs))
         ortho_mine = slot_orthogonalize(
             place, x_wide, (gram_low, near, far, back), square_slots, moment_slots
         )
         blocks, outs = grad_blocks(
-            [attn_part, parts[1][0]], [mlp_part, parts[1][1]], dp_rows, square_slots
+            [attn_part, parts[1][0]], [mlp_part, parts[1][1]], dp_rows, square_slots, near, back, far
         )
         ortho_mine, blocks = lax.optimization_barrier((ortho_mine, blocks))
         returned = slot_exchange(ortho_mine.reshape(dp_size, dp_rows, D))
@@ -1147,6 +1137,9 @@
         ortho = jnp.stack(ortho_list).reshape(LAYERS, 3, dp_rows, cols_dev).astype(f32)
         grad_mats = jnp.stack(grad_list).reshape(weights.shape)
         moment_new = jnp.stack(moment_list).reshape(weights.shape)
+    grad_vecs = lax.dynamic_slice_in_dim(
+        sum_group(vec_sums), dp_index * vectors.shape[2], vectors.shape[2], axis=2
+    )
     factor = jnp.array([0.2 * math.sqrt(D), 0.2 * math.sqrt(FF), 0.2 * math.sqrt(FF)], f32)
     weights_new = weights * (1.0 - matrix_rate * matrix_decay) - matrix_rate * (
         ortho * factor[None, :, None, None]

time: 530 us -> 531 us (level)
  waiting for transfers between devices: 178 us -> 166 us
  starting transfers between devices: 175 us -> 186 us
    ppermute x30, starting transfers between devices: 54.9 us -> 66.3 us  [rotate(): lax.ppermute(block, axis, [((i + step) % size, i) for i in range(size)])]
    ppermute x4, waiting for transfers between devices: 21.8 us -> 11.1 us  [half_sum(): return mine + lax.ppermute(give, 'g', SWAP).astype(f32)]
    all_to_all x4, waiting for transfers between devices: 13.7 us -> 5.23 us  [slot_exchange(): return lax.all_to_all(blocks, DP, split_axis=0, concat_axis=0, tiled=True)]
    ppermute x2, waiting for transfers between devices: 4.61 us -> 12.8 us  [the longest x1 12 us: sum_group(): return total + lax.ppermute(total, 'jx', SWAP)]
    all_to_all x3, waiting for transfers between devices: 9.66 us -> 17.6 us  [group_exchange(): lax.all_to_all(blocks, GROUP, split_axis=0, concat_axis=0, tiled=True)]
    ppermute x8, waiting for transfers between devices: 35.7 us -> 28.1 us  [group_sum(): return (mine, lax.ppermute(mine.astype(bf16), 'jx', SWAP))]
    ppermute x6, starting transfers between devices: 25 us -> 18 us  [core_shift(): lax.ppermute(block, ('jc', 'ctx'), [((i + step) % size, i) for i in range...]
    ppermute x1, starting transfers between devices: 1.78 us -> 7.4 us  [local(): lax.ppermute(after(ends, near, back, far), axes, from_seq)]
  transfers between devices with their start and end apart: 97 -> 97, of which waited for: 39 -> 35; matrix products, arithmetic and copies ran while one was open for 8% -> 9% of each run, Pallas kernels for 16% -> 15%
where the time goes in v10:
time: 531 us; the launch traced here: 521 us
  starting transfers between devices  186 us (35%)
  waiting for transfers between devices  166 us (31%)
  Pallas kernels  95.6 us (18%)
  other arithmetic  37.2 us (7%)
  local copies, waits for them, and re-layouts  33.2 us (6%)
    pallas_call x24, Pallas kernels, call(): pl.pallas_call(kernel, out_shape=[jax.ShapeDtypeStruct(shape, kind) for s...  95.6 us
    ppermute x30, starting transfers between devices, rotate(): lax.ppermute(block, axis, [((i + step) % size, i) for i in range(size)])  66.3 us
    ppermute x30, waiting for transfers between devices, rotate(): lax.ppermute(block, axis, [((i + step) % size, i) for i in range(size)])  56.8 us
    ppermute x8, waiting for transfers between devices, group_sum(): return (mine, lax.ppermute(mine.astype(bf16), 'jx', SWAP))  28.1 us
    unnamed x156, local copies, waits for them, and re-layouts  20.7 us
    ppermute x6, starting transfers between devices, core_shift(): lax.ppermute(block, ('jc', 'ctx'), [((i + step) % size, i) for i in range...  18 us
    all_to_all x4, starting transfers between devices, slot_exchange(): return lax.all_to_all(blocks, DP, split_axis=0, concat_axis=0, tiled=True)  17.9 us
    all_to_all x3, waiting for transfers between devices, group_exchange(): lax.all_to_all(blocks, GROUP, split_axis=0, concat_axis=0, tiled=True)  17.6 us
  transfers between devices with their start and end apart: 97, of which 35 were waited for; matrix products, arithmetic and copies ran while one was open for 9% of the time, Pallas kernels for 15%

profile of v10, /device:TPU:0, one launch (start us, length us, event | category | flops | bytes accessed | tf_op | source)
XLA Modules:
  0.0 520.7 jit_solution(1515475673719296991)
XLA Ops:
  12.4 6.8 %all-to-all-start = ((bf16[4,1,192,96]{3,2,1,0:T(8,128)(2,1)}), bf16[4,1,192,96]{3,2,1,0:T(8,128)(2,1)S(1)}, u32[]{:S(2)}, u32[]{:S(2)}) async-start(bf16[4,1,192,96]{3,2,1,0:T(8,128)(2,1)} %shard_map.152), calls=%async_computation | async-start | bytes 393216 | tf_op jit(solution)/shard_map/all_to_all | solution.py:174
  30.5 12.4 %collective-permute-start.11 = (bf16[192,384]{1,0:T(8,128)(2,1)S(1)}, bf16[192,384]{1,0:T(8,128)(2,1)S(1)}, u32[]{:S(2)}, u32[]{:S(2)}) collective-permute-start(bf16[192,384]{1,0:T(8,128)(2,1)S(1)} %shard_map.153.refs_0_), channel_id=1, source_target_pairs={{1,0},{2,1},{3,2},{0,3},{5,4},{6,5},{7,6},{4,7},{9,8},{10,9},{11,1... | collective-permute-start | bytes 442376 | tf_op jit(solution)/shard_map/ppermute | solution.py:70
  57.7 9.7 %all-to-all-done.1.blocks_ref = bf16[4,5,192,96]{3,2,1,0:T(8,128)(2,1)S(1)} async-done(((bf16[4,5,192,96]{3,2,1,0:T(8,128)(2,1)}), bf16[4,5,192,96]{3,2,1,0:T(8,128)(2,1)S(1)}, u32[]{:S(2)}, u32[]{:S(2)}) %all-to-all-start.1) | async-done | bytes 737312 | tf_op jit(solution)/shard_map/all_to_all | solution.py:174
  74.8 6.5 %shard_map.155 = (bf16[768,768]{1,0:T(8,128)(2,1)}, bf16[512,576]{1,0:T(8,128)(2,1)}, f32[512,128]{1,0:T(8,128)S(1)}, bf16[512,192]{1,0:T(8,128)(2,1)S(1)}, f32[...) custom-call(s32[3]{0:T(128)S(1)} %pad_add_fusion.place_ref, f32[8,512]{1,0:T(8,128)S(1)} %pad.13.row_ref, ...), custom_call_target="tpu_custom_call" | custom-call | tf_op jit(solution)/shard_map/pallas_call | solution.py:320
  88.5 9.1 %collective-permute-done.19.refs_1_ = bf16[256,768]{1,0:T(8,128)(2,1)S(1)} collective-permute-done((bf16[256,768]{1,0:T(8,128)(2,1)S(1)}, bf16[256,768]{1,0:T(8,128)(2,1)S(1)}, u32[]{:S(2)}, u32[]{:S(2)}) %collective-permute-start.19) | collective-permute-done | bytes 393248 | tf_op jit(solution)/shard_map/ppermute | solution.py:677
  114.1 7.1 %collective-permute-done.25.refs_2_ = bf16[192,384]{1,0:T(8,128)(2,1)S(1)} collective-permute-done((bf16[192,384]{1,0:T(8,128)(2,1)S(1)}, bf16[192,384]{1,0:T(8,128)(2,1)S(1)}, u32[]{:S(2)}, u32[]{:S(2)}) %collective-permute-start.25) | collective-permute-done | bytes 147488 | tf_op jit(solution)/shard_map/ppermute | solution.py:70
  134.7 6.9 %collective-permute-done.30.refs_1_ = bf16[256,768]{1,0:T(8,128)(2,1)S(1)} collective-permute-done((bf16[256,768]{1,0:T(8,128)(2,1)S(1)}, bf16[256,768]{1,0:T(8,128)(2,1)S(1)}, u32[]{:S(2)}, u32[]{:S(2)}) %collective-permute-start.30) | collective-permute-done | bytes 393248 | tf_op jit(solution)/shard_map/ppermute | solution.py:677
  175.3 6.9 %collective-permute-start.45 = (f32[128,768]{1,0:T(8,128)}, f32[128,768]{1,0:T(8,128)}, u32[]{:S(2)}, u32[]{:S(2)}) collective-permute-start(f32[128,768]{1,0:T(8,128)} %collective-permute-done.39), channel_id=1, source_target_pairs={{0,8},{8,0},{1,9},{9,1},{2,10},{10,2},{3,11},{11,3},{4,12},{12,4},... | collective-permute-start | bytes 1179656 | tf_op jit(solution)/shard_map/ppermute | solution.py:74
  201.6 7.5 %shard_map.164 = (f32[256,768]{1,0:T(8,128)}, bf16[256,768]{1,0:T(8,128)(2,1)S(1)}, f32[8,768]{1,0:T(8,128)S(1)}, f32[4,2,192,384]{3,2,1,0:T(8,128)}, bf16[4,2,192,384]{3,2,1,0:T(8,128)(2,1)}) custom-call(s32[3]{0:T(128)S(1)} %pad_add_fusion.place_ref, bf16[256,768]{1,0:T(8,128)(2,1)S(1)} %pad_maximum_fusion.6.own_gy_ref, ...), custom_call_target="tpu_custom_call" | custom-call | tf_op jit(solution)/shard_map/pallas_call | solution.py:320
  234.7 8.5 %shard_map.166 = (f32[256,768]{1,0:T(8,128)}, bf16[256,768]{1,0:T(8,128)(2,1)S(1)}, f32[8,576]{1,0:T(8,128)S(1)}, f32[4,192,384]{2,1,0:T(8,128)}, bf16[4,192,384]{2,1,0:T(8,128)(2,1)}) custom-call(s32[3]{0:T(128)S(1)} %pad_add_fusion.place_ref, f32[8,512]{1,0:T(8,128)S(1)} %pad.13.row_ref, f32[512,128]{1,0:T(8,128)S(1)} %pad.14.column_ref, ...), custom_call_target="tpu_custom_call" | custom-call | tf_op jit(solution)/shard_map/pallas_call | solution.py:320
  258.1 7.1 %collective-permute-done.52 = bf16[4,192,384]{2,1,0:T(8,128)(2,1)S(1)} collective-permute-done((bf16[4,192,384]{2,1,0:T(8,128)(2,1)}, bf16[4,192,384]{2,1,0:T(8,128)(2,1)S(1)}, u32[]{:S(2)}, u32[]{:S(2)}) %collective-permute-start.52) | collective-permute-done | bytes 589856 | tf_op jit(solution)/shard_map/ppermute | solution.py:232
  276.0 7.4 %shard_map.168 = (f32[256,768]{1,0:T(8,128)}, bf16[256,768]{1,0:T(8,128)(2,1)S(1)}, f32[8,768]{1,0:T(8,128)S(1)}, f32[4,2,192,384]{3,2,1,0:T(8,128)}, bf16[4,2,192,384]{3,2,1,0:T(8,128)(2,1)}) custom-call(s32[3]{0:T(128)S(1)} %pad_add_fusion.place_ref, bf16[256,768]{1,0:T(8,128)(2,1)S(1)} %get-tuple-element.194.own_gy_ref, ...), custom_call_target="tpu_custom_call" | custom-call | tf_op jit(solution)/shard_map/pallas_call | solution.py:320
  286.9 7.3 %collective-permute-done.56 = bf16[2,192,384]{2,1,0:T(8,128)(2,1)S(1)} collective-permute-done((bf16[2,192,384]{2,1,0:T(8,128)(2,1)S(1)}, bf16[2,192,384]{2,1,0:T(8,128)(2,1)S(1)}, u32[]{:S(2)}, u32[]{:S(2)}) %collective-permute-start.56) | collective-permute-done | bytes 294944 | tf_op jit(solution)/shard_map/ppermute | solution.py:70
  299.1 7.1 %collective-permute-start.64 = (bf16[192,384]{1,0:T(8,128)(2,1)S(1)}, bf16[192,384]{1,0:T(8,128)(2,1)S(1)}, u32[]{:S(2)}, u32[]{:S(2)}) collective-permute-start(bf16[192,384]{1,0:T(8,128)(2,1)S(1)} %get-tuple-element.294), channel_id=1, source_target_pairs={{2,0},{3,1},{0,2},{1,3},{6,4},{7,5},{4,6},{5,7},{10,8},{11,9},{8,1... | collective-permute-start | bytes 442376 | tf_op jit(solution)/shard_map/ppermute | solution.py:70
  326.0 8.4 %shard_map.170 = (f32[256,768]{1,0:T(8,128)}, bf16[256,768]{1,0:T(8,128)(2,1)S(1)}, f32[8,576]{1,0:T(8,128)S(1)}, f32[4,192,384]{2,1,0:T(8,128)}, bf16[4,192,384]{2,1,0:T(8,128)(2,1)}) custom-call(s32[3]{0:T(128)S(1)} %pad_add_fusion.place_ref, f32[8,512]{1,0:T(8,128)S(1)} %pad.13.row_ref, f32[512,128]{1,0:T(8,128)S(1)} %pad.14.column_ref, ...), custom_call_target="tpu_custom_call" | custom-call | tf_op jit(solution)/shard_map/pallas_call | solution.py:320
  335.3 7.5 %collective-permute-start.68 = (bf16[2,192,384]{2,1,0:T(8,128)(2,1)}, bf16[2,192,384]{2,1,0:T(8,128)(2,1)S(1)}, u32[]{:S(2)}, u32[]{:S(2)}) collective-permute-start(bf16[2,192,384]{2,1,0:T(8,128)(2,1)} %get-tuple-element.279), channel_id=1, source_target_pairs={{2,0},{3,1},{0,2},{1,3},{6,4},{7,5},{4,6},{5,7},{10,8},{11,9},{8,1... | collective-permute-start | bytes 884744 | tf_op jit(solution)/shard_map/ppermute | solution.py:70
  350.2 7.4 %collective-permute-done.68 = bf16[2,192,384]{2,1,0:T(8,128)(2,1)S(1)} collective-permute-done((bf16[2,192,384]{2,1,0:T(8,128)(2,1)}, bf16[2,192,384]{2,1,0:T(8,128)(2,1)S(1)}, u32[]{:S(2)}, u32[]{:S(2)}) %collective-permute-start.68) | collective-permute-done | bytes 294944 | tf_op jit(solution)/shard_map/ppermute | solution.py:70
  357.7 7.0 %collective-permute-done.67 = bf16[2,192,384]{2,1,0:T(8,128)(2,1)} collective-permute-done((bf16[2,192,384]{2,1,0:T(8,128)(2,1)}, bf16[2,192,384]{2,1,0:T(8,128)(2,1)}, u32[]{:S(2)}, u32[]{:S(2)}) %collective-permute-start.67) | collective-permute-done | bytes 294944 | tf_op jit(solution)/shard_map/ppermute | solution.py:70
  379.1 10.4 %collective-permute-done.82 = f32[2,12,768]{2,1,0:T(8,128)S(1)} collective-permute-done((f32[2,12,768]{2,1,0:T(8,128)S(1)}, f32[2,12,768]{2,1,0:T(8,128)S(1)}, u32[]{:S(2)}, u32[]{:S(2)}) %collective-permute-start.82) | collective-permute-done | bytes 73760 | tf_op jit(solution)/shard_map/ppermute | solution.py:303
  389.8 7.2 %collective-permute-start.84 = (f32[2,3,768]{2,0,1:T(2,128)S(1)}, f32[2,3,768]{2,0,1:T(2,128)S(1)}, u32[]{:S(2)}, u32[]{:S(2)}) collective-permute-start(f32[2,3,768]{2,0,1:T(2,128)S(1)} %get-tuple-element.306), channel_id=1, source_target_pairs={{2,0},{3,1},{0,2},{1,3},{6,4},{7,5},{4,6},{5,7},{10,8},{11,9},{8,1... | collective-permute-start | bytes 55304 | tf_op jit(solution)/shard_map/ppermute | solution.py:70
  461.2 7.4 %collective-permute-start.77 = (f32[2,128,768]{2,1,0:T(8,128)}, f32[2,128,768]{2,1,0:T(8,128)}, u32[]{:S(2)}, u32[]{:S(2)}) collective-permute-start(f32[2,128,768]{2,1,0:T(8,128)} %fusion.2), channel_id=1, source_target_pairs={{0,0},{8,1},{4,2},{12,3},{1,4},{9,5},{5,6},{13,7},{2,8},{10,9},{6,... | collective-permute-start | bytes 2359304 | tf_op jit(solution)/shard_map/ppermute | solution.py:1100
  468.6 11.9 %shard_map.173 = bf16[768,768]{1,0:T(8,128)(2,1)} custom-call(s32[3]{0:T(128)S(1)} %pad_add_fusion.place_ref, bf16[768,768]{1,0:T(8,128)(2,1)} %copy-done.17, bf16[192,768]{1,0:T(8,128)(2,1)S(1)} %fusion.5.gram0_ref, bf16[192,768]{1,0:T(8,128)(2,1)S(1)} %collective-permute-done.74.gram1_ref, bf16[192,768]{1,0:T(8,128)(2,1)S(1)} %copy-done.24, ...), custom_call_target="tpu_custom_call" | custom-call | tf_op jit(solution)/shard_map/pallas_call | solution.py:320
  480.5 8.0 %all-to-all-done.5.blocks_ref = bf16[4,6,96,192]{3,2,1,0:T(8,128)(2,1)S(1)} async-done(((bf16[4,6,96,192]{3,2,1,0:T(8,128)(2,1)}), bf16[4,6,96,192]{3,2,1,0:T(8,128)(2,1)S(1)}, u32[]{:S(2)}, u32[]{:S(2)}) %all-to-all-start.5) | async-done | bytes 884768 | tf_op jit(solution)/shard_map/all_to_all | solution.py:174
  497.9 12.0 %collective-permute-done.89 = f32[2,3,768]{2,0,1:T(2,128)S(1)} collective-permute-done((f32[2,3,768]{2,0,1:T(2,128)S(1)}, f32[2,3,768]{2,0,1:T(2,128)S(1)}, u32[]{:S(2)}, u32[]{:S(2)}) %collective-permute-start.89) | collective-permute-done | bytes 18464 | tf_op jit(solution)/shard_map/ppermute | solution.py:316
  (465 shorter events, 320.9 us)
Async XLA Ops:
  43.6 24.9 %collective-permute-start.14 = (bf16[192,384]{1,0:T(8,128)(2,1)S(1)}, bf16[192,384]{1,0:T(8,128)(2,1)}, u32[]{:S(2)}, u32[]{:S(2)}) collective-permute-start(bf16[192,384]{1,0:T(8,128)(2,1)S(1)} %shard_map.153.refs_0_), channel_id=1, source_target_pairs={{0,16},{16,0},{1,17},{17,1},{2,18},{18,2},{3,19},{19,3},{4,20},{20... | collective-permute-start | bytes 442376 | tf_op jit(solution)/shard_map/ppermute | solution.py:196
  86.1 20.7 %collective-permute-start.27 = (bf16[3,2,192,384]{3,2,1,0:T(8,128)(2,1)S(1)}, bf16[3,2,192,384]{3,2,1,0:T(8,128)(2,1)S(1)}, u32[]{:S(2)}, u32[]{:S(2)}) collective-permute-start(bf16[3,2,192,384]{3,2,1,0:T(8,128)(2,1)S(1)} %pad_maximum_fusion), channel_id=1, source_target_pairs={{0,16},{16,0},{1,17},{17,1},{2,18},{18,2},{3,19},{19,3},{4,20},{20... | collective-permute-start | bytes 2654216 | tf_op jit(solution)/shard_map/ppermute | solution.py:209
  100.2 21.0 %collective-permute-start.20 = (bf16[256,768]{1,0:T(8,128)(2,1)S(1)}, bf16[256,768]{1,0:T(8,128)(2,1)S(1)}, u32[]{:S(2)}, u32[]{:S(2)}) collective-permute-start(bf16[256,768]{1,0:T(8,128)(2,1)S(1)} %get-tuple-element.134.own_c_ref), channel_id=1, source_target_pairs={{0,4},{4,0},{1,5},{5,1},{2,6},{6,2},{3,7},{7,3},{8,12},{12,8},{9,1... | collective-permute-start | bytes 1179656 | tf_op jit(solution)/shard_map/ppermute | solution.py:672
  133.1 20.3 %collective-permute-start.35 = (bf16[4,192,384]{2,1,0:T(8,128)(2,1)S(1)}, bf16[4,192,384]{2,1,0:T(8,128)(2,1)S(1)}, u32[]{:S(2)}, u32[]{:S(2)}) collective-permute-start(bf16[4,192,384]{2,1,0:T(8,128)(2,1)S(1)} %pad_maximum_fusion.4), channel_id=1, source_target_pairs={{0,16},{16,0},{1,17},{17,1},{2,18},{18,2},{3,19},{19,3},{4,20},{20... | collective-permute-start | bytes 1769480 | tf_op jit(solution)/shard_map/ppermute | solution.py:939
  160.7 22.1 %collective-permute-start.43 = (bf16[3,2,192,384]{3,2,1,0:T(8,128)(2,1)S(1)}, bf16[3,2,192,384]{3,2,1,0:T(8,128)(2,1)S(1)}, u32[]{:S(2)}, u32[]{:S(2)}) collective-permute-start(bf16[3,2,192,384]{3,2,1,0:T(8,128)(2,1)S(1)} %pad_maximum_fusion.1), channel_id=1, source_target_pairs={{0,16},{16,0},{1,17},{17,1},{2,18},{18,2},{3,19},{19,3},{4,20},{20... | collective-permute-start | bytes 2654216 | tf_op jit(solution)/shard_map/ppermute | solution.py:209
  175.3 34.4 %collective-permute-start.45 = (f32[128,768]{1,0:T(8,128)}, f32[128,768]{1,0:T(8,128)}, u32[]{:S(2)}, u32[]{:S(2)}) collective-permute-start(f32[128,768]{1,0:T(8,128)} %collective-permute-done.39), channel_id=1, source_target_pairs={{0,8},{8,0},{1,9},{9,1},{2,10},{10,2},{3,11},{11,3},{4,12},{12,4},... | collective-permute-start | bytes 1179656 | tf_op jit(solution)/shard_map/ppermute | solution.py:74
  211.8 33.5 %collective-permute-start.49 = (bf16[4,2,192,384]{3,2,1,0:T(8,128)(2,1)}, bf16[4,2,192,384]{3,2,1,0:T(8,128)(2,1)}, u32[]{:S(2)}, u32[]{:S(2)}) collective-permute-start(bf16[4,2,192,384]{3,2,1,0:T(8,128)(2,1)} %get-tuple-element.187), channel_id=1, source_target_pairs={{0,16},{16,0},{1,17},{17,1},{2,18},{18,2},{3,19},{19,3},{4,20},{20... | collective-permute-start | bytes 3538952 | tf_op jit(solution)/shard_map/ppermute | solution.py:232
  228.8 24.8 %all-to-all-start.2 = ((bf16[8,96,768]{2,1,0:T(8,128)(2,1)}), bf16[8,96,768]{2,1,0:T(8,128)(2,1)S(1)}, u32[]{:S(2)}, u32[]{:S(2)}) async-start(bf16[8,96,768]{2,1,0:T(8,128)(2,1)} %fusion.21), calls=%async_computation.2 | async-start | bytes 2359296 | tf_op jit(solution)/shard_map/all_to_all | solution.py:840
  243.6 21.6 %collective-permute-start.52 = (bf16[4,192,384]{2,1,0:T(8,128)(2,1)}, bf16[4,192,384]{2,1,0:T(8,128)(2,1)S(1)}, u32[]{:S(2)}, u32[]{:S(2)}) collective-permute-start(bf16[4,192,384]{2,1,0:T(8,128)(2,1)} %get-tuple-element.193), channel_id=1, source_target_pairs={{0,16},{16,0},{1,17},{17,1},{2,18},{18,2},{3,19},{19,3},{4,20},{20... | collective-permute-start | bytes 1769480 | tf_op jit(solution)/shard_map/ppermute | solution.py:232
  273.9 20.3 %collective-permute-start.56 = (bf16[2,192,384]{2,1,0:T(8,128)(2,1)S(1)}, bf16[2,192,384]{2,1,0:T(8,128)(2,1)S(1)}, u32[]{:S(2)}, u32[]{:S(2)}) collective-permute-start(bf16[2,192,384]{2,1,0:T(8,128)(2,1)S(1)} %get-tuple-element.281), channel_id=1, source_target_pairs={{3,0},{0,1},{1,2},{2,3},{7,4},{4,5},{5,6},{6,7},{11,8},{8,9},{9,10... | collective-permute-start | bytes 884744 | tf_op jit(solution)/shard_map/ppermute | solution.py:70
  274.3 21.5 %collective-permute-start.55 = (bf16[256,768]{1,0:T(8,128)(2,1)S(1)}, bf16[256,768]{1,0:T(8,128)(2,1)S(1)}, u32[]{:S(2)}, u32[]{:S(2)}) collective-permute-start(bf16[256,768]{1,0:T(8,128)(2,1)S(1)} %fusion.10), channel_id=1, source_target_pairs={{0,8},{8,0},{1,9},{9,1},{2,10},{10,2},{3,11},{11,3},{4,12},{12,4},... | collective-permute-start | bytes 1179656 | tf_op jit(solution)/shard_map/ppermute | solution.py:677
  294.3 28.0 %collective-permute-start.65 = (bf16[4,2,192,384]{3,2,1,0:T(8,128)(2,1)}, bf16[4,2,192,384]{3,2,1,0:T(8,128)(2,1)}, u32[]{:S(2)}, u32[]{:S(2)}) collective-permute-start(bf16[4,2,192,384]{3,2,1,0:T(8,128)(2,1)} %get-tuple-element.211), channel_id=1, source_target_pairs={{0,16},{16,0},{1,17},{17,1},{2,18},{18,2},{3,19},{19,3},{4,20},{20... | collective-permute-start | bytes 3538952 | tf_op jit(solution)/shard_map/ppermute | solution.py:232
  335.3 22.4 %collective-permute-start.68 = (bf16[2,192,384]{2,1,0:T(8,128)(2,1)}, bf16[2,192,384]{2,1,0:T(8,128)(2,1)S(1)}, u32[]{:S(2)}, u32[]{:S(2)}) collective-permute-start(bf16[2,192,384]{2,1,0:T(8,128)(2,1)} %get-tuple-element.279), channel_id=1, source_target_pairs={{2,0},{3,1},{0,2},{1,3},{6,4},{7,5},{4,6},{5,7},{10,8},{11,9},{8,1... | collective-permute-start | bytes 884744 | tf_op jit(solution)/shard_map/ppermute | solution.py:70
  342.8 21.8 %collective-permute-start.67 = (bf16[2,192,384]{2,1,0:T(8,128)(2,1)}, bf16[2,192,384]{2,1,0:T(8,128)(2,1)}, u32[]{:S(2)}, u32[]{:S(2)}) collective-permute-start(bf16[2,192,384]{2,1,0:T(8,128)(2,1)} %get-tuple-element.280), channel_id=1, source_target_pairs={{1,0},{2,1},{3,2},{0,3},{5,4},{6,5},{7,6},{4,7},{9,8},{10,9},{11,1... | collective-permute-start | bytes 884744 | tf_op jit(solution)/shard_map/ppermute | solution.py:70
  343.3 21.4 %collective-permute-start.66 = (bf16[2,192,384]{2,1,0:T(8,128)(2,1)}, bf16[2,192,384]{2,1,0:T(8,128)(2,1)}, u32[]{:S(2)}, u32[]{:S(2)}) collective-permute-start(bf16[2,192,384]{2,1,0:T(8,128)(2,1)} %get-tuple-element.278), channel_id=1, source_target_pairs={{3,0},{0,1},{1,2},{2,3},{7,4},{4,5},{5,6},{6,7},{11,8},{8,9},{9,10... | collective-permute-start | bytes 884744 | tf_op jit(solution)/shard_map/ppermute | solution.py:70
  345.9 30.9 %collective-permute-start.78 = (bf16[4,192,384]{2,1,0:T(8,128)(2,1)}, bf16[4,192,384]{2,1,0:T(8,128)(2,1)}, u32[]{:S(2)}, u32[]{:S(2)}) collective-permute-start(bf16[4,192,384]{2,1,0:T(8,128)(2,1)} %get-tuple-element.231), channel_id=1, source_target_pairs={{0,16},{16,0},{1,17},{17,1},{2,18},{18,2},{3,19},{19,3},{4,20},{20... | collective-permute-start | bytes 1769480 | tf_op jit(solution)/shard_map/ppermute | solution.py:232
  349.5 22.1 %collective-permute-start.70 = (bf16[256,768]{1,0:T(8,128)(2,1)}, bf16[256,768]{1,0:T(8,128)(2,1)S(1)}, u32[]{:S(2)}, u32[]{:S(2)}) collective-permute-start(bf16[256,768]{1,0:T(8,128)(2,1)} %get-tuple-element.259), channel_id=1, source_target_pairs={{0,8},{8,0},{1,9},{9,1},{2,10},{10,2},{3,11},{11,3},{4,12},{12,4},... | collective-permute-start | bytes 1179656 | tf_op jit(solution)/shard_map/ppermute | solution.py:677
  367.3 35.5 %all-to-all-start.3 = ((bf16[8,192,384]{2,1,0:T(8,128)(2,1)}), bf16[8,192,384]{2,1,0:T(8,128)(2,1)}, u32[]{:S(2)}, u32[]{:S(2)}) async-start(bf16[8,192,384]{2,1,0:T(8,128)(2,1)} %bitcast.194), calls=%async_computation.3 | async-start | bytes 2359296 | tf_op jit(solution)/shard_map/all_to_all | solution.py:840
  397.7 20.2 %collective-permute-start.80 = (bf16[192,384]{1,0:T(8,128)(2,1)S(1)}, bf16[192,384]{1,0:T(8,128)(2,1)S(1)}, u32[]{:S(2)}, u32[]{:S(2)}) collective-permute-start(bf16[192,384]{1,0:T(8,128)(2,1)S(1)} %get-tuple-element.291), channel_id=1, source_target_pairs={{1,0},{2,1},{3,2},{0,3},{5,4},{6,5},{7,6},{4,7},{9,8},{10,9},{11,1... | collective-permute-start | bytes 442376 | tf_op jit(solution)/shard_map/ppermute | solution.py:70
  429.0 25.3 %all-to-all-start.4 = ((bf16[8,192,384]{2,1,0:T(8,128)(2,1)}), bf16[8,192,384]{2,1,0:T(8,128)(2,1)}, u32[]{:S(2)}, u32[]{:S(2)}) async-start(bf16[8,192,384]{2,1,0:T(8,128)(2,1)} %bitcast.195), calls=%async_computation.4 | async-start | bytes 2359296 | tf_op jit(solution)/shard_map/all_to_all | solution.py:840
  454.3 34.2 %all-to-all-start.5 = ((bf16[4,6,96,192]{3,2,1,0:T(8,128)(2,1)}), bf16[4,6,96,192]{3,2,1,0:T(8,128)(2,1)S(1)}, u32[]{:S(2)}, u32[]{:S(2)}) async-start(bf16[4,6,96,192]{3,2,1,0:T(8,128)(2,1)} %shard_map.174), calls=%async_computation.5 | async-start | bytes 2359296 | tf_op jit(solution)/shard_map/all_to_all | solution.py:174
  457.8 39.1 %collective-permute-start.86 = (bf16[2,192,384]{2,1,0:T(8,128)(2,1)}, bf16[2,192,384]{2,1,0:T(8,128)(2,1)}, u32[]{:S(2)}, u32[]{:S(2)}) collective-permute-start(bf16[2,192,384]{2,1,0:T(8,128)(2,1)} %get-tuple-element.302), channel_id=1, source_target_pairs={{3,3},{19,7},{7,11},{23,15},{11,19},{27,23},{15,27},{31,31}} | collective-permute-start | bytes 884744 | tf_op jit(solution)/shard_map/ppermute | solution.py:128
  461.2 50.4 %collective-permute-start.77 = (f32[2,128,768]{2,1,0:T(8,128)}, f32[2,128,768]{2,1,0:T(8,128)}, u32[]{:S(2)}, u32[]{:S(2)}) collective-permute-start(f32[2,128,768]{2,1,0:T(8,128)} %fusion.2), channel_id=1, source_target_pairs={{0,0},{8,1},{4,2},{12,3},{1,4},{9,5},{5,6},{13,7},{2,8},{10,9},{6,... | collective-permute-start | bytes 2359304 | tf_op jit(solution)/shard_map/ppermute | solution.py:1100
  488.5 28.8 %all-to-all-start.6 = ((bf16[8,96,768]{2,1,0:T(8,128)(2,1)}), bf16[8,96,768]{2,1,0:T(8,128)(2,1)S(1)}, u32[]{:S(2)}, u32[]{:S(2)}) async-start(bf16[8,96,768]{2,1,0:T(8,128)(2,1)} %bitcast.196), calls=%async_computation.6 | async-start | bytes 2359296 | tf_op jit(solution)/shard_map/all_to_all | solution.py:840
  (145 other events, 1356.8 us)

commit v11 on v10

--- a/solution.py
+++ b/solution.py
@@ -968,7 +968,7 @@
         grad_hidden = x_join(lax.ppermute(out_grad[0], axes, to_seq))
         hidden_out = send_back(last_hidden())
         gy_own = grad_hidden.astype(bf16)
-    attn_half = mlp_half = None
+    attn_half = None
 
     mat_list = [None] * LAYERS
     sum_list = [None] * LAYERS
@@ -980,6 +980,7 @@
         if relative and attn_half is not None:
             gy_own, attn_half = lax.optimization_barrier((gy_own, attn_half))
             hidden = last_hidden(gy_own)
+            attn_part = ctx_sum(attn_half)
         gy_other = core_swap(gy_own)
         if relative and attn_half is None:
             gy_other, moved_grad = lax.optimization_barrier((gy_other, moved_grad))
@@ -988,12 +989,13 @@
             place, gy_own, gy_other, c_own, c_other, preact, act, w_mlp, relative
         )
         if relative:
+            mlp_mine, mlp_give = mlp_grads
+            mlp_recv = lax.ppermute(mlp_give, "g", SWAP)
             if attn_half is None:
                 mine, grad_hidden = lax.optimization_barrier((mine, grad_hidden))
             else:
-                mine, hidden, wide_part = lax.optimization_barrier((mine, hidden, mlp_part))
-                attn_part = ctx_sum(attn_half)
-            mlp_half = half_sum(*mlp_grads)
+                mine, hidden, attn_part = lax.optimization_barrier((mine, hidden, attn_part))
+                wide_part = ctx_sum(late_half[0] + after(late_half[1], mine).astype(f32))
         mine, recv = group_sum(mine, give)
         grad_middle, gb_own, mid_sums = norm_back_stage(
             vec_rows, layer, 2, grad_hidden, mine, recv, middle
@@ -1006,11 +1008,7 @@
             ).reshape(D, D)
         gb_other = core_swap(gb_own)
         if relative and layer < LAYERS - 1:
-            gb_other, attn_part, mlp_half = lax.optimization_barrier(
-                (gb_other, attn_part, mlp_half)
-            )
-            parts[layer + 1] = (attn_part, wide_part)
-            mlp_part = ctx_sum(mlp_half)
+            gb_other, wide_part = lax.optimization_barrier((gb_other, wide_part))
         mine, give, qkv_sums, *attn_grads = attend_back_stage(
             place,
             row_info,
@@ -1027,9 +1025,11 @@
         )
         if relative:
             if layer == LAYERS - 1:
-                mine, mlp_half, moment_slots = lax.optimization_barrier(
-                    (mine, mlp_half, moment_slots)
-                )
+                mine, moment_slots = lax.optimization_barrier((mine, moment_slots))
+                late_half = (mlp_mine, mlp_recv)
+            else:
+                parts[layer + 1] = (attn_part, wide_part)
+                mlp_half = mlp_mine + after(mlp_recv, give).astype(f32)
                 mlp_part = ctx_sum(mlp_half)
             attn_half = half_sum(*attn_grads)
         else:
@@ -1068,15 +1068,17 @@
     vec_terms = jnp.concatenate(
         [shared[:, 0:4], placed[:, 0:2], shared[:, 4:6], placed[:, 2:6]], axis=1
     )
-    vec_sums = sum_vectors(vec_terms)
     if relative:
         attn_low = attn_half.astype(bf16)
         attn_sums = [rotate(attn_low[step], "ctx", -step) for step in (1, 3, 2)]
         wide_low = jnp.concatenate([parts[1][1], mlp_part]).astype(bf16)
-        wide_slots = slot_exchange(jnp.repeat(after(wide_low, give), 2, axis=0))
-        wide_slots, grad_hidden = lax.optimization_barrier((wide_slots, grad_hidden))
+        wide_low = after(wide_low, attn_half)
+        wide_slots = slot_exchange(jnp.repeat(wide_low, 2, axis=0))
+        wide_slots, grad_hidden, attn_sums = lax.optimization_barrier(
+            (wide_slots, grad_hidden, attn_sums)
+        )
         x_wide, gram_blocks = slot_gram(place, wide_slots, moment_slots)
-        attn_sums, unused = lax.optimization_barrier((attn_sums, gram_blocks))
+        vec_sums = sum_group(sum_vectors(after(vec_terms, gram_blocks)))
         attn_part = attn_half[0] + sum(block.astype(f32) for block in attn_sums)
         total = gram_blocks[0].astype(f32)
         for step in (1, 3, 2):
@@ -1093,7 +1095,6 @@
         blocks, outs = grad_blocks(
             [attn_part, parts[1][0]], [mlp_part, parts[1][1]], dp_rows, square_slots, near, back, far
         )
-        ortho_mine, blocks = lax.optimization_barrier((ortho_mine, blocks))
         returned = slot_exchange(ortho_mine.reshape(dp_size, dp_rows, D))
         ends = jnp.stack([hidden, grad_hidden])
         ends = lax.dynamic_slice_in_dim(ends, x_index * tokens_dev, tokens_dev, axis=1)
@@ -1102,6 +1103,7 @@
         ortho = ortho.reshape(weights.shape).astype(f32)
         grad_mats, moment_new = grad_rows(place, blocks, outs, mat_momentum)
     else:
+        vec_sums = sum_group(sum_vectors(vec_terms))
         cols_dev = weights.shape[3]
         grad_list, moment_list, low_list = [], [], []
         for layer in range(LAYERS):
@@ -1138,7 +1140,7 @@
         grad_mats = jnp.stack(grad_list).reshape(weights.shape)
         moment_new = jnp.stack(moment_list).reshape(weights.shape)
     grad_vecs = lax.dynamic_slice_in_dim(
-        sum_group(vec_sums), dp_index * vectors.shape[2], vectors.shape[2], axis=2
+        vec_sums, dp_index * vectors.shape[2], vectors.shape[2], axis=2
     )
     factor = jnp.array([0.2 * math.sqrt(D), 0.2 * math.sqrt(FF), 0.2 * math.sqrt(FF)], f32)
     weights_new = weights * (1.0 - matrix_rate * matrix_decay) - matrix_rate * (

time: 531 us -> 522 us (0.983)
  other arithmetic: 37.2 us -> 28 us
  waiting for transfers between devices: 166 us -> 173 us
    ppermute x8, waiting for transfers between devices: 28.1 us -> 39.6 us  [group_sum(): return (mine, lax.ppermute(mine.astype(bf16), 'jx', SWAP))]
    ppermute x1, waiting for transfers between devices: 12 us -> 2.59 us  [sum_group(): return total + lax.ppermute(total, 'jx', SWAP)]
    ppermute x0 -> x2, waiting for transfers between devices: none -> 8.29 us  [local(): mlp_recv = lax.ppermute(mlp_give, 'g', SWAP)]
    ppermute x1, waiting for transfers between devices: 10.4 us -> 3.11 us  [sum_vectors(): terms = terms + lax.ppermute(terms, 'g', SWAP)]
    all_to_all x4, waiting for transfers between devices: 5.23 us -> 12.2 us  [slot_exchange(): return lax.all_to_all(blocks, DP, split_axis=0, concat_axis=0, tiled=True)]
    ppermute x4 -> x2, waiting for transfers between devices: 11.1 us -> 9.17 us  [half_sum(): return mine + lax.ppermute(give, 'g', SWAP).astype(f32)]
    unnamed x156 -> x160, local copies, waits for them, and re-layouts: 20.7 us -> 19.9 us
  transfers between devices with their start and end apart: 97 -> 97, of which waited for: 35 -> 34; matrix products, arithmetic and copies ran while one was open for 9% -> 7% of each run, Pallas kernels for 15% -> 16%
where the time goes in v11:
time: 522 us; the launch traced here: 512 us
  starting transfers between devices  183 us (35%)
  waiting for transfers between devices  173 us (33%)
  Pallas kernels  95.5 us (18%)
  local copies, waits for them, and re-layouts  30 us (6%)
  other arithmetic  28 us (5%)
    pallas_call x24, Pallas kernels, call(): pl.pallas_call(kernel, out_shape=[jax.ShapeDtypeStruct(shape, kind) for s...  95.5 us
    ppermute x30, starting transfers between devices, rotate(): lax.ppermute(block, axis, [((i + step) % size, i) for i in range(size)])  63.1 us
    ppermute x30, waiting for transfers between devices, rotate(): lax.ppermute(block, axis, [((i + step) % size, i) for i in range(size)])  59.7 us
    ppermute x8, waiting for transfers between devices, group_sum(): return (mine, lax.ppermute(mine.astype(bf16), 'jx', SWAP))  39.6 us
    ppermute x6, starting transfers between devices, core_shift(): lax.ppermute(block, ('jc', 'ctx'), [((i + step) % size, i) for i in range...  20.4 us
    unnamed x160, local copies, waits for them, and re-layouts  19.9 us
    all_to_all x4, starting transfers between devices, slot_exchange(): return lax.all_to_all(blocks, DP, split_axis=0, concat_axis=0, tiled=True)  18 us
    all_to_all x3, waiting for transfers between devices, group_exchange(): lax.all_to_all(blocks, GROUP, split_axis=0, concat_axis=0, tiled=True)  17.6 us
  transfers between devices with their start and end apart: 97, of which 34 were waited for; matrix products, arithmetic and copies ran while one was open for 7% of the time, Pallas kernels for 16%

profile of v11, /device:TPU:0, one launch (start us, length us, event | category | flops | bytes accessed | tf_op | source)
XLA Modules:
  0.0 511.8 jit_solution(593722424307714504)
XLA Ops:
  12.4 6.8 %all-to-all-start = ((bf16[4,1,192,96]{3,2,1,0:T(8,128)(2,1)}), bf16[4,1,192,96]{3,2,1,0:T(8,128)(2,1)S(1)}, u32[]{:S(2)}, u32[]{:S(2)}) async-start(bf16[4,1,192,96]{3,2,1,0:T(8,128)(2,1)} %shard_map.152), calls=%async_computation | async-start | bytes 393216 | tf_op jit(solution)/shard_map/all_to_all | solution.py:174
  30.5 12.4 %collective-permute-start.11 = (bf16[192,384]{1,0:T(8,128)(2,1)S(1)}, bf16[192,384]{1,0:T(8,128)(2,1)S(1)}, u32[]{:S(2)}, u32[]{:S(2)}) collective-permute-start(bf16[192,384]{1,0:T(8,128)(2,1)S(1)} %shard_map.153.refs_0_), channel_id=1, source_target_pairs={{1,0},{2,1},{3,2},{0,3},{5,4},{6,5},{7,6},{4,7},{9,8},{10,9},{11,1... | collective-permute-start | bytes 442376 | tf_op jit(solution)/shard_map/ppermute | solution.py:70
  57.7 9.7 %all-to-all-done.1.blocks_ref = bf16[4,5,192,96]{3,2,1,0:T(8,128)(2,1)S(1)} async-done(((bf16[4,5,192,96]{3,2,1,0:T(8,128)(2,1)}), bf16[4,5,192,96]{3,2,1,0:T(8,128)(2,1)S(1)}, u32[]{:S(2)}, u32[]{:S(2)}) %all-to-all-start.1) | async-done | bytes 737312 | tf_op jit(solution)/shard_map/all_to_all | solution.py:174
  74.8 6.5 %shard_map.155 = (bf16[768,768]{1,0:T(8,128)(2,1)}, bf16[512,576]{1,0:T(8,128)(2,1)}, f32[512,128]{1,0:T(8,128)S(1)}, bf16[512,192]{1,0:T(8,128)(2,1)S(1)}, f32[...) custom-call(s32[3]{0:T(128)S(1)} %pad_add_fusion.place_ref, f32[8,512]{1,0:T(8,128)S(1)} %pad.13.row_ref, ...), custom_call_target="tpu_custom_call" | custom-call | tf_op jit(solution)/shard_map/pallas_call | solution.py:320
  88.5 9.1 %collective-permute-done.19.refs_1_ = bf16[256,768]{1,0:T(8,128)(2,1)S(1)} collective-permute-done((bf16[256,768]{1,0:T(8,128)(2,1)S(1)}, bf16[256,768]{1,0:T(8,128)(2,1)S(1)}, u32[]{:S(2)}, u32[]{:S(2)}) %collective-permute-start.19) | collective-permute-done | bytes 393248 | tf_op jit(solution)/shard_map/ppermute | solution.py:677
  114.1 7.1 %collective-permute-done.25.refs_2_ = bf16[192,384]{1,0:T(8,128)(2,1)S(1)} collective-permute-done((bf16[192,384]{1,0:T(8,128)(2,1)S(1)}, bf16[192,384]{1,0:T(8,128)(2,1)S(1)}, u32[]{:S(2)}, u32[]{:S(2)}) %collective-permute-start.25) | collective-permute-done | bytes 147488 | tf_op jit(solution)/shard_map/ppermute | solution.py:70
  134.7 6.9 %collective-permute-done.30.refs_1_ = bf16[256,768]{1,0:T(8,128)(2,1)S(1)} collective-permute-done((bf16[256,768]{1,0:T(8,128)(2,1)S(1)}, bf16[256,768]{1,0:T(8,128)(2,1)S(1)}, u32[]{:S(2)}, u32[]{:S(2)}) %collective-permute-start.30) | collective-permute-done | bytes 393248 | tf_op jit(solution)/shard_map/ppermute | solution.py:677
  175.3 6.9 %collective-permute-start.45 = (f32[128,768]{1,0:T(8,128)}, f32[128,768]{1,0:T(8,128)}, u32[]{:S(2)}, u32[]{:S(2)}) collective-permute-start(f32[128,768]{1,0:T(8,128)} %collective-permute-done.39), channel_id=1, source_target_pairs={{0,8},{8,0},{1,9},{9,1},{2,10},{10,2},{3,11},{11,3},{4,12},{12,4},... | collective-permute-start | bytes 1179656 | tf_op jit(solution)/shard_map/ppermute | solution.py:74
  201.6 7.5 %shard_map.164 = (f32[256,768]{1,0:T(8,128)}, bf16[256,768]{1,0:T(8,128)(2,1)S(1)}, f32[8,768]{1,0:T(8,128)S(1)}, f32[4,2,192,384]{3,2,1,0:T(8,128)}, bf16[4,2,192,384]{3,2,1,0:T(8,128)(2,1)}) custom-call(s32[3]{0:T(128)S(1)} %pad_add_fusion.place_ref, bf16[256,768]{1,0:T(8,128)(2,1)S(1)} %pad_maximum_fusion.6.own_gy_ref, ...), custom_call_target="tpu_custom_call" | custom-call | tf_op jit(solution)/shard_map/pallas_call | solution.py:320
  218.6 6.4 %collective-permute-done.47.recv_ref = bf16[256,768]{1,0:T(8,128)(2,1)S(1)} collective-permute-done((bf16[256,768]{1,0:T(8,128)(2,1)S(1)}, bf16[256,768]{1,0:T(8,128)(2,1)S(1)}, u32[]{:S(2)}, u32[]{:S(2)}) %collective-permute-start.47) | collective-permute-done | bytes 393248 | tf_op jit(solution)/shard_map/ppermute | solution.py:677
  234.5 8.4 %shard_map.166 = (f32[256,768]{1,0:T(8,128)}, bf16[256,768]{1,0:T(8,128)(2,1)S(1)}, f32[8,576]{1,0:T(8,128)S(1)}, f32[4,192,384]{2,1,0:T(8,128)}, bf16[4,192,384]{2,1,0:T(8,128)(2,1)}) custom-call(s32[3]{0:T(128)S(1)} %pad_add_fusion.place_ref, f32[8,512]{1,0:T(8,128)S(1)} %pad.13.row_ref, f32[512,128]{1,0:T(8,128)S(1)} %pad.14.column_ref, ...), custom_call_target="tpu_custom_call" | custom-call | tf_op jit(solution)/shard_map/pallas_call | solution.py:320
  252.7 9.2 %collective-permute-done.51 = bf16[4,192,384]{2,1,0:T(8,128)(2,1)S(1)} collective-permute-done((bf16[4,192,384]{2,1,0:T(8,128)(2,1)}, bf16[4,192,384]{2,1,0:T(8,128)(2,1)S(1)}, u32[]{:S(2)}, u32[]{:S(2)}) %collective-permute-start.51) | collective-permute-done | bytes 589856 | tf_op jit(solution)/shard_map/ppermute | solution.py:232
  271.8 7.4 %shard_map.168 = (f32[256,768]{1,0:T(8,128)}, bf16[256,768]{1,0:T(8,128)(2,1)S(1)}, f32[8,768]{1,0:T(8,128)S(1)}, f32[4,2,192,384]{3,2,1,0:T(8,128)}, bf16[4,2,192,384]{3,2,1,0:T(8,128)(2,1)}) custom-call(s32[3]{0:T(128)S(1)} %pad_add_fusion.place_ref, bf16[256,768]{1,0:T(8,128)(2,1)S(1)} %get-tuple-element.191.own_gy_ref, ...), custom_call_target="tpu_custom_call" | custom-call | tf_op jit(solution)/shard_map/pallas_call | solution.py:320
  285.9 8.3 %collective-permute-done.61 = bf16[4,2,192,384]{3,2,1,0:T(8,128)(2,1)S(1)} collective-permute-done((bf16[4,2,192,384]{3,2,1,0:T(8,128)(2,1)S(1)}, bf16[4,2,192,384]{3,2,1,0:T(8,128)(2,1)S(1)}, u32[]{:S(2)}, u32[]{:S(2)}) %collective-permute-start.61) | collective-permute-done | bytes 1179680 | tf_op jit(solution)/shard_map/ppermute | solution.py:993
  301.9 15.4 %collective-permute-done.64 = bf16[2,192,384]{2,1,0:T(8,128)(2,1)S(1)} collective-permute-done((bf16[2,192,384]{2,1,0:T(8,128)(2,1)S(1)}, bf16[2,192,384]{2,1,0:T(8,128)(2,1)S(1)}, u32[]{:S(2)}, u32[]{:S(2)}) %collective-permute-start.64) | collective-permute-done | bytes 294944 | tf_op jit(solution)/shard_map/ppermute | solution.py:70
  317.4 8.5 %shard_map.170 = (f32[256,768]{1,0:T(8,128)}, bf16[256,768]{1,0:T(8,128)(2,1)S(1)}, f32[8,576]{1,0:T(8,128)S(1)}, f32[4,192,384]{2,1,0:T(8,128)}, bf16[4,192,384]{2,1,0:T(8,128)(2,1)}) custom-call(s32[3]{0:T(128)S(1)} %pad_add_fusion.place_ref, f32[8,512]{1,0:T(8,128)S(1)} %pad.13.row_ref, f32[512,128]{1,0:T(8,128)S(1)} %pad.14.column_ref, ...), custom_call_target="tpu_custom_call" | custom-call | tf_op jit(solution)/shard_map/pallas_call | solution.py:320
  326.5 7.3 %collective-permute-start.68 = (bf16[2,192,384]{2,1,0:T(8,128)(2,1)S(1)}, bf16[2,192,384]{2,1,0:T(8,128)(2,1)S(1)}, u32[]{:S(2)}, u32[]{:S(2)}) collective-permute-start(bf16[2,192,384]{2,1,0:T(8,128)(2,1)S(1)} %get-tuple-element.281), channel_id=1, source_target_pairs={{2,0},{3,1},{0,2},{1,3},{6,4},{7,5},{4,6},{5,7},{10,8},{11,9},{8,1... | collective-permute-start | bytes 884744 | tf_op jit(solution)/shard_map/ppermute | solution.py:70
  336.5 12.7 %collective-permute-done.68 = bf16[2,192,384]{2,1,0:T(8,128)(2,1)S(1)} collective-permute-done((bf16[2,192,384]{2,1,0:T(8,128)(2,1)S(1)}, bf16[2,192,384]{2,1,0:T(8,128)(2,1)S(1)}, u32[]{:S(2)}, u32[]{:S(2)}) %collective-permute-start.68) | collective-permute-done | bytes 294944 | tf_op jit(solution)/shard_map/ppermute | solution.py:70
  375.0 12.2 %collective-permute-done.71.recv_ref = bf16[256,768]{1,0:T(8,128)(2,1)S(1)} collective-permute-done((bf16[256,768]{1,0:T(8,128)(2,1)}, bf16[256,768]{1,0:T(8,128)(2,1)S(1)}, u32[]{:S(2)}, u32[]{:S(2)}) %collective-permute-start.71) | collective-permute-done | bytes 393248 | tf_op jit(solution)/shard_map/ppermute | solution.py:677
  400.5 6.5 %collective-permute-start.84 = (f32[2,3,768]{2,0,1:T(2,128)S(1)}, f32[2,3,768]{2,0,1:T(2,128)S(1)}, u32[]{:S(2)}, u32[]{:S(2)}) collective-permute-start(f32[2,3,768]{2,0,1:T(2,128)S(1)} %get-tuple-element.308), channel_id=1, source_target_pairs={{2,0},{3,1},{0,2},{1,3},{6,4},{7,5},{4,6},{5,7},{10,8},{11,9},{8,1... | collective-permute-start | bytes 55304 | tf_op jit(solution)/shard_map/ppermute | solution.py:70
  460.4 7.4 %collective-permute-start.81 = (f32[2,128,768]{2,1,0:T(8,128)}, f32[2,128,768]{2,1,0:T(8,128)}, u32[]{:S(2)}, u32[]{:S(2)}) collective-permute-start(f32[2,128,768]{2,1,0:T(8,128)} %fusion.2), channel_id=1, source_target_pairs={{0,0},{8,1},{4,2},{12,3},{1,4},{9,5},{5,6},{13,7},{2,8},{10,9},{6,... | collective-permute-start | bytes 2359304 | tf_op jit(solution)/shard_map/ppermute | solution.py:1101
  467.8 11.9 %shard_map.175 = bf16[768,768]{1,0:T(8,128)(2,1)} custom-call(s32[3]{0:T(128)S(1)} %pad_add_fusion.place_ref, bf16[768,768]{1,0:T(8,128)(2,1)} %copy-done.17, bf16[192,768]{1,0:T(8,128)(2,1)S(1)} %fusion.11.gram0_ref, bf16[192,768]{1,0:T(8,128)(2,1)S(1)} %collective-permute-done.78.gram1_ref, bf16[192,768]{1,0:T(8,128)(2,1)S(1)} %copy-done.24, ...), custom_call_target="tpu_custom_call" | custom-call | tf_op jit(solution)/shard_map/pallas_call | solution.py:320
  479.7 8.0 %all-to-all-done.5.blocks_ref = bf16[4,6,96,192]{3,2,1,0:T(8,128)(2,1)S(1)} async-done(((bf16[4,6,96,192]{3,2,1,0:T(8,128)(2,1)}), bf16[4,6,96,192]{3,2,1,0:T(8,128)(2,1)S(1)}, u32[]{:S(2)}, u32[]{:S(2)}) %all-to-all-start.5) | async-done | bytes 884768 | tf_op jit(solution)/shard_map/all_to_all | solution.py:174
  502.0 7.7 %all-to-all-done.6 = bf16[8,96,768]{2,1,0:T(8,128)(2,1)S(1)} async-done(((bf16[8,96,768]{2,1,0:T(8,128)(2,1)}), bf16[8,96,768]{2,1,0:T(8,128)(2,1)S(1)}, u32[]{:S(2)}, u32[]{:S(2)}) %all-to-all-start.6) | async-done | bytes 1179680 | tf_op jit(solution)/shard_map/all_to_all | solution.py:840
  (468 shorter events, 299.3 us)
Async XLA Ops:
  43.6 24.9 %collective-permute-start.14 = (bf16[192,384]{1,0:T(8,128)(2,1)S(1)}, bf16[192,384]{1,0:T(8,128)(2,1)}, u32[]{:S(2)}, u32[]{:S(2)}) collective-permute-start(bf16[192,384]{1,0:T(8,128)(2,1)S(1)} %shard_map.153.refs_0_), channel_id=1, source_target_pairs={{0,16},{16,0},{1,17},{17,1},{2,18},{18,2},{3,19},{19,3},{4,20},{20... | collective-permute-start | bytes 442376 | tf_op jit(solution)/shard_map/ppermute | solution.py:196
  86.1 20.7 %collective-permute-start.27 = (bf16[3,2,192,384]{3,2,1,0:T(8,128)(2,1)S(1)}, bf16[3,2,192,384]{3,2,1,0:T(8,128)(2,1)S(1)}, u32[]{:S(2)}, u32[]{:S(2)}) collective-permute-start(bf16[3,2,192,384]{3,2,1,0:T(8,128)(2,1)S(1)} %pad_maximum_fusion), channel_id=1, source_target_pairs={{0,16},{16,0},{1,17},{17,1},{2,18},{18,2},{3,19},{19,3},{4,20},{20... | collective-permute-start | bytes 2654216 | tf_op jit(solution)/shard_map/ppermute | solution.py:209
  100.2 21.0 %collective-permute-start.20 = (bf16[256,768]{1,0:T(8,128)(2,1)S(1)}, bf16[256,768]{1,0:T(8,128)(2,1)S(1)}, u32[]{:S(2)}, u32[]{:S(2)}) collective-permute-start(bf16[256,768]{1,0:T(8,128)(2,1)S(1)} %get-tuple-element.133.own_c_ref), channel_id=1, source_target_pairs={{0,4},{4,0},{1,5},{5,1},{2,6},{6,2},{3,7},{7,3},{8,12},{12,8},{9,1... | collective-permute-start | bytes 1179656 | tf_op jit(solution)/shard_map/ppermute | solution.py:672
  133.1 20.3 %collective-permute-start.35 = (bf16[4,192,384]{2,1,0:T(8,128)(2,1)S(1)}, bf16[4,192,384]{2,1,0:T(8,128)(2,1)S(1)}, u32[]{:S(2)}, u32[]{:S(2)}) collective-permute-start(bf16[4,192,384]{2,1,0:T(8,128)(2,1)S(1)} %pad_maximum_fusion.4), channel_id=1, source_target_pairs={{0,16},{16,0},{1,17},{17,1},{2,18},{18,2},{3,19},{19,3},{4,20},{20... | collective-permute-start | bytes 1769480 | tf_op jit(solution)/shard_map/ppermute | solution.py:939
  160.7 22.1 %collective-permute-start.43 = (bf16[3,2,192,384]{3,2,1,0:T(8,128)(2,1)S(1)}, bf16[3,2,192,384]{3,2,1,0:T(8,128)(2,1)S(1)}, u32[]{:S(2)}, u32[]{:S(2)}) collective-permute-start(bf16[3,2,192,384]{3,2,1,0:T(8,128)(2,1)S(1)} %pad_maximum_fusion.1), channel_id=1, source_target_pairs={{0,16},{16,0},{1,17},{17,1},{2,18},{18,2},{3,19},{19,3},{4,20},{20... | collective-permute-start | bytes 2654216 | tf_op jit(solution)/shard_map/ppermute | solution.py:209
  175.3 34.4 %collective-permute-start.45 = (f32[128,768]{1,0:T(8,128)}, f32[128,768]{1,0:T(8,128)}, u32[]{:S(2)}, u32[]{:S(2)}) collective-permute-start(f32[128,768]{1,0:T(8,128)} %collective-permute-done.39), channel_id=1, source_target_pairs={{0,8},{8,0},{1,9},{9,1},{2,10},{10,2},{3,11},{11,3},{4,12},{12,4},... | collective-permute-start | bytes 1179656 | tf_op jit(solution)/shard_map/ppermute | solution.py:74
  228.2 21.3 %all-to-all-start.2 = ((bf16[8,96,768]{2,1,0:T(8,128)(2,1)}), bf16[8,96,768]{2,1,0:T(8,128)(2,1)S(1)}, u32[]{:S(2)}, u32[]{:S(2)}) async-start(bf16[8,96,768]{2,1,0:T(8,128)(2,1)} %fusion.23), calls=%async_computation.2 | async-start | bytes 2359296 | tf_op jit(solution)/shard_map/all_to_all | solution.py:840
  265.3 28.8 %collective-permute-start.61 = (bf16[4,2,192,384]{3,2,1,0:T(8,128)(2,1)S(1)}, bf16[4,2,192,384]{3,2,1,0:T(8,128)(2,1)S(1)}, u32[]{:S(2)}, u32[]{:S(2)}) collective-permute-start(bf16[4,2,192,384]{3,2,1,0:T(8,128)(2,1)S(1)} %copy-done.72), channel_id=1, source_target_pairs={{0,16},{16,0},{1,17},{17,1},{2,18},{18,2},{3,19},{19,3},{4,20},{20... | collective-permute-start | bytes 3538952 | tf_op jit(solution)/shard_map/ppermute | solution.py:993
  280.7 45.2 %collective-permute-start.65 = (bf16[4,2,192,384]{3,2,1,0:T(8,128)(2,1)}, bf16[4,2,192,384]{3,2,1,0:T(8,128)(2,1)S(1)}, u32[]{:S(2)}, u32[]{:S(2)}) collective-permute-start(bf16[4,2,192,384]{3,2,1,0:T(8,128)(2,1)} %get-tuple-element.210), channel_id=1, source_target_pairs={{0,16},{16,0},{1,17},{17,1},{2,18},{18,2},{3,19},{19,3},{4,20},{20... | collective-permute-start | bytes 3538952 | tf_op jit(solution)/shard_map/ppermute | solution.py:993
  294.6 22.7 %collective-permute-start.64 = (bf16[2,192,384]{2,1,0:T(8,128)(2,1)S(1)}, bf16[2,192,384]{2,1,0:T(8,128)(2,1)S(1)}, u32[]{:S(2)}, u32[]{:S(2)}) collective-permute-start(bf16[2,192,384]{2,1,0:T(8,128)(2,1)S(1)} %get-tuple-element.284), channel_id=1, source_target_pairs={{2,0},{3,1},{0,2},{1,3},{6,4},{7,5},{4,6},{5,7},{10,8},{11,9},{8,1... | collective-permute-start | bytes 884744 | tf_op jit(solution)/shard_map/ppermute | solution.py:70
  296.4 20.8 %collective-permute-start.63 = (bf16[2,192,384]{2,1,0:T(8,128)(2,1)S(1)}, bf16[2,192,384]{2,1,0:T(8,128)(2,1)S(1)}, u32[]{:S(2)}, u32[]{:S(2)}) collective-permute-start(bf16[2,192,384]{2,1,0:T(8,128)(2,1)S(1)} %get-tuple-element.285), channel_id=1, source_target_pairs={{1,0},{2,1},{3,2},{0,3},{5,4},{6,5},{7,6},{4,7},{9,8},{10,9},{11,1... | collective-permute-start | bytes 884744 | tf_op jit(solution)/shard_map/ppermute | solution.py:70
  326.5 22.7 %collective-permute-start.68 = (bf16[2,192,384]{2,1,0:T(8,128)(2,1)S(1)}, bf16[2,192,384]{2,1,0:T(8,128)(2,1)S(1)}, u32[]{:S(2)}, u32[]{:S(2)}) collective-permute-start(bf16[2,192,384]{2,1,0:T(8,128)(2,1)S(1)} %get-tuple-element.281), channel_id=1, source_target_pairs={{2,0},{3,1},{0,2},{1,3},{6,4},{7,5},{4,6},{5,7},{10,8},{11,9},{8,1... | collective-permute-start | bytes 884744 | tf_op jit(solution)/shard_map/ppermute | solution.py:70
  333.7 21.0 %collective-permute-start.67 = (bf16[2,192,384]{2,1,0:T(8,128)(2,1)S(1)}, bf16[2,192,384]{2,1,0:T(8,128)(2,1)S(1)}, u32[]{:S(2)}, u32[]{:S(2)}) collective-permute-start(bf16[2,192,384]{2,1,0:T(8,128)(2,1)S(1)} %get-tuple-element.282), channel_id=1, source_target_pairs={{1,0},{2,1},{3,2},{0,3},{5,4},{6,5},{7,6},{4,7},{9,8},{10,9},{11,1... | collective-permute-start | bytes 884744 | tf_op jit(solution)/shard_map/ppermute | solution.py:70
  334.8 19.9 %collective-permute-start.66 = (bf16[2,192,384]{2,1,0:T(8,128)(2,1)S(1)}, bf16[2,192,384]{2,1,0:T(8,128)(2,1)S(1)}, u32[]{:S(2)}, u32[]{:S(2)}) collective-permute-start(bf16[2,192,384]{2,1,0:T(8,128)(2,1)S(1)} %get-tuple-element.280), channel_id=1, source_target_pairs={{3,0},{0,1},{1,2},{2,3},{7,4},{4,5},{5,6},{6,7},{11,8},{8,9},{9,10... | collective-permute-start | bytes 884744 | tf_op jit(solution)/shard_map/ppermute | solution.py:70
  335.7 19.3 %collective-permute-start.69 = (bf16[4,192,384]{2,1,0:T(8,128)(2,1)S(1)}, bf16[4,192,384]{2,1,0:T(8,128)(2,1)S(1)}, u32[]{:S(2)}, u32[]{:S(2)}) collective-permute-start(bf16[4,192,384]{2,1,0:T(8,128)(2,1)S(1)} %copy-done.73), channel_id=1, source_target_pairs={{0,16},{16,0},{1,17},{17,1},{2,18},{18,2},{3,19},{19,3},{4,20},{20... | collective-permute-start | bytes 1769480 | tf_op jit(solution)/shard_map/ppermute | solution.py:232
  336.4 26.5 %collective-permute-start.70 = (bf16[256,768]{1,0:T(8,128)(2,1)S(1)}, bf16[256,768]{1,0:T(8,128)(2,1)S(1)}, u32[]{:S(2)}, u32[]{:S(2)}) collective-permute-start(bf16[256,768]{1,0:T(8,128)(2,1)S(1)} %get-tuple-element.216), channel_id=1, source_target_pairs={{0,4},{4,0},{1,5},{5,1},{2,6},{6,2},{3,7},{7,3},{8,12},{12,8},{9,1... | collective-permute-start | bytes 1179656 | tf_op jit(solution)/shard_map/ppermute | solution.py:672
  358.7 31.6 %all-to-all-start.3 = ((bf16[8,192,384]{2,1,0:T(8,128)(2,1)}), bf16[8,192,384]{2,1,0:T(8,128)(2,1)}, u32[]{:S(2)}, u32[]{:S(2)}) async-start(bf16[8,192,384]{2,1,0:T(8,128)(2,1)} %bitcast.198), calls=%async_computation.3 | async-start | bytes 2359296 | tf_op jit(solution)/shard_map/all_to_all | solution.py:840
  365.2 21.9 %collective-permute-start.71 = (bf16[256,768]{1,0:T(8,128)(2,1)}, bf16[256,768]{1,0:T(8,128)(2,1)S(1)}, u32[]{:S(2)}, u32[]{:S(2)}) collective-permute-start(bf16[256,768]{1,0:T(8,128)(2,1)} %get-tuple-element.257), channel_id=1, source_target_pairs={{0,8},{8,0},{1,9},{9,1},{2,10},{10,2},{3,11},{11,3},{4,12},{12,4},... | collective-permute-start | bytes 1179656 | tf_op jit(solution)/shard_map/ppermute | solution.py:677
  367.7 22.6 %collective-permute-start.72 = (bf16[192,384]{1,0:T(8,128)(2,1)S(1)}, bf16[192,384]{1,0:T(8,128)(2,1)S(1)}, u32[]{:S(2)}, u32[]{:S(2)}) collective-permute-start(bf16[192,384]{1,0:T(8,128)(2,1)S(1)} %get-tuple-element.294), channel_id=1, source_target_pairs={{3,0},{0,1},{1,2},{2,3},{7,4},{4,5},{5,6},{6,7},{11,8},{8,9},{9,10... | collective-permute-start | bytes 442376 | tf_op jit(solution)/shard_map/ppermute | solution.py:70
  426.7 26.8 %all-to-all-start.4 = ((bf16[8,192,384]{2,1,0:T(8,128)(2,1)}), bf16[8,192,384]{2,1,0:T(8,128)(2,1)}, u32[]{:S(2)}, u32[]{:S(2)}) async-start(bf16[8,192,384]{2,1,0:T(8,128)(2,1)} %bitcast.199), calls=%async_computation.4 | async-start | bytes 2359296 | tf_op jit(solution)/shard_map/all_to_all | solution.py:840
  453.5 34.2 %all-to-all-start.5 = ((bf16[4,6,96,192]{3,2,1,0:T(8,128)(2,1)}), bf16[4,6,96,192]{3,2,1,0:T(8,128)(2,1)S(1)}, u32[]{:S(2)}, u32[]{:S(2)}) async-start(bf16[4,6,96,192]{3,2,1,0:T(8,128)(2,1)} %shard_map.173), calls=%async_computation.5 | async-start | bytes 2359296 | tf_op jit(solution)/shard_map/all_to_all | solution.py:174
  457.0 35.8 %collective-permute-start.88 = (bf16[2,192,384]{2,1,0:T(8,128)(2,1)}, bf16[2,192,384]{2,1,0:T(8,128)(2,1)}, u32[]{:S(2)}, u32[]{:S(2)}) collective-permute-start(bf16[2,192,384]{2,1,0:T(8,128)(2,1)} %get-tuple-element.304), channel_id=1, source_target_pairs={{3,3},{19,7},{7,11},{23,15},{11,19},{27,23},{15,27},{31,31}} | collective-permute-start | bytes 884744 | tf_op jit(solution)/shard_map/ppermute | solution.py:128
  460.4 35.9 %collective-permute-start.81 = (f32[2,128,768]{2,1,0:T(8,128)}, f32[2,128,768]{2,1,0:T(8,128)}, u32[]{:S(2)}, u32[]{:S(2)}) collective-permute-start(f32[2,128,768]{2,1,0:T(8,128)} %fusion.2), channel_id=1, source_target_pairs={{0,0},{8,1},{4,2},{12,3},{1,4},{9,5},{5,6},{13,7},{2,8},{10,9},{6,... | collective-permute-start | bytes 2359304 | tf_op jit(solution)/shard_map/ppermute | solution.py:1101
  487.7 21.9 %all-to-all-start.6 = ((bf16[8,96,768]{2,1,0:T(8,128)(2,1)}), bf16[8,96,768]{2,1,0:T(8,128)(2,1)S(1)}, u32[]{:S(2)}, u32[]{:S(2)}) async-start(bf16[8,96,768]{2,1,0:T(8,128)(2,1)} %bitcast.200), calls=%async_computation.6 | async-start | bytes 2359296 | tf_op jit(solution)/shard_map/all_to_all | solution.py:840
  (147 other events, 1330.1 us)

commit v12 on v11

--- a/solution.py
+++ b/solution.py
@@ -921,7 +921,6 @@
         )
         if relative and not following:
             mine, gy_own = lax.optimization_barrier((mine, gy_own))
-            moved_grad = lax.ppermute(after(out_grad[0], far), axes, to_seq)
         mine, recv = group_sum(mine, give)
         middle, c_own = norm_stage(vec_rows, layer, 2, hidden, mine, recv, (layer, 6))
         if relative:
@@ -968,6 +967,8 @@
         grad_hidden = x_join(lax.ppermute(out_grad[0], axes, to_seq))
         hidden_out = send_back(last_hidden())
         gy_own = grad_hidden.astype(bf16)
+    else:
+        grad_hidden = gy_own.astype(f32)
     attn_half = None
 
     mat_list = [None] * LAYERS
@@ -982,18 +983,13 @@
             hidden = last_hidden(gy_own)
             attn_part = ctx_sum(attn_half)
         gy_other = core_swap(gy_own)
-        if relative and attn_half is None:
-            gy_other, moved_grad = lax.optimization_barrier((gy_other, moved_grad))
-            grad_hidden = x_join(moved_grad)
         mine, give, up_sums, *mlp_grads = feed_back_stage(
             place, gy_own, gy_other, c_own, c_other, preact, act, w_mlp, relative
         )
         if relative:
             mlp_mine, mlp_give = mlp_grads
             mlp_recv = lax.ppermute(mlp_give, "g", SWAP)
-            if attn_half is None:
-                mine, grad_hidden = lax.optimization_barrier((mine, grad_hidden))
-            else:
+            if attn_half is not None:
                 mine, hidden, attn_part = lax.optimization_barrier((mine, hidden, attn_part))
                 wide_part = ctx_sum(late_half[0] + after(late_half[1], mine).astype(f32))
         mine, recv = group_sum(mine, give)
@@ -1025,7 +1021,9 @@
         )
         if relative:
             if layer == LAYERS - 1:
-                mine, moment_slots = lax.optimization_barrier((mine, moment_slots))
+                mine, mlp_recv, moment_slots = lax.optimization_barrier(
+                    (mine, mlp_recv, moment_slots)
+                )
                 late_half = (mlp_mine, mlp_recv)
             else:
                 parts[layer + 1] = (attn_part, wide_part)
@@ -1072,11 +1070,9 @@
         attn_low = attn_half.astype(bf16)
         attn_sums = [rotate(attn_low[step], "ctx", -step) for step in (1, 3, 2)]
         wide_low = jnp.concatenate([parts[1][1], mlp_part]).astype(bf16)
-        wide_low = after(wide_low, attn_half)
+        wide_low = after(wide_low, attn_half, grad_hidden)
         wide_slots = slot_exchange(jnp.repeat(wide_low, 2, axis=0))
-        wide_slots, grad_hidden, attn_sums = lax.optimization_barrier(
-            (wide_slots, grad_hidden, attn_sums)
-        )
+        wide_slots, attn_sums = lax.optimization_barrier((wide_slots, attn_sums))
         x_wide, gram_blocks = slot_gram(place, wide_slots, moment_slots)
         vec_sums = sum_group(sum_vectors(after(vec_terms, gram_blocks)))
         attn_part = attn_half[0] + sum(block.astype(f32) for block in attn_sums)
@@ -1084,24 +1080,25 @@
         for step in (1, 3, 2):
             total = total + core_shift(gram_blocks[step], -step).astype(f32)
         gram_low = total.astype(bf16)
-        square_low, vec_sums, unused = lax.optimization_barrier(
-            (jnp.stack([parts[1][0], attn_part]).astype(bf16), vec_sums, gram_low)
+        blocks, outs = grad_blocks(
+            [attn_part, parts[1][0]], [mlp_part, parts[1][1]], dp_rows, gram_blocks
+        )
+        square_low, vec_sums, blocks, unused = lax.optimization_barrier(
+            (jnp.stack([parts[1][0], attn_part]).astype(bf16), vec_sums, blocks, gram_low)
         )
         square_slots = slot_exchange(jnp.tile(jnp.repeat(square_low, 2, axis=0), (2, 1, 1)))
         near, back, far = [core_shift(gram_low, step) for step in (1, 3, 2)]
         ortho_mine = slot_orthogonalize(
             place, x_wide, (gram_low, near, far, back), square_slots, moment_slots
         )
-        blocks, outs = grad_blocks(
-            [attn_part, parts[1][0]], [mlp_part, parts[1][1]], dp_rows, square_slots, near, back, far
-        )
+        grad_mats, moment_new = grad_rows(place, blocks, outs, mat_momentum)
         returned = slot_exchange(ortho_mine.reshape(dp_size, dp_rows, D))
-        ends = jnp.stack([hidden, grad_hidden])
+        ends = jnp.stack([hidden, grad_hidden]).astype(bf16)
         ends = lax.dynamic_slice_in_dim(ends, x_index * tokens_dev, tokens_dev, axis=1)
-        hidden_out, input_grad = lax.ppermute(after(ends, near, back, far), axes, from_seq)
+        ends = lax.ppermute(after(ends, near, back, far), axes, from_seq)
+        hidden_out, input_grad = ends.astype(f32)
         ortho = jnp.stack([returned[slot] for slot in (3, 4, 6, 1, 0, 2)])
         ortho = ortho.reshape(weights.shape).astype(f32)
-        grad_mats, moment_new = grad_rows(place, blocks, outs, mat_momentum)
     else:
         vec_sums = sum_group(sum_vectors(vec_terms))
         cols_dev = weights.shape[3]

time: 522 us -> 526 us (level)
  waiting for transfers between devices: 173 us -> 205 us
  starting transfers between devices: 183 us -> 153 us
    ppermute x30, waiting for transfers between devices: 59.7 us -> 89.5 us  [rotate(): lax.ppermute(block, axis, [((i + step) % size, i) for i in range(size)])]
    ppermute x30, starting transfers between devices: 63.1 us -> 51.5 us  [rotate(): lax.ppermute(block, axis, [((i + step) % size, i) for i in range(size)])]
    all_to_all x4, waiting for transfers between devices: 12.2 us -> 21.7 us  [slot_exchange(): return lax.all_to_all(blocks, DP, split_axis=0, concat_axis=0, tiled=True)]
    all_to_all x3, waiting for transfers between devices: 17.6 us -> 8.76 us  [group_exchange(): lax.all_to_all(blocks, GROUP, split_axis=0, concat_axis=0, tiled=True)]
    ppermute x2 -> x1, starting transfers between devices: 8.8 us -> 0.69 us  [local(): ends = lax.ppermute(after(ends, near, back, far), axes, from_seq)]
    ppermute x8, starting transfers between devices: 14.2 us -> 6.57 us  [group_sum(): return (mine, lax.ppermute(mine.astype(bf16), 'jx', SWAP))]
    ppermute x8, waiting for transfers between devices: 39.6 us -> 32.4 us  [group_sum(): return (mine, lax.ppermute(mine.astype(bf16), 'jx', SWAP))]
    unnamed x160 -> x140, local copies, waits for them, and re-layouts: 19.9 us -> 22.8 us
  transfers between devices with their start and end apart: 97 -> 95, of which waited for: 34 -> 41; matrix products, arithmetic and copies ran while one was open for 7% -> 6% of each run, Pallas kernels for 16% -> 14%
where the time goes in v12:
time: 526 us; the launch traced here: 516 us
  waiting for transfers between devices  205 us (39%)
  starting transfers between devices  153 us (29%)
  Pallas kernels  95.4 us (18%)
  local copies, waits for them, and re-layouts  33.7 us (6%)
  other arithmetic  26.1 us (5%)
    pallas_call x24, Pallas kernels, call(): pl.pallas_call(kernel, out_shape=[jax.ShapeDtypeStruct(shape, kind) for s...  95.4 us
    ppermute x30, waiting for transfers between devices, rotate(): lax.ppermute(block, axis, [((i + step) % size, i) for i in range(size)])  89.5 us
    ppermute x30, starting transfers between devices, rotate(): lax.ppermute(block, axis, [((i + step) % size, i) for i in range(size)])  51.5 us
    ppermute x8, waiting for transfers between devices, group_sum(): return (mine, lax.ppermute(mine.astype(bf16), 'jx', SWAP))  32.4 us
    unnamed x140, local copies, waits for them, and re-layouts  22.8 us
    all_to_all x4, waiting for transfers between devices, slot_exchange(): return lax.all_to_all(blocks, DP, split_axis=0, concat_axis=0, tiled=True)  21.7 us
    ppermute x6, starting transfers between devices, core_shift(): lax.ppermute(block, ('jc', 'ctx'), [((i + step) % size, i) for i in range...  21 us
    all_to_all x4, starting transfers between devices, slot_exchange(): return lax.all_to_all(blocks, DP, split_axis=0, concat_axis=0, tiled=True)  17.5 us
  transfers between devices with their start and end apart: 95, of which 41 were waited for; matrix products, arithmetic and copies ran while one was open for 6% of the time, Pallas kernels for 14%

profile of v12, /device:TPU:0, one launch (start us, length us, event | category | flops | bytes accessed | tf_op | source)
XLA Modules:
  0.0 515.7 jit_solution(3205524342600628200)
XLA Ops:
  20.7 10.7 %collective-permute-start.6 = (bf16[4,2,3,192]{3,1,2,0:T(2,128)(2,1)S(1)}, bf16[4,2,3,192]{3,1,2,0:T(2,128)(2,1)S(1)}, u32[]{:S(2)}, u32[]{:S(2)}) collective-permute-start(bf16[4,2,3,192]{3,1,2,0:T(2,128)(2,1)S(1)} %pad_maximum_fusion.14), channel_id=1, source_target_pairs={{0,8},{8,0},{1,9},{9,1},{2,10},{10,2},{3,11},{11,3},{4,12},{12,4},... | collective-permute-start | bytes 27656 | tf_op jit(solution)/shard_map/ppermute | solution.py:74
  35.8 9.7 %collective-permute-start.11 = (bf16[192,384]{1,0:T(8,128)(2,1)S(1)}, bf16[192,384]{1,0:T(8,128)(2,1)S(1)}, u32[]{:S(2)}, u32[]{:S(2)}) collective-permute-start(bf16[192,384]{1,0:T(8,128)(2,1)S(1)} %shard_map.153.refs_0_), channel_id=1, source_target_pairs={{1,0},{2,1},{3,2},{0,3},{5,4},{6,5},{7,6},{4,7},{9,8},{10,9},{11,1... | collective-permute-start | bytes 442376 | tf_op jit(solution)/shard_map/ppermute | solution.py:70
  61.2 8.8 %all-to-all-done.1.blocks_ref = bf16[4,5,192,96]{3,2,1,0:T(8,128)(2,1)S(1)} async-done(((bf16[4,5,192,96]{3,2,1,0:T(8,128)(2,1)}), bf16[4,5,192,96]{3,2,1,0:T(8,128)(2,1)S(1)}, u32[]{:S(2)}, u32[]{:S(2)}) %all-to-all-start.1) | async-done | bytes 737312 | tf_op jit(solution)/shard_map/all_to_all | solution.py:174
  78.1 6.5 %shard_map.155 = (bf16[768,768]{1,0:T(8,128)(2,1)}, bf16[512,576]{1,0:T(8,128)(2,1)}, f32[512,128]{1,0:T(8,128)S(1)}, bf16[512,192]{1,0:T(8,128)(2,1)S(1)}, f32[...) custom-call(s32[3]{0:T(128)S(1)} %pad_add_fusion.place_ref, f32[8,512]{1,0:T(8,128)S(1)} %pad.13.row_ref, ...), custom_call_target="tpu_custom_call" | custom-call | tf_op jit(solution)/shard_map/pallas_call | solution.py:320
  84.7 6.4 %collective-permute-done.21.refs_1_ = bf16[2,192,384]{2,1,0:T(8,128)(2,1)S(1)} collective-permute-done((bf16[2,192,384]{2,1,0:T(8,128)(2,1)S(1)}, bf16[2,192,384]{2,1,0:T(8,128)(2,1)S(1)}, u32[]{:S(2)}, u32[]{:S(2)}) %collective-permute-start.21) | collective-permute-done | bytes 294944 | tf_op jit(solution)/shard_map/ppermute | solution.py:70
  94.2 8.3 %collective-permute-done.19.refs_1_ = bf16[256,768]{1,0:T(8,128)(2,1)S(1)} collective-permute-done((bf16[256,768]{1,0:T(8,128)(2,1)S(1)}, bf16[256,768]{1,0:T(8,128)(2,1)S(1)}, u32[]{:S(2)}, u32[]{:S(2)}) %collective-permute-start.19) | collective-permute-done | bytes 393248 | tf_op jit(solution)/shard_map/ppermute | solution.py:677
  118.6 8.1 %collective-permute-done.25.refs_2_ = bf16[192,384]{1,0:T(8,128)(2,1)S(1)} collective-permute-done((bf16[192,384]{1,0:T(8,128)(2,1)S(1)}, bf16[192,384]{1,0:T(8,128)(2,1)S(1)}, u32[]{:S(2)}, u32[]{:S(2)}) %collective-permute-start.25) | collective-permute-done | bytes 147488 | tf_op jit(solution)/shard_map/ppermute | solution.py:70
  162.7 6.1 %shard_map.161 = (bf16[768,768]{1,0:T(8,128)(2,1)}, bf16[512,576]{1,0:T(8,128)(2,1)}, f32[512,128]{1,0:T(8,128)S(1)}, bf16[512,192]{1,0:T(8,128)(2,1)S(1)}, f32[...) custom-call(s32[3]{0:T(128)S(1)} %pad_add_fusion.place_ref, f32[8,512]{1,0:T(8,128)S(1)} %pad.13.row_ref, ...), custom_call_target="tpu_custom_call" | custom-call | tf_op jit(solution)/shard_map/pallas_call | solution.py:320
  175.7 10.5 %collective-permute-done.41.refs_2_ = bf16[2,192,384]{2,1,0:T(8,128)(2,1)S(1)} collective-permute-done((bf16[2,192,384]{2,1,0:T(8,128)(2,1)S(1)}, bf16[2,192,384]{2,1,0:T(8,128)(2,1)S(1)}, u32[]{:S(2)}, u32[]{:S(2)}) %collective-permute-start.41) | collective-permute-done | bytes 294944 | tf_op jit(solution)/shard_map/ppermute | solution.py:70
  207.3 7.6 %shard_map.164 = (f32[256,768]{1,0:T(8,128)}, bf16[256,768]{1,0:T(8,128)(2,1)S(1)}, f32[8,768]{1,0:T(8,128)S(1)}, f32[4,2,192,384]{3,2,1,0:T(8,128)}, bf16[4,2,192,384]{3,2,1,0:T(8,128)(2,1)}) custom-call(s32[3]{0:T(128)S(1)} %pad_add_fusion.place_ref, bf16[256,768]{1,0:T(8,128)(2,1)S(1)} %pad_maximum_fusion.5.own_gy_ref, ...), custom_call_target="tpu_custom_call" | custom-call | tf_op jit(solution)/shard_map/pallas_call | solution.py:320
  223.4 6.5 %collective-permute-done.45.recv_ref = bf16[256,768]{1,0:T(8,128)(2,1)S(1)} collective-permute-done((bf16[256,768]{1,0:T(8,128)(2,1)S(1)}, bf16[256,768]{1,0:T(8,128)(2,1)S(1)}, u32[]{:S(2)}, u32[]{:S(2)}) %collective-permute-start.45) | collective-permute-done | bytes 393248 | tf_op jit(solution)/shard_map/ppermute | solution.py:677
  239.8 8.4 %shard_map.166 = (f32[256,768]{1,0:T(8,128)}, bf16[256,768]{1,0:T(8,128)(2,1)S(1)}, f32[8,576]{1,0:T(8,128)S(1)}, f32[4,192,384]{2,1,0:T(8,128)}, bf16[4,192,384]{2,1,0:T(8,128)(2,1)}) custom-call(s32[3]{0:T(128)S(1)} %pad_add_fusion.place_ref, f32[8,512]{1,0:T(8,128)S(1)} %pad.13.row_ref, f32[512,128]{1,0:T(8,128)S(1)} %pad.14.column_ref, ...), custom_call_target="tpu_custom_call" | custom-call | tf_op jit(solution)/shard_map/pallas_call | solution.py:320
  256.3 6.4 %all-to-all-done.2 = bf16[8,96,768]{2,1,0:T(8,128)(2,1)} async-done(((bf16[8,96,768]{2,1,0:T(8,128)(2,1)}), bf16[8,96,768]{2,1,0:T(8,128)(2,1)}, u32[]{:S(2)}, u32[]{:S(2)}) %all-to-all-start.2) | async-done | bytes 1179680 | tf_op jit(solution)/shard_map/all_to_all | solution.py:840
  265.5 8.7 %collective-permute-done.50 = bf16[4,192,384]{2,1,0:T(8,128)(2,1)} collective-permute-done((bf16[4,192,384]{2,1,0:T(8,128)(2,1)}, bf16[4,192,384]{2,1,0:T(8,128)(2,1)}, u32[]{:S(2)}, u32[]{:S(2)}) %collective-permute-start.50) | collective-permute-done | bytes 589856 | tf_op jit(solution)/shard_map/ppermute | solution.py:232
  284.0 7.4 %shard_map.168 = (f32[256,768]{1,0:T(8,128)}, bf16[256,768]{1,0:T(8,128)(2,1)S(1)}, f32[8,768]{1,0:T(8,128)S(1)}, f32[4,2,192,384]{3,2,1,0:T(8,128)}, bf16[4,2,192,384]{3,2,1,0:T(8,128)(2,1)}) custom-call(s32[3]{0:T(128)S(1)} %pad_add_fusion.place_ref, bf16[256,768]{1,0:T(8,128)(2,1)S(1)} %get-tuple-element.183.own_gy_ref, ...), custom_call_target="tpu_custom_call" | custom-call | tf_op jit(solution)/shard_map/pallas_call | solution.py:320
  318.0 9.8 %collective-permute-done.62 = bf16[2,192,384]{2,1,0:T(8,128)(2,1)S(1)} collective-permute-done((bf16[2,192,384]{2,1,0:T(8,128)(2,1)S(1)}, bf16[2,192,384]{2,1,0:T(8,128)(2,1)S(1)}, u32[]{:S(2)}, u32[]{:S(2)}) %collective-permute-start.62) | collective-permute-done | bytes 294944 | tf_op jit(solution)/shard_map/ppermute | solution.py:70
  328.0 8.6 %shard_map.170 = (f32[256,768]{1,0:T(8,128)}, bf16[256,768]{1,0:T(8,128)(2,1)S(1)}, f32[8,576]{1,0:T(8,128)S(1)}, f32[4,192,384]{2,1,0:T(8,128)}, bf16[4,192,384]{2,1,0:T(8,128)(2,1)}) custom-call(s32[3]{0:T(128)S(1)} %pad_add_fusion.place_ref, f32[8,512]{1,0:T(8,128)S(1)} %pad.13.row_ref, f32[512,128]{1,0:T(8,128)S(1)} %pad.14.column_ref, ...), custom_call_target="tpu_custom_call" | custom-call | tf_op jit(solution)/shard_map/pallas_call | solution.py:320
  341.4 7.5 %collective-permute-done.66 = bf16[2,192,384]{2,1,0:T(8,128)(2,1)S(1)} collective-permute-done((bf16[2,192,384]{2,1,0:T(8,128)(2,1)S(1)}, bf16[2,192,384]{2,1,0:T(8,128)(2,1)S(1)}, u32[]{:S(2)}, u32[]{:S(2)}) %collective-permute-start.66) | collective-permute-done | bytes 294944 | tf_op jit(solution)/shard_map/ppermute | solution.py:70
  351.7 11.6 %collective-permute-done.68 = bf16[2,192,384]{2,1,0:T(8,128)(2,1)S(1)} collective-permute-done((bf16[2,192,384]{2,1,0:T(8,128)(2,1)S(1)}, bf16[2,192,384]{2,1,0:T(8,128)(2,1)S(1)}, u32[]{:S(2)}, u32[]{:S(2)}) %collective-permute-start.68) | collective-permute-done | bytes 294944 | tf_op jit(solution)/shard_map/ppermute | solution.py:70
  368.0 6.8 %collective-permute-done.64.recv_ref = bf16[256,768]{1,0:T(8,128)(2,1)S(1)} collective-permute-done((bf16[256,768]{1,0:T(8,128)(2,1)S(1)}, bf16[256,768]{1,0:T(8,128)(2,1)S(1)}, u32[]{:S(2)}, u32[]{:S(2)}) %collective-permute-start.64) | collective-permute-done | bytes 393248 | tf_op jit(solution)/shard_map/ppermute | solution.py:677
  447.3 6.6 %collective-permute-start.76 = (bf16[192,768]{1,0:T(8,128)(2,1)S(1)}, bf16[192,768]{1,0:T(8,128)(2,1)S(1)}, u32[]{:S(2)}, u32[]{:S(2)}) collective-permute-start(bf16[192,768]{1,0:T(8,128)(2,1)S(1)} %fusion.10.gram0_ref), channel_id=1, source_target_pairs={{1,0},{2,1},{3,2},{0,3},{9,8},{10,9},{11,10},{8,11},{17,16},{18,17... | collective-permute-start | bytes 884744 | tf_op jit(solution)/shard_map/ppermute | solution.py:845
  464.5 6.2 %collective-permute-done.78.gram2_ref = bf16[192,768]{1,0:T(8,128)(2,1)S(1)} collective-permute-done((bf16[192,768]{1,0:T(8,128)(2,1)S(1)}, bf16[192,768]{1,0:T(8,128)(2,1)S(1)}, u32[]{:S(2)}, u32[]{:S(2)}) %collective-permute-start.78) | collective-permute-done | bytes 294944 | tf_op jit(solution)/shard_map/ppermute | solution.py:845
  470.7 11.9 %shard_map.175 = bf16[768,768]{1,0:T(8,128)(2,1)} custom-call(s32[3]{0:T(128)S(1)} %pad_add_fusion.place_ref, bf16[768,768]{1,0:T(8,128)(2,1)} %copy-done.17, bf16[192,768]{1,0:T(8,128)(2,1)S(1)} %fusion.10.gram0_ref, bf16[192,768]{1,0:T(8,128)(2,1)S(1)} %collective-permute-done.76.gram1_ref, bf16[192,768]{1,0:T(8,128)(2,1)S(1)} %collective-permute-done.78.gram2_ref, ...), custom_call_target="tpu_custom_call" | custom-call | tf_op jit(solution)/shard_map/pallas_call | solution.py:320
  494.9 14.2 %all-to-all-done.6 = bf16[8,96,768]{2,1,0:T(8,128)(2,1)} async-done(((bf16[8,96,768]{2,1,0:T(8,128)(2,1)}), bf16[8,96,768]{2,1,0:T(8,128)(2,1)}, u32[]{:S(2)}, u32[]{:S(2)}) %all-to-all-start.6) | async-done | bytes 1179680 | tf_op jit(solution)/shard_map/all_to_all | solution.py:840
  (444 shorter events, 309.8 us)
Async XLA Ops:
  10.9 24.2 %all-to-all-start = ((bf16[4,1,192,96]{3,2,1,0:T(8,128)(2,1)}), bf16[4,1,192,96]{3,2,1,0:T(8,128)(2,1)S(1)}, u32[]{:S(2)}, u32[]{:S(2)}) async-start(bf16[4,1,192,96]{3,2,1,0:T(8,128)(2,1)} %shard_map.152), calls=%async_computation | async-start | bytes 393216 | tf_op jit(solution)/shard_map/all_to_all | solution.py:174
  47.2 23.9 %collective-permute-start.14 = (bf16[192,384]{1,0:T(8,128)(2,1)S(1)}, bf16[192,384]{1,0:T(8,128)(2,1)}, u32[]{:S(2)}, u32[]{:S(2)}) collective-permute-start(bf16[192,384]{1,0:T(8,128)(2,1)S(1)} %shard_map.153.refs_0_), channel_id=1, source_target_pairs={{0,16},{16,0},{1,17},{17,1},{2,18},{18,2},{3,19},{19,3},{4,20},{20... | collective-permute-start | bytes 442376 | tf_op jit(solution)/shard_map/ppermute | solution.py:196
  56.2 19.1 %collective-permute-start.15 = (bf16[192,384]{1,0:T(8,128)(2,1)S(1)}, bf16[192,384]{1,0:T(8,128)(2,1)}, u32[]{:S(2)}, u32[]{:S(2)}) collective-permute-start(bf16[192,384]{1,0:T(8,128)(2,1)S(1)} %collective-permute-done.11.refs_1_), channel_id=1, source_target_pairs={{0,16},{16,0},{1,17},{17,1},{2,18},{18,2},{3,19},{19,3},{4,20},{20... | collective-permute-start | bytes 442376 | tf_op jit(solution)/shard_map/ppermute | solution.py:196
  58.3 19.8 %collective-permute-start.10 = (bf16[256,768]{1,0:T(8,128)(2,1)S(1)}, bf16[256,768]{1,0:T(8,128)(2,1)}, u32[]{:S(2)}, u32[]{:S(2)}) collective-permute-start(bf16[256,768]{1,0:T(8,128)(2,1)S(1)} %shard_map.154.own_a_ref), channel_id=1, source_target_pairs={{0,4},{4,0},{1,5},{5,1},{2,6},{6,2},{3,7},{7,3},{8,12},{12,8},{9,1... | collective-permute-start | bytes 1179656 | tf_op jit(solution)/shard_map/ppermute | solution.py:672
  71.1 20.0 %collective-permute-start.21 = (bf16[2,192,384]{2,1,0:T(8,128)(2,1)S(1)}, bf16[2,192,384]{2,1,0:T(8,128)(2,1)S(1)}, u32[]{:S(2)}, u32[]{:S(2)}) collective-permute-start(bf16[2,192,384]{2,1,0:T(8,128)(2,1)S(1)} %pad_maximum_fusion.7.refs_0_), channel_id=1, source_target_pairs={{1,0},{2,1},{3,2},{0,3},{5,4},{6,5},{7,6},{4,7},{9,8},{10,9},{11,1... | collective-permute-start | bytes 884744 | tf_op jit(solution)/shard_map/ppermute | solution.py:70
  91.2 20.7 %collective-permute-start.27 = (bf16[3,2,192,384]{3,2,1,0:T(8,128)(2,1)S(1)}, bf16[3,2,192,384]{3,2,1,0:T(8,128)(2,1)S(1)}, u32[]{:S(2)}, u32[]{:S(2)}) collective-permute-start(bf16[3,2,192,384]{3,2,1,0:T(8,128)(2,1)S(1)} %pad_maximum_fusion), channel_id=1, source_target_pairs={{0,16},{16,0},{1,17},{17,1},{2,18},{18,2},{3,19},{19,3},{4,20},{20... | collective-permute-start | bytes 2654216 | tf_op jit(solution)/shard_map/ppermute | solution.py:209
  105.2 21.5 %collective-permute-start.20 = (bf16[256,768]{1,0:T(8,128)(2,1)S(1)}, bf16[256,768]{1,0:T(8,128)(2,1)S(1)}, u32[]{:S(2)}, u32[]{:S(2)}) collective-permute-start(bf16[256,768]{1,0:T(8,128)(2,1)S(1)} %get-tuple-element.129.own_c_ref), channel_id=1, source_target_pairs={{0,4},{4,0},{1,5},{5,1},{2,6},{6,2},{3,7},{7,3},{8,12},{12,8},{9,1... | collective-permute-start | bytes 1179656 | tf_op jit(solution)/shard_map/ppermute | solution.py:672
  139.8 20.9 %collective-permute-start.35 = (bf16[4,192,384]{2,1,0:T(8,128)(2,1)S(1)}, bf16[4,192,384]{2,1,0:T(8,128)(2,1)S(1)}, u32[]{:S(2)}, u32[]{:S(2)}) collective-permute-start(bf16[4,192,384]{2,1,0:T(8,128)(2,1)S(1)} %pad_maximum_fusion.3), channel_id=1, source_target_pairs={{0,16},{16,0},{1,17},{17,1},{2,18},{18,2},{3,19},{19,3},{4,20},{20... | collective-permute-start | bytes 1769480 | tf_op jit(solution)/shard_map/ppermute | solution.py:938
  169.3 21.8 %collective-permute-start.42 = (bf16[3,2,192,384]{3,2,1,0:T(8,128)(2,1)S(1)}, bf16[3,2,192,384]{3,2,1,0:T(8,128)(2,1)S(1)}, u32[]{:S(2)}, u32[]{:S(2)}) collective-permute-start(bf16[3,2,192,384]{3,2,1,0:T(8,128)(2,1)S(1)} %pad_maximum_fusion.1), channel_id=1, source_target_pairs={{0,16},{16,0},{1,17},{17,1},{2,18},{18,2},{3,19},{19,3},{4,20},{20... | collective-permute-start | bytes 2654216 | tf_op jit(solution)/shard_map/ppermute | solution.py:209
  175.7 29.6 %collective-permute-start.37 = (bf16[256,768]{1,0:T(8,128)(2,1)S(1)}, bf16[256,768]{1,0:T(8,128)(2,1)S(1)}, u32[]{:S(2)}, u32[]{:S(2)}) collective-permute-start(bf16[256,768]{1,0:T(8,128)(2,1)S(1)} %pad_maximum_fusion.5.own_gy_ref), channel_id=1, source_target_pairs={{0,4},{4,0},{1,5},{5,1},{2,6},{6,2},{3,7},{7,3},{8,12},{12,8},{9,1... | collective-permute-start | bytes 1179656 | tf_op jit(solution)/shard_map/ppermute | solution.py:672
  220.9 35.4 %collective-permute-start.47 = (bf16[4,2,192,384]{3,2,1,0:T(8,128)(2,1)}, bf16[4,2,192,384]{3,2,1,0:T(8,128)(2,1)S(1)}, u32[]{:S(2)}, u32[]{:S(2)}) collective-permute-start(bf16[4,2,192,384]{3,2,1,0:T(8,128)(2,1)} %get-tuple-element.176), channel_id=1, source_target_pairs={{0,16},{16,0},{1,17},{17,1},{2,18},{18,2},{3,19},{19,3},{4,20},{20... | collective-permute-start | bytes 3538952 | tf_op jit(solution)/shard_map/ppermute | solution.py:991
  233.2 29.5 %all-to-all-start.2 = ((bf16[8,96,768]{2,1,0:T(8,128)(2,1)}), bf16[8,96,768]{2,1,0:T(8,128)(2,1)}, u32[]{:S(2)}, u32[]{:S(2)}) async-start(bf16[8,96,768]{2,1,0:T(8,128)(2,1)} %fusion.23), calls=%async_computation.2 | async-start | bytes 2359296 | tf_op jit(solution)/shard_map/all_to_all | solution.py:840
  248.6 25.6 %collective-permute-start.50 = (bf16[4,192,384]{2,1,0:T(8,128)(2,1)}, bf16[4,192,384]{2,1,0:T(8,128)(2,1)}, u32[]{:S(2)}, u32[]{:S(2)}) collective-permute-start(bf16[4,192,384]{2,1,0:T(8,128)(2,1)} %get-tuple-element.182), channel_id=1, source_target_pairs={{0,16},{16,0},{1,17},{17,1},{2,18},{18,2},{3,19},{19,3},{4,20},{20... | collective-permute-start | bytes 1769480 | tf_op jit(solution)/shard_map/ppermute | solution.py:232
  295.9 40.7 %collective-permute-start.65 = (bf16[4,2,192,384]{3,2,1,0:T(8,128)(2,1)}, bf16[4,2,192,384]{3,2,1,0:T(8,128)(2,1)S(1)}, u32[]{:S(2)}, u32[]{:S(2)}) collective-permute-start(bf16[4,2,192,384]{3,2,1,0:T(8,128)(2,1)} %get-tuple-element.211), channel_id=1, source_target_pairs={{0,16},{16,0},{1,17},{17,1},{2,18},{18,2},{3,19},{19,3},{4,20},{20... | collective-permute-start | bytes 3538952 | tf_op jit(solution)/shard_map/ppermute | solution.py:991
  304.9 23.0 %collective-permute-start.62 = (bf16[2,192,384]{2,1,0:T(8,128)(2,1)S(1)}, bf16[2,192,384]{2,1,0:T(8,128)(2,1)S(1)}, u32[]{:S(2)}, u32[]{:S(2)}) collective-permute-start(bf16[2,192,384]{2,1,0:T(8,128)(2,1)S(1)} %get-tuple-element.276), channel_id=1, source_target_pairs={{2,0},{3,1},{0,2},{1,3},{6,4},{7,5},{4,6},{5,7},{10,8},{11,9},{8,1... | collective-permute-start | bytes 884744 | tf_op jit(solution)/shard_map/ppermute | solution.py:70
  341.0 22.4 %collective-permute-start.68 = (bf16[2,192,384]{2,1,0:T(8,128)(2,1)S(1)}, bf16[2,192,384]{2,1,0:T(8,128)(2,1)S(1)}, u32[]{:S(2)}, u32[]{:S(2)}) collective-permute-start(bf16[2,192,384]{2,1,0:T(8,128)(2,1)S(1)} %get-tuple-element.273), channel_id=1, source_target_pairs={{2,0},{3,1},{0,2},{1,3},{6,4},{7,5},{4,6},{5,7},{10,8},{11,9},{8,1... | collective-permute-start | bytes 884744 | tf_op jit(solution)/shard_map/ppermute | solution.py:70
  341.0 22.6 %collective-permute-start.63 = (bf16[256,768]{1,0:T(8,128)(2,1)S(1)}, bf16[256,768]{1,0:T(8,128)(2,1)S(1)}, u32[]{:S(2)}, u32[]{:S(2)}) collective-permute-start(bf16[256,768]{1,0:T(8,128)(2,1)S(1)} %get-tuple-element.207), channel_id=1, source_target_pairs={{0,4},{4,0},{1,5},{5,1},{2,6},{6,2},{3,7},{7,3},{8,12},{12,8},{9,1... | collective-permute-start | bytes 1179656 | tf_op jit(solution)/shard_map/ppermute | solution.py:672
  341.0 25.1 %collective-permute-start.69 = (bf16[4,192,384]{2,1,0:T(8,128)(2,1)S(1)}, bf16[4,192,384]{2,1,0:T(8,128)(2,1)S(1)}, u32[]{:S(2)}, u32[]{:S(2)}) collective-permute-start(bf16[4,192,384]{2,1,0:T(8,128)(2,1)S(1)} %copy-done.63), channel_id=1, source_target_pairs={{0,16},{16,0},{1,17},{17,1},{2,18},{18,2},{3,19},{19,3},{4,20},{20... | collective-permute-start | bytes 1769480 | tf_op jit(solution)/shard_map/ppermute | solution.py:232
  378.9 21.1 %all-to-all-start.3 = ((bf16[8,192,384]{2,1,0:T(8,128)(2,1)}), bf16[8,192,384]{2,1,0:T(8,128)(2,1)}, u32[]{:S(2)}, u32[]{:S(2)}) async-start(bf16[8,192,384]{2,1,0:T(8,128)(2,1)} %bitcast.199), calls=%async_computation.3 | async-start | bytes 2359296 | tf_op jit(solution)/shard_map/all_to_all | solution.py:840
  409.5 19.8 %collective-permute-start.82 = (f32[2,3,768]{2,0,1:T(2,128)S(1)}, f32[2,3,768]{2,0,1:T(2,128)}, u32[]{:S(2)}, u32[]{:S(2)}) collective-permute-start(f32[2,3,768]{2,0,1:T(2,128)S(1)} %get-tuple-element.298), channel_id=1, source_target_pairs={{2,0},{3,1},{0,2},{1,3},{6,4},{7,5},{4,6},{5,7},{10,8},{11,9},{8,1... | collective-permute-start | bytes 55304 | tf_op jit(solution)/shard_map/ppermute | solution.py:70
  415.7 24.8 %all-to-all-start.4 = ((bf16[4,6,96,192]{3,2,1,0:T(8,128)(2,1)}), bf16[4,6,96,192]{3,2,1,0:T(8,128)(2,1)S(1)}, u32[]{:S(2)}, u32[]{:S(2)}) async-start(bf16[4,6,96,192]{3,2,1,0:T(8,128)(2,1)} %shard_map.173), calls=%async_computation.4 | async-start | bytes 2359296 | tf_op jit(solution)/shard_map/all_to_all | solution.py:174
  441.7 29.0 %all-to-all-start.5 = ((bf16[8,192,384]{2,1,0:T(8,128)(2,1)}), bf16[8,192,384]{2,1,0:T(8,128)(2,1)}, u32[]{:S(2)}, u32[]{:S(2)}) async-start(bf16[8,192,384]{2,1,0:T(8,128)(2,1)} %bitcast.198), calls=%async_computation.5 | async-start | bytes 2359296 | tf_op jit(solution)/shard_map/all_to_all | solution.py:840
  459.3 29.2 %collective-permute-start.87 = (bf16[2,96,384]{2,1,0:T(8,128)(2,1)S(1)}, bf16[2,96,384]{2,1,0:T(8,128)(2,1)}, u32[]{:S(2)}, u32[]{:S(2)}) collective-permute-start(bf16[2,96,384]{2,1,0:T(8,128)(2,1)S(1)} %constant_dynamic-slice_fusion.3), channel_id=1, source_target_pairs={{0,4},{4,0},{1,5},{5,1},{2,6},{6,2},{3,7},{7,3},{8,12},{12,8},{9,1... | collective-permute-start | bytes 442376 | tf_op jit(solution)/shard_map/ppermute | solution.py:132
  482.6 26.5 %all-to-all-start.6 = ((bf16[8,96,768]{2,1,0:T(8,128)(2,1)}), bf16[8,96,768]{2,1,0:T(8,128)(2,1)}, u32[]{:S(2)}, u32[]{:S(2)}) async-start(bf16[8,96,768]{2,1,0:T(8,128)(2,1)} %bitcast.200), calls=%async_computation.6 | async-start | bytes 2359296 | tf_op jit(solution)/shard_map/all_to_all | solution.py:840
  (135 other events, 1197.3 us)

commit v13 on v12

--- a/solution.py
+++ b/solution.py
@@ -1070,9 +1070,11 @@
         attn_low = attn_half.astype(bf16)
         attn_sums = [rotate(attn_low[step], "ctx", -step) for step in (1, 3, 2)]
         wide_low = jnp.concatenate([parts[1][1], mlp_part]).astype(bf16)
-        wide_low = after(wide_low, attn_half, grad_hidden)
+        wide_low = after(wide_low, attn_half)
         wide_slots = slot_exchange(jnp.repeat(wide_low, 2, axis=0))
-        wide_slots, attn_sums = lax.optimization_barrier((wide_slots, attn_sums))
+        wide_slots, grad_hidden, attn_sums = lax.optimization_barrier(
+            (wide_slots, grad_hidden, attn_sums)
+        )
         x_wide, gram_blocks = slot_gram(place, wide_slots, moment_slots)
         vec_sums = sum_group(sum_vectors(after(vec_terms, gram_blocks)))
         attn_part = attn_half[0] + sum(block.astype(f32) for block in attn_sums)

time: 526 us -> 525 us (level)
    ppermute x30, waiting for transfers between devices: 89.5 us -> 80.9 us  [rotate(): lax.ppermute(block, axis, [((i + step) % size, i) for i in range(size)])]
    ppermute x8, waiting for transfers between devices: 32.4 us -> 40 us  [group_sum(): return (mine, lax.ppermute(mine.astype(bf16), 'jx', SWAP))]
    unnamed x140 -> x144, local copies, waits for them, and re-layouts: 22.8 us -> 20.6 us
  transfers between devices with their start and end apart: 95 -> 95, of which waited for: 41 -> 38; matrix products, arithmetic and copies ran while one was open for 6% -> 6% of each run, Pallas kernels for 14% -> 15%
where the time goes in v13:
time: 525 us; the launch traced here: 515 us
  waiting for transfers between devices  204 us (39%)
  starting transfers between devices  154 us (29%)
  Pallas kernels  95.5 us (18%)
  local copies, waits for them, and re-layouts  31.5 us (6%)
  other arithmetic  27.3 us (5%)
    pallas_call x24, Pallas kernels, call(): pl.pallas_call(kernel, out_shape=[jax.ShapeDtypeStruct(shape, kind) for s...  95.5 us
    ppermute x30, waiting for transfers between devices, rotate(): lax.ppermute(block, axis, [((i + step) % size, i) for i in range(size)])  80.9 us
    ppermute x30, starting transfers between devices, rotate(): lax.ppermute(block, axis, [((i + step) % size, i) for i in range(size)])  51.5 us
    ppermute x8, waiting for transfers between devices, group_sum(): return (mine, lax.ppermute(mine.astype(bf16), 'jx', SWAP))  40 us
    ppermute x6, starting transfers between devices, core_shift(): lax.ppermute(block, ('jc', 'ctx'), [((i + step) % size, i) for i in range...  21 us
    unnamed x144, local copies, waits for them, and re-layouts  20.6 us
    all_to_all x4, waiting for transfers between devices, slot_exchange(): return lax.all_to_all(blocks, DP, split_axis=0, concat_axis=0, tiled=True)  20.4 us
    ppermute x5, starting transfers between devices, pair_join(): other = lax.ppermute(block, axis, SWAP)  17.3 us
  transfers between devices with their start and end apart: 95, of which 38 were waited for; matrix products, arithmetic and copies ran while one was open for 6% of the time, Pallas kernels for 15%

profile of v13, /device:TPU:0, one launch (start us, length us, event | category | flops | bytes accessed | tf_op | source)
XLA Modules:
  0.0 514.8 jit_solution(15643314493305620932)
XLA Ops:
  20.7 10.7 %collective-permute-start.6 = (bf16[4,2,3,192]{3,1,2,0:T(2,128)(2,1)S(1)}, bf16[4,2,3,192]{3,1,2,0:T(2,128)(2,1)S(1)}, u32[]{:S(2)}, u32[]{:S(2)}) collective-permute-start(bf16[4,2,3,192]{3,1,2,0:T(2,128)(2,1)S(1)} %pad_maximum_fusion.14), channel_id=1, source_target_pairs={{0,8},{8,0},{1,9},{9,1},{2,10},{10,2},{3,11},{11,3},{4,12},{12,4},... | collective-permute-start | bytes 27656 | tf_op jit(solution)/shard_map/ppermute | solution.py:74
  35.8 9.7 %collective-permute-start.11 = (bf16[192,384]{1,0:T(8,128)(2,1)S(1)}, bf16[192,384]{1,0:T(8,128)(2,1)S(1)}, u32[]{:S(2)}, u32[]{:S(2)}) collective-permute-start(bf16[192,384]{1,0:T(8,128)(2,1)S(1)} %shard_map.153.refs_0_), channel_id=1, source_target_pairs={{1,0},{2,1},{3,2},{0,3},{5,4},{6,5},{7,6},{4,7},{9,8},{10,9},{11,1... | collective-permute-start | bytes 442376 | tf_op jit(solution)/shard_map/ppermute | solution.py:70
  61.2 8.8 %all-to-all-done.1.blocks_ref = bf16[4,5,192,96]{3,2,1,0:T(8,128)(2,1)S(1)} async-done(((bf16[4,5,192,96]{3,2,1,0:T(8,128)(2,1)}), bf16[4,5,192,96]{3,2,1,0:T(8,128)(2,1)S(1)}, u32[]{:S(2)}, u32[]{:S(2)}) %all-to-all-start.1) | async-done | bytes 737312 | tf_op jit(solution)/shard_map/all_to_all | solution.py:174
  78.1 6.5 %shard_map.155 = (bf16[768,768]{1,0:T(8,128)(2,1)}, bf16[512,576]{1,0:T(8,128)(2,1)}, f32[512,128]{1,0:T(8,128)S(1)}, bf16[512,192]{1,0:T(8,128)(2,1)S(1)}, f32[...) custom-call(s32[3]{0:T(128)S(1)} %pad_add_fusion.place_ref, f32[8,512]{1,0:T(8,128)S(1)} %pad.13.row_ref, ...), custom_call_target="tpu_custom_call" | custom-call | tf_op jit(solution)/shard_map/pallas_call | solution.py:320
  84.7 6.4 %collective-permute-done.21.refs_1_ = bf16[2,192,384]{2,1,0:T(8,128)(2,1)S(1)} collective-permute-done((bf16[2,192,384]{2,1,0:T(8,128)(2,1)S(1)}, bf16[2,192,384]{2,1,0:T(8,128)(2,1)S(1)}, u32[]{:S(2)}, u32[]{:S(2)}) %collective-permute-start.21) | collective-permute-done | bytes 294944 | tf_op jit(solution)/shard_map/ppermute | solution.py:70
  94.2 8.3 %collective-permute-done.19.refs_1_ = bf16[256,768]{1,0:T(8,128)(2,1)S(1)} collective-permute-done((bf16[256,768]{1,0:T(8,128)(2,1)S(1)}, bf16[256,768]{1,0:T(8,128)(2,1)S(1)}, u32[]{:S(2)}, u32[]{:S(2)}) %collective-permute-start.19) | collective-permute-done | bytes 393248 | tf_op jit(solution)/shard_map/ppermute | solution.py:677
  118.6 8.1 %collective-permute-done.25.refs_2_ = bf16[192,384]{1,0:T(8,128)(2,1)S(1)} collective-permute-done((bf16[192,384]{1,0:T(8,128)(2,1)S(1)}, bf16[192,384]{1,0:T(8,128)(2,1)S(1)}, u32[]{:S(2)}, u32[]{:S(2)}) %collective-permute-start.25) | collective-permute-done | bytes 147488 | tf_op jit(solution)/shard_map/ppermute | solution.py:70
  174.5 11.7 %collective-permute-done.41.refs_2_ = bf16[2,192,384]{2,1,0:T(8,128)(2,1)S(1)} collective-permute-done((bf16[2,192,384]{2,1,0:T(8,128)(2,1)S(1)}, bf16[2,192,384]{2,1,0:T(8,128)(2,1)S(1)}, u32[]{:S(2)}, u32[]{:S(2)}) %collective-permute-start.41) | collective-permute-done | bytes 294944 | tf_op jit(solution)/shard_map/ppermute | solution.py:70
  207.3 7.6 %shard_map.164 = (f32[256,768]{1,0:T(8,128)}, bf16[256,768]{1,0:T(8,128)(2,1)S(1)}, f32[8,768]{1,0:T(8,128)S(1)}, f32[4,2,192,384]{3,2,1,0:T(8,128)}, bf16[4,2,192,384]{3,2,1,0:T(8,128)(2,1)}) custom-call(s32[3]{0:T(128)S(1)} %pad_add_fusion.place_ref, bf16[256,768]{1,0:T(8,128)(2,1)S(1)} %pad_maximum_fusion.5.own_gy_ref, ...), custom_call_target="tpu_custom_call" | custom-call | tf_op jit(solution)/shard_map/pallas_call | solution.py:320
  223.4 6.5 %collective-permute-done.45.recv_ref = bf16[256,768]{1,0:T(8,128)(2,1)S(1)} collective-permute-done((bf16[256,768]{1,0:T(8,128)(2,1)S(1)}, bf16[256,768]{1,0:T(8,128)(2,1)S(1)}, u32[]{:S(2)}, u32[]{:S(2)}) %collective-permute-start.45) | collective-permute-done | bytes 393248 | tf_op jit(solution)/shard_map/ppermute | solution.py:677
  239.2 8.4 %shard_map.166 = (f32[256,768]{1,0:T(8,128)}, bf16[256,768]{1,0:T(8,128)(2,1)S(1)}, f32[8,576]{1,0:T(8,128)S(1)}, f32[4,192,384]{2,1,0:T(8,128)}, bf16[4,192,384]{2,1,0:T(8,128)(2,1)}) custom-call(s32[3]{0:T(128)S(1)} %pad_add_fusion.place_ref, f32[8,512]{1,0:T(8,128)S(1)} %pad.13.row_ref, f32[512,128]{1,0:T(8,128)S(1)} %pad.14.column_ref, ...), custom_call_target="tpu_custom_call" | custom-call | tf_op jit(solution)/shard_map/pallas_call | solution.py:320
  249.6 6.8 %collective-permute-done.47 = bf16[4,2,192,384]{3,2,1,0:T(8,128)(2,1)} collective-permute-done((bf16[4,2,192,384]{3,2,1,0:T(8,128)(2,1)}, bf16[4,2,192,384]{3,2,1,0:T(8,128)(2,1)}, u32[]{:S(2)}, u32[]{:S(2)}) %collective-permute-start.47) | collective-permute-done | bytes 1179680 | tf_op jit(solution)/shard_map/ppermute | solution.py:991
  256.4 6.2 %all-to-all-done.2 = bf16[8,96,768]{2,1,0:T(8,128)(2,1)S(1)} async-done(((bf16[8,96,768]{2,1,0:T(8,128)(2,1)}), bf16[8,96,768]{2,1,0:T(8,128)(2,1)S(1)}, u32[]{:S(2)}, u32[]{:S(2)}) %all-to-all-start.2) | async-done | bytes 1179680 | tf_op jit(solution)/shard_map/all_to_all | solution.py:840
  265.7 8.4 %collective-permute-done.50 = bf16[4,192,384]{2,1,0:T(8,128)(2,1)S(1)} collective-permute-done((bf16[4,192,384]{2,1,0:T(8,128)(2,1)}, bf16[4,192,384]{2,1,0:T(8,128)(2,1)S(1)}, u32[]{:S(2)}, u32[]{:S(2)}) %collective-permute-start.50) | collective-permute-done | bytes 589856 | tf_op jit(solution)/shard_map/ppermute | solution.py:232
  282.8 7.4 %shard_map.168 = (f32[256,768]{1,0:T(8,128)}, bf16[256,768]{1,0:T(8,128)(2,1)S(1)}, f32[8,768]{1,0:T(8,128)S(1)}, f32[4,2,192,384]{3,2,1,0:T(8,128)}, bf16[4,2,192,384]{3,2,1,0:T(8,128)(2,1)}) custom-call(s32[3]{0:T(128)S(1)} %pad_add_fusion.place_ref, bf16[256,768]{1,0:T(8,128)(2,1)S(1)} %get-tuple-element.184.own_gy_ref, ...), custom_call_target="tpu_custom_call" | custom-call | tf_op jit(solution)/shard_map/pallas_call | solution.py:320
  318.1 9.9 %collective-permute-done.62 = bf16[2,192,384]{2,1,0:T(8,128)(2,1)S(1)} collective-permute-done((bf16[2,192,384]{2,1,0:T(8,128)(2,1)S(1)}, bf16[2,192,384]{2,1,0:T(8,128)(2,1)S(1)}, u32[]{:S(2)}, u32[]{:S(2)}) %collective-permute-start.62) | collective-permute-done | bytes 294944 | tf_op jit(solution)/shard_map/ppermute | solution.py:70
  328.1 8.5 %shard_map.170 = (f32[256,768]{1,0:T(8,128)}, bf16[256,768]{1,0:T(8,128)(2,1)S(1)}, f32[8,576]{1,0:T(8,128)S(1)}, f32[4,192,384]{2,1,0:T(8,128)}, bf16[4,192,384]{2,1,0:T(8,128)(2,1)}) custom-call(s32[3]{0:T(128)S(1)} %pad_add_fusion.place_ref, f32[8,512]{1,0:T(8,128)S(1)} %pad.13.row_ref, f32[512,128]{1,0:T(8,128)S(1)} %pad.14.column_ref, ...), custom_call_target="tpu_custom_call" | custom-call | tf_op jit(solution)/shard_map/pallas_call | solution.py:320
  341.4 7.5 %collective-permute-done.64 = bf16[2,192,384]{2,1,0:T(8,128)(2,1)S(1)} collective-permute-done((bf16[2,192,384]{2,1,0:T(8,128)(2,1)S(1)}, bf16[2,192,384]{2,1,0:T(8,128)(2,1)S(1)}, u32[]{:S(2)}, u32[]{:S(2)}) %collective-permute-start.64) | collective-permute-done | bytes 294944 | tf_op jit(solution)/shard_map/ppermute | solution.py:70
  351.8 11.7 %collective-permute-done.66 = bf16[2,192,384]{2,1,0:T(8,128)(2,1)S(1)} collective-permute-done((bf16[2,192,384]{2,1,0:T(8,128)(2,1)S(1)}, bf16[2,192,384]{2,1,0:T(8,128)(2,1)S(1)}, u32[]{:S(2)}, u32[]{:S(2)}) %collective-permute-start.66) | collective-permute-done | bytes 294944 | tf_op jit(solution)/shard_map/ppermute | solution.py:70
  380.2 15.6 %collective-permute-done.69.recv_ref = bf16[256,768]{1,0:T(8,128)(2,1)S(1)} collective-permute-done((bf16[256,768]{1,0:T(8,128)(2,1)}, bf16[256,768]{1,0:T(8,128)(2,1)S(1)}, u32[]{:S(2)}, u32[]{:S(2)}) %collective-permute-start.69) | collective-permute-done | bytes 393248 | tf_op jit(solution)/shard_map/ppermute | solution.py:677
  446.4 6.6 %collective-permute-start.76 = (bf16[192,768]{1,0:T(8,128)(2,1)S(1)}, bf16[192,768]{1,0:T(8,128)(2,1)S(1)}, u32[]{:S(2)}, u32[]{:S(2)}) collective-permute-start(bf16[192,768]{1,0:T(8,128)(2,1)S(1)} %fusion.10.gram0_ref), channel_id=1, source_target_pairs={{1,0},{2,1},{3,2},{0,3},{9,8},{10,9},{11,10},{8,11},{17,16},{18,17... | collective-permute-start | bytes 884744 | tf_op jit(solution)/shard_map/ppermute | solution.py:845
  463.6 6.2 %collective-permute-done.78.gram2_ref = bf16[192,768]{1,0:T(8,128)(2,1)S(1)} collective-permute-done((bf16[192,768]{1,0:T(8,128)(2,1)S(1)}, bf16[192,768]{1,0:T(8,128)(2,1)S(1)}, u32[]{:S(2)}, u32[]{:S(2)}) %collective-permute-start.78) | collective-permute-done | bytes 294944 | tf_op jit(solution)/shard_map/ppermute | solution.py:845
  469.8 11.9 %shard_map.175 = bf16[768,768]{1,0:T(8,128)(2,1)} custom-call(s32[3]{0:T(128)S(1)} %pad_add_fusion.place_ref, bf16[768,768]{1,0:T(8,128)(2,1)} %copy-done.17, bf16[192,768]{1,0:T(8,128)(2,1)S(1)} %fusion.10.gram0_ref, bf16[192,768]{1,0:T(8,128)(2,1)S(1)} %collective-permute-done.76.gram1_ref, bf16[192,768]{1,0:T(8,128)(2,1)S(1)} %collective-permute-done.78.gram2_ref, ...), custom_call_target="tpu_custom_call" | custom-call | tf_op jit(solution)/shard_map/pallas_call | solution.py:320
  493.9 14.2 %all-to-all-done.6 = bf16[8,96,768]{2,1,0:T(8,128)(2,1)} async-done(((bf16[8,96,768]{2,1,0:T(8,128)(2,1)}), bf16[8,96,768]{2,1,0:T(8,128)(2,1)}, u32[]{:S(2)}, u32[]{:S(2)}) %all-to-all-start.6) | async-done | bytes 1179680 | tf_op jit(solution)/shard_map/all_to_all | solution.py:840
  (448 shorter events, 298.6 us)
Async XLA Ops:
  10.9 24.2 %all-to-all-start = ((bf16[4,1,192,96]{3,2,1,0:T(8,128)(2,1)}), bf16[4,1,192,96]{3,2,1,0:T(8,128)(2,1)S(1)}, u32[]{:S(2)}, u32[]{:S(2)}) async-start(bf16[4,1,192,96]{3,2,1,0:T(8,128)(2,1)} %shard_map.152), calls=%async_computation | async-start | bytes 393216 | tf_op jit(solution)/shard_map/all_to_all | solution.py:174
  47.2 23.9 %collective-permute-start.14 = (bf16[192,384]{1,0:T(8,128)(2,1)S(1)}, bf16[192,384]{1,0:T(8,128)(2,1)}, u32[]{:S(2)}, u32[]{:S(2)}) collective-permute-start(bf16[192,384]{1,0:T(8,128)(2,1)S(1)} %shard_map.153.refs_0_), channel_id=1, source_target_pairs={{0,16},{16,0},{1,17},{17,1},{2,18},{18,2},{3,19},{19,3},{4,20},{20... | collective-permute-start | bytes 442376 | tf_op jit(solution)/shard_map/ppermute | solution.py:196
  71.1 20.0 %collective-permute-start.21 = (bf16[2,192,384]{2,1,0:T(8,128)(2,1)S(1)}, bf16[2,192,384]{2,1,0:T(8,128)(2,1)S(1)}, u32[]{:S(2)}, u32[]{:S(2)}) collective-permute-start(bf16[2,192,384]{2,1,0:T(8,128)(2,1)S(1)} %pad_maximum_fusion.7.refs_0_), channel_id=1, source_target_pairs={{1,0},{2,1},{3,2},{0,3},{5,4},{6,5},{7,6},{4,7},{9,8},{10,9},{11,1... | collective-permute-start | bytes 884744 | tf_op jit(solution)/shard_map/ppermute | solution.py:70
  91.2 20.7 %collective-permute-start.27 = (bf16[3,2,192,384]{3,2,1,0:T(8,128)(2,1)S(1)}, bf16[3,2,192,384]{3,2,1,0:T(8,128)(2,1)S(1)}, u32[]{:S(2)}, u32[]{:S(2)}) collective-permute-start(bf16[3,2,192,384]{3,2,1,0:T(8,128)(2,1)S(1)} %pad_maximum_fusion), channel_id=1, source_target_pairs={{0,16},{16,0},{1,17},{17,1},{2,18},{18,2},{3,19},{19,3},{4,20},{20... | collective-permute-start | bytes 2654216 | tf_op jit(solution)/shard_map/ppermute | solution.py:209
  105.2 21.5 %collective-permute-start.20 = (bf16[256,768]{1,0:T(8,128)(2,1)S(1)}, bf16[256,768]{1,0:T(8,128)(2,1)S(1)}, u32[]{:S(2)}, u32[]{:S(2)}) collective-permute-start(bf16[256,768]{1,0:T(8,128)(2,1)S(1)} %get-tuple-element.130.own_c_ref), channel_id=1, source_target_pairs={{0,4},{4,0},{1,5},{5,1},{2,6},{6,2},{3,7},{7,3},{8,12},{12,8},{9,1... | collective-permute-start | bytes 1179656 | tf_op jit(solution)/shard_map/ppermute | solution.py:672
  139.8 20.9 %collective-permute-start.35 = (bf16[4,192,384]{2,1,0:T(8,128)(2,1)S(1)}, bf16[4,192,384]{2,1,0:T(8,128)(2,1)S(1)}, u32[]{:S(2)}, u32[]{:S(2)}) collective-permute-start(bf16[4,192,384]{2,1,0:T(8,128)(2,1)S(1)} %pad_maximum_fusion.3), channel_id=1, source_target_pairs={{0,16},{16,0},{1,17},{17,1},{2,18},{18,2},{3,19},{19,3},{4,20},{20... | collective-permute-start | bytes 1769480 | tf_op jit(solution)/shard_map/ppermute | solution.py:938
  169.3 21.8 %collective-permute-start.42 = (bf16[3,2,192,384]{3,2,1,0:T(8,128)(2,1)S(1)}, bf16[3,2,192,384]{3,2,1,0:T(8,128)(2,1)S(1)}, u32[]{:S(2)}, u32[]{:S(2)}) collective-permute-start(bf16[3,2,192,384]{3,2,1,0:T(8,128)(2,1)S(1)} %pad_maximum_fusion.1), channel_id=1, source_target_pairs={{0,16},{16,0},{1,17},{17,1},{2,18},{18,2},{3,19},{19,3},{4,20},{20... | collective-permute-start | bytes 2654216 | tf_op jit(solution)/shard_map/ppermute | solution.py:209
  174.4 30.9 %collective-permute-start.37 = (bf16[256,768]{1,0:T(8,128)(2,1)S(1)}, bf16[256,768]{1,0:T(8,128)(2,1)S(1)}, u32[]{:S(2)}, u32[]{:S(2)}) collective-permute-start(bf16[256,768]{1,0:T(8,128)(2,1)S(1)} %pad_maximum_fusion.5.own_gy_ref), channel_id=1, source_target_pairs={{0,4},{4,0},{1,5},{5,1},{2,6},{6,2},{3,7},{7,3},{8,12},{12,8},{9,1... | collective-permute-start | bytes 1179656 | tf_op jit(solution)/shard_map/ppermute | solution.py:672
  220.9 35.5 %collective-permute-start.47 = (bf16[4,2,192,384]{3,2,1,0:T(8,128)(2,1)}, bf16[4,2,192,384]{3,2,1,0:T(8,128)(2,1)}, u32[]{:S(2)}, u32[]{:S(2)}) collective-permute-start(bf16[4,2,192,384]{3,2,1,0:T(8,128)(2,1)} %get-tuple-element.177), channel_id=1, source_target_pairs={{0,16},{16,0},{1,17},{17,1},{2,18},{18,2},{3,19},{19,3},{4,20},{20... | collective-permute-start | bytes 3538952 | tf_op jit(solution)/shard_map/ppermute | solution.py:991
  233.2 29.4 %all-to-all-start.2 = ((bf16[8,96,768]{2,1,0:T(8,128)(2,1)}), bf16[8,96,768]{2,1,0:T(8,128)(2,1)S(1)}, u32[]{:S(2)}, u32[]{:S(2)}) async-start(bf16[8,96,768]{2,1,0:T(8,128)(2,1)} %fusion.23), calls=%async_computation.2 | async-start | bytes 2359296 | tf_op jit(solution)/shard_map/all_to_all | solution.py:840
  247.9 26.2 %collective-permute-start.50 = (bf16[4,192,384]{2,1,0:T(8,128)(2,1)}, bf16[4,192,384]{2,1,0:T(8,128)(2,1)S(1)}, u32[]{:S(2)}, u32[]{:S(2)}) collective-permute-start(bf16[4,192,384]{2,1,0:T(8,128)(2,1)} %get-tuple-element.183), channel_id=1, source_target_pairs={{0,16},{16,0},{1,17},{17,1},{2,18},{18,2},{3,19},{19,3},{4,20},{20... | collective-permute-start | bytes 1769480 | tf_op jit(solution)/shard_map/ppermute | solution.py:232
  294.7 41.9 %collective-permute-start.63 = (bf16[4,2,192,384]{3,2,1,0:T(8,128)(2,1)}, bf16[4,2,192,384]{3,2,1,0:T(8,128)(2,1)S(1)}, u32[]{:S(2)}, u32[]{:S(2)}) collective-permute-start(bf16[4,2,192,384]{3,2,1,0:T(8,128)(2,1)} %get-tuple-element.203), channel_id=1, source_target_pairs={{0,16},{16,0},{1,17},{17,1},{2,18},{18,2},{3,19},{19,3},{4,20},{20... | collective-permute-start | bytes 3538952 | tf_op jit(solution)/shard_map/ppermute | solution.py:991
  305.0 23.0 %collective-permute-start.62 = (bf16[2,192,384]{2,1,0:T(8,128)(2,1)S(1)}, bf16[2,192,384]{2,1,0:T(8,128)(2,1)S(1)}, u32[]{:S(2)}, u32[]{:S(2)}) collective-permute-start(bf16[2,192,384]{2,1,0:T(8,128)(2,1)S(1)} %get-tuple-element.278), channel_id=1, source_target_pairs={{2,0},{3,1},{0,2},{1,3},{6,4},{7,5},{4,6},{5,7},{10,8},{11,9},{8,1... | collective-permute-start | bytes 884744 | tf_op jit(solution)/shard_map/ppermute | solution.py:70
  341.0 22.4 %collective-permute-start.66 = (bf16[2,192,384]{2,1,0:T(8,128)(2,1)S(1)}, bf16[2,192,384]{2,1,0:T(8,128)(2,1)S(1)}, u32[]{:S(2)}, u32[]{:S(2)}) collective-permute-start(bf16[2,192,384]{2,1,0:T(8,128)(2,1)S(1)} %get-tuple-element.275), channel_id=1, source_target_pairs={{2,0},{3,1},{0,2},{1,3},{6,4},{7,5},{4,6},{5,7},{10,8},{11,9},{8,1... | collective-permute-start | bytes 884744 | tf_op jit(solution)/shard_map/ppermute | solution.py:70
  341.0 22.7 %collective-permute-start.67 = (bf16[4,192,384]{2,1,0:T(8,128)(2,1)S(1)}, bf16[4,192,384]{2,1,0:T(8,128)(2,1)S(1)}, u32[]{:S(2)}, u32[]{:S(2)}) collective-permute-start(bf16[4,192,384]{2,1,0:T(8,128)(2,1)S(1)} %copy-done.65), channel_id=1, source_target_pairs={{0,16},{16,0},{1,17},{17,1},{2,18},{18,2},{3,19},{19,3},{4,20},{20... | collective-permute-start | bytes 1769480 | tf_op jit(solution)/shard_map/ppermute | solution.py:232
  341.4 30.2 %collective-permute-start.68 = (bf16[256,768]{1,0:T(8,128)(2,1)S(1)}, bf16[256,768]{1,0:T(8,128)(2,1)S(1)}, u32[]{:S(2)}, u32[]{:S(2)}) collective-permute-start(bf16[256,768]{1,0:T(8,128)(2,1)S(1)} %get-tuple-element.209), channel_id=1, source_target_pairs={{0,4},{4,0},{1,5},{5,1},{2,6},{6,2},{3,7},{7,3},{8,12},{12,8},{9,1... | collective-permute-start | bytes 1179656 | tf_op jit(solution)/shard_map/ppermute | solution.py:672
  367.4 31.6 %all-to-all-start.3 = ((bf16[8,192,384]{2,1,0:T(8,128)(2,1)}), bf16[8,192,384]{2,1,0:T(8,128)(2,1)}, u32[]{:S(2)}, u32[]{:S(2)}) async-start(bf16[8,192,384]{2,1,0:T(8,128)(2,1)} %bitcast.200), calls=%async_computation.3 | async-start | bytes 2359296 | tf_op jit(solution)/shard_map/all_to_all | solution.py:840
  373.9 21.9 %collective-permute-start.69 = (bf16[256,768]{1,0:T(8,128)(2,1)}, bf16[256,768]{1,0:T(8,128)(2,1)S(1)}, u32[]{:S(2)}, u32[]{:S(2)}) collective-permute-start(bf16[256,768]{1,0:T(8,128)(2,1)} %get-tuple-element.251), channel_id=1, source_target_pairs={{0,8},{8,0},{1,9},{9,1},{2,10},{10,2},{3,11},{11,3},{4,12},{12,4},... | collective-permute-start | bytes 1179656 | tf_op jit(solution)/shard_map/ppermute | solution.py:677
  376.4 22.6 %collective-permute-start.70 = (bf16[192,384]{1,0:T(8,128)(2,1)S(1)}, bf16[192,384]{1,0:T(8,128)(2,1)S(1)}, u32[]{:S(2)}, u32[]{:S(2)}) collective-permute-start(bf16[192,384]{1,0:T(8,128)(2,1)S(1)} %get-tuple-element.284), channel_id=1, source_target_pairs={{3,0},{0,1},{1,2},{2,3},{7,4},{4,5},{5,6},{6,7},{11,8},{8,9},{9,10... | collective-permute-start | bytes 442376 | tf_op jit(solution)/shard_map/ppermute | solution.py:70
  376.4 22.5 %collective-permute-start.71 = (bf16[192,384]{1,0:T(8,128)(2,1)S(1)}, bf16[192,384]{1,0:T(8,128)(2,1)S(1)}, u32[]{:S(2)}, u32[]{:S(2)}) collective-permute-start(bf16[192,384]{1,0:T(8,128)(2,1)S(1)} %get-tuple-element.283), channel_id=1, source_target_pairs={{1,0},{2,1},{3,2},{0,3},{5,4},{6,5},{7,6},{4,7},{9,8},{10,9},{11,1... | collective-permute-start | bytes 442376 | tf_op jit(solution)/shard_map/ppermute | solution.py:70
  414.8 24.8 %all-to-all-start.4 = ((bf16[4,6,96,192]{3,2,1,0:T(8,128)(2,1)}), bf16[4,6,96,192]{3,2,1,0:T(8,128)(2,1)S(1)}, u32[]{:S(2)}, u32[]{:S(2)}) async-start(bf16[4,6,96,192]{3,2,1,0:T(8,128)(2,1)} %shard_map.173), calls=%async_computation.4 | async-start | bytes 2359296 | tf_op jit(solution)/shard_map/all_to_all | solution.py:174
  440.8 29.0 %all-to-all-start.5 = ((bf16[8,192,384]{2,1,0:T(8,128)(2,1)}), bf16[8,192,384]{2,1,0:T(8,128)(2,1)}, u32[]{:S(2)}, u32[]{:S(2)}) async-start(bf16[8,192,384]{2,1,0:T(8,128)(2,1)} %bitcast.201), calls=%async_computation.5 | async-start | bytes 2359296 | tf_op jit(solution)/shard_map/all_to_all | solution.py:840
  458.4 29.2 %collective-permute-start.87 = (bf16[2,96,384]{2,1,0:T(8,128)(2,1)S(1)}, bf16[2,96,384]{2,1,0:T(8,128)(2,1)S(1)}, u32[]{:S(2)}, u32[]{:S(2)}) collective-permute-start(bf16[2,96,384]{2,1,0:T(8,128)(2,1)S(1)} %constant_dynamic-slice_fusion.3), channel_id=1, source_target_pairs={{0,4},{4,0},{1,5},{5,1},{2,6},{6,2},{3,7},{7,3},{8,12},{12,8},{9,1... | collective-permute-start | bytes 442376 | tf_op jit(solution)/shard_map/ppermute | solution.py:132
  481.7 26.5 %all-to-all-start.6 = ((bf16[8,96,768]{2,1,0:T(8,128)(2,1)}), bf16[8,96,768]{2,1,0:T(8,128)(2,1)}, u32[]{:S(2)}, u32[]{:S(2)}) async-start(bf16[8,96,768]{2,1,0:T(8,128)(2,1)} %bitcast.202), calls=%async_computation.6 | async-start | bytes 2359296 | tf_op jit(solution)/shard_map/all_to_all | solution.py:840
  (137 other events, 1243.8 us)
